TPU v7x, 128 devices: a whole 4x4x4 slice. The times are simulated.
128 devices in a mesh: rep: 16 (over y, z_lo, core), fsdp: 8 (over z_hi, x).
Axes of the slice: x: 4, y: 4, z: 4 (z_hi: 2, z_lo: 2; z = z_hi * 2 + z_lo), core: 2. Of those that a mesh axis runs over, the one named last changes fastest.
Arguments:
- tokens: bfloat16 [22528, 960], P(('rep', 'fsdp')), may hold values from -6 to 6
- seq_lengths: int32 [16, 3], P('rep'), may hold values from 1 to 1406, as said below
- attn_gain: bfloat16 [2, 960], P(None, 'fsdp'), may hold values from 0.5 to 1.5
- query_weight: bfloat16 [2, 960, 960], P(None, 'fsdp'), may hold values from -0.1875 to 0.1875
- key_projection: bfloat16 [2, 960, 320], P(None, 'fsdp'), may hold values from -0.1875 to 0.1875
- value_projection: bfloat16 [2, 960, 320], P(None, 'fsdp'), may hold values from -0.1875 to 0.1875
- out_weight: bfloat16 [2, 960, 960], P(None, 'fsdp'), may hold values from -0.75 to 0.75
- mlp_gain: bfloat16 [2, 960], P(None, 'fsdp'), may hold values from 0.5 to 1.5
- gate_weight: bfloat16 [2, 960, 2560], P(None, 'fsdp'), may hold values from -0.1875 to 0.1875
- up_weight: bfloat16 [2, 960, 2560], P(None, 'fsdp'), may hold values from -0.1875 to 0.1875
- down_weight: bfloat16 [2, 2560, 960], P(None, 'fsdp'), may hold values from -0.125 to 0.125
- cotangent: bfloat16 [22528, 960], P(('rep', 'fsdp')), may hold values from -6 to 6
Outputs:
- output: bfloat16 [22528, 960], P(('rep', 'fsdp'))
- grad_tokens: float32 [22528, 960], P(('rep', 'fsdp'))
- grad_attn_gain: float32 [2, 960], P(None, 'fsdp')
- grad_query_weight: float32 [2, 960, 960], P(None, 'fsdp')
- grad_key_weight: float32 [2, 960, 320], P(None, 'fsdp')
- grad_value_weight: float32 [2, 960, 320], P(None, 'fsdp')
- grad_out_weight: float32 [2, 960, 960], P(None, 'fsdp')
- grad_mlp_gain: float32 [2, 960], P(None, 'fsdp')
- grad_gate_weight: float32 [2, 960, 2560], P(None, 'fsdp')
- grad_up_weight: float32 [2, 960, 2560], P(None, 'fsdp')
- grad_down_weight: float32 [2, 2560, 960], P(None, 'fsdp')
Inputs may be any that keep to these rules, and one draw needn't show every extreme that they name: `seq_lengths`: row r gives the lengths of the 3 sequences of pack r in order; they sum to 1408, and the first and the last are under 176.
All inputs are finite; a program needn't handle non-finite values.
Results may differ from a plain program's by a relative error of at most 0.03.
Values may be sent and summed in bfloat16 or wider, within the bound.
No kernel may reach another device: no remote copies, remote signals or barrier semaphores. Data moves between devices by JAX's collectives and lax.ppermute only.
A program may use at most 256 MiB of HBM per device.

v0:
```python
import jax
import jax.numpy as jnp
from jax import lax
from jax.sharding import PartitionSpec as P

QUERY_HEADS = 15
KEY_VALUE_HEADS = 5
HEAD_SIZE = 64
DECODER_LAYERS = 2


epsilon_norm = 1e-05
rope_base = 100000.0
masked_score = -1e30


def for_sending(array):
    return jax.tree.map(lambda a: a.astype(jnp.bfloat16) if a.dtype == jnp.float32 else a, array)


def rms_scale(stream, gain):
    return (
        stream * lax.rsqrt(jnp.mean(stream * stream, axis=-1, keepdims=True) + epsilon_norm) * gain
    )


def rotary(head_values, cosine_table, sine_values):
    half_dim = head_values.shape[-1] // 2
    turned = jnp.concatenate([-head_values[..., half_dim:], head_values[..., :half_dim]], axis=-1)
    return head_values * cosine_table[:, None, :] + turned * sine_values[:, None, :]


def rope_tables(positions):
    frequency = rope_base ** (-(jnp.arange(HEAD_SIZE // 2, dtype=jnp.float32) * 2.0) / HEAD_SIZE)
    angles = positions[:, None] * frequency[None, :]
    angles = jnp.concatenate([angles, angles], axis=1)
    return (jnp.cos(angles), jnp.sin(angles))


def segment_layout(lengths, group_pos):
    seq_ends = jnp.cumsum(lengths)
    seq_starts = seq_ends - lengths
    segment = jnp.sum((group_pos[:, None] >= seq_ends[None, :-1]).astype(jnp.int32), axis=1)
    chosen = (segment[:, None] == jnp.arange(lengths.shape[0], dtype=jnp.int32)[None, :]).astype(
        jnp.int32
    )
    offsets = group_pos - jnp.sum(chosen * seq_starts[None, :], axis=1)
    return (segment, offsets.astype(jnp.float32))


def projection_rotary(normalized_input, weight, heads_count, cosine_table, sine_values):
    count_of_rows = normalized_input.shape[0]
    projected = jnp.dot(normalized_input, weight, preferred_element_type=jnp.float32).reshape(
        count_of_rows, heads_count, HEAD_SIZE
    )
    return (
        rotary(projected, cosine_table, sine_values)
        .reshape(count_of_rows, heads_count * HEAD_SIZE)
        .astype(jnp.bfloat16)
    )


def inverse_rotation(gradient, heads_count, cosine_table, sine_values):
    count_of_rows = gradient.shape[0]
    shaped = gradient.reshape(count_of_rows, heads_count, HEAD_SIZE)
    turned_back = jax.vjp(lambda values_in: rotary(values_in, cosine_table, sine_values), shaped)[
        1
    ](shaped)[0]
    return turned_back.reshape(count_of_rows, heads_count * HEAD_SIZE)


def cross_rows(left, right):
    return jnp.einsum("td,te->de", left, right, preferred_element_type=jnp.float32)


def attend(query_rows, gathered_keys, gathered_values, allowed):
    count_of_rows = query_rows.shape[0]
    pack_rows = gathered_keys.shape[0]
    heads_of_queries = query_rows.reshape(
        count_of_rows, KEY_VALUE_HEADS, QUERY_HEADS // KEY_VALUE_HEADS, HEAD_SIZE
    )
    heads_of_keys = gathered_keys.reshape(pack_rows, KEY_VALUE_HEADS, HEAD_SIZE)
    heads_of_values = gathered_values.reshape(pack_rows, KEY_VALUE_HEADS, HEAD_SIZE)
    scores = jnp.einsum(
        "qhgd,khd->hgqk", heads_of_queries, heads_of_keys, preferred_element_type=jnp.float32
    ) * HEAD_SIZE ** (-0.5)
    scores = jnp.where(allowed, scores, masked_score)
    row_top = jnp.max(scores, axis=-1, keepdims=True)
    exponent = jnp.exp(scores - row_top)
    row_total = jnp.sum(exponent, axis=-1, keepdims=True)
    log_totals = (row_top + jnp.log(row_total))[..., 0]
    soft_weights = (exponent / row_total).astype(jnp.bfloat16)
    combined_heads = jnp.einsum(
        "hgqk,khd->qhgd", soft_weights, heads_of_values, preferred_element_type=jnp.float32
    )
    return (
        combined_heads.reshape(count_of_rows, QUERY_HEADS * HEAD_SIZE).astype(jnp.bfloat16),
        log_totals,
    )


def attention_back(
    query_rows, gathered_keys, gathered_values, log_totals, combined_gradient, allowed
):
    count_of_rows = query_rows.shape[0]
    pack_rows = gathered_keys.shape[0]
    scale = HEAD_SIZE ** (-0.5)
    heads_of_queries = query_rows.reshape(
        count_of_rows, KEY_VALUE_HEADS, QUERY_HEADS // KEY_VALUE_HEADS, HEAD_SIZE
    )
    heads_of_keys = gathered_keys.reshape(pack_rows, KEY_VALUE_HEADS, HEAD_SIZE)
    heads_of_values = gathered_values.reshape(pack_rows, KEY_VALUE_HEADS, HEAD_SIZE)
    heads_gradient = combined_gradient.reshape(
        count_of_rows, KEY_VALUE_HEADS, QUERY_HEADS // KEY_VALUE_HEADS, HEAD_SIZE
    )
    scores = (
        jnp.einsum(
            "qhgd,khd->hgqk", heads_of_queries, heads_of_keys, preferred_element_type=jnp.float32
        )
        * scale
    )
    soft_weights = jnp.exp(jnp.where(allowed, scores, masked_score) - log_totals[..., None])
    weights_low = soft_weights.astype(jnp.bfloat16)
    grad_soft = jnp.einsum(
        "qhgd,khd->hgqk", heads_gradient, heads_of_values, preferred_element_type=jnp.float32
    )
    value_shard = jnp.einsum(
        "hgqk,qhgd->khd", weights_low, heads_gradient, preferred_element_type=jnp.float32
    )
    grad_scores = soft_weights * (
        grad_soft - jnp.sum(grad_soft * soft_weights, axis=-1, keepdims=True)
    )
    grad_scores = grad_scores.astype(jnp.bfloat16)
    query_grad = (
        jnp.einsum("hgqk,khd->qhgd", grad_scores, heads_of_keys, preferred_element_type=jnp.float32)
        * scale
    )
    key_shard = (
        jnp.einsum(
            "hgqk,qhgd->khd", grad_scores, heads_of_queries, preferred_element_type=jnp.float32
        )
        * scale
    )
    return (
        query_grad.reshape(count_of_rows, QUERY_HEADS * HEAD_SIZE),
        key_shard.reshape(pack_rows, KEY_VALUE_HEADS * HEAD_SIZE),
        value_shard.reshape(pack_rows, KEY_VALUE_HEADS * HEAD_SIZE),
    )


def forward_block(stream, whole_weights, cosine_table, sine_values, allowed):
    (
        gain_attn,
        query_full,
        gathered_key_weight,
        value_full,
        out_full,
        gain_mlp,
        gate_full,
        up_full,
        down_full,
    ) = whole_weights
    normalized_attention = rms_scale(stream, gain_attn).astype(jnp.bfloat16)
    query_rows = projection_rotary(
        normalized_attention, query_full, QUERY_HEADS, cosine_table, sine_values
    )
    shard_keys = projection_rotary(
        normalized_attention, gathered_key_weight, KEY_VALUE_HEADS, cosine_table, sine_values
    )
    values_local = jnp.dot(
        normalized_attention, value_full, preferred_element_type=jnp.float32
    ).astype(jnp.bfloat16)
    gathered = (
        lax.all_gather(shard_keys, "fsdp", axis=0, tiled=True),
        lax.all_gather(values_local, "fsdp", axis=0, tiled=True),
    )
    combined_heads, log_totals = attend(query_rows, gathered[0], gathered[1], allowed)
    middle = stream + jnp.dot(combined_heads, out_full, preferred_element_type=jnp.float32)
    normed_mlp = rms_scale(middle, gain_mlp).astype(jnp.bfloat16)
    gate_value = jnp.dot(normed_mlp, gate_full, preferred_element_type=jnp.float32)
    up_value = jnp.dot(normed_mlp, up_full, preferred_element_type=jnp.float32)
    hidden = (jax.nn.silu(gate_value) * up_value).astype(jnp.bfloat16)
    output = middle + jnp.dot(hidden, down_full, preferred_element_type=jnp.float32)
    record = (
        stream,
        normalized_attention,
        query_rows,
        shard_keys,
        values_local,
        log_totals,
        combined_heads,
        middle,
        normed_mlp,
        gate_value,
        up_value,
        hidden,
    )
    return (output, record, gathered)


def backward_block(
    grad_stream, whole_weights, gathered, record, cosine_table, sine_values, allowed
):
    (
        gain_attn,
        query_full,
        gathered_key_weight,
        value_full,
        out_full,
        gain_mlp,
        gate_full,
        up_full,
        down_full,
    ) = whole_weights
    (
        stream,
        normalized_attention,
        query_rows,
        shard_keys,
        values_local,
        log_totals,
        combined_heads,
        middle,
        normed_mlp,
        gate_value,
        up_value,
        hidden,
    ) = record
    down_grad = grad_stream.astype(jnp.bfloat16)
    grad_hidden = jnp.einsum("td,fd->tf", down_grad, down_full, preferred_element_type=jnp.float32)
    sigmoid_gate = jax.nn.sigmoid(gate_value)
    gate_grad = (
        grad_hidden * up_value * sigmoid_gate * (1.0 + gate_value * (1.0 - sigmoid_gate))
    ).astype(jnp.bfloat16)
    up_grad = (grad_hidden * gate_value * sigmoid_gate).astype(jnp.bfloat16)
    grad_normed = jnp.einsum("tf,df->td", gate_grad, gate_full, preferred_element_type=jnp.float32)
    grad_normed = grad_normed + jnp.einsum(
        "tf,df->td", up_grad, up_full, preferred_element_type=jnp.float32
    )
    norm_back = jax.vjp(rms_scale, middle, gain_mlp.astype(jnp.float32))[1]
    grad_middle, grad_mlp_gain = norm_back(grad_normed)
    grad_middle = grad_middle + grad_stream
    attn_grad = grad_middle.astype(jnp.bfloat16)
    combined_gradient = jnp.einsum(
        "td,ed->te", attn_grad, out_full, preferred_element_type=jnp.float32
    ).astype(jnp.bfloat16)
    query_grad, key_shard, value_shard = attention_back(
        query_rows, gathered[0], gathered[1], log_totals, combined_gradient, allowed
    )
    key_gradient_total, value_sum = (
        lax.psum_scatter(
            key_shard.astype(jnp.bfloat16), "fsdp", scatter_dimension=0, tiled=True
        ).astype(jnp.float32),
        lax.psum_scatter(
            value_shard.astype(jnp.bfloat16), "fsdp", scatter_dimension=0, tiled=True
        ).astype(jnp.float32),
    )
    query_grad = inverse_rotation(query_grad, QUERY_HEADS, cosine_table, sine_values).astype(
        jnp.bfloat16
    )
    key_gradient = inverse_rotation(
        key_gradient_total, KEY_VALUE_HEADS, cosine_table, sine_values
    ).astype(jnp.bfloat16)
    value_grad = value_sum.astype(jnp.bfloat16)
    grad_normed = jnp.einsum(
        "te,de->td", query_grad, query_full, preferred_element_type=jnp.float32
    )
    grad_normed = grad_normed + jnp.einsum(
        "te,de->td", key_gradient, gathered_key_weight, preferred_element_type=jnp.float32
    )
    grad_normed = grad_normed + jnp.einsum(
        "te,de->td", value_grad, value_full, preferred_element_type=jnp.float32
    )
    norm_back = jax.vjp(rms_scale, stream, gain_attn.astype(jnp.float32))[1]
    grad_input, grad_attn_gain = norm_back(grad_normed)
    inputs = (normalized_attention, combined_heads, normed_mlp, hidden)
    outputs = (query_grad, key_gradient, value_grad, attn_grad, gate_grad, up_grad, down_grad)
    return (grad_input + grad_middle, (grad_attn_gain, grad_mlp_gain), inputs, outputs)


def body(
    tokens,
    seq_lengths,
    attn_gain,
    query_weight,
    key_projection,
    value_projection,
    out_weight,
    mlp_gain,
    gate_weight,
    up_weight,
    down_weight,
    cotangent,
):
    local_rows = tokens.shape[0]
    pack_rows = local_rows * lax.axis_size("fsdp")
    first_row = lax.axis_index("fsdp") * local_rows
    group_pos = jnp.arange(pack_rows, dtype=jnp.int32)
    query_pos = first_row + jnp.arange(local_rows, dtype=jnp.int32)
    key_segment = segment_layout(seq_lengths[0], group_pos)[0]
    query_segment, query_offsets = segment_layout(seq_lengths[0], query_pos)
    allowed = (query_segment[:, None] == key_segment[None, :]) & (
        group_pos[None, :] <= query_pos[:, None]
    )
    cosine_table, sine_values = rope_tables(query_offsets)
    stream = tokens.astype(jnp.float32)
    saved_state = []
    for layer_index in range(DECODER_LAYERS):
        shards = (
            attn_gain[layer_index],
            query_weight[layer_index],
            key_projection[layer_index],
            value_projection[layer_index],
            out_weight[layer_index],
            mlp_gain[layer_index],
            gate_weight[layer_index],
            up_weight[layer_index],
            down_weight[layer_index],
        )
        whole_weights = (
            lax.all_gather(shards[0], "fsdp", axis=0, tiled=True),
            lax.all_gather(shards[1], "fsdp", axis=0, tiled=True),
            lax.all_gather(shards[2], "fsdp", axis=0, tiled=True),
            lax.all_gather(shards[3], "fsdp", axis=0, tiled=True),
            lax.all_gather(shards[4], "fsdp", axis=0, tiled=True),
            lax.all_gather(shards[5], "fsdp", axis=0, tiled=True),
            lax.all_gather(shards[6], "fsdp", axis=0, tiled=True),
            lax.all_gather(shards[7], "fsdp", axis=0, tiled=True),
            lax.all_gather(shards[8], "fsdp", axis=0, tiled=True),
        )
        stream, record, gathered = forward_block(
            stream, whole_weights, cosine_table, sine_values, allowed
        )
        saved_state.append((shards, record))
    grad_stream = cotangent.astype(jnp.float32)
    layer_grads = [None] * DECODER_LAYERS
    for layer_index in reversed(range(DECODER_LAYERS)):
        shards, record = saved_state[layer_index]
        whole_weights = jax.tree.map(
            lambda part, own: part.astype(own.dtype),
            lax.all_gather(for_sending(shards), "fsdp", axis=0, tiled=True),
            shards,
        )
        gathered = (
            lax.all_gather(record[3], "fsdp", axis=0, tiled=True),
            lax.all_gather(record[4], "fsdp", axis=0, tiled=True),
        )
        grad_stream, gain_terms, inputs, outputs = backward_block(
            grad_stream, whole_weights, gathered, record, cosine_table, sine_values, allowed
        )
        normalized_attention, combined_heads, normed_mlp, hidden = inputs
        query_grad, key_gradient, value_grad, attn_grad, gate_grad, up_grad, down_grad = outputs
        layer_terms = (
            gain_terms[0],
            cross_rows(normalized_attention, query_grad),
            cross_rows(normalized_attention, key_gradient),
            cross_rows(normalized_attention, value_grad),
            cross_rows(combined_heads, attn_grad),
            gain_terms[1],
            cross_rows(normed_mlp, gate_grad),
            cross_rows(normed_mlp, up_grad),
            cross_rows(hidden, down_grad),
        )
        owned_grads = (
            lax.psum_scatter(
                layer_terms[0].astype(jnp.bfloat16), "fsdp", scatter_dimension=0, tiled=True
            ).astype(jnp.float32),
            lax.psum_scatter(
                layer_terms[1].astype(jnp.bfloat16), "fsdp", scatter_dimension=0, tiled=True
            ).astype(jnp.float32),
            lax.psum_scatter(
                layer_terms[2].astype(jnp.bfloat16), "fsdp", scatter_dimension=0, tiled=True
            ).astype(jnp.float32),
            lax.psum_scatter(
                layer_terms[3].astype(jnp.bfloat16), "fsdp", scatter_dimension=0, tiled=True
            ).astype(jnp.float32),
            lax.psum_scatter(
                layer_terms[4].astype(jnp.bfloat16), "fsdp", scatter_dimension=0, tiled=True
            ).astype(jnp.float32),
            lax.psum_scatter(
                layer_terms[5].astype(jnp.bfloat16), "fsdp", scatter_dimension=0, tiled=True
            ).astype(jnp.float32),
            lax.psum_scatter(
                layer_terms[6].astype(jnp.bfloat16), "fsdp", scatter_dimension=0, tiled=True
            ).astype(jnp.float32),
            lax.psum_scatter(
                layer_terms[7].astype(jnp.bfloat16), "fsdp", scatter_dimension=0, tiled=True
            ).astype(jnp.float32),
            lax.psum_scatter(
                layer_terms[8].astype(jnp.bfloat16), "fsdp", scatter_dimension=0, tiled=True
            ).astype(jnp.float32),
        )
        layer_grads[layer_index] = (
            lax.psum(owned_grads[0].astype(jnp.bfloat16), "rep").astype(jnp.float32),
            lax.psum(owned_grads[1].astype(jnp.bfloat16), "rep").astype(jnp.float32),
            lax.psum(owned_grads[2].astype(jnp.bfloat16), "rep").astype(jnp.float32),
            lax.psum(owned_grads[3].astype(jnp.bfloat16), "rep").astype(jnp.float32),
            lax.psum(owned_grads[4].astype(jnp.bfloat16), "rep").astype(jnp.float32),
            lax.psum(owned_grads[5].astype(jnp.bfloat16), "rep").astype(jnp.float32),
            lax.psum(owned_grads[6].astype(jnp.bfloat16), "rep").astype(jnp.float32),
            lax.psum(owned_grads[7].astype(jnp.bfloat16), "rep").astype(jnp.float32),
            lax.psum(owned_grads[8].astype(jnp.bfloat16), "rep").astype(jnp.float32),
        )
    stacked = [
        jnp.stack(
            [layer_grads[layer_index][member] for layer_index in range(DECODER_LAYERS)], axis=0
        )
        for member in range(9)
    ]
    return (
        stream.astype(jnp.bfloat16),
        grad_stream,
        stacked[0],
        stacked[1],
        stacked[2],
        stacked[3],
        stacked[4],
        stacked[5],
        stacked[6],
        stacked[7],
        stacked[8],
    )


def solution(mesh):
    in_specs = (
        P(("rep", "fsdp"), None),
        P("rep", None),
        P(None, "fsdp"),
        P(None, "fsdp", None),
        P(None, "fsdp", None),
        P(None, "fsdp", None),
        P(None, "fsdp", None),
        P(None, "fsdp"),
        P(None, "fsdp", None),
        P(None, "fsdp", None),
        P(None, "fsdp", None),
        P(("rep", "fsdp"), None),
    )
    out_specs = (
        P(("rep", "fsdp"), None),
        P(("rep", "fsdp"), None),
        P(None, "fsdp"),
        P(None, "fsdp", None),
        P(None, "fsdp", None),
        P(None, "fsdp", None),
        P(None, "fsdp", None),
        P(None, "fsdp"),
        P(None, "fsdp", None),
        P(None, "fsdp", None),
        P(None, "fsdp", None),
    )
    return jax.shard_map(body, mesh=mesh, in_specs=in_specs, out_specs=out_specs, check_vma=False)
```

profile of v0, /device:TPU:5, one launch (start us, length us, event | category | flops | bytes accessed | tf_op | source)
XLA Modules:
  0.0 2265.5 jit_solution(5979825594006726664)
XLA Ops:
  23.0 17.2 all-reduce.23
  46.7 33.6 %all-gather.2 = bf16[1,960,320]{2,0,1:T(2,128)(2,1)S(1)} all-gather(bf16[1,120,320]{2,0,1:T(2,128)(2,1)} %copy.170), channel_id=4, replica_groups=mesh['rep'=16,'fsdp'=8] {'fsdp'}, dimensions={1}, use_global_device_ids=true | all-gather | bytes 691200 | tf_op jit(solution)/shard_map/all_gather | solution.py:323
  85.7 34.1 %all_gather.92 = bf16[1408,320]{1,0:T(8,128)(2,1)} all-gather(bf16[176,320]{1,0:T(8,128)(2,1)S(1)} %add_convert_fusion.3), channel_id=1, replica_groups=mesh['rep'=16,'fsdp'=8] {'fsdp'}, dimensions={0}, use_global_device_ids=true | all-gather | bytes 1013760 | tf_op jit(solution)/shard_map/all_gather | solution.py:174
  121.5 34.9 %all-gather.1 = bf16[1,960,320]{2,0,1:T(2,128)(2,1)} all-gather(bf16[1,120,320]{2,0,1:T(2,128)(2,1)S(1)} %copy-done.60), channel_id=3, replica_groups=mesh['rep'=16,'fsdp'=8] {'fsdp'}, dimensions={1}, use_global_device_ids=true | all-gather | bytes 691200 | tf_op jit(solution)/shard_map/all_gather | solution.py:324
  160.5 35.1 %all_gather.90 = bf16[1408,320]{1,0:T(8,128)(2,1)} all-gather(bf16[176,320]{1,0:T(8,128)(2,1)S(1)} %convolution_convert_fusion.15), channel_id=1, replica_groups=mesh['rep'=16,'fsdp'=8] {'fsdp'}, dimensions={0}, use_global_device_ids=true | all-gather | bytes 1013760 | tf_op jit(solution)/shard_map/all_gather | solution.py:175
  197.9 35.3 %all-gather.10 = bf16[1,960,320]{2,0,1:T(2,128)(2,1)} all-gather(bf16[1,120,320]{2,0,1:T(2,128)(2,1)S(1)} %copy-done.59), channel_id=12, replica_groups=mesh['rep'=16,'fsdp'=8] {'fsdp'}, dimensions={1}, use_global_device_ids=true | all-gather | bytes 691200 | tf_op jit(solution)/shard_map/all_gather | solution.py:324
  237.8 37.9 %all-gather.11 = bf16[1,960,320]{2,0,1:T(2,128)(2,1)} all-gather(bf16[1,120,320]{2,0,1:T(2,128)(2,1)S(1)} %copy-done.58), channel_id=13, replica_groups=mesh['rep'=16,'fsdp'=8] {'fsdp'}, dimensions={1}, use_global_device_ids=true | all-gather | bytes 691200 | tf_op jit(solution)/shard_map/all_gather | solution.py:323
  290.2 7.8 fusion.168
  298.0 7.7 fusion.6
  305.8 8.2 fusion.75
  327.0 70.8 %all-gather.37.cloned.1.call-done = bf16[1,2560,960]{2,1,0:T(8,128)(2,1)} async-done(((bf16[1,320,960]{2,1,0:T(8,128)(2,1)}), bf16[1,2560,960]{2,1,0:T(8,128)(2,1)}) %all-gather.37.cloned.1.call-update) | async-done | bytes 4915216 | tf_op jit(solution)/shard_map/all_gather | solution.py:329
  406.3 31.6 %all_gather.103 = bf16[1408,320]{1,0:T(8,128)(2,1)} all-gather(bf16[176,320]{1,0:T(8,128)(2,1)S(1)} %add_convert_fusion.2), channel_id=1, replica_groups=mesh['rep'=16,'fsdp'=8] {'fsdp'}, dimensions={0}, use_global_device_ids=true | all-gather | bytes 1013760 | tf_op jit(solution)/shard_map/all_gather | solution.py:174
  441.1 34.1 %all_gather.101 = bf16[1408,320]{1,0:T(8,128)(2,1)} all-gather(bf16[176,320]{1,0:T(8,128)(2,1)S(1)} %convolution_convert_fusion.14), channel_id=1, replica_groups=mesh['rep'=16,'fsdp'=8] {'fsdp'}, dimensions={0}, use_global_device_ids=true | all-gather | bytes 1013760 | tf_op jit(solution)/shard_map/all_gather | solution.py:175
  490.9 9.1 fusion.169
  500.0 7.5 fusion.7
  507.5 9.0 fusion.74
  520.4 70.2 %all-gather.45.cloned.1.call-done = bf16[1,960,2560]{2,1,0:T(8,128)(2,1)} async-done(((bf16[1,120,2560]{2,1,0:T(8,128)(2,1)}), bf16[1,960,2560]{2,1,0:T(8,128)(2,1)}) %all-gather.45.cloned.1.call-update) | async-done | bytes 4915216 | tf_op jit(solution)/shard_map/all_gather | solution.py:328
  595.3 75.7 %all-gather.47.cloned.1.call-done = bf16[1,2560,960]{2,1,0:T(8,128)(2,1)} async-done(((bf16[1,320,960]{2,1,0:T(8,128)(2,1)}), bf16[1,2560,960]{2,1,0:T(8,128)(2,1)}) %all-gather.47.cloned.1.call-update) | async-done | bytes 4915216 | tf_op jit(solution)/shard_map/all_gather | solution.py:329
  671.0 5.7 fusion.18
  676.7 71.8 %all-gather.43.cloned.1.call-done = bf16[1,960,2560]{2,1,0:T(8,128)(2,1)} async-done(((bf16[1,120,2560]{2,1,0:T(8,128)(2,1)}), bf16[1,960,2560]{2,1,0:T(8,128)(2,1)}) %all-gather.43.cloned.1.call-update) | async-done | bytes 4915216 | tf_op jit(solution)/shard_map/all_gather | solution.py:327
  748.5 6.2 multiply_convert_fusion.3
  766.5 14.0 fusion.3
  780.6 7.7 fusion.5
  797.6 8.6 fusion.52
  808.7 5.8 convolution_multiply_fusion.1
  821.9 41.0 %reduce-scatter.47.cloned.1.call-done = bf16[176,320]{1,0:T(8,128)(2,1)} async-done(((bf16[1408,320]{1,0:T(8,128)(2,1)}), bf16[176,320]{1,0:T(8,128)(2,1)}) %reduce-scatter.47.cloned.1.call-update) | async-done | bytes 112656
  868.2 67.6 %reduce-scatter.49.cloned.1.call-done = bf16[176,320]{1,0:T(8,128)(2,1)} async-done(((bf16[1408,320]{1,0:T(8,128)(2,1)}), bf16[176,320]{1,0:T(8,128)(2,1)}) %reduce-scatter.49.cloned.1.call-update) | async-done | bytes 112656
  938.7 6.1 multiply_convert_fusion.1
  951.9 14.2 fusion
  966.2 7.7 fusion.2
  982.3 8.5 fusion.55
  995.6 55.1 %reduce-scatter.51.cloned.1.call-done = bf16[176,320]{1,0:T(8,128)(2,1)} async-done(((bf16[1408,320]{1,0:T(8,128)(2,1)}), bf16[176,320]{1,0:T(8,128)(2,1)}) %reduce-scatter.51.cloned.1.call-update) | async-done | bytes 112656
  1053.2 70.9 %reduce-scatter.53.cloned.1.call-done = bf16[176,320]{1,0:T(8,128)(2,1)} async-done(((bf16[1408,320]{1,0:T(8,128)(2,1)}), bf16[176,320]{1,0:T(8,128)(2,1)}) %reduce-scatter.53.cloned.1.call-update) | async-done | bytes 112656
  1135.8 6.0 convolution_multiply_fusion
  1174.4 45.2 %all-reduce.30.cloned.1.call-done = (bf16[960,320]{0,1:T(8,128)(2,1)}, bf16[960,320]{0,1:T(8,128)(2,1)}, bf16[960,320]{0,1:T(8,128)(2,1)}, bf16[960,320]{0,1:T(8,128)(2,1)}) async-done(((bf16[960,320]{0,1:T(8,128)(2,1)}, bf16[960,320]{0,1:T(8,128)(2,1)}, bf16[960,320]{0,1:T(8,128)(2,1)}, bf16[960,320]{0,1:T(8,128)(2,1)}), (bf16[960,320]{0,1:T(8,128)(2,1)}, bf16[960,320]{0,1:T(8,128)(2,1)}, ...) | async-done | bytes 2457616
  1223.2 77.8 %reduce-scatter.33.cloned.1.call-done = bf16[120,960]{1,0:T(8,128)(2,1)} async-done(((bf16[960,960]{1,0:T(8,128)(2,1)}), bf16[120,960]{1,0:T(8,128)(2,1)}) %reduce-scatter.33.cloned.1.call-update) | async-done | bytes 230416 | tf_op jit(solution)/shard_map/reduce_scatter | solution.py:377
  1301.0 78.3 %reduce-scatter.29.cloned.1.call-done = bf16[120,960]{1,0:T(8,128)(2,1)} async-done(((bf16[960,960]{1,0:T(8,128)(2,1)}), bf16[120,960]{1,0:T(8,128)(2,1)}) %reduce-scatter.29.cloned.1.call-update) | async-done | bytes 230416 | tf_op jit(solution)/shard_map/reduce_scatter | solution.py:368
  1379.3 77.7 %reduce-scatter.31.cloned.1.call-done = bf16[120,960]{1,0:T(8,128)(2,1)} async-done(((bf16[960,960]{1,0:T(8,128)(2,1)}), bf16[120,960]{1,0:T(8,128)(2,1)}) %reduce-scatter.31.cloned.1.call-update) | async-done | bytes 230416 | tf_op jit(solution)/shard_map/reduce_scatter | solution.py:377
  1457.1 78.5 %reduce-scatter.27.cloned.1.call-done = bf16[120,960]{1,0:T(8,128)(2,1)} async-done(((bf16[960,960]{1,0:T(8,128)(2,1)}), bf16[120,960]{1,0:T(8,128)(2,1)}) %reduce-scatter.27.cloned.1.call-update) | async-done | bytes 230416 | tf_op jit(solution)/shard_map/reduce_scatter | solution.py:368
  1535.5 93.0 %reduce-scatter.37.cloned.1.call-done = bf16[120,2560]{1,0:T(8,128)(2,1)} async-done(((bf16[960,2560]{1,0:T(8,128)(2,1)}), bf16[120,2560]{1,0:T(8,128)(2,1)}) %reduce-scatter.37.cloned.1.call-update) | async-done | bytes 614416 | tf_op jit(solution)/shard_map/reduce_scatter | solution.py:383
  1628.5 93.1 %reduce-scatter.41.cloned.1.call-done = bf16[120,2560]{1,0:T(8,128)(2,1)} async-done(((bf16[960,2560]{1,0:T(8,128)(2,1)}), bf16[120,2560]{1,0:T(8,128)(2,1)}) %reduce-scatter.41.cloned.1.call-update) | async-done | bytes 614416 | tf_op jit(solution)/shard_map/reduce_scatter | solution.py:386
  1721.6 94.7 %reduce-scatter.45.cloned.1.call-done = bf16[320,960]{1,0:T(8,128)(2,1)} async-done(((bf16[2560,960]{1,0:T(8,128)(2,1)}), bf16[320,960]{1,0:T(8,128)(2,1)}) %reduce-scatter.45.cloned.1.call-update) | async-done | bytes 614416 | tf_op jit(solution)/shard_map/reduce_scatter | solution.py:389
  1816.2 94.9 %reduce-scatter.43.cloned.1.call-done = bf16[320,960]{1,0:T(8,128)(2,1)} async-done(((bf16[2560,960]{1,0:T(8,128)(2,1)}), bf16[320,960]{1,0:T(8,128)(2,1)}) %reduce-scatter.43.cloned.1.call-update) | async-done | bytes 614416 | tf_op jit(solution)/shard_map/reduce_scatter | solution.py:389
  1911.1 92.2 %reduce-scatter.35.cloned.1.call-done = bf16[120,2560]{1,0:T(8,128)(2,1)} async-done(((bf16[960,2560]{1,0:T(8,128)(2,1)}), bf16[120,2560]{1,0:T(8,128)(2,1)}) %reduce-scatter.35.cloned.1.call-update) | async-done | bytes 614416 | tf_op jit(solution)/shard_map/reduce_scatter | solution.py:383
  2003.3 92.9 %reduce-scatter.39.cloned.1.call-done = bf16[120,2560]{1,0:T(8,128)(2,1)} async-done(((bf16[960,2560]{1,0:T(8,128)(2,1)}), bf16[120,2560]{1,0:T(8,128)(2,1)}) %reduce-scatter.39.cloned.1.call-update) | async-done | bytes 614416 | tf_op jit(solution)/shard_map/reduce_scatter | solution.py:386
  2102.7 14.9 all-reduce.22
  2117.7 32.0 %all-reduce.20 = (bf16[1,120]{1,0:T(2,128)(2,1)S(1)}, bf16[1,120]{1,0:T(2,128)(2,1)S(1)}, bf16[1,120]{1,0:T(2,128)(2,1)S(1)}, bf16[1,120]{1,0:T(2,128)(2,1)S(1)}) all-reduce(bf16[1,120]{1,0:T(2,128)(2,1)S(1)} %get-tuple-element.114, bf16[1,120]{1,0:T(2,128)(2,1)S(1)} %get-tuple-element.115, ...), channel_id=1, replica_groups=mesh['rep'=16,'fsdp'=8] {'rep'}, use_global_device_ids=true, to_apply=%region_27.28 | all-reduce | flops 480 | bytes 1920 | tf_op jit(solution)/shard_map/psum | solution.py:394
  2151.9 92.9 %all-reduce.28.cloned.1.call-done = (bf16[1,120,960]{2,1,0:T(8,128)(2,1)}, bf16[1,120,960]{2,1,0:T(8,128)(2,1)}, bf16[1,120,320]{1,2,0:T(8,128)(2,1)}, bf16[1,12...) async-done(((bf16[1,120,960]{2,1,0:T(8,128)(2,1)}, ...) | async-done | bytes 4915216 | tf_op jit(solution)/shard_map/psum | solution.py:395
  (476 shorter events, 233.0 us)
Async XLA Ops:
  7.2 273.4 %all-gather.29.cloned.1.call-start = ((), (), s32[]{:S(2)}) async-start(), calls=%async_computation.24 | async-start | bytes 2211840 | tf_op jit(solution)/shard_map/all_gather | solution.py:322
  9.3 304.8 %all-gather.31.cloned.1.call-start = ((), (), s32[]{:S(2)}) async-start(), calls=%async_computation.25 | async-start | bytes 2211840 | tf_op jit(solution)/shard_map/all_gather | solution.py:325
  11.2 305.5 %all-gather.33.cloned.1.call-start = ((), (), s32[]{:S(2)}) async-start(), calls=%async_computation.26 | async-start | bytes 5529600 | tf_op jit(solution)/shard_map/all_gather | solution.py:327
  13.7 307.9 %all-gather.35.cloned.1.call-start = ((), (), s32[]{:S(2)}) async-start(), calls=%async_computation.27 | async-start | bytes 5529600 | tf_op jit(solution)/shard_map/all_gather | solution.py:328
  14.9 382.8 %all-gather.37.cloned.1.call-start = ((), (), s32[]{:S(2)}) async-start(), calls=%async_computation.28 | async-start | bytes 5898240 | tf_op jit(solution)/shard_map/all_gather | solution.py:329
  16.1 461.3 %all-gather.39.cloned.1.call-start = ((), (), s32[]{:S(2)}) async-start(), calls=%async_computation.29 | async-start | bytes 2211840 | tf_op jit(solution)/shard_map/all_gather | solution.py:322
  16.7 499.8 %all-gather.41.cloned.1.call-start = ((), (), s32[]{:S(2)}) async-start(), calls=%async_computation.30 | async-start | bytes 2211840 | tf_op jit(solution)/shard_map/all_gather | solution.py:325
  17.5 573.2 %all-gather.45.cloned.1.call-start = ((), (), s32[]{:S(2)}) async-start(), calls=%async_computation.32 | async-start | bytes 5529600 | tf_op jit(solution)/shard_map/all_gather | solution.py:328
  18.2 652.8 %all-gather.47.cloned.1.call-start = ((), (), s32[]{:S(2)}) async-start(), calls=%async_computation.33 | async-start | bytes 5898240 | tf_op jit(solution)/shard_map/all_gather | solution.py:329
  19.0 729.5 %all-gather.43.cloned.1.call-start = ((), (), s32[]{:S(2)}) async-start(), calls=%async_computation.31 | async-start | bytes 5529600 | tf_op jit(solution)/shard_map/all_gather | solution.py:327
  19.5 843.4 %reduce-scatter.47.cloned.1.call-start = ((), (), s32[]{:S(2)}) async-start(), calls=%async_computation.34 | async-start | bytes 1216512
  20.0 140.1 %copy-start.82 = (f32[176]{0:T(256)}, f32[176]{0:T(256)S(1)}, u32[]{:S(2)}) copy-start(f32[176]{0:T(256)S(1)} %fusion.145) | copy-start | bytes 2116
  40.2 119.8 %copy-start.69 = (f32[960]{0:T(1024)}, f32[960]{0:T(1024)S(1)}, u32[]{:S(2)}) copy-start(f32[960]{0:T(1024)S(1)} %convert_element_type.398) | copy-start | bytes 11524
  46.1 244.1 %copy-start.28 = (pred[176,1408]{1,0:T(8,128)(4,1)}, pred[176,1408]{1,0:T(8,128)(4,1)S(1)}, u32[]{:S(2)}) copy-start(pred[176,1408]{1,0:T(8,128)(4,1)S(1)} %fusion.102) | copy-start | bytes 743428
  119.8 78.2 %copy-start.59 = (bf16[1,120,320]{2,0,1:T(2,128)(2,1)S(1)}, bf16[1,120,320]{2,0,1:T(2,128)(2,1)}, u32[]{:S(2)}) copy-start(bf16[1,120,320]{2,0,1:T(2,128)(2,1)} %copy.171) | copy-start | bytes 230404
  121.5 168.7 %copy-start.3 = (bf16[1408,320]{0,1:T(8,128)(2,1)}, bf16[1408,320]{0,1:T(8,128)(2,1)S(1)}, u32[]{:S(2)}) copy-start(bf16[1408,320]{0,1:T(8,128)(2,1)S(1)} %copy.125) | copy-start | bytes 2703364
  156.4 81.4 %copy-start.58 = (bf16[1,120,320]{2,0,1:T(2,128)(2,1)S(1)}, bf16[1,120,320]{2,0,1:T(2,128)(2,1)}, u32[]{:S(2)}) copy-start(bf16[1,120,320]{2,0,1:T(2,128)(2,1)} %copy.172) | copy-start | bytes 230404
  160.1 115.6 %copy-start.45 = (bf16[1,960,320]{1,2,0:T(8,128)(2,1)}, bf16[1,960,320]{1,2,0:T(8,128)(2,1)S(1)}, u32[]{:S(2)}) copy-start(bf16[1,960,320]{1,2,0:T(8,128)(2,1)S(1)} %copy.118) | copy-start | bytes 1843204
  195.6 85.0 %copy-start.70 = (f32[960]{0:T(1024)S(1)}, f32[960]{0:T(1024)}, u32[]{:S(2)}) copy-start(f32[960]{0:T(1024)} %copy-done.69) | copy-start | bytes 11524
  195.6 85.0 %copy-start.83 = (f32[176]{0:T(256)S(1)}, f32[176]{0:T(256)}, u32[]{:S(2)}) copy-start(f32[176]{0:T(256)} %copy-done.82) | copy-start | bytes 2116
  316.5 81.3 %copy-start.5 = (f32[176,960]{1,0:T(8,128)}, f32[176,960]{1,0:T(8,128)S(1)}, u32[]{:S(2)}) copy-start(f32[176,960]{1,0:T(8,128)S(1)} %get-tuple-element.95) | copy-start | bytes 2027524
  327.0 76.2 %copy-start.20 = (bf16[176,2560]{1,0:T(8,128)(2,1)}, bf16[176,2560]{1,0:T(8,128)(2,1)S(1)}, u32[]{:S(2)}) copy-start(bf16[176,2560]{1,0:T(8,128)(2,1)S(1)} %get-tuple-element.96) | copy-start | bytes 2703364
  796.2 139.5 %reduce-scatter.49.cloned.1.call-start = ((), (), s32[]{:S(2)}) async-start(), calls=%async_computation.35 | async-start | bytes 1216512
  816.6 234.1 %reduce-scatter.51.cloned.1.call-start = ((), (), s32[]{:S(2)}) async-start(), calls=%async_computation.36 | async-start | bytes 1216512
  818.1 117.7 %copy-start.81 = (f32[960]{0:T(1024)S(1)}, f32[960]{0:T(1024)}, u32[]{:S(2)}) copy-start(f32[960]{0:T(1024)} %convert_element_type.400) | copy-start | bytes 11524
  818.1 117.7 %copy-start.92 = (f32[176]{0:T(256)S(1)}, f32[176]{0:T(256)}, u32[]{:S(2)}) copy-start(f32[176]{0:T(256)} %copy-done.91) | copy-start | bytes 2116
  820.3 118.1 %copy-start.102 = (f32[176]{0:T(256)S(1)}, f32[176]{0:T(256)}, u32[]{:S(2)}) copy-start(f32[176]{0:T(256)} %copy-done.101) | copy-start | bytes 2116
  820.3 118.1 %copy-start.14 = (f32[176,960]{1,0:T(8,128)S(1)}, f32[176,960]{1,0:T(8,128)}, u32[]{:S(2)}) copy-start(f32[176,960]{1,0:T(8,128)} %copy-done.13) | copy-start | bytes 2027524
  865.6 73.0 %copy-start.49 = (bf16[176,5,64]{0,2,1:T(8,128)(2,1)}, bf16[176,5,64]{0,2,1:T(8,128)(2,1)S(1)}, u32[]{:S(2)}) copy-start(bf16[176,5,64]{0,2,1:T(8,128)(2,1)S(1)} %fusion.131) | copy-start | bytes 337924
  981.8 142.3 %reduce-scatter.53.cloned.1.call-start = ((), (), s32[]{:S(2)}) async-start(), calls=%async_computation.37 | async-start | bytes 1216512
  990.8 61.0 %copy-start.71 = (f32[960]{0:T(1024)S(1)}, f32[960]{0:T(1024)}, u32[]{:S(2)}) copy-start(f32[960]{0:T(1024)} %copy-done.69) | copy-start | bytes 11524
  990.8 61.0 %copy-start.84 = (f32[176]{0:T(256)S(1)}, f32[176]{0:T(256)}, u32[]{:S(2)}) copy-start(f32[176]{0:T(256)} %copy-done.82) | copy-start | bytes 2116
  993.2 133.2 %copy-start.15 = (f32[176,960]{1,0:T(8,128)S(1)}, f32[176,960]{1,0:T(8,128)}, u32[]{:S(2)}) copy-start(f32[176,960]{1,0:T(8,128)} %copy-done.13) | copy-start | bytes 2027524
  993.2 226.5 %all-reduce.30.cloned.1.call-start = ((), (), s32[]{:S(2)}) async-start(), calls=%async_computation.39 | async-start | bytes 5242880
  1051.8 77.6 %copy-start.51 = (bf16[176,5,64]{0,2,1:T(8,128)(2,1)}, bf16[176,5,64]{0,2,1:T(8,128)(2,1)S(1)}, u32[]{:S(2)}) copy-start(bf16[176,5,64]{0,2,1:T(8,128)(2,1)S(1)} %fusion.134) | copy-start | bytes 337924
  1126.3 174.7 %reduce-scatter.33.cloned.1.call-start = ((), (), s32[]{:S(2)}) async-start(), calls=%async_computation.17 | async-start | bytes 2211840 | tf_op jit(solution)/shard_map/reduce_scatter | solution.py:377
  1129.4 249.9 %reduce-scatter.29.cloned.1.call-start = ((), (), s32[]{:S(2)}) async-start(), calls=%async_computation.15 | async-start | bytes 2211840 | tf_op jit(solution)/shard_map/reduce_scatter | solution.py:368
  1132.6 324.4 %reduce-scatter.31.cloned.1.call-start = ((), (), s32[]{:S(2)}) async-start(), calls=%async_computation.16 | async-start | bytes 2211840 | tf_op jit(solution)/shard_map/reduce_scatter | solution.py:377
  1135.7 399.8 %reduce-scatter.27.cloned.1.call-start = ((), (), s32[]{:S(2)}) async-start(), calls=%async_computation.14 | async-start | bytes 2211840 | tf_op jit(solution)/shard_map/reduce_scatter | solution.py:368
  1144.6 483.9 %reduce-scatter.37.cloned.1.call-start = ((), (), s32[]{:S(2)}) async-start(), calls=%async_computation.19 | async-start | bytes 5529600 | tf_op jit(solution)/shard_map/reduce_scatter | solution.py:383
  1149.5 572.1 %reduce-scatter.41.cloned.1.call-start = ((), (), s32[]{:S(2)}) async-start(), calls=%async_computation.21 | async-start | bytes 5529600 | tf_op jit(solution)/shard_map/reduce_scatter | solution.py:386
  1154.6 661.6 %reduce-scatter.45.cloned.1.call-start = ((), (), s32[]{:S(2)}) async-start(), calls=%async_computation.23 | async-start | bytes 5898240 | tf_op jit(solution)/shard_map/reduce_scatter | solution.py:389
  1158.8 752.4 %reduce-scatter.43.cloned.1.call-start = ((), (), s32[]{:S(2)}) async-start(), calls=%async_computation.22 | async-start | bytes 5898240 | tf_op jit(solution)/shard_map/reduce_scatter | solution.py:389
  1164.0 839.3 %reduce-scatter.35.cloned.1.call-start = ((), (), s32[]{:S(2)}) async-start(), calls=%async_computation.18 | async-start | bytes 5529600 | tf_op jit(solution)/shard_map/reduce_scatter | solution.py:383
  1169.9 926.4 %reduce-scatter.39.cloned.1.call-start = ((), (), s32[]{:S(2)}) async-start(), calls=%async_computation.20 | async-start | bytes 5529600 | tf_op jit(solution)/shard_map/reduce_scatter | solution.py:386
  1173.7 922.6 %copy-start.30 = (bf16[176,2560]{1,0:T(8,128)(2,1)S(1)}, bf16[176,2560]{1,0:T(8,128)(2,1)}, u32[]{:S(2)}) copy-start(bf16[176,2560]{1,0:T(8,128)(2,1)} %get-tuple-element.52) | copy-start | bytes 2703364
  1173.7 1071.1 %all-reduce.28.cloned.1.call-start = ((), (), s32[]{:S(2)}) async-start(), calls=%async_computation.38 | async-start | bytes 10158080 | tf_op jit(solution)/shard_map/psum | solution.py:395
  2100.8 50.0 %copy-start.12 = (f32[176,960]{1,0:T(8,128)S(1)}, f32[176,960]{1,0:T(8,128)}, u32[]{:S(2)}) copy-start(f32[176,960]{1,0:T(8,128)} %copy-done.10) | copy-start | bytes 2027524
  (103 other events, 884.2 us)
Sparse Core Ops, SparseCore 0:
  10.9 57.6 all-gather.28
  71.5 59.4 all-gather.30
  133.9 91.3 all-gather.32
  228.0 88.2 all-gather.34
  319.1 78.6 all-gather.36
  400.5 54.7 all-gather.38
  457.6 53.5 all-gather.40
  513.5 77.1 all-gather.44
  593.0 78.0 all-gather.46
  673.2 75.2 all-gather.42
  796.3 66.5 reduce-scatter.46
  867.0 68.7 reduce-scatter.48
  981.9 68.7 reduce-scatter.50
  1055.3 68.7 reduce-scatter.52
  1127.3 92.3 all-reduce.29
  1223.9 77.0 reduce-scatter.32
  1305.3 74.0 reduce-scatter.28
  1383.0 74.0 reduce-scatter.30
  1461.4 74.0 reduce-scatter.26
  1539.4 89.0 reduce-scatter.36
  1633.1 88.4 reduce-scatter.40
  1725.5 90.7 reduce-scatter.44
  1820.7 90.4 reduce-scatter.42
  1915.0 88.2 reduce-scatter.34
  2007.8 88.3 reduce-scatter.38
  2100.5 144.2 all-reduce.27
where the time goes:
time: 2280 us; the launch traced here: 2270 us
  waiting for transfers between devices  1540 us (68%)
  blocking collectives  341 us (15%)
  matrix products  218 us (10%)
  local copies, waits for them, and re-layouts  81.1 us (4%)
  other arithmetic  69 us (3%)
    unnamed x31, waiting for transfers between devices  283 us
    reduce_scatter x2, waiting for transfers between devices, body(): lax.psum_scatter(layer_terms[8].astype(jnp.bfloat16), 'fsdp', scatter_dim...  190 us
    reduce_scatter x2, waiting for transfers between devices, body(): lax.psum_scatter(layer_terms[7].astype(jnp.bfloat16), 'fsdp', scatter_dim...  186 us
    reduce_scatter x2, waiting for transfers between devices, body(): lax.psum_scatter(layer_terms[6].astype(jnp.bfloat16), 'fsdp', scatter_dim...  185 us
    reduce_scatter x2, waiting for transfers between devices, body(): lax.psum_scatter(layer_terms[1].astype(jnp.bfloat16), 'fsdp', scatter_dim...  157 us
    reduce_scatter x2, waiting for transfers between devices, body(): lax.psum_scatter(layer_terms[4].astype(jnp.bfloat16), 'fsdp', scatter_dim...  156 us
    all_gather x2, waiting for transfers between devices, body(): lax.all_gather(shards[8], 'fsdp', axis=0, tiled=True)  146 us
    psum x1, waiting for transfers between devices, body(): lax.psum(owned_grads[1].astype(jnp.bfloat16), 'rep').astype(jnp.float32)  92.9 us
  transfers between devices with their start and end apart: 26, of which 20 were waited for; matrix products, arithmetic and copies ran while one was open for 11% of the time, Pallas kernels for 0%

commit v1 on v0

v1 whole, which is shorter than its diff:
```python
import functools

import jax
import jax.numpy as jnp
from jax import lax
from jax.experimental import pallas as pl
from jax.experimental.pallas import tpu as pltpu
from jax.sharding import PartitionSpec as P

QUERY_HEADS = 15
KEY_VALUE_HEADS = 5
GROUP = QUERY_HEADS // KEY_VALUE_HEADS
HEAD = 64
DECODER_LAYERS = 2
X_SIZE = 4

epsilon_norm = 1e-05
rope_base = 100000.0
masked_score = -1e30

f32 = jnp.float32
bf16 = jnp.bfloat16

NT = (((1,), (1,)), ((), ()))


def swap(array, axis, mask):
    count = lax.axis_size(axis)
    return lax.ppermute(array, axis, [(i, i ^ mask) for i in range(count)])


def swap_core(array):
    return swap(array, "rep", 1)


def gather_pack(rows):
    pair = jnp.stack([rows, swap(rows, "fsdp", 4)])
    parts = [pair] + [swap(pair, "fsdp", m) for m in range(1, X_SIZE)]
    return jnp.concatenate(parts, axis=0).reshape(-1, rows.shape[-1])


BLOCK_ORDER = (0, 4, 1, 5, 2, 6, 3, 7)


def scatter_pack(rows):
    blocks = rows.reshape(X_SIZE, 2, -1, rows.shape[-1])
    total = blocks[0].astype(f32)
    for m in range(1, X_SIZE):
        total = total + swap(blocks[m], "fsdp", m).astype(f32)
    return total[0] + swap(total[1].astype(bf16), "fsdp", 4).astype(f32)


def x_groups():
    return [[z * X_SIZE + x for x in range(X_SIZE)] for z in range(2)]


def sum_over_x(rows):
    return lax.psum_scatter(
        rows, "fsdp", scatter_dimension=0, tiled=True, axis_index_groups=x_groups()
    )


def finish_sum(pair):
    mine_first = lax.axis_index("fsdp") < X_SIZE
    own = jnp.where(mine_first, pair[0], pair[1])
    away = jnp.where(mine_first, pair[1], pair[0])
    total = own.astype(f32) + swap(away, "fsdp", 4).astype(f32)
    total = total.astype(bf16)
    total = (total.astype(f32) + swap(total, "rep", 2).astype(f32)).astype(bf16)
    parts = [total] + [swap(total, "rep", 4 * m) for m in range(1, 4)]
    parts = [part.astype(f32) for part in parts]
    return ((parts[0] + parts[1]) + (parts[2] + parts[3])).astype(bf16)


def stacked_heads(array, kv_head):
    first = kv_head * GROUP
    return jnp.concatenate(
        [array[:, (first + g) * HEAD : (first + g + 1) * HEAD] for g in range(GROUP)], axis=0
    )


def attention_forward_kernel(q_ref, kv_ref, key_place_ref, bounds_ref, mixed_ref, log_ref, bias):
    rows = q_ref.shape[0]
    keys = kv_ref.shape[0]
    width = KEY_VALUE_HEADS * HEAD
    place = key_place_ref[...]
    bias[...] = jnp.where(
        (place >= bounds_ref[0:1, :]) & (place <= bounds_ref[1:2, :]), 0.0, masked_score
    )
    for h in range(KEY_VALUE_HEADS):
        queries = stacked_heads(q_ref[...], h)
        keys_h = kv_ref[:, h * HEAD : (h + 1) * HEAD]
        values_h = kv_ref[:, width + h * HEAD : width + (h + 1) * HEAD]
        scores = lax.dot_general(keys_h, queries, NT, preferred_element_type=f32) + bias[...]
        top = jnp.max(scores, axis=0, keepdims=True)
        weights = jnp.exp(scores - top)
        total = jnp.sum(weights, axis=0, keepdims=True)
        mixed = jnp.dot(
            values_h.T, weights.astype(bf16), preferred_element_type=f32
        ) * (1.0 / total)
        mixed = mixed.T.astype(bf16)
        for g in range(GROUP):
            j = h * GROUP + g
            mixed_ref[:, j * HEAD : (j + 1) * HEAD] = mixed[g * rows : (g + 1) * rows]
        log_ref[h : h + 1, :] = top + jnp.log(total)


def attention_backward_kernel(
    q_ref, kv_ref, key_place_ref, bounds_ref, mixed_ref, log_ref, grad_ref, dq_ref, dkv_ref
):
    rows = q_ref.shape[0]
    keys = kv_ref.shape[0]
    width = KEY_VALUE_HEADS * HEAD
    chunk = keys // 4
    for h in range(KEY_VALUE_HEADS):
        queries = stacked_heads(q_ref[...], h)
        grads = stacked_heads(grad_ref[...], h)
        mixed = stacked_heads(mixed_ref[...], h)
        product = (grads.astype(f32) * mixed.astype(f32)).T
        delta = jnp.sum(product, axis=0, keepdims=True)
        logs = log_ref[h : h + 1, :]
        dq = jnp.zeros((HEAD, GROUP * rows), f32)
        for part in range(4):
            span = slice(part * chunk, (part + 1) * chunk)
            place = key_place_ref[span, :]
            allowed = (place >= bounds_ref[0:1, :]) & (place <= bounds_ref[1:2, :])
            keys_h = kv_ref[span, h * HEAD : (h + 1) * HEAD]
            values_h = kv_ref[span, width + h * HEAD : width + (h + 1) * HEAD]
            scores = lax.dot_general(keys_h, queries, NT, preferred_element_type=f32)
            weights = jnp.exp(jnp.where(allowed, scores, masked_score) - logs)
            dweights = lax.dot_general(values_h, grads, NT, preferred_element_type=f32)
            dscores = (weights * (dweights - delta)).astype(bf16)
            dvalues = jnp.dot(weights.astype(bf16), grads, preferred_element_type=f32)
            dkeys = jnp.dot(dscores, queries, preferred_element_type=f32)
            dq = dq + jnp.dot(keys_h.T, dscores, preferred_element_type=f32)
            dkv_ref[span, h * HEAD : (h + 1) * HEAD] = dkeys.astype(bf16)
            dkv_ref[span, width + h * HEAD : width + (h + 1) * HEAD] = dvalues.astype(bf16)
        dq = dq.T * HEAD ** (-0.5)
        for g in range(GROUP):
            j = h * GROUP + g
            dq_ref[:, j * HEAD : (j + 1) * HEAD] = dq[g * rows : (g + 1) * rows]


def kernel_params():
    return pltpu.CompilerParams(vmem_limit_bytes=48 * 1024 * 1024)


def attend(queries, kv, key_place, bounds):
    rows, keys = queries.shape[0], kv.shape[0]
    pairs = QUERY_HEADS * rows * keys
    return pl.pallas_call(
        attention_forward_kernel,
        out_shape=(
            jax.ShapeDtypeStruct(queries.shape, bf16),
            jax.ShapeDtypeStruct((8, GROUP * rows), f32),
        ),
        scratch_shapes=[pltpu.VMEM((keys, GROUP * rows), f32)],
        compiler_params=kernel_params(),
        cost_estimate=pl.CostEstimate(
            flops=4 * pairs * HEAD, bytes_accessed=4 * 1024 * 1024, transcendentals=pairs
        ),
        name="attention_forward",
    )(queries, kv, key_place, bounds)


def attend_back(queries, kv, key_place, bounds, mixed, logs, grads):
    rows, keys = queries.shape[0], kv.shape[0]
    pairs = QUERY_HEADS * rows * keys
    return pl.pallas_call(
        attention_backward_kernel,
        out_shape=(
            jax.ShapeDtypeStruct(queries.shape, f32),
            jax.ShapeDtypeStruct(kv.shape, bf16),
        ),
        compiler_params=kernel_params(),
        cost_estimate=pl.CostEstimate(
            flops=10 * pairs * HEAD, bytes_accessed=6 * 1024 * 1024, transcendentals=pairs
        ),
        name="attention_backward",
    )(queries, kv, key_place, bounds, mixed, logs, grads)


def normalize(stream):
    return stream * lax.rsqrt(jnp.mean(stream * stream, axis=-1, keepdims=True) + epsilon_norm)


def normalize_back(stream, gain, grad):
    inverse = lax.rsqrt(jnp.mean(stream * stream, axis=-1, keepdims=True) + epsilon_norm)
    unit = stream * inverse
    scaled = grad * gain
    gain_grad = jnp.sum(grad * unit, axis=0)
    return inverse * (scaled - unit * jnp.mean(scaled * unit, axis=-1, keepdims=True)), gain_grad


def turn(flat):
    half = HEAD // 2
    ahead = jnp.concatenate([flat[:, half:], flat[:, :half]], axis=1)
    behind = jnp.concatenate([flat[:, -half:], flat[:, :-half]], axis=1)
    lane = lax.broadcasted_iota(jnp.int32, flat.shape, 1) % HEAD
    return jnp.where(lane < half, -ahead, behind)


def rotary(flat, cosine, sine):
    return flat * cosine[:, : flat.shape[1]] + turn(flat) * sine[:, : flat.shape[1]]


def rotary_back(flat, cosine, sine):
    return flat * cosine[:, : flat.shape[1]] - turn(flat * sine[:, : flat.shape[1]])


def matmul(left, right):
    return jnp.dot(left, right, preferred_element_type=f32)


def matmul_nt(left, right):
    return lax.dot_general(left, right, NT, preferred_element_type=f32)


def cross_rows(left, right):
    return lax.dot_general(left, right, (((0,), (0,)), ((), ())), preferred_element_type=f32)


def by_x(columns):
    rows, width = columns.shape
    blocks = columns.reshape(rows, 2, X_SIZE, width // (2 * X_SIZE))
    return blocks.swapaxes(1, 2).reshape(rows, width)


def body(
    tokens,
    seq_lengths,
    attn_gain,
    query_weight,
    key_projection,
    value_projection,
    out_weight,
    mlp_gain,
    gate_weight,
    up_weight,
    down_weight,
    cotangent,
):
    rows, width = tokens.shape
    shard = query_weight.shape[1]
    key_width = key_projection.shape[2]
    att_width = width + key_width
    half_width = width // 2
    me = lax.axis_index("fsdp")
    first_core = lax.axis_index("rep") % 2 == 0

    def pick(a, b):
        return jnp.where(first_core, a, b)

    def gathered(part):
        mine = lax.all_gather(part, "fsdp", axis=0, tiled=True)
        return mine, swap_core(mine)

    layers = []
    for l in range(DECODER_LAYERS):
        gains = jnp.stack([attn_gain[l], mlp_gain[l]])
        gains = jnp.pad(gains, ((0, 6), (0, att_width - shard)))
        own = pick(
            jnp.concatenate([query_weight[l], key_projection[l]], axis=1),
            jnp.concatenate([out_weight[l], value_projection[l]], axis=1),
        )
        mine, other = gathered(jnp.concatenate([own, gains], axis=0))
        blocks = mine.reshape(-1, shard + 8, att_width)
        gain_attn = blocks[:, shard, :shard].reshape(width).astype(f32)
        gain_mlp = blocks[:, shard + 1, :shard].reshape(width).astype(f32)
        mine = blocks[:, :shard].reshape(width, att_width)
        other = other.reshape(-1, shard + 8, att_width)[:, :shard].reshape(width, att_width)
        query_key = pick(mine, other)
        out_value = pick(other, mine)
        gate_up = gathered(pick(gate_weight[l], up_weight[l]))
        down = gathered(pick(down_weight[l][:, :half_width], down_weight[l][:, half_width:]))
        layers.append((gain_attn, gain_mlp, query_key, out_value, gate_up, down))

    lengths = seq_lengths[0]
    ends = jnp.cumsum(lengths)
    starts = ends - lengths
    places = me * rows + jnp.arange(rows, dtype=jnp.int32)
    segment = jnp.sum((places[:, None] >= ends[None, :-1]).astype(jnp.int32), axis=1)
    chosen = segment[:, None] == jnp.arange(lengths.shape[0], dtype=jnp.int32)[None, :]
    start = jnp.sum(chosen.astype(jnp.int32) * starts[None, :], axis=1)
    offsets = (places - start).astype(f32)
    frequency = rope_base ** (-(jnp.arange(HEAD // 2, dtype=f32) * 2.0) / HEAD)
    angles = offsets[:, None] * frequency[None, :]
    cosine = jnp.tile(jnp.cos(angles), (1, 2 * QUERY_HEADS))
    sine = jnp.tile(jnp.sin(angles), (1, 2 * QUERY_HEADS))
    bounds = jnp.stack([jnp.tile(start, GROUP), jnp.tile(places, GROUP)])
    bounds = jnp.pad(bounds, ((0, 6), (0, 0)))
    blocks = jnp.bitwise_xor(me, jnp.array(BLOCK_ORDER, jnp.int32))
    key_place = blocks[:, None] * rows + jnp.arange(rows, dtype=jnp.int32)[None, :]
    key_place = key_place.reshape(-1, 1)

    stream = tokens.astype(f32)
    saved = []
    for l in range(DECODER_LAYERS):
        gain_attn, gain_mlp, query_key, out_value, gate_up, down = layers[l]
        normed = (normalize(stream) * gain_attn).astype(bf16)
        values = matmul(normed, out_value[:, width:]).astype(bf16)
        projected = matmul(normed, query_key)
        keys = rotary(projected[:, width:], cosine, sine).astype(bf16)
        kv = gather_pack(jnp.concatenate([keys, values], axis=1))
        queries = rotary(projected[:, :width], cosine, sine).astype(bf16)
        queries = queries * jnp.asarray(HEAD ** (-0.5), bf16)
        mixed, logs = attend(queries, kv, key_place, bounds)
        middle = stream + matmul(mixed, out_value[:, :width])
        normed_mlp = (normalize(middle) * gain_mlp).astype(bf16)
        mine = matmul(normed_mlp, gate_up[0])
        other = matmul(normed_mlp, gate_up[1])
        gate, up = pick(mine, other), pick(other, mine)
        sigmoid = jax.nn.sigmoid(gate)
        hidden = (gate * sigmoid * up).astype(bf16)
        mine = matmul(hidden, down[0])
        other = matmul(hidden, down[1])
        saved.append((stream, normed, queries, kv, logs, mixed, middle, normed_mlp, gate, up, hidden))
        stream = middle + jnp.concatenate([pick(mine, other), pick(other, mine)], axis=1)
    output = stream.astype(bf16)

    def finish(pair_parts, names):
        widths = [part.shape[-1] for part in pair_parts]
        joined = jnp.concatenate(pair_parts, axis=-1) if len(pair_parts) > 1 else pair_parts[0]
        return finish_sum(joined)

    grad = cotangent.astype(f32)
    results = [None] * DECODER_LAYERS
    for l in reversed(range(DECODER_LAYERS)):
        gain_attn, gain_mlp, query_key, out_value, gate_up, down = layers[l]
        stream, normed, queries, kv, logs, mixed, middle, normed_mlp, gate, up, hidden = saved[l]
        grad_low = grad.astype(bf16)
        grad_a, grad_b = grad_low[:, :half_width], grad_low[:, half_width:]
        grad_mine, grad_other = pick(grad_a, grad_b), pick(grad_b, grad_a)
        hidden_x = by_x(hidden)
        received = swap_core(cross_rows(hidden_x, grad_other).astype(bf16))
        down_sum = (cross_rows(hidden_x, grad_mine) + received.astype(f32)).astype(bf16)
        down_sum = sum_over_x(down_sum)

        dhidden = matmul_nt(grad_mine, down[0]) + matmul_nt(grad_other, down[1])
        sigmoid = jax.nn.sigmoid(gate)
        dgate = (dhidden * up * sigmoid * (1.0 + gate * (1.0 - sigmoid))).astype(bf16)
        dup = (dhidden * gate * sigmoid).astype(bf16)
        dmine, dother = pick(dgate, dup), pick(dup, dgate)
        mlp_x = by_x(normed_mlp)
        received = swap_core(cross_rows(mlp_x, dother).astype(bf16))
        gate_up_sum = (cross_rows(mlp_x, dmine) + received.astype(f32)).astype(bf16)
        gate_up_sum = sum_over_x(gate_up_sum)

        dnormed = matmul_nt(dmine, gate_up[0]) + matmul_nt(dother, gate_up[1])
        dmiddle, mlp_gain_grad = normalize_back(middle, gain_mlp, dnormed)
        dmiddle = dmiddle + grad
        dmiddle_low = dmiddle.astype(bf16)
        dmixed = matmul_nt(dmiddle_low, out_value[:, :width]).astype(bf16)
        dq, dkv = attend_back(queries, kv, key_place, bounds, mixed, logs, dmixed)
        dkv = scatter_pack(dkv)
        dq = rotary_back(dq, cosine, sine).astype(bf16)
        dk = rotary_back(dkv[:, :key_width], cosine, sine).astype(bf16)
        dv = dkv[:, key_width:].astype(bf16)

        dqk = jnp.concatenate([dq, dk], axis=1)
        dnormed = matmul_nt(dqk, query_key) + matmul_nt(dv, out_value[:, width:])
        dstream, attn_gain_grad = normalize_back(stream, gain_attn, dnormed)
        grad = dstream + dmiddle

        normed_x, mixed_x = by_x(normed), by_x(mixed)

        def att_terms(first):
            wide = cross_rows(
                jnp.where(first, normed_x, mixed_x), jnp.where(first, dq, dmiddle_low)
            )
            return jnp.concatenate([wide, cross_rows(normed_x, jnp.where(first, dk, dv))], axis=1)

        received = swap_core(att_terms(jnp.logical_not(first_core)).astype(bf16))
        att_sum = (att_terms(first_core) + received.astype(f32)).astype(bf16)
        gain_grads = jnp.stack([attn_gain_grad, mlp_gain_grad]).astype(bf16)
        received = swap_core(gain_grads)
        gain_grads = by_x((gain_grads.astype(f32) + received.astype(f32)).astype(bf16))
        gain_grads = gain_grads.reshape(2, -1, shard).swapaxes(0, 1)
        gain_grads = jnp.pad(gain_grads, ((0, 0), (0, 6), (0, att_width - shard)))
        att_sum = jnp.concatenate([att_sum.reshape(-1, shard, att_width), gain_grads], axis=1)
        att_sum = sum_over_x(att_sum.reshape(-1, att_width))

        ffn = jnp.concatenate(
            [
                gate_up_sum.reshape(2, shard, -1),
                down_sum.reshape(2, -1, half_width).reshape(2, shard, -1),
            ],
            axis=2,
        )
        ffn = finish_sum(ffn)
        att = finish_sum(att_sum.reshape(2, shard + 8, att_width))
        ffn_other, att_other = swap_core(ffn), swap_core(att)
        ffn_a, ffn_b = pick(ffn, ffn_other), pick(ffn_other, ffn)
        att_a, att_b = pick(att, att_other), pick(att_other, att)
        hidden_width = gate_weight.shape[2]
        down_shape = (down_weight.shape[1], half_width)
        results[l] = (
            att[shard, :shard],
            att_a[:shard, :width],
            att_a[:shard, width:],
            att_b[:shard, width:],
            att_b[:shard, :width],
            att[shard + 1, :shard],
            ffn_a[:, :hidden_width],
            ffn_b[:, :hidden_width],
            jnp.concatenate(
                [
                    ffn_a[:, hidden_width:].reshape(down_shape),
                    ffn_b[:, hidden_width:].reshape(down_shape),
                ],
                axis=1,
            ),
        )
    stacked = [
        jnp.stack([results[l][m].astype(f32) for l in range(DECODER_LAYERS)], axis=0)
        for m in range(9)
    ]
    return (output, grad, *stacked)


def solution(mesh):
    weights = P(None, "fsdp", None)
    gains = P(None, "fsdp")
    packed = P(("rep", "fsdp"), None)
    in_specs = (
        packed,
        P("rep", None),
        gains,
        weights,
        weights,
        weights,
        weights,
        gains,
        weights,
        weights,
        weights,
        packed,
    )
    out_specs = (
        packed,
        packed,
        gains,
        weights,
        weights,
        weights,
        weights,
        gains,
        weights,
        weights,
        weights,
    )
    return jax.shard_map(body, mesh=mesh, in_specs=in_specs, out_specs=out_specs, check_vma=False)
```

time: 2280 us -> 1060 us (0.46)
  waiting for transfers between devices: 1540 us -> 614 us
  blocking collectives: 341 us -> 0 us
  matrix products: 218 us -> 112 us
  starting transfers between devices: 1.64 us -> 78.8 us
  Pallas kernels: 0 us -> 44 us
  local copies, waits for them, and re-layouts: 81.1 us -> 109 us
    reduce_scatter x10 -> x6, waiting for transfers between devices: 873 us -> 45.2 us  [sum_over_x(): lax.psum_scatter(rows, 'fsdp', scatter_dimension=0, tiled=True, axis_inde...]
    unnamed x31 -> x12, waiting for transfers between devices: 283 us -> 0.7 us
    all_gather x8 -> x0, blocking collectives: 277 us -> none  [the longest x2 71.5 us: body(): lax.all_gather(shards[2], 'fsdp', axis=0, tiled=True)]
    ppermute x0 -> x54, waiting for transfers between devices: none -> 246 us  [swap(): return lax.ppermute(array, axis, [(i, i ^ mask) for i in range(count)])]
    dot_general x54 -> x44, matrix products: 218 us -> 112 us  [the longest x16 43.6 us: cross_rows(): lax.dot_general(left, right, (((0,), (0,)), ((), ())), preferred_element_...]
    psum x1 -> x0, waiting for transfers between devices: 92.9 us -> none  [body(): lax.psum(owned_grads[1].astype(jnp.bfloat16), 'rep').astype(jnp.float32)]
    ppermute x0 -> x54, starting transfers between devices: none -> 77.9 us  [swap(): return lax.ppermute(array, axis, [(i, i ^ mask) for i in range(count)])]
    pallas_call x0 -> x4, Pallas kernels: none -> 44 us  [the longest x2 28.4 us: attend_back(): pl.pallas_call(attention_backward_kernel, out_shape=(jax.ShapeDtypeStruct...]
  transfers between devices with their start and end apart: 26 -> 66, of which waited for: 20 -> 40; matrix products, arithmetic and copies ran while one was open for 11% -> 22% of each run, Pallas kernels for 0% -> 3%
where the time goes in v1:
time: 1060 us; the launch traced here: 1050 us
  waiting for transfers between devices  614 us (58%)
  matrix products  112 us (11%)
  local copies, waits for them, and re-layouts  109 us (10%)
  starting transfers between devices  78.8 us (7%)
  other arithmetic  72.9 us (7%)
  Pallas kernels  44 us (4%)
  between operations  16.6 us (2%)
    all_gather x6, waiting for transfers between devices, gathered(): mine = lax.all_gather(part, 'fsdp', axis=0, tiled=True)  321 us
    ppermute x54, waiting for transfers between devices, swap(): return lax.ppermute(array, axis, [(i, i ^ mask) for i in range(count)])  246 us
    ppermute x54, starting transfers between devices, swap(): return lax.ppermute(array, axis, [(i, i ^ mask) for i in range(count)])  77.9 us
    reduce_scatter x6, waiting for transfers between devices, sum_over_x(): lax.psum_scatter(rows, 'fsdp', scatter_dimension=0, tiled=True, axis_inde...  45.2 us
    dot_general x16, matrix products, cross_rows(): lax.dot_general(left, right, (((0,), (0,)), ((), ())), preferred_element_...  43.6 us
    dot_general x14, matrix products, matmul_nt(): return lax.dot_general(left, right, NT, preferred_element_type=f32)  38.4 us
    dot_general x14, matrix products, matmul(): return jnp.dot(left, right, preferred_element_type=f32)  29.6 us
    pallas_call x2, Pallas kernels, attend_back(): pl.pallas_call(attention_backward_kernel, out_shape=(jax.ShapeDtypeStruct...  28.4 us
  transfers between devices with their start and end apart: 66, of which 40 were waited for; matrix products, arithmetic and copies ran while one was open for 22% of the time, Pallas kernels for 3%

profile of v1, /device:TPU:5, one launch (start us, length us, event | category | flops | bytes accessed | tf_op | source)
XLA Modules:
  0.0 1046.7 jit_solution(2780399224658982)
XLA Ops:
  18.7 52.4 %all-gather.9.cloned.1.call-done = bf16[1024,1280]{1,0:T(8,128)(2,1)} async-done(((bf16[128,1280]{1,0:T(8,128)(2,1)}), bf16[1024,1280]{1,0:T(8,128)(2,1)}) %all-gather.9.cloned.1.call-update) | async-done | bytes 2621456 | tf_op jit(solution)/shard_map/all_gather | solution.py:255
  74.4 57.1 %all-gather.11.cloned.1.call-done = bf16[2560,480]{1,0:T(8,128)(2,1)} async-done(((bf16[320,480]{1,0:T(8,128)(2,1)}), bf16[2560,480]{1,0:T(8,128)(2,1)}) %all-gather.11.cloned.1.call-update) | async-done | bytes 2457616 | tf_op jit(solution)/shard_map/all_gather | solution.py:255
  131.5 4.4 copy.237
  137.2 54.7 %all-gather.15.cloned.1.call-done = bf16[2560,480]{1,0:T(8,128)(2,1)} async-done(((bf16[320,480]{1,0:T(8,128)(2,1)}), bf16[2560,480]{1,0:T(8,128)(2,1)}) %all-gather.15.cloned.1.call-update) | async-done | bytes 2457616 | tf_op jit(solution)/shard_map/all_gather | solution.py:255
  191.9 4.5 copy.243
  201.4 50.8 %all-gather.13.cloned.1.call-done = bf16[1024,1280]{1,0:T(8,128)(2,1)} async-done(((bf16[128,1280]{1,0:T(8,128)(2,1)}), bf16[1024,1280]{1,0:T(8,128)(2,1)}) %all-gather.13.cloned.1.call-update) | async-done | bytes 2621456 | tf_op jit(solution)/shard_map/all_gather | solution.py:255
  255.8 75.6 %all-gather.17.cloned.1.call-done = bf16[1,960,2560]{2,1,0:T(8,128)(2,1)} async-done(((bf16[1,120,2560]{2,1,0:T(8,128)(2,1)}), bf16[1,960,2560]{2,1,0:T(8,128)(2,1)}) %all-gather.17.cloned.1.call-update) | async-done | bytes 4915216 | tf_op jit(solution)/shard_map/all_gather | solution.py:255
  338.6 4.3 broadcast_select_fusion
  349.9 15.9 %collective-permute-done.2 = bf16[2,176,640]{2,1,0:T(8,128)(2,1)S(1)} collective-permute-done((bf16[2,176,640]{2,1,0:T(8,128)(2,1)S(1)}, bf16[2,176,640]{2,1,0:T(8,128)(2,1)S(1)}, u32[]{:S(2)}, u32[]{:S(2)}) %collective-permute-start.2) | collective-permute-done | bytes 450592 | tf_op jit(solution)/shard_map/ppermute | solution.py:29
  367.3 7.5 collective-permute-done.3
  375.9 7.8 attention_forward.2
  385.4 30.8 %all-gather.19.cloned.1.call-done = bf16[1,960,2560]{2,1,0:T(8,128)(2,1)} async-done(((bf16[1,120,2560]{2,1,0:T(8,128)(2,1)}), bf16[1,960,2560]{2,1,0:T(8,128)(2,1)}) %all-gather.19.cloned.1.call-update) | async-done | bytes 4915216 | tf_op jit(solution)/shard_map/all_gather | solution.py:255
  421.3 6.2 multiply_convert_fusion.5
  437.0 8.3 collective-permute-done.8
  452.9 4.6 collective-permute-done.9
  459.4 8.1 collective-permute-done.10
  473.9 7.8 attention_forward.3
  498.6 4.9 multiply_reduce_fusion
  509.9 14.3 %attention_backward.2 = (f32[176,960]{1,0:T(8,128)S(1)}, bf16[1408,640]{1,0:T(8,128)(2,1)S(1)}) custom-call(bf16[176,960]{1,0:T(8,128)(2,1)S(1)} %fusion.85.q_ref, bf16[1408,640]{1,0:T(8,128)(2,1)S(1)} %bitcast.196, s32[1408,1]{1,0:T(8,128)S(1)} %add.387.key_place_ref, s32[8,528]{1,0:T(8,128)S(1)} %pad.19.bounds_ref, ...), custom_call_target="tpu_custom_call" | custom-call | flops 2378956800 | bytes 6291456 | tf_op jit(solution)/shard_map/attention_backward/pallas_call | solution.py:169
  539.0 9.4 collective-permute-done.15
  564.4 5.9 collective-permute-start.29
  631.6 4.4 copy.274
  636.4 4.7 multiply_convert_fusion
  641.2 4.7 fusion.93
  646.0 4.4 multiply_reduce_fusion.2
  652.8 14.1 %attention_backward.3 = (f32[176,960]{1,0:T(8,128)S(1)}, bf16[1408,640]{1,0:T(8,128)(2,1)S(1)}) custom-call(bf16[176,960]{1,0:T(8,128)(2,1)S(1)} %fusion.84.q_ref, bf16[1408,640]{1,0:T(8,128)(2,1)S(1)} %bitcast.194, s32[1408,1]{1,0:T(8,128)S(1)} %add.387.key_place_ref, s32[8,528]{1,0:T(8,128)S(1)} %pad.19.bounds_ref, ...), custom_call_target="tpu_custom_call" | custom-call | flops 2378956800 | bytes 6291456 | tf_op jit(solution)/shard_map/attention_backward/pallas_call | solution.py:169
  672.7 8.1 collective-permute-done.18
  680.8 10.9 %collective-permute-done.19 = bf16[2,176,640]{2,1,0:T(8,128)(2,1)S(1)} collective-permute-done((bf16[2,176,640]{2,1,0:T(8,128)(2,1)S(1)}, bf16[2,176,640]{2,1,0:T(8,128)(2,1)S(1)}, u32[]{:S(2)}, u32[]{:S(2)}) %collective-permute-start.19) | collective-permute-done | bytes 450592 | tf_op jit(solution)/shard_map/ppermute | solution.py:29
  695.0 4.9 collective-permute-done.21
  700.0 4.3 add_convert_fusion.3
  704.3 4.4 copy.272
  731.2 4.3 fusion.2
  738.3 6.1 add_convert_fusion
  750.3 8.2 collective-permute-done.38
  763.5 10.6 %collective-permute-done.31 = bf16[128,1280]{1,0:T(8,128)(2,1)S(1)} collective-permute-done((bf16[128,1280]{1,0:T(8,128)(2,1)S(1)}, bf16[128,1280]{1,0:T(8,128)(2,1)S(1)}, u32[]{:S(2)}, u32[]{:S(2)}) %collective-permute-start.31) | collective-permute-done | bytes 327712 | tf_op jit(solution)/shard_map/ppermute | solution.py:29
  791.2 9.3 collective-permute-done.34
  807.6 8.2 collective-permute-done.25
  819.9 4.7 collective-permute-done.26
  824.6 6.9 collective-permute-done.27
  844.5 45.2 %reduce-scatter.15.cloned.1.call-done = bf16[240,2560]{1,0:T(8,128)(2,1)} async-done(((bf16[960,2560]{1,0:T(8,128)(2,1)}), bf16[240,2560]{1,0:T(8,128)(2,1)}) %reduce-scatter.15.cloned.1.call-update) | async-done | bytes 1228816 | tf_op jit(solution)/shard_map/reduce_scatter | solution.py:58
  896.1 18.0 %collective-permute-done.40 = bf16[120,3840]{1,0:T(8,128)(2,1)S(1)} collective-permute-done((bf16[120,3840]{1,0:T(8,128)(2,1)S(1)}, bf16[120,3840]{1,0:T(8,128)(2,1)S(1)}, u32[]{:S(2)}, u32[]{:S(2)}) %collective-permute-start.40) | collective-permute-done | bytes 921632 | tf_op jit(solution)/shard_map/ppermute | solution.py:29
  916.0 18.2 %collective-permute-done.49 = bf16[120,3840]{1,0:T(8,128)(2,1)S(1)} collective-permute-done((bf16[120,3840]{1,0:T(8,128)(2,1)S(1)}, bf16[120,3840]{1,0:T(8,128)(2,1)S(1)}, u32[]{:S(2)}, u32[]{:S(2)}) %collective-permute-start.49) | collective-permute-done | bytes 921632 | tf_op jit(solution)/shard_map/ppermute | solution.py:29
  938.3 15.6 %collective-permute-done.41 = bf16[120,3840]{1,0:T(8,128)(2,1)S(1)} collective-permute-done((bf16[120,3840]{1,0:T(8,128)(2,1)S(1)}, bf16[120,3840]{1,0:T(8,128)(2,1)S(1)}, u32[]{:S(2)}, u32[]{:S(2)}) %collective-permute-start.41) | collective-permute-done | bytes 921632 | tf_op jit(solution)/shard_map/ppermute | solution.py:29
  958.1 17.8 %collective-permute-done.51 = bf16[120,3840]{1,0:T(8,128)(2,1)S(1)} collective-permute-done((bf16[120,3840]{1,0:T(8,128)(2,1)S(1)}, bf16[120,3840]{1,0:T(8,128)(2,1)S(1)}, u32[]{:S(2)}, u32[]{:S(2)}) %collective-permute-start.51) | collective-permute-done | bytes 921632 | tf_op jit(solution)/shard_map/ppermute | solution.py:29
  976.4 9.0 collective-permute-start.53
  985.4 8.1 collective-permute-done.42
  993.4 22.0 %collective-permute-done.43 = bf16[120,3840]{1,0:T(8,128)(2,1)S(1)} collective-permute-done((bf16[120,3840]{1,0:T(8,128)(2,1)S(1)}, bf16[120,3840]{1,0:T(8,128)(2,1)S(1)}, u32[]{:S(2)}, u32[]{:S(2)}) %collective-permute-start.43) | collective-permute-done | bytes 921632 | tf_op jit(solution)/shard_map/ppermute | solution.py:29
  1015.9 6.1 collective-permute-start.45
  (600 shorter events, 311.6 us)
Async XLA Ops:
  7.2 63.9 %all-gather.9.cloned.1.call-start = ((), (), s32[]{:S(2)}) async-start(), calls=%async_computation.6 | async-start | bytes 2949120 | tf_op jit(solution)/shard_map/all_gather | solution.py:255
  11.9 119.6 %all-gather.11.cloned.1.call-start = ((), (), s32[]{:S(2)}) async-start(), calls=%async_computation.7 | async-start | bytes 2949120 | tf_op jit(solution)/shard_map/all_gather | solution.py:255
  12.9 179.0 %all-gather.15.cloned.1.call-start = ((), (), s32[]{:S(2)}) async-start(), calls=%async_computation.9 | async-start | bytes 2949120 | tf_op jit(solution)/shard_map/all_gather | solution.py:255
  13.9 238.3 %all-gather.13.cloned.1.call-start = ((), (), s32[]{:S(2)}) async-start(), calls=%async_computation.8 | async-start | bytes 2949120 | tf_op jit(solution)/shard_map/all_gather | solution.py:255
  15.1 316.3 %all-gather.17.cloned.1.call-start = ((), (), s32[]{:S(2)}) async-start(), calls=%async_computation.14 | async-start | bytes 5529600 | tf_op jit(solution)/shard_map/all_gather | solution.py:255
  17.7 398.5 %all-gather.19.cloned.1.call-start = ((), (), s32[]{:S(2)}) async-start(), calls=%async_computation.15 | async-start | bytes 5529600 | tf_op jit(solution)/shard_map/all_gather | solution.py:255
  18.2 743.9 %reduce-scatter.13.cloned.1.call-start = ((), (), s32[]{:S(2)}) async-start(), calls=%async_computation.11 | async-start | bytes 3276800 | tf_op jit(solution)/shard_map/reduce_scatter | solution.py:58
  71.1 261.4 %collective-permute-start = (bf16[1024,1280]{1,0:T(8,128)(2,1)}, bf16[1024,1280]{1,0:T(8,128)(2,1)}, u32[]{:S(2)}, u32[]{:S(2)}) collective-permute-start(bf16[1024,1280]{1,0:T(8,128)(2,1)} %all-gather.9.cloned.1.call-done), channel_id=1, source_target_pairs={{0,8},{8,0},{16,24},{24,16},{32,40},{40,32},{48,56},{56,48},{64,72... | collective-permute-start | bytes 7864328 | tf_op jit(solution)/shard_map/ppermute | solution.py:29
  135.9 292.3 %collective-permute-start.6 = (bf16[2560,480]{0,1:T(8,128)(2,1)}, bf16[2560,480]{0,1:T(8,128)(2,1)}, u32[]{:S(2)}, u32[]{:S(2)}) collective-permute-start(bf16[2560,480]{0,1:T(8,128)(2,1)} %copy.237), channel_id=1, source_target_pairs={{0,8},{8,0},{16,24},{24,16},{32,40},{40,32},{48,56},{56,48},{64,72... | collective-permute-start | bytes 7372808 | tf_op jit(solution)/shard_map/ppermute | solution.py:29
  252.2 85.9 %collective-permute-start.7 = (bf16[1024,1280]{1,0:T(8,128)(2,1)}, bf16[1024,1280]{1,0:T(8,128)(2,1)}, u32[]{:S(2)}, u32[]{:S(2)}) collective-permute-start(bf16[1024,1280]{1,0:T(8,128)(2,1)} %all-gather.13.cloned.1.call-done), channel_id=1, source_target_pairs={{0,8},{8,0},{16,24},{24,16},{32,40},{40,32},{48,56},{56,48},{64,72... | collective-permute-start | bytes 7864328 | tf_op jit(solution)/shard_map/ppermute | solution.py:29
  331.4 89.9 %collective-permute-start.5 = (bf16[960,2560]{1,0:T(8,128)(2,1)}, bf16[960,2560]{1,0:T(8,128)(2,1)}, u32[]{:S(2)}, u32[]{:S(2)}) collective-permute-start(bf16[960,2560]{1,0:T(8,128)(2,1)} %bitcast.197), channel_id=1, source_target_pairs={{0,8},{8,0},{16,24},{24,16},{32,40},{40,32},{48,56},{56,48},{64,72... | collective-permute-start | bytes 14745608 | tf_op jit(solution)/shard_map/ppermute | solution.py:29
  346.7 19.1 %collective-permute-start.2 = (bf16[2,176,640]{2,1,0:T(8,128)(2,1)S(1)}, bf16[2,176,640]{2,1,0:T(8,128)(2,1)S(1)}, u32[]{:S(2)}, u32[]{:S(2)}) collective-permute-start(bf16[2,176,640]{2,1,0:T(8,128)(2,1)S(1)} %pad_maximum_fusion.4), channel_id=1, source_target_pairs={{0,1},{1,0},{2,3},{3,2},{4,5},{5,4},{6,7},{7,6},{8,9},{9,8},{10,11... | collective-permute-start | bytes 1351688 | tf_op jit(solution)/shard_map/ppermute | solution.py:29
  347.3 27.6 %collective-permute-start.3 = (bf16[2,176,640]{2,1,0:T(8,128)(2,1)S(1)}, bf16[2,176,640]{2,1,0:T(8,128)(2,1)S(1)}, u32[]{:S(2)}, u32[]{:S(2)}) collective-permute-start(bf16[2,176,640]{2,1,0:T(8,128)(2,1)S(1)} %pad_maximum_fusion.4), channel_id=1, source_target_pairs={{0,2},{1,3},{2,0},{3,1},{4,6},{5,7},{6,4},{7,5},{8,10},{9,11},{10,... | collective-permute-start | bytes 1351688 | tf_op jit(solution)/shard_map/ppermute | solution.py:29
  349.0 26.8 %collective-permute-start.4 = (bf16[2,176,640]{2,1,0:T(8,128)(2,1)S(1)}, bf16[2,176,640]{2,1,0:T(8,128)(2,1)S(1)}, u32[]{:S(2)}, u32[]{:S(2)}) collective-permute-start(bf16[2,176,640]{2,1,0:T(8,128)(2,1)S(1)} %pad_maximum_fusion.4), channel_id=1, source_target_pairs={{0,3},{1,2},{2,1},{3,0},{4,7},{5,6},{6,5},{7,4},{8,11},{9,10},{10,... | collective-permute-start | bytes 1351688 | tf_op jit(solution)/shard_map/ppermute | solution.py:29
  365.8 126.9 %collective-permute-start.13 = (bf16[2560,480]{0,1:T(8,128)(2,1)}, bf16[2560,480]{0,1:T(8,128)(2,1)}, u32[]{:S(2)}, u32[]{:S(2)}) collective-permute-start(bf16[2560,480]{0,1:T(8,128)(2,1)} %copy.243), channel_id=1, source_target_pairs={{0,8},{8,0},{16,24},{24,16},{32,40},{40,32},{48,56},{56,48},{64,72... | collective-permute-start | bytes 7372808 | tf_op jit(solution)/shard_map/ppermute | solution.py:29
  416.2 72.8 %collective-permute-start.12 = (bf16[960,2560]{1,0:T(8,128)(2,1)}, bf16[960,2560]{1,0:T(8,128)(2,1)}, u32[]{:S(2)}, u32[]{:S(2)}) collective-permute-start(bf16[960,2560]{1,0:T(8,128)(2,1)} %bitcast.198), channel_id=1, source_target_pairs={{0,8},{8,0},{16,24},{24,16},{32,40},{40,32},{48,56},{56,48},{64,72... | collective-permute-start | bytes 14745608 | tf_op jit(solution)/shard_map/ppermute | solution.py:29
  446.6 20.9 %collective-permute-start.10 = (bf16[2,176,640]{2,1,0:T(8,128)(2,1)}, bf16[2,176,640]{2,1,0:T(8,128)(2,1)}, u32[]{:S(2)}, u32[]{:S(2)}) collective-permute-start(bf16[2,176,640]{2,1,0:T(8,128)(2,1)} %pad_maximum_fusion.5), channel_id=1, source_target_pairs={{0,2},{1,3},{2,0},{3,1},{4,6},{5,7},{6,4},{7,5},{8,10},{9,11},{10,... | collective-permute-start | bytes 1351688 | tf_op jit(solution)/shard_map/ppermute | solution.py:29
  451.1 20.5 %collective-permute-start.11 = (bf16[2,176,640]{2,1,0:T(8,128)(2,1)}, bf16[2,176,640]{2,1,0:T(8,128)(2,1)S(1)}, u32[]{:S(2)}, u32[]{:S(2)}) collective-permute-start(bf16[2,176,640]{2,1,0:T(8,128)(2,1)} %pad_maximum_fusion.5), channel_id=1, source_target_pairs={{0,3},{1,2},{2,1},{3,0},{4,7},{5,6},{6,5},{7,4},{8,11},{9,10},{10,... | collective-permute-start | bytes 1351688 | tf_op jit(solution)/shard_map/ppermute | solution.py:29
  530.3 18.1 %collective-permute-start.15 = (bf16[2,176,640]{2,1,0:T(8,128)(2,1)}, bf16[2,176,640]{2,1,0:T(8,128)(2,1)}, u32[]{:S(2)}, u32[]{:S(2)}) collective-permute-start(bf16[2,176,640]{2,1,0:T(8,128)(2,1)} %bitcast.34), channel_id=1, source_target_pairs={{0,2},{1,3},{2,0},{3,1},{4,6},{5,7},{6,4},{7,5},{8,10},{9,11},{10,... | collective-permute-start | bytes 1351688 | tf_op jit(solution)/shard_map/ppermute | solution.py:29
  530.3 18.1 %collective-permute-start.16 = (bf16[2,176,640]{2,1,0:T(8,128)(2,1)}, bf16[2,176,640]{2,1,0:T(8,128)(2,1)}, u32[]{:S(2)}, u32[]{:S(2)}) collective-permute-start(bf16[2,176,640]{2,1,0:T(8,128)(2,1)} %bitcast.35), channel_id=1, source_target_pairs={{0,3},{1,2},{2,1},{3,0},{4,7},{5,6},{6,5},{7,4},{8,11},{9,10},{10,... | collective-permute-start | bytes 1351688 | tf_op jit(solution)/shard_map/ppermute | solution.py:29
  564.4 14.5 %collective-permute-start.29 = (bf16[960,1280]{1,0:T(8,128)(2,1)}, bf16[960,1280]{1,0:T(8,128)(2,1)}, u32[]{:S(2)}, u32[]{:S(2)}) collective-permute-start(bf16[960,1280]{1,0:T(8,128)(2,1)} %pad_maximum_fusion.1), channel_id=1, source_target_pairs={{0,8},{8,0},{16,24},{24,16},{32,40},{40,32},{48,56},{56,48},{64,72... | collective-permute-start | bytes 7372808 | tf_op jit(solution)/shard_map/ppermute | solution.py:29
  584.8 192.4 %reduce-scatter.21.cloned.1.call-start = ((), (), s32[]{:S(2)}) async-start(), calls=%async_computation.17 | async-start | bytes 3276800 | tf_op jit(solution)/shard_map/reduce_scatter | solution.py:58
  599.3 28.1 %collective-permute-start.47 = (bf16[2560,480]{0,1:T(8,128)(2,1)}, bf16[2560,480]{0,1:T(8,128)(2,1)}, u32[]{:S(2)}, u32[]{:S(2)}) collective-permute-start(bf16[2560,480]{0,1:T(8,128)(2,1)} %convolution_convert_fusion.2), channel_id=1, source_target_pairs={{0,8},{8,0},{16,24},{24,16},{32,40},{40,32},{48,56},{56,48},{64,72... | collective-permute-start | bytes 7372808 | tf_op jit(solution)/shard_map/ppermute | solution.py:29
  625.2 74.9 %collective-permute-start.39 = (bf16[2560,480]{0,1:T(8,128)(2,1)}, bf16[2560,480]{0,1:T(8,128)(2,1)}, u32[]{:S(2)}, u32[]{:S(2)}) collective-permute-start(bf16[2560,480]{0,1:T(8,128)(2,1)} %convolution_convert_fusion.3), channel_id=1, source_target_pairs={{0,8},{8,0},{16,24},{24,16},{32,40},{40,32},{48,56},{56,48},{64,72... | collective-permute-start | bytes 7372808 | tf_op jit(solution)/shard_map/ppermute | solution.py:29
  636.0 143.7 %reduce-scatter.19.cloned.1.call-start = ((), (), s32[]{:S(2)}) async-start(), calls=%async_computation.16 | async-start | bytes 3276800 | tf_op jit(solution)/shard_map/reduce_scatter | solution.py:58
  670.7 21.1 %collective-permute-start.19 = (bf16[2,176,640]{2,1,0:T(8,128)(2,1)S(1)}, bf16[2,176,640]{2,1,0:T(8,128)(2,1)S(1)}, u32[]{:S(2)}, u32[]{:S(2)}) collective-permute-start(bf16[2,176,640]{2,1,0:T(8,128)(2,1)S(1)} %bitcast.242), channel_id=1, source_target_pairs={{0,2},{1,3},{2,0},{3,1},{4,6},{5,7},{6,4},{7,5},{8,10},{9,11},{10,... | collective-permute-start | bytes 1351688 | tf_op jit(solution)/shard_map/ppermute | solution.py:29
  671.7 20.9 %collective-permute-start.20 = (bf16[2,176,640]{2,1,0:T(8,128)(2,1)S(1)}, bf16[2,176,640]{2,1,0:T(8,128)(2,1)S(1)}, u32[]{:S(2)}, u32[]{:S(2)}) collective-permute-start(bf16[2,176,640]{2,1,0:T(8,128)(2,1)S(1)} %bitcast.241), channel_id=1, source_target_pairs={{0,3},{1,2},{2,1},{3,0},{4,7},{5,6},{6,5},{7,4},{8,11},{9,10},{10,... | collective-permute-start | bytes 1351688 | tf_op jit(solution)/shard_map/ppermute | solution.py:29
  708.7 79.0 %reduce-scatter.11.cloned.1.call-start = ((), (), s32[]{:S(2)}) async-start(), calls=%async_computation.10 | async-start | bytes 3276800 | tf_op jit(solution)/shard_map/reduce_scatter | solution.py:58
  715.2 16.0 %collective-permute-start.22 = (bf16[960,1280]{1,0:T(8,128)(2,1)}, bf16[960,1280]{1,0:T(8,128)(2,1)}, u32[]{:S(2)}, u32[]{:S(2)}) collective-permute-start(bf16[960,1280]{1,0:T(8,128)(2,1)} %pad_maximum_fusion), channel_id=1, source_target_pairs={{0,8},{8,0},{16,24},{24,16},{32,40},{40,32},{48,56},{56,48},{64,72... | collective-permute-start | bytes 7372808 | tf_op jit(solution)/shard_map/ppermute | solution.py:29
  722.7 14.6 %collective-permute-start.46 = (bf16[960,2560]{1,0:T(8,128)(2,1)}, bf16[960,2560]{1,0:T(8,128)(2,1)}, u32[]{:S(2)}, u32[]{:S(2)}) collective-permute-start(bf16[960,2560]{1,0:T(8,128)(2,1)} %convolution_convert_fusion), channel_id=1, source_target_pairs={{0,8},{8,0},{16,24},{24,16},{32,40},{40,32},{48,56},{56,48},{64,72... | collective-permute-start | bytes 14745608 | tf_op jit(solution)/shard_map/ppermute | solution.py:29
  737.3 102.0 %reduce-scatter.17.cloned.1.call-start = ((), (), s32[]{:S(2)}) async-start(), calls=%async_computation.13 | async-start | bytes 6144000 | tf_op jit(solution)/shard_map/reduce_scatter | solution.py:58
  744.4 145.3 %reduce-scatter.15.cloned.1.call-start = ((), (), s32[]{:S(2)}) async-start(), calls=%async_computation.12 | async-start | bytes 6144000 | tf_op jit(solution)/shard_map/reduce_scatter | solution.py:58
  785.1 15.3 %collective-permute-start.34 = (bf16[128,1280]{1,0:T(8,128)(2,1)S(1)}, bf16[128,1280]{1,0:T(8,128)(2,1)S(1)}, u32[]{:S(2)}, u32[]{:S(2)}) collective-permute-start(bf16[128,1280]{1,0:T(8,128)(2,1)S(1)} %add_convert_fusion.9), channel_id=1, source_target_pairs={{0,64},{8,72},{16,80},{24,88},{32,96},{40,104},{48,112},{56,120},{... | collective-permute-start | bytes 983048 | tf_op jit(solution)/shard_map/ppermute | solution.py:29
  787.5 15.5 %collective-permute-start.35 = (bf16[128,1280]{1,0:T(8,128)(2,1)S(1)}, bf16[128,1280]{1,0:T(8,128)(2,1)S(1)}, u32[]{:S(2)}, u32[]{:S(2)}) collective-permute-start(bf16[128,1280]{1,0:T(8,128)(2,1)S(1)} %add_convert_fusion.9), channel_id=1, source_target_pairs={{0,96},{8,104},{16,112},{24,120},{32,64},{40,72},{48,80},{56,88},{... | collective-permute-start | bytes 983048 | tf_op jit(solution)/shard_map/ppermute | solution.py:29
  788.9 17.3 %collective-permute-start.24 = (bf16[128,1280]{1,0:T(8,128)(2,1)S(1)}, bf16[128,1280]{1,0:T(8,128)(2,1)S(1)}, u32[]{:S(2)}, u32[]{:S(2)}) collective-permute-start(bf16[128,1280]{1,0:T(8,128)(2,1)S(1)} %broadcast_select_fusion.33), channel_id=1, source_target_pairs={{0,4},{1,5},{2,6},{3,7},{4,0},{5,1},{6,2},{7,3},{8,12},{9,13},{10,... | collective-permute-start | bytes 983048 | tf_op jit(solution)/shard_map/ppermute | solution.py:29
  816.0 15.5 %collective-permute-start.27 = (bf16[128,1280]{1,0:T(8,128)(2,1)S(1)}, bf16[128,1280]{1,0:T(8,128)(2,1)S(1)}, u32[]{:S(2)}, u32[]{:S(2)}) collective-permute-start(bf16[128,1280]{1,0:T(8,128)(2,1)S(1)} %add_convert_fusion.12), channel_id=1, source_target_pairs={{0,64},{8,72},{16,80},{24,88},{32,96},{40,104},{48,112},{56,120},{... | collective-permute-start | bytes 983048 | tf_op jit(solution)/shard_map/ppermute | solution.py:29
  817.3 16.2 %collective-permute-start.28 = (bf16[128,1280]{1,0:T(8,128)(2,1)S(1)}, bf16[128,1280]{1,0:T(8,128)(2,1)S(1)}, u32[]{:S(2)}, u32[]{:S(2)}) collective-permute-start(bf16[128,1280]{1,0:T(8,128)(2,1)S(1)} %add_convert_fusion.12), channel_id=1, source_target_pairs={{0,96},{8,104},{16,112},{24,120},{32,64},{40,72},{48,80},{56,88},{... | collective-permute-start | bytes 983048 | tf_op jit(solution)/shard_map/ppermute | solution.py:29
  841.8 52.4 %collective-permute-start.48 = (bf16[120,3840]{1,0:T(8,128)(2,1)}, bf16[120,3840]{1,0:T(8,128)(2,1)}, u32[]{:S(2)}, u32[]{:S(2)}) collective-permute-start(bf16[120,3840]{1,0:T(8,128)(2,1)} %select_bitcast_fusion), channel_id=1, source_target_pairs={{0,4},{1,5},{2,6},{3,7},{4,0},{5,1},{6,2},{7,3},{8,12},{9,13},{10,... | collective-permute-start | bytes 2764808 | tf_op jit(solution)/shard_map/ppermute | solution.py:29
  891.2 23.0 %collective-permute-start.40 = (bf16[120,3840]{1,0:T(8,128)(2,1)S(1)}, bf16[120,3840]{1,0:T(8,128)(2,1)S(1)}, u32[]{:S(2)}, u32[]{:S(2)}) collective-permute-start(bf16[120,3840]{1,0:T(8,128)(2,1)S(1)} %select_bitcast_fusion.1), channel_id=1, source_target_pairs={{0,4},{1,5},{2,6},{3,7},{4,0},{5,1},{6,2},{7,3},{8,12},{9,13},{10,... | collective-permute-start | bytes 2764808 | tf_op jit(solution)/shard_map/ppermute | solution.py:29
  895.7 38.5 %collective-permute-start.49 = (bf16[120,3840]{1,0:T(8,128)(2,1)S(1)}, bf16[120,3840]{1,0:T(8,128)(2,1)S(1)}, u32[]{:S(2)}, u32[]{:S(2)}) collective-permute-start(bf16[120,3840]{1,0:T(8,128)(2,1)S(1)} %fusion.6), channel_id=1, source_target_pairs={{0,16},{8,24},{16,0},{24,8},{32,48},{40,56},{48,32},{56,40},{64,80... | collective-permute-start | bytes 2764808 | tf_op jit(solution)/shard_map/ppermute | solution.py:29
  914.5 39.4 %collective-permute-start.41 = (bf16[120,3840]{1,0:T(8,128)(2,1)S(1)}, bf16[120,3840]{1,0:T(8,128)(2,1)S(1)}, u32[]{:S(2)}, u32[]{:S(2)}) collective-permute-start(bf16[120,3840]{1,0:T(8,128)(2,1)S(1)} %fusion.7), channel_id=1, source_target_pairs={{0,16},{8,24},{16,0},{24,8},{32,48},{40,56},{48,32},{56,40},{64,80... | collective-permute-start | bytes 2764808 | tf_op jit(solution)/shard_map/ppermute | solution.py:29
  934.4 23.5 %collective-permute-start.50 = (bf16[120,3840]{1,0:T(8,128)(2,1)S(1)}, bf16[120,3840]{1,0:T(8,128)(2,1)S(1)}, u32[]{:S(2)}, u32[]{:S(2)}) collective-permute-start(bf16[120,3840]{1,0:T(8,128)(2,1)S(1)} %add_convert_fusion.5), channel_id=1, source_target_pairs={{0,32},{8,40},{16,48},{24,56},{32,0},{40,8},{48,16},{56,24},{64,96... | collective-permute-start | bytes 2764808 | tf_op jit(solution)/shard_map/ppermute | solution.py:29
  935.7 40.2 %collective-permute-start.51 = (bf16[120,3840]{1,0:T(8,128)(2,1)S(1)}, bf16[120,3840]{1,0:T(8,128)(2,1)S(1)}, u32[]{:S(2)}, u32[]{:S(2)}) collective-permute-start(bf16[120,3840]{1,0:T(8,128)(2,1)S(1)} %add_convert_fusion.5), channel_id=1, source_target_pairs={{0,64},{8,72},{16,80},{24,88},{32,96},{40,104},{48,112},{56,120},{... | collective-permute-start | bytes 2764808 | tf_op jit(solution)/shard_map/ppermute | solution.py:29
  938.1 37.7 %collective-permute-start.52 = (bf16[120,3840]{1,0:T(8,128)(2,1)S(1)}, bf16[120,3840]{1,0:T(8,128)(2,1)S(1)}, u32[]{:S(2)}, u32[]{:S(2)}) collective-permute-start(bf16[120,3840]{1,0:T(8,128)(2,1)S(1)} %add_convert_fusion.5), channel_id=1, source_target_pairs={{0,96},{8,104},{16,112},{24,120},{32,64},{40,72},{48,80},{56,88},{... | collective-permute-start | bytes 2764808 | tf_op jit(solution)/shard_map/ppermute | solution.py:29
  954.1 39.3 %collective-permute-start.42 = (bf16[120,3840]{1,0:T(8,128)(2,1)S(1)}, bf16[120,3840]{1,0:T(8,128)(2,1)S(1)}, u32[]{:S(2)}, u32[]{:S(2)}) collective-permute-start(bf16[120,3840]{1,0:T(8,128)(2,1)S(1)} %add_convert_fusion.7), channel_id=1, source_target_pairs={{0,32},{8,40},{16,48},{24,56},{32,0},{40,8},{48,16},{56,24},{64,96... | collective-permute-start | bytes 2764808 | tf_op jit(solution)/shard_map/ppermute | solution.py:29
  955.4 60.0 %collective-permute-start.43 = (bf16[120,3840]{1,0:T(8,128)(2,1)S(1)}, bf16[120,3840]{1,0:T(8,128)(2,1)S(1)}, u32[]{:S(2)}, u32[]{:S(2)}) collective-permute-start(bf16[120,3840]{1,0:T(8,128)(2,1)S(1)} %add_convert_fusion.7), channel_id=1, source_target_pairs={{0,64},{8,72},{16,80},{24,88},{32,96},{40,104},{48,112},{56,120},{... | collective-permute-start | bytes 2764808 | tf_op jit(solution)/shard_map/ppermute | solution.py:29
  957.9 57.5 %collective-permute-start.44 = (bf16[120,3840]{1,0:T(8,128)(2,1)S(1)}, bf16[120,3840]{1,0:T(8,128)(2,1)S(1)}, u32[]{:S(2)}, u32[]{:S(2)}) collective-permute-start(bf16[120,3840]{1,0:T(8,128)(2,1)S(1)} %add_convert_fusion.7), channel_id=1, source_target_pairs={{0,96},{8,104},{16,112},{24,120},{32,64},{40,72},{48,80},{56,88},{... | collective-permute-start | bytes 2764808 | tf_op jit(solution)/shard_map/ppermute | solution.py:29
  976.4 45.6 %collective-permute-start.53 = (bf16[120,3840]{1,0:T(8,128)(2,1)S(1)}, bf16[120,3840]{1,0:T(8,128)(2,1)S(1)}, u32[]{:S(2)}, u32[]{:S(2)}) collective-permute-start(bf16[120,3840]{1,0:T(8,128)(2,1)S(1)} %add_convert_fusion.4), channel_id=1, source_target_pairs={{0,8},{8,0},{16,24},{24,16},{32,40},{40,32},{48,56},{56,48},{64,72... | collective-permute-start | bytes 2764808 | tf_op jit(solution)/shard_map/ppermute | solution.py:29
  (134 other events, 3277.5 us)
Sparse Core Ops, SparseCore 0:
  12.0 59.0 all-gather.8
  74.0 57.4 all-gather.10
  134.4 57.4 all-gather.14
  194.6 57.4 all-gather.12
  254.9 76.4 all-gather.16
  334.1 81.9 all-gather.18
  585.0 33.2 reduce-scatter.12
  636.1 33.2 reduce-scatter.20
  708.8 35.0 reduce-scatter.18
  746.2 33.6 reduce-scatter.10
  782.4 52.4 reduce-scatter.16
  837.3 52.4 reduce-scatter.14

commit v2 on v1

--- a/solution.py
+++ b/solution.py
@@ -60,16 +60,86 @@
     )
 
 
+def to_owners(pair):
+    z_hi = lax.axis_index("fsdp") // X_SIZE
+    even = jnp.where(z_hi == 0, pair[0], pair[1])
+    odd = jnp.where(z_hi == 0, pair[1], pair[0])
+    reps, count = lax.axis_size("rep"), lax.axis_size("fsdp")
+
+    def send(block, flip, z_lo):
+        moves = []
+        for rep in range(reps):
+            for f in range(count):
+                owner = 2 * (f % X_SIZE) + ((f // X_SIZE) ^ flip)
+                moves.append((rep * count + f, (rep ^ (2 * z_lo)) * count + owner))
+        return lax.ppermute(block, ("rep", "fsdp"), moves).astype(f32)
+
+    near = send(even, 0, 0) + send(odd, 1, 0)
+    far = send(even, 0, 1) + send(odd, 1, 1)
+    return (near + far).astype(bf16)
+
+
 def finish_sum(pair):
-    mine_first = lax.axis_index("fsdp") < X_SIZE
-    own = jnp.where(mine_first, pair[0], pair[1])
-    away = jnp.where(mine_first, pair[1], pair[0])
-    total = own.astype(f32) + swap(away, "fsdp", 4).astype(f32)
-    total = total.astype(bf16)
-    total = (total.astype(f32) + swap(total, "rep", 2).astype(f32)).astype(bf16)
+    total = to_owners(pair)
     parts = [total] + [swap(total, "rep", 4 * m) for m in range(1, 4)]
     parts = [part.astype(f32) for part in parts]
     return ((parts[0] + parts[1]) + (parts[2] + parts[3])).astype(bf16)
+
+
+def assemble_kernel(count, y_parts, *refs):
+    parts, out, sems = refs[:count], refs[count], refs[count + 1]
+    me = lax.axis_index("fsdp")
+    copies = []
+    if y_parts:
+        y = lax.axis_index("rep") // 4
+        columns = parts[0].shape[-1]
+        for m in range(count):
+            first = pl.multiple_of(jnp.bitwise_xor(y, m) * columns, 128)
+            for k, block in enumerate(BLOCK_ORDER):
+                place = out.at[jnp.bitwise_xor(me, block), :, pl.ds(first, columns)]
+                copies.append((parts[m].at[k], place))
+    else:
+        for k, block in enumerate(BLOCK_ORDER):
+            copies.append((parts[k // 2].at[k % 2], out.at[jnp.bitwise_xor(me, block)]))
+    copies = [
+        pltpu.make_async_copy(source, place, sems.at[i])
+        for i, (source, place) in enumerate(copies)
+    ]
+    for copy in copies:
+        copy.start()
+    for copy in copies:
+        copy.wait()
+
+
+def assemble(parts, y_parts):
+    rows, columns = parts[0].shape[1:]
+    blocks = len(BLOCK_ORDER)
+    columns = columns * len(parts) if y_parts else columns
+    size = blocks * rows * columns * 4
+    return pl.pallas_call(
+        functools.partial(assemble_kernel, len(parts), y_parts),
+        out_shape=jax.ShapeDtypeStruct((blocks, rows, columns), parts[0].dtype),
+        in_specs=[pl.BlockSpec(memory_space=pl.ANY)] * len(parts),
+        out_specs=pl.BlockSpec(memory_space=pl.ANY),
+        scratch_shapes=[pltpu.SemaphoreType.DMA((blocks * (len(parts) if y_parts else 1),))],
+        cost_estimate=pl.CostEstimate(flops=0, bytes_accessed=size, transcendentals=0),
+        name="assemble",
+    )(*parts)
+
+
+def gather_blocks(part):
+    pair = jnp.stack([part, swap(part, "fsdp", 4)])
+    return [pair] + [swap(pair, "fsdp", m) for m in range(1, X_SIZE)]
+
+
+def gather_by_y(part):
+    columns = part.shape[1] // 4
+    y = lax.axis_index("rep") // 4
+    quarter = lax.dynamic_slice_in_dim(part, y * columns, columns, axis=1)
+    blocks = gather_blocks(quarter)
+    joined = jnp.concatenate(blocks, axis=0)
+    parts = [joined] + [swap(joined, "rep", 4 * m) for m in range(1, 4)]
+    return parts, blocks
 
 
 def stacked_heads(array, kv_head):
@@ -220,12 +290,6 @@
     return lax.dot_general(left, right, (((0,), (0,)), ((), ())), preferred_element_type=f32)
 
 
-def by_x(columns):
-    rows, width = columns.shape
-    blocks = columns.reshape(rows, 2, X_SIZE, width // (2 * X_SIZE))
-    return blocks.swapaxes(1, 2).reshape(rows, width)
-
-
 def body(
     tokens,
     seq_lengths,
@@ -251,28 +315,41 @@
     def pick(a, b):
         return jnp.where(first_core, a, b)
 
-    def gathered(part):
-        mine = lax.all_gather(part, "fsdp", axis=0, tiled=True)
-        return mine, swap_core(mine)
+    def after(part, earlier):
+        return lax.optimization_barrier((part, earlier))[0]
 
     layers = []
+    last = None
     for l in range(DECODER_LAYERS):
         gains = jnp.stack([attn_gain[l], mlp_gain[l]])
         gains = jnp.pad(gains, ((0, 6), (0, att_width - shard)))
-        own = pick(
+        att = pick(
             jnp.concatenate([query_weight[l], key_projection[l]], axis=1),
             jnp.concatenate([out_weight[l], value_projection[l]], axis=1),
         )
-        mine, other = gathered(jnp.concatenate([own, gains], axis=0))
-        blocks = mine.reshape(-1, shard + 8, att_width)
-        gain_attn = blocks[:, shard, :shard].reshape(width).astype(f32)
-        gain_mlp = blocks[:, shard + 1, :shard].reshape(width).astype(f32)
-        mine = blocks[:, :shard].reshape(width, att_width)
-        other = other.reshape(-1, shard + 8, att_width)[:, :shard].reshape(width, att_width)
+        att = jnp.concatenate([att, gains], axis=0)
+        gate_up = pick(gate_weight[l], up_weight[l])
+        down = pick(down_weight[l][:, :half_width], down_weight[l][:, half_width:])
+
+        if last is not None:
+            gate_up = after(gate_up, last[-1])
+        by_y, last = gather_by_y(gate_up)
+        att_parts = gather_blocks(after(att, last[-1]))
+        down_parts = gather_blocks(after(down, att_parts[-1]))
+        last = down_parts
+
+        mine = assemble(att_parts, False)
+        other = swap_core(mine)
+        gain_attn = mine[:, shard, :shard].reshape(width).astype(f32)
+        gain_mlp = mine[:, shard + 1, :shard].reshape(width).astype(f32)
+        mine = mine[:, :shard].reshape(width, att_width)
+        other = other[:, :shard].reshape(width, att_width)
         query_key = pick(mine, other)
         out_value = pick(other, mine)
-        gate_up = gathered(pick(gate_weight[l], up_weight[l]))
-        down = gathered(pick(down_weight[l][:, :half_width], down_weight[l][:, half_width:]))
+        mine = assemble(by_y, True).reshape(width, -1)
+        gate_up = (mine, swap_core(mine))
+        mine = assemble(down_parts, False).reshape(-1, half_width)
+        down = (mine, swap_core(mine))
         layers.append((gain_attn, gain_mlp, query_key, out_value, gate_up, down))
 
     lengths = seq_lengths[0]
@@ -318,11 +395,6 @@
         stream = middle + jnp.concatenate([pick(mine, other), pick(other, mine)], axis=1)
     output = stream.astype(bf16)
 
-    def finish(pair_parts, names):
-        widths = [part.shape[-1] for part in pair_parts]
-        joined = jnp.concatenate(pair_parts, axis=-1) if len(pair_parts) > 1 else pair_parts[0]
-        return finish_sum(joined)
-
     grad = cotangent.astype(f32)
     results = [None] * DECODER_LAYERS
     for l in reversed(range(DECODER_LAYERS)):
@@ -331,9 +403,8 @@
         grad_low = grad.astype(bf16)
         grad_a, grad_b = grad_low[:, :half_width], grad_low[:, half_width:]
         grad_mine, grad_other = pick(grad_a, grad_b), pick(grad_b, grad_a)
-        hidden_x = by_x(hidden)
-        received = swap_core(cross_rows(hidden_x, grad_other).astype(bf16))
-        down_sum = (cross_rows(hidden_x, grad_mine) + received.astype(f32)).astype(bf16)
+        received = swap_core(cross_rows(hidden, grad_other).astype(bf16))
+        down_sum = (cross_rows(hidden, grad_mine) + received.astype(f32)).astype(bf16)
         down_sum = sum_over_x(down_sum)
 
         dhidden = matmul_nt(grad_mine, down[0]) + matmul_nt(grad_other, down[1])
@@ -341,9 +412,8 @@
         dgate = (dhidden * up * sigmoid * (1.0 + gate * (1.0 - sigmoid))).astype(bf16)
         dup = (dhidden * gate * sigmoid).astype(bf16)
         dmine, dother = pick(dgate, dup), pick(dup, dgate)
-        mlp_x = by_x(normed_mlp)
-        received = swap_core(cross_rows(mlp_x, dother).astype(bf16))
-        gate_up_sum = (cross_rows(mlp_x, dmine) + received.astype(f32)).astype(bf16)
+        received = swap_core(cross_rows(normed_mlp, dother).astype(bf16))
+        gate_up_sum = (cross_rows(normed_mlp, dmine) + received.astype(f32)).astype(bf16)
         gate_up_sum = sum_over_x(gate_up_sum)
 
         dnormed = matmul_nt(dmine, gate_up[0]) + matmul_nt(dother, gate_up[1])
@@ -362,54 +432,40 @@
         dstream, attn_gain_grad = normalize_back(stream, gain_attn, dnormed)
         grad = dstream + dmiddle
 
-        normed_x, mixed_x = by_x(normed), by_x(mixed)
-
         def att_terms(first):
             wide = cross_rows(
-                jnp.where(first, normed_x, mixed_x), jnp.where(first, dq, dmiddle_low)
+                jnp.where(first, normed, mixed), jnp.where(first, dq, dmiddle_low)
             )
-            return jnp.concatenate([wide, cross_rows(normed_x, jnp.where(first, dk, dv))], axis=1)
+            return jnp.concatenate([wide, cross_rows(normed, jnp.where(first, dk, dv))], axis=1)
 
         received = swap_core(att_terms(jnp.logical_not(first_core)).astype(bf16))
         att_sum = (att_terms(first_core) + received.astype(f32)).astype(bf16)
         gain_grads = jnp.stack([attn_gain_grad, mlp_gain_grad]).astype(bf16)
         received = swap_core(gain_grads)
-        gain_grads = by_x((gain_grads.astype(f32) + received.astype(f32)).astype(bf16))
+        gain_grads = (gain_grads.astype(f32) + received.astype(f32)).astype(bf16)
         gain_grads = gain_grads.reshape(2, -1, shard).swapaxes(0, 1)
         gain_grads = jnp.pad(gain_grads, ((0, 0), (0, 6), (0, att_width - shard)))
         att_sum = jnp.concatenate([att_sum.reshape(-1, shard, att_width), gain_grads], axis=1)
         att_sum = sum_over_x(att_sum.reshape(-1, att_width))
 
-        ffn = jnp.concatenate(
-            [
-                gate_up_sum.reshape(2, shard, -1),
-                down_sum.reshape(2, -1, half_width).reshape(2, shard, -1),
-            ],
-            axis=2,
-        )
-        ffn = finish_sum(ffn)
-        att = finish_sum(att_sum.reshape(2, shard + 8, att_width))
-        ffn_other, att_other = swap_core(ffn), swap_core(att)
-        ffn_a, ffn_b = pick(ffn, ffn_other), pick(ffn_other, ffn)
-        att_a, att_b = pick(att, att_other), pick(att_other, att)
-        hidden_width = gate_weight.shape[2]
-        down_shape = (down_weight.shape[1], half_width)
+        def whole(pair):
+            own = finish_sum(pair)
+            return own, swap_core(own)
+
+        gate_up_own, gate_up_other = whole(gate_up_sum.reshape(2, shard, -1))
+        down_own, down_other = whole(down_sum.reshape(2, -1, half_width))
+        att_own, att_other = whole(att_sum.reshape(2, shard + 8, att_width))
+        att_a, att_b = pick(att_own, att_other), pick(att_other, att_own)
         results[l] = (
-            att[shard, :shard],
+            att_own[shard, :shard],
             att_a[:shard, :width],
             att_a[:shard, width:],
             att_b[:shard, width:],
             att_b[:shard, :width],
-            att[shard + 1, :shard],
-            ffn_a[:, :hidden_width],
-            ffn_b[:, :hidden_width],
-            jnp.concatenate(
-                [
-                    ffn_a[:, hidden_width:].reshape(down_shape),
-                    ffn_b[:, hidden_width:].reshape(down_shape),
-                ],
-                axis=1,
-            ),
+            att_own[shard + 1, :shard],
+            pick(gate_up_own, gate_up_other),
+            pick(gate_up_other, gate_up_own),
+            jnp.concatenate([pick(down_own, down_other), pick(down_other, down_own)], axis=1),
         )
     stacked = [
         jnp.stack([results[l][m].astype(f32) for l in range(DECODER_LAYERS)], axis=0)

time: 1060 us -> 1570 us (1.48)
  Pallas kernels: 44 us -> 667 us
  waiting for transfers between devices: 614 us -> 419 us
  starting transfers between devices: 78.8 us -> 216 us
  local copies, waits for them, and re-layouts: 109 us -> 54.5 us
    pallas_call x0 -> x6, Pallas kernels: none -> 623 us  [assemble(): pl.pallas_call(functools.partial(assemble_kernel, len(parts), y_parts), o...]
    all_gather x6 -> x0, waiting for transfers between devices: 321 us -> none  [gathered(): mine = lax.all_gather(part, 'fsdp', axis=0, tiled=True)]
    ppermute x0 -> x24, waiting for transfers between devices: none -> 125 us  [send(): return lax.ppermute(block, ('rep', 'fsdp'), moves).astype(f32)]
    ppermute x54 -> x84, starting transfers between devices: 77.9 us -> 156 us  [swap(): return lax.ppermute(array, axis, [(i, i ^ mask) for i in range(count)])]
    ppermute x0 -> x24, starting transfers between devices: none -> 59.2 us  [send(): return lax.ppermute(block, ('rep', 'fsdp'), moves).astype(f32)]
    ppermute x54 -> x84, waiting for transfers between devices: 246 us -> 293 us  [swap(): return lax.ppermute(array, axis, [(i, i ^ mask) for i in range(count)])]
    reduce_scatter x6, waiting for transfers between devices: 45.2 us -> 0.03 us  [sum_over_x(): lax.psum_scatter(rows, 'fsdp', scatter_dimension=0, tiled=True, axis_inde...]
    reshape x26 -> x4, local copies, waits for them, and re-layouts: 42.1 us -> 9.14 us  [the longest x2 8.96 us: body(): mine = assemble(down_parts, False).reshape(-1, half_width)]
  transfers between devices with their start and end apart: 66 -> 114, of which waited for: 40 -> 66; matrix products, arithmetic and copies ran while one was open for 22% -> 12% of each run, Pallas kernels for 3% -> 42%
where the time goes in v2:
time: 1570 us; the launch traced here: 1560 us
  Pallas kernels  667 us (42%)
  waiting for transfers between devices  419 us (27%)
  starting transfers between devices  216 us (14%)
  matrix products  104 us (7%)
  other arithmetic  87 us (6%)
  local copies, waits for them, and re-layouts  54.5 us (3%)
  between operations  16.4 us (1%)
    pallas_call x6, Pallas kernels, assemble(): pl.pallas_call(functools.partial(assemble_kernel, len(parts), y_parts), o...  623 us
    ppermute x84, waiting for transfers between devices, swap(): return lax.ppermute(array, axis, [(i, i ^ mask) for i in range(count)])  293 us
    ppermute x84, starting transfers between devices, swap(): return lax.ppermute(array, axis, [(i, i ^ mask) for i in range(count)])  156 us
    ppermute x24, waiting for transfers between devices, send(): return lax.ppermute(block, ('rep', 'fsdp'), moves).astype(f32)  125 us
    ppermute x24, starting transfers between devices, send(): return lax.ppermute(block, ('rep', 'fsdp'), moves).astype(f32)  59.2 us
    dot_general x16, matrix products, cross_rows(): lax.dot_general(left, right, (((0,), (0,)), ((), ())), preferred_element_...  43.1 us
    dot_general x14, matrix products, matmul_nt(): return lax.dot_general(left, right, NT, preferred_element_type=f32)  33.9 us
  transfers between devices with their start and end apart: 114, of which 66 were waited for; matrix products, arithmetic and copies ran while one was open for 12% of the time, Pallas kernels for 42%

profile of v2, /device:TPU:5, one launch (start us, length us, event | category | flops | bytes accessed | tf_op | source)
XLA Modules:
  0.0 1563.1 jit_solution(9481307731502581915)
XLA Ops:
  17.8 7.2 collective-permute-done.1
  27.4 6.2 collective-permute-done.2
  35.6 11.3 collective-permute-done.5.refs_3_
  57.6 8.2 collective-permute-done.20.refs_3_
  104.4 11.9 collective-permute-done.4.refs_2_
  118.3 11.9 collective-permute-done.25.refs_1_
  131.4 80.6 %assemble.6 = bf16[8,128,1280]{2,1,0:T(8,128)(2,1)} custom-call(bf16[2,128,1280]{2,1,0:T(8,128)(2,1)} %copy-done.60, bf16[2,128,1280]{2,1,0:T(8,128)(2,1)} %copy-done.79, bf16[2,128,1280]{2,1,0:T(8,128)(2,1)} %copy-done.80, bf16[2,128,1280]{2,1,0:T(8,128)(2,1)} %copy-done.77), custom_call_target="tpu_custom_call" | custom-call | bytes 5242880 | tf_op jit(solution)/shard_map/assemble/pallas_call | solution.py:119
  212.1 18.0 %collective-permute-start.6 = (bf16[8,128,1280]{2,1,0:T(8,128)(2,1)}, bf16[8,128,1280]{2,1,0:T(8,128)(2,1)}, u32[]{:S(2)}, u32[]{:S(2)}) collective-permute-start(bf16[8,128,1280]{2,1,0:T(8,128)(2,1)} %assemble.6), channel_id=1, source_target_pairs={{0,8},{8,0},{16,24},{24,16},{32,40},{40,32},{48,56},{56,48},{64,72... | collective-permute-start | bytes 7864328 | tf_op jit(solution)/shard_map/ppermute | solution.py:29
  230.1 80.6 %assemble.9 = bf16[8,128,1280]{2,1,0:T(8,128)(2,1)} custom-call(bf16[2,128,1280]{2,1,0:T(8,128)(2,1)} %copy-done.61, bf16[2,128,1280]{2,1,0:T(8,128)(2,1)} %copy-done.82, bf16[2,128,1280]{2,1,0:T(8,128)(2,1)} %collective-permute-done.26.refs_2_, bf16[2,128,1280]{2,1,0:T(8,128)(2,1)} %copy-done.81), custom_call_target="tpu_custom_call" | custom-call | bytes 5242880 | tf_op jit(solution)/shard_map/assemble/pallas_call | solution.py:119
  316.1 30.4 %collective-permute-done.34 = bf16[2,120,640]{2,1,0:T(8,128)(2,1)} collective-permute-done((bf16[2,120,640]{2,1,0:T(8,128)(2,1)}, bf16[2,120,640]{2,1,0:T(8,128)(2,1)}, u32[]{:S(2)}, u32[]{:S(2)}) %collective-permute-start.34) | collective-permute-done | bytes 307232 | tf_op jit(solution)/shard_map/ppermute | solution.py:29
  360.4 17.5 %collective-permute-done.35.refs_1_ = bf16[8,120,640]{2,1,0:T(8,128)(2,1)S(1)} collective-permute-done((bf16[8,120,640]{2,1,0:T(8,128)(2,1)S(1)}, bf16[8,120,640]{2,1,0:T(8,128)(2,1)S(1)}, u32[]{:S(2)}, u32[]{:S(2)}) %collective-permute-start.35) | collective-permute-done | bytes 1228832 | tf_op jit(solution)/shard_map/ppermute | solution.py:29
  379.6 27.1 %collective-permute-done.36.refs_2_ = bf16[8,120,640]{2,1,0:T(8,128)(2,1)S(1)} collective-permute-done((bf16[8,120,640]{2,1,0:T(8,128)(2,1)S(1)}, bf16[8,120,640]{2,1,0:T(8,128)(2,1)S(1)}, u32[]{:S(2)}, u32[]{:S(2)}) %collective-permute-start.36) | collective-permute-done | bytes 1228832 | tf_op jit(solution)/shard_map/ppermute | solution.py:29
  416.4 150.3 %assemble.7 = bf16[8,120,2560]{2,1,0:T(8,128)(2,1)} custom-call(bf16[8,120,640]{2,1,0:T(8,128)(2,1)} %constant_dynamic-update-slice_fusion.5.refs_0_, bf16[8,120,640]{2,1,0:T(8,128)(2,1)} %collective-permute-done.13.refs_1_, bf16[8,120,640]{2,1,0:T(8,128)(2,1)} %collective-permute-done.14.refs_2_, bf16[8,120,640]{2,1,0:T(8,128)(2,1)} %collective-permute-done.15.refs_3_), custom_call_target="tpu_custom_call" | custom-call | bytes 9830400 | tf_op jit(solution)/shard_map/assemble/pallas_call | solution.py:119
  566.7 80.6 %assemble.8 = bf16[8,320,480]{2,1,0:T(8,128)(2,1)} custom-call(bf16[2,320,480]{2,1,0:T(8,128)(2,1)} %copy-done.59, bf16[2,320,480]{2,1,0:T(8,128)(2,1)} %copy-done.78, bf16[2,320,480]{2,1,0:T(8,128)(2,1)} %collective-permute-done.19.refs_2_, bf16[2,320,480]{2,1,0:T(8,128)(2,1)} %collective-permute-done.20.refs_3_), custom_call_target="tpu_custom_call" | custom-call | bytes 4915200 | tf_op jit(solution)/shard_map/assemble/pallas_call | solution.py:119
  652.7 150.3 %assemble.10 = bf16[8,120,2560]{2,1,0:T(8,128)(2,1)} custom-call(bf16[8,120,640]{2,1,0:T(8,128)(2,1)} %copy-done.69, bf16[8,120,640]{2,1,0:T(8,128)(2,1)} %copy-done.71, bf16[8,120,640]{2,1,0:T(8,128)(2,1)} %copy-done.72, bf16[8,120,640]{2,1,0:T(8,128)(2,1)} %copy-done.73), custom_call_target="tpu_custom_call" | custom-call | bytes 9830400 | tf_op jit(solution)/shard_map/assemble/pallas_call | solution.py:119
  806.1 80.6 %assemble.11 = bf16[8,320,480]{2,1,0:T(8,128)(2,1)} custom-call(bf16[2,320,480]{2,1,0:T(8,128)(2,1)} %pad_maximum_fusion.5.refs_0_, bf16[2,320,480]{2,1,0:T(8,128)(2,1)} %collective-permute-done.40.refs_1_, bf16[2,320,480]{2,1,0:T(8,128)(2,1)} %collective-permute-done.41.refs_2_, bf16[2,320,480]{2,1,0:T(8,128)(2,1)} %collective-permute-done.42.refs_3_), custom_call_target="tpu_custom_call" | custom-call | bytes 4915200 | tf_op jit(solution)/shard_map/assemble/pallas_call | solution.py:119
  901.8 6.5 collective-permute-done.7
  911.8 7.4 collective-permute-done.8
  931.6 7.9 attention_forward.2
  943.1 6.1 multiply_convert_fusion.5
  974.2 10.0 collective-permute-done.31
  984.3 6.6 collective-permute-done.32
  991.0 7.7 attention_forward.3
  1020.7 14.0 attention_backward.2
  1051.0 9.3 collective-permute-done.45
  1076.4 6.4 add_convert_fusion.2
  1091.3 6.4 collective-permute-start.90
  1120.6 6.6 add_convert_fusion.3
  1138.9 14.2 attention_backward.3
  1162.3 7.7 collective-permute-done.48
  1170.0 9.0 collective-permute-done.49
  1221.2 6.2 add_convert_fusion
  1234.1 6.1 collective-permute-start.100
  1243.5 10.9 collective-permute-done.100
  1259.0 9.4 collective-permute-done.102
  1277.5 6.0 add_convert_fusion.1
  1306.8 9.3 collective-permute-done.93
  1363.8 9.0 collective-permute-done.68
  1388.8 11.0 collective-permute-done.54
  1404.5 9.4 collective-permute-done.56
  1426.4 6.9 collective-permute-done.59
  1469.2 6.9 collective-permute-done.84
  1482.4 6.9 collective-permute-done.73
  1497.1 6.3 collective-permute-done.75
  1511.9 9.7 collective-permute-done.88
  1522.0 6.2 collective-permute-start.89
  1528.2 10.2 collective-permute-done.78
  1538.4 9.6 collective-permute-done.79
  (659 shorter events, 508.0 us)
Async XLA Ops:
  7.2 1225.8 %reduce-scatter.17.cloned.1.call-start = ((), (), s32[]{:S(2)}) async-start(), calls=%async_computation.11 | async-start | bytes 3276800 | tf_op jit(solution)/shard_map/reduce_scatter | solution.py:58
  85.9 30.4 %collective-permute-start.4 = (bf16[2,128,1280]{2,1,0:T(8,128)(2,1)S(1)}, bf16[2,128,1280]{2,1,0:T(8,128)(2,1)S(1)}, u32[]{:S(2)}, u32[]{:S(2)}) collective-permute-start(bf16[2,128,1280]{2,1,0:T(8,128)(2,1)S(1)} %pad_maximum_fusion.2.refs_0_), channel_id=1, source_target_pairs={{0,2},{1,3},{2,0},{3,1},{4,6},{5,7},{6,4},{7,5},{8,10},{9,11},{10,... | collective-permute-start | bytes 1966088 | tf_op jit(solution)/shard_map/ppermute | solution.py:29
  91.1 27.0 %collective-permute-start.27 = (bf16[2,128,1280]{2,1,0:T(8,128)(2,1)S(1)}, bf16[2,128,1280]{2,1,0:T(8,128)(2,1)S(1)}, u32[]{:S(2)}, u32[]{:S(2)}) collective-permute-start(bf16[2,128,1280]{2,1,0:T(8,128)(2,1)S(1)} %pad_maximum_fusion.4.refs_0_), channel_id=1, source_target_pairs={{0,3},{1,2},{2,1},{3,0},{4,7},{5,6},{6,5},{7,4},{8,11},{9,10},{10,... | collective-permute-start | bytes 1966088 | tf_op jit(solution)/shard_map/ppermute | solution.py:29
  92.3 218.3 %collective-permute-start.13 = (bf16[8,120,640]{2,1,0:T(8,128)(2,1)}, bf16[8,120,640]{2,1,0:T(8,128)(2,1)}, u32[]{:S(2)}, u32[]{:S(2)}) collective-permute-start(bf16[8,120,640]{2,1,0:T(8,128)(2,1)} %constant_dynamic-update-slice_fusion.5.refs_0_), channel_id=1, source_target_pairs={{0,32},{8,40},{16,48},{24,56},{32,0},{40,8},{48,16},{56,24},{64,96... | collective-permute-start | bytes 3686408 | tf_op jit(solution)/shard_map/ppermute | solution.py:29
  93.6 217.5 %collective-permute-start.14 = (bf16[8,120,640]{2,1,0:T(8,128)(2,1)}, bf16[8,120,640]{2,1,0:T(8,128)(2,1)}, u32[]{:S(2)}, u32[]{:S(2)}) collective-permute-start(bf16[8,120,640]{2,1,0:T(8,128)(2,1)} %constant_dynamic-update-slice_fusion.5.refs_0_), channel_id=1, source_target_pairs={{0,64},{8,72},{16,80},{24,88},{32,96},{40,104},{48,112},{56,120},{... | collective-permute-start | bytes 3686408 | tf_op jit(solution)/shard_map/ppermute | solution.py:29
  101.6 209.5 %collective-permute-start.15 = (bf16[8,120,640]{2,1,0:T(8,128)(2,1)}, bf16[8,120,640]{2,1,0:T(8,128)(2,1)}, u32[]{:S(2)}, u32[]{:S(2)}) collective-permute-start(bf16[8,120,640]{2,1,0:T(8,128)(2,1)} %constant_dynamic-update-slice_fusion.5.refs_0_), channel_id=1, source_target_pairs={{0,96},{8,104},{16,112},{24,120},{32,64},{40,72},{48,80},{56,88},{... | collective-permute-start | bytes 3686408 | tf_op jit(solution)/shard_map/ppermute | solution.py:29
  118.1 94.0 %collective-permute-start.26 = (bf16[2,128,1280]{2,1,0:T(8,128)(2,1)S(1)}, bf16[2,128,1280]{2,1,0:T(8,128)(2,1)}, u32[]{:S(2)}, u32[]{:S(2)}) collective-permute-start(bf16[2,128,1280]{2,1,0:T(8,128)(2,1)S(1)} %pad_maximum_fusion.4.refs_0_), channel_id=1, source_target_pairs={{0,2},{1,3},{2,0},{3,1},{4,6},{5,7},{6,4},{7,5},{8,10},{9,11},{10,... | collective-permute-start | bytes 1966088 | tf_op jit(solution)/shard_map/ppermute | solution.py:29
  130.1 184.0 %collective-permute-start.33 = (bf16[2,120,640]{2,1,0:T(8,128)(2,1)}, bf16[2,120,640]{2,1,0:T(8,128)(2,1)}, u32[]{:S(2)}, u32[]{:S(2)}) collective-permute-start(bf16[2,120,640]{2,1,0:T(8,128)(2,1)} %pad_maximum_fusion.11), channel_id=1, source_target_pairs={{0,1},{1,0},{2,3},{3,2},{4,5},{5,4},{6,7},{7,6},{8,9},{9,8},{10,11... | collective-permute-start | bytes 921608 | tf_op jit(solution)/shard_map/ppermute | solution.py:29
  212.1 679.1 %collective-permute-start.6 = (bf16[8,128,1280]{2,1,0:T(8,128)(2,1)}, bf16[8,128,1280]{2,1,0:T(8,128)(2,1)}, u32[]{:S(2)}, u32[]{:S(2)}) collective-permute-start(bf16[8,128,1280]{2,1,0:T(8,128)(2,1)} %assemble.6), channel_id=1, source_target_pairs={{0,8},{8,0},{16,24},{24,16},{32,40},{40,32},{48,56},{56,48},{64,72... | collective-permute-start | bytes 7864328 | tf_op jit(solution)/shard_map/ppermute | solution.py:29
  310.7 39.7 %collective-permute-start.18 = (bf16[2,320,480]{2,1,0:T(8,128)(2,1)S(1)}, bf16[2,320,480]{2,1,0:T(8,128)(2,1)S(1)}, u32[]{:S(2)}, u32[]{:S(2)}) collective-permute-start(bf16[2,320,480]{2,1,0:T(8,128)(2,1)S(1)} %pad_maximum_fusion.3.refs_0_), channel_id=1, source_target_pairs={{0,1},{1,0},{2,3},{3,2},{4,5},{5,4},{6,7},{7,6},{8,9},{9,8},{10,11... | collective-permute-start | bytes 1843208 | tf_op jit(solution)/shard_map/ppermute | solution.py:29
  311.1 40.6 %collective-permute-start.19 = (bf16[2,320,480]{2,1,0:T(8,128)(2,1)S(1)}, bf16[2,320,480]{2,1,0:T(8,128)(2,1)}, u32[]{:S(2)}, u32[]{:S(2)}) collective-permute-start(bf16[2,320,480]{2,1,0:T(8,128)(2,1)S(1)} %pad_maximum_fusion.3.refs_0_), channel_id=1, source_target_pairs={{0,2},{1,3},{2,0},{3,1},{4,6},{5,7},{6,4},{7,5},{8,10},{9,11},{10,... | collective-permute-start | bytes 1843208 | tf_op jit(solution)/shard_map/ppermute | solution.py:29
  311.1 35.4 %collective-permute-start.34 = (bf16[2,120,640]{2,1,0:T(8,128)(2,1)}, bf16[2,120,640]{2,1,0:T(8,128)(2,1)}, u32[]{:S(2)}, u32[]{:S(2)}) collective-permute-start(bf16[2,120,640]{2,1,0:T(8,128)(2,1)} %pad_maximum_fusion.11), channel_id=1, source_target_pairs={{0,2},{1,3},{2,0},{3,1},{4,6},{5,7},{6,4},{7,5},{8,10},{9,11},{10,... | collective-permute-start | bytes 921608 | tf_op jit(solution)/shard_map/ppermute | solution.py:29
  314.1 577.1 %collective-permute-start.28 = (bf16[8,128,1280]{2,1,0:T(8,128)(2,1)}, bf16[8,128,1280]{2,1,0:T(8,128)(2,1)}, u32[]{:S(2)}, u32[]{:S(2)}) collective-permute-start(bf16[8,128,1280]{2,1,0:T(8,128)(2,1)} %assemble.9), channel_id=1, source_target_pairs={{0,8},{8,0},{16,24},{24,16},{32,40},{40,32},{48,56},{56,48},{64,72... | collective-permute-start | bytes 7864328 | tf_op jit(solution)/shard_map/ppermute | solution.py:29
  350.4 27.5 %collective-permute-start.35 = (bf16[8,120,640]{2,1,0:T(8,128)(2,1)S(1)}, bf16[8,120,640]{2,1,0:T(8,128)(2,1)S(1)}, u32[]{:S(2)}, u32[]{:S(2)}) collective-permute-start(bf16[8,120,640]{2,1,0:T(8,128)(2,1)S(1)} %constant_dynamic-update-slice_fusion.15.refs_0_), channel_id=1, source_target_pairs={{0,32},{8,40},{16,48},{24,56},{32,0},{40,8},{48,16},{56,24},{64,96... | collective-permute-start | bytes 3686408 | tf_op jit(solution)/shard_map/ppermute | solution.py:29
  351.8 55.0 %collective-permute-start.36 = (bf16[8,120,640]{2,1,0:T(8,128)(2,1)S(1)}, bf16[8,120,640]{2,1,0:T(8,128)(2,1)S(1)}, u32[]{:S(2)}, u32[]{:S(2)}) collective-permute-start(bf16[8,120,640]{2,1,0:T(8,128)(2,1)S(1)} %constant_dynamic-update-slice_fusion.15.refs_0_), channel_id=1, source_target_pairs={{0,64},{8,72},{16,80},{24,88},{32,96},{40,104},{48,112},{56,120},{... | collective-permute-start | bytes 3686408 | tf_op jit(solution)/shard_map/ppermute | solution.py:29
  356.4 54.5 %collective-permute-start.37 = (bf16[8,120,640]{2,1,0:T(8,128)(2,1)S(1)}, bf16[8,120,640]{2,1,0:T(8,128)(2,1)S(1)}, u32[]{:S(2)}, u32[]{:S(2)}) collective-permute-start(bf16[8,120,640]{2,1,0:T(8,128)(2,1)S(1)} %constant_dynamic-update-slice_fusion.15.refs_0_), channel_id=1, source_target_pairs={{0,96},{8,104},{16,112},{24,120},{32,64},{40,72},{48,80},{56,88},{... | collective-permute-start | bytes 3686408 | tf_op jit(solution)/shard_map/ppermute | solution.py:29
  377.9 425.2 %collective-permute-start.40 = (bf16[2,320,480]{2,1,0:T(8,128)(2,1)}, bf16[2,320,480]{2,1,0:T(8,128)(2,1)}, u32[]{:S(2)}, u32[]{:S(2)}) collective-permute-start(bf16[2,320,480]{2,1,0:T(8,128)(2,1)} %pad_maximum_fusion.5.refs_0_), channel_id=1, source_target_pairs={{0,1},{1,0},{2,3},{3,2},{4,5},{5,4},{6,7},{7,6},{8,9},{9,8},{10,11... | collective-permute-start | bytes 1843208 | tf_op jit(solution)/shard_map/ppermute | solution.py:29
  406.7 399.3 %collective-permute-start.41 = (bf16[2,320,480]{2,1,0:T(8,128)(2,1)}, bf16[2,320,480]{2,1,0:T(8,128)(2,1)}, u32[]{:S(2)}, u32[]{:S(2)}) collective-permute-start(bf16[2,320,480]{2,1,0:T(8,128)(2,1)} %pad_maximum_fusion.5.refs_0_), channel_id=1, source_target_pairs={{0,2},{1,3},{2,0},{3,1},{4,6},{5,7},{6,4},{7,5},{8,10},{9,11},{10,... | collective-permute-start | bytes 1843208 | tf_op jit(solution)/shard_map/ppermute | solution.py:29
  410.9 395.2 %collective-permute-start.42 = (bf16[2,320,480]{2,1,0:T(8,128)(2,1)}, bf16[2,320,480]{2,1,0:T(8,128)(2,1)}, u32[]{:S(2)}, u32[]{:S(2)}) collective-permute-start(bf16[2,320,480]{2,1,0:T(8,128)(2,1)} %pad_maximum_fusion.5.refs_0_), channel_id=1, source_target_pairs={{0,3},{1,2},{2,1},{3,0},{4,7},{5,6},{6,5},{7,4},{8,11},{9,10},{10,... | collective-permute-start | bytes 1843208 | tf_op jit(solution)/shard_map/ppermute | solution.py:29
  803.1 140.1 %collective-permute-start.16 = (bf16[960,2560]{1,0:T(8,128)(2,1)}, bf16[960,2560]{1,0:T(8,128)(2,1)}, u32[]{:S(2)}, u32[]{:S(2)}) collective-permute-start(bf16[960,2560]{1,0:T(8,128)(2,1)} %bitcast.168), channel_id=1, source_target_pairs={{0,8},{8,0},{16,24},{24,16},{32,40},{40,32},{48,56},{56,48},{64,72... | collective-permute-start | bytes 14745608 | tf_op jit(solution)/shard_map/ppermute | solution.py:29
  806.0 143.3 %collective-permute-start.21 = (bf16[2560,480]{0,1:T(8,128)(2,1)}, bf16[2560,480]{0,1:T(8,128)(2,1)}, u32[]{:S(2)}, u32[]{:S(2)}) collective-permute-start(bf16[2560,480]{0,1:T(8,128)(2,1)} %copy.139), channel_id=1, source_target_pairs={{0,8},{8,0},{16,24},{24,16},{32,40},{40,32},{48,56},{56,48},{64,72... | collective-permute-start | bytes 7372808 | tf_op jit(solution)/shard_map/ppermute | solution.py:29
  919.3 82.9 %collective-permute-start.38 = (bf16[960,2560]{1,0:T(8,128)(2,1)S(1)}, bf16[960,2560]{1,0:T(8,128)(2,1)}, u32[]{:S(2)}, u32[]{:S(2)}) collective-permute-start(bf16[960,2560]{1,0:T(8,128)(2,1)S(1)} %bitcast.175), channel_id=1, source_target_pairs={{0,8},{8,0},{16,24},{24,16},{32,40},{40,32},{48,56},{56,48},{64,72... | collective-permute-start | bytes 14745608 | tf_op jit(solution)/shard_map/ppermute | solution.py:29
  929.1 38.8 %collective-permute-start.43 = (bf16[2560,480]{0,1:T(8,128)(2,1)}, bf16[2560,480]{0,1:T(8,128)(2,1)}, u32[]{:S(2)}, u32[]{:S(2)}) collective-permute-start(bf16[2560,480]{0,1:T(8,128)(2,1)} %copy.145), channel_id=1, source_target_pairs={{0,8},{8,0},{16,24},{24,16},{32,40},{40,32},{48,56},{56,48},{64,72... | collective-permute-start | bytes 7372808 | tf_op jit(solution)/shard_map/ppermute | solution.py:29
  1044.4 27.2 %collective-permute-start.99 = (bf16[2560,480]{0,1:T(8,128)(2,1)S(1)}, bf16[2560,480]{0,1:T(8,128)(2,1)}, u32[]{:S(2)}, u32[]{:S(2)}) collective-permute-start(bf16[2560,480]{0,1:T(8,128)(2,1)S(1)} %convolution_convert_fusion.2), channel_id=1, source_target_pairs={{0,8},{8,0},{16,24},{24,16},{32,40},{40,32},{48,56},{56,48},{64,72... | collective-permute-start | bytes 7372808 | tf_op jit(solution)/shard_map/ppermute | solution.py:29
  1082.9 200.8 %reduce-scatter.15.cloned.1.call-start = ((), (), s32[]{:S(2)}) async-start(), calls=%async_computation.10 | async-start | bytes 3276800 | tf_op jit(solution)/shard_map/reduce_scatter | solution.py:58
  1105.2 79.1 %collective-permute-start.61 = (bf16[960,1280]{1,0:T(8,128)(2,1)}, bf16[960,1280]{1,0:T(8,128)(2,1)}, u32[]{:S(2)}, u32[]{:S(2)}) collective-permute-start(bf16[960,1280]{1,0:T(8,128)(2,1)} %pad_maximum_fusion.1), channel_id=1, source_target_pairs={{0,8},{8,0},{16,24},{24,16},{32,40},{40,32},{48,56},{56,48},{64,72... | collective-permute-start | bytes 7372808 | tf_op jit(solution)/shard_map/ppermute | solution.py:29
  1127.2 197.9 %reduce-scatter.9.cloned.1.call-start = ((), (), s32[]{:S(2)}) async-start(), calls=%async_computation.7 | async-start | bytes 3276800 | tf_op jit(solution)/shard_map/reduce_scatter | solution.py:58
  1189.8 188.8 %reduce-scatter.7.cloned.1.call-start = ((), (), s32[]{:S(2)}) async-start(), calls=%async_computation.6 | async-start | bytes 3276800 | tf_op jit(solution)/shard_map/reduce_scatter | solution.py:58
  1221.1 222.7 %reduce-scatter.13.cloned.1.call-start = ((), (), s32[]{:S(2)}) async-start(), calls=%async_computation.9 | async-start | bytes 6144000 | tf_op jit(solution)/shard_map/reduce_scatter | solution.py:58
  1227.4 226.8 %reduce-scatter.11.cloned.1.call-start = ((), (), s32[]{:S(2)}) async-start(), calls=%async_computation.8 | async-start | bytes 6144000 | tf_op jit(solution)/shard_map/reduce_scatter | solution.py:58
  1232.6 44.9 %collective-permute-start.72 = (bf16[960,2560]{1,0:T(8,128)(2,1)}, bf16[960,2560]{1,0:T(8,128)(2,1)}, u32[]{:S(2)}, u32[]{:S(2)}) collective-permute-start(bf16[960,2560]{1,0:T(8,128)(2,1)} %convolution_convert_fusion.1), channel_id=1, source_target_pairs={{0,8},{8,0},{16,24},{24,16},{32,40},{40,32},{48,56},{56,48},{64,72... | collective-permute-start | bytes 14745608 | tf_op jit(solution)/shard_map/ppermute | solution.py:29
  1243.3 29.1 %collective-permute-start.103 = (bf16[320,480]{1,0:T(8,128)(2,1)S(1)}, bf16[320,480]{1,0:T(8,128)(2,1)S(1)}, u32[]{:S(2)}, u32[]{:S(2)}) collective-permute-start(bf16[320,480]{1,0:T(8,128)(2,1)S(1)} %get-tuple-element.186), channel_id=1, source_target_pairs={{0,17},{1,19},{2,21},{3,23},{4,16},{5,18},{6,20},{7,22},{8,25},{9,... | collective-permute-start | bytes 921608 | tf_op jit(solution)/shard_map/ppermute | solution.py:75
  1288.1 28.1 %collective-permute-start.93 = (bf16[320,480]{1,0:T(8,128)(2,1)S(1)}, bf16[320,480]{1,0:T(8,128)(2,1)S(1)}, u32[]{:S(2)}, u32[]{:S(2)}) collective-permute-start(bf16[320,480]{1,0:T(8,128)(2,1)S(1)} %get-tuple-element.181), channel_id=1, source_target_pairs={{0,16},{1,18},{2,20},{3,22},{4,17},{5,19},{6,21},{7,23},{8,24},{9,... | collective-permute-start | bytes 921608 | tf_op jit(solution)/shard_map/ppermute | solution.py:75
  1292.2 28.8 %collective-permute-start.94 = (bf16[320,480]{1,0:T(8,128)(2,1)S(1)}, bf16[320,480]{1,0:T(8,128)(2,1)S(1)}, u32[]{:S(2)}, u32[]{:S(2)}) collective-permute-start(bf16[320,480]{1,0:T(8,128)(2,1)S(1)} %get-tuple-element.182), channel_id=1, source_target_pairs={{0,17},{1,19},{2,21},{3,23},{4,16},{5,18},{6,20},{7,22},{8,25},{9,... | collective-permute-start | bytes 921608 | tf_op jit(solution)/shard_map/ppermute | solution.py:75
  1301.1 30.5 %collective-permute-start.107 = (bf16[320,480]{1,0:T(8,128)(2,1)S(1)}, bf16[320,480]{1,0:T(8,128)(2,1)S(1)}, u32[]{:S(2)}, u32[]{:S(2)}) collective-permute-start(bf16[320,480]{1,0:T(8,128)(2,1)S(1)} %add_convert_fusion.8), channel_id=1, source_target_pairs={{0,8},{8,0},{16,24},{24,16},{32,40},{40,32},{48,56},{56,48},{64,72... | collective-permute-start | bytes 921608 | tf_op jit(solution)/shard_map/ppermute | solution.py:29
  1385.2 28.6 %collective-permute-start.56 = (bf16[128,1280]{1,0:T(8,128)(2,1)S(1)}, bf16[128,1280]{1,0:T(8,128)(2,1)S(1)}, u32[]{:S(2)}, u32[]{:S(2)}) collective-permute-start(bf16[128,1280]{1,0:T(8,128)(2,1)S(1)} %get-tuple-element.191), channel_id=1, source_target_pairs={{0,16},{1,18},{2,20},{3,22},{4,17},{5,19},{6,21},{7,23},{8,24},{9,... | collective-permute-start | bytes 983048 | tf_op jit(solution)/shard_map/ppermute | solution.py:75
  1387.4 30.6 %collective-permute-start.57 = (bf16[128,1280]{1,0:T(8,128)(2,1)S(1)}, bf16[128,1280]{1,0:T(8,128)(2,1)S(1)}, u32[]{:S(2)}, u32[]{:S(2)}) collective-permute-start(bf16[128,1280]{1,0:T(8,128)(2,1)S(1)} %get-tuple-element.192), channel_id=1, source_target_pairs={{0,17},{1,19},{2,21},{3,23},{4,16},{5,18},{6,20},{7,22},{8,25},{9,... | collective-permute-start | bytes 983048 | tf_op jit(solution)/shard_map/ppermute | solution.py:75
  1449.6 26.4 %collective-permute-start.84 = (bf16[120,2560]{1,0:T(8,128)(2,1)S(1)}, bf16[120,2560]{1,0:T(8,128)(2,1)S(1)}, u32[]{:S(2)}, u32[]{:S(2)}) collective-permute-start(bf16[120,2560]{1,0:T(8,128)(2,1)S(1)} %get-tuple-element.144), channel_id=1, source_target_pairs={{0,16},{1,18},{2,20},{3,22},{4,17},{5,19},{6,21},{7,23},{8,24},{9,... | collective-permute-start | bytes 1843208 | tf_op jit(solution)/shard_map/ppermute | solution.py:75
  1452.0 28.9 %collective-permute-start.85 = (bf16[120,2560]{1,0:T(8,128)(2,1)S(1)}, bf16[120,2560]{1,0:T(8,128)(2,1)}, u32[]{:S(2)}, u32[]{:S(2)}) collective-permute-start(bf16[120,2560]{1,0:T(8,128)(2,1)S(1)} %get-tuple-element.145), channel_id=1, source_target_pairs={{0,17},{1,19},{2,21},{3,23},{4,16},{5,18},{6,20},{7,22},{8,25},{9,... | collective-permute-start | bytes 1843208 | tf_op jit(solution)/shard_map/ppermute | solution.py:75
  1455.5 33.8 %collective-permute-start.73 = (bf16[120,2560]{1,0:T(8,128)(2,1)S(1)}, bf16[120,2560]{1,0:T(8,128)(2,1)S(1)}, u32[]{:S(2)}, u32[]{:S(2)}) collective-permute-start(bf16[120,2560]{1,0:T(8,128)(2,1)S(1)} %get-tuple-element.142), channel_id=1, source_target_pairs={{0,0},{1,2},{2,4},{3,6},{4,1},{5,3},{6,5},{7,7},{8,8},{9,10},{10,1... | collective-permute-start | bytes 1843208 | tf_op jit(solution)/shard_map/ppermute | solution.py:75
  1462.5 40.9 %collective-permute-start.75 = (bf16[120,2560]{1,0:T(8,128)(2,1)S(1)}, bf16[120,2560]{1,0:T(8,128)(2,1)S(1)}, u32[]{:S(2)}, u32[]{:S(2)}) collective-permute-start(bf16[120,2560]{1,0:T(8,128)(2,1)S(1)} %get-tuple-element.142), channel_id=1, source_target_pairs={{0,16},{1,18},{2,20},{3,22},{4,17},{5,19},{6,21},{7,23},{8,24},{9,... | collective-permute-start | bytes 1843208 | tf_op jit(solution)/shard_map/ppermute | solution.py:75
  1468.1 26.6 %collective-permute-start.74 = (bf16[120,2560]{1,0:T(8,128)(2,1)S(1)}, bf16[120,2560]{1,0:T(8,128)(2,1)S(1)}, u32[]{:S(2)}, u32[]{:S(2)}) collective-permute-start(bf16[120,2560]{1,0:T(8,128)(2,1)S(1)} %get-tuple-element.143), channel_id=1, source_target_pairs={{0,1},{1,3},{2,5},{3,7},{4,0},{5,2},{6,4},{7,6},{8,9},{9,11},{10,1... | collective-permute-start | bytes 1843208 | tf_op jit(solution)/shard_map/ppermute | solution.py:75
  1476.1 31.6 %collective-permute-start.76 = (bf16[120,2560]{1,0:T(8,128)(2,1)S(1)}, bf16[120,2560]{1,0:T(8,128)(2,1)S(1)}, u32[]{:S(2)}, u32[]{:S(2)}) collective-permute-start(bf16[120,2560]{1,0:T(8,128)(2,1)S(1)} %get-tuple-element.143), channel_id=1, source_target_pairs={{0,17},{1,19},{2,21},{3,23},{4,16},{5,18},{6,20},{7,22},{8,25},{9,... | collective-permute-start | bytes 1843208 | tf_op jit(solution)/shard_map/ppermute | solution.py:75
  1482.3 29.4 %collective-permute-start.86 = (bf16[120,2560]{1,0:T(8,128)(2,1)S(1)}, bf16[120,2560]{1,0:T(8,128)(2,1)S(1)}, u32[]{:S(2)}, u32[]{:S(2)}) collective-permute-start(bf16[120,2560]{1,0:T(8,128)(2,1)S(1)} %add_convert_fusion.5), channel_id=1, source_target_pairs={{0,32},{8,40},{16,48},{24,56},{32,0},{40,8},{48,16},{56,24},{64,96... | collective-permute-start | bytes 1843208 | tf_op jit(solution)/shard_map/ppermute | solution.py:29
  1494.6 27.0 %collective-permute-start.88 = (bf16[120,2560]{1,0:T(8,128)(2,1)S(1)}, bf16[120,2560]{1,0:T(8,128)(2,1)S(1)}, u32[]{:S(2)}, u32[]{:S(2)}) collective-permute-start(bf16[120,2560]{1,0:T(8,128)(2,1)S(1)} %add_convert_fusion.5), channel_id=1, source_target_pairs={{0,96},{8,104},{16,112},{24,120},{32,64},{40,72},{48,80},{56,88},{... | collective-permute-start | bytes 1843208 | tf_op jit(solution)/shard_map/ppermute | solution.py:29
  1508.1 30.3 %collective-permute-start.78 = (bf16[120,2560]{1,0:T(8,128)(2,1)S(1)}, bf16[120,2560]{1,0:T(8,128)(2,1)S(1)}, u32[]{:S(2)}, u32[]{:S(2)}) collective-permute-start(bf16[120,2560]{1,0:T(8,128)(2,1)S(1)} %add_convert_fusion.7), channel_id=1, source_target_pairs={{0,64},{8,72},{16,80},{24,88},{32,96},{40,104},{48,112},{56,120},{... | collective-permute-start | bytes 1843208 | tf_op jit(solution)/shard_map/ppermute | solution.py:29
  1511.7 36.2 %collective-permute-start.79 = (bf16[120,2560]{1,0:T(8,128)(2,1)S(1)}, bf16[120,2560]{1,0:T(8,128)(2,1)S(1)}, u32[]{:S(2)}, u32[]{:S(2)}) collective-permute-start(bf16[120,2560]{1,0:T(8,128)(2,1)S(1)} %add_convert_fusion.7), channel_id=1, source_target_pairs={{0,96},{8,104},{16,112},{24,120},{32,64},{40,72},{48,80},{56,88},{... | collective-permute-start | bytes 1843208 | tf_op jit(solution)/shard_map/ppermute | solution.py:29
  1522.0 29.1 %collective-permute-start.89 = (bf16[120,2560]{1,0:T(8,128)(2,1)S(1)}, bf16[120,2560]{1,0:T(8,128)(2,1)S(1)}, u32[]{:S(2)}, u32[]{:S(2)}) collective-permute-start(bf16[120,2560]{1,0:T(8,128)(2,1)S(1)} %add_convert_fusion.4), channel_id=1, source_target_pairs={{0,8},{8,0},{16,24},{24,16},{32,40},{40,32},{48,56},{56,48},{64,72... | collective-permute-start | bytes 1843208 | tf_op jit(solution)/shard_map/ppermute | solution.py:29
  (171 other events, 3538.2 us)
Sparse Core Ops, SparseCore 0:
  1083.0 39.9 reduce-scatter.16
  1127.4 35.2 reduce-scatter.14
  1190.0 34.8 reduce-scatter.8
  1227.1 47.7 reduce-scatter.6
  1277.1 74.1 reduce-scatter.12
  1353.8 67.7 reduce-scatter.10

commit v3 on v2

--- a/solution.py
+++ b/solution.py
@@ -84,6 +84,10 @@
     parts = [total] + [swap(total, "rep", 4 * m) for m in range(1, 4)]
     parts = [part.astype(f32) for part in parts]
     return ((parts[0] + parts[1]) + (parts[2] + parts[3])).astype(bf16)
+
+
+def kernel_params():
+    return pltpu.CompilerParams(vmem_limit_bytes=48 * 1024 * 1024)
 
 
 def assemble_kernel(count, y_parts, *refs):
@@ -120,23 +124,29 @@
         functools.partial(assemble_kernel, len(parts), y_parts),
         out_shape=jax.ShapeDtypeStruct((blocks, rows, columns), parts[0].dtype),
         in_specs=[pl.BlockSpec(memory_space=pl.ANY)] * len(parts),
-        out_specs=pl.BlockSpec(memory_space=pl.ANY),
+        out_specs=pl.BlockSpec(memory_space=pltpu.VMEM),
+        compiler_params=kernel_params(),
         scratch_shapes=[pltpu.SemaphoreType.DMA((blocks * (len(parts) if y_parts else 1),))],
         cost_estimate=pl.CostEstimate(flops=0, bytes_accessed=size, transcendentals=0),
         name="assemble",
     )(*parts)
 
 
-def gather_blocks(part):
+def after(array, earlier):
+    return lax.optimization_barrier((array, earlier))[0]
+
+
+def gather_blocks(part, earlier):
     pair = jnp.stack([part, swap(part, "fsdp", 4)])
+    pair = pair if earlier is None else after(pair, earlier)
     return [pair] + [swap(pair, "fsdp", m) for m in range(1, X_SIZE)]
 
 
-def gather_by_y(part):
+def gather_by_y(part, earlier):
     columns = part.shape[1] // 4
     y = lax.axis_index("rep") // 4
     quarter = lax.dynamic_slice_in_dim(part, y * columns, columns, axis=1)
-    blocks = gather_blocks(quarter)
+    blocks = gather_blocks(quarter, earlier)
     joined = jnp.concatenate(blocks, axis=0)
     parts = [joined] + [swap(joined, "rep", 4 * m) for m in range(1, 4)]
     return parts, blocks
@@ -211,10 +221,6 @@
             dq_ref[:, j * HEAD : (j + 1) * HEAD] = dq[g * rows : (g + 1) * rows]
 
 
-def kernel_params():
-    return pltpu.CompilerParams(vmem_limit_bytes=48 * 1024 * 1024)
-
-
 def attend(queries, kv, key_place, bounds):
     rows, keys = queries.shape[0], kv.shape[0]
     pairs = QUERY_HEADS * rows * keys
@@ -315,43 +321,6 @@
     def pick(a, b):
         return jnp.where(first_core, a, b)
 
-    def after(part, earlier):
-        return lax.optimization_barrier((part, earlier))[0]
-
-    layers = []
-    last = None
-    for l in range(DECODER_LAYERS):
-        gains = jnp.stack([attn_gain[l], mlp_gain[l]])
-        gains = jnp.pad(gains, ((0, 6), (0, att_width - shard)))
-        att = pick(
-            jnp.concatenate([query_weight[l], key_projection[l]], axis=1),
-            jnp.concatenate([out_weight[l], value_projection[l]], axis=1),
-        )
-        att = jnp.concatenate([att, gains], axis=0)
-        gate_up = pick(gate_weight[l], up_weight[l])
-        down = pick(down_weight[l][:, :half_width], down_weight[l][:, half_width:])
-
-        if last is not None:
-            gate_up = after(gate_up, last[-1])
-        by_y, last = gather_by_y(gate_up)
-        att_parts = gather_blocks(after(att, last[-1]))
-        down_parts = gather_blocks(after(down, att_parts[-1]))
-        last = down_parts
-
-        mine = assemble(att_parts, False)
-        other = swap_core(mine)
-        gain_attn = mine[:, shard, :shard].reshape(width).astype(f32)
-        gain_mlp = mine[:, shard + 1, :shard].reshape(width).astype(f32)
-        mine = mine[:, :shard].reshape(width, att_width)
-        other = other[:, :shard].reshape(width, att_width)
-        query_key = pick(mine, other)
-        out_value = pick(other, mine)
-        mine = assemble(by_y, True).reshape(width, -1)
-        gate_up = (mine, swap_core(mine))
-        mine = assemble(down_parts, False).reshape(-1, half_width)
-        down = (mine, swap_core(mine))
-        layers.append((gain_attn, gain_mlp, query_key, out_value, gate_up, down))
-
     lengths = seq_lengths[0]
     ends = jnp.cumsum(lengths)
     starts = ends - lengths
@@ -370,18 +339,59 @@
     key_place = blocks[:, None] * rows + jnp.arange(rows, dtype=jnp.int32)[None, :]
     key_place = key_place.reshape(-1, 1)
 
+    def own_weights(l):
+        gains = jnp.stack([attn_gain[l], mlp_gain[l]])
+        gains = jnp.pad(gains, ((0, 6), (0, att_width - shard)))
+        att = pick(
+            jnp.concatenate([query_weight[l], key_projection[l]], axis=1),
+            jnp.concatenate([out_weight[l], value_projection[l]], axis=1),
+        )
+        att = jnp.concatenate([att, gains], axis=0)
+        gate_up = pick(gate_weight[l], up_weight[l])
+        down = pick(down_weight[l][:, :half_width], down_weight[l][:, half_width:])
+        return att, gate_up, down
+
+    def gather_parts(own, earlier):
+        att, gate_up, down = own
+        by_y, blocks = gather_by_y(gate_up, earlier)
+        att_parts = gather_blocks(att, blocks)
+        down_parts = gather_blocks(down, att_parts)
+        return att_parts, by_y, down_parts
+
+    def whole_weights(parts, earlier):
+        att_parts, by_y, down_parts = parts if earlier is None else after(parts, earlier)
+        mine = assemble(att_parts, False)
+        other = swap_core(mine)
+        gain_attn = mine[:, shard, :shard].reshape(width).astype(f32)
+        gain_mlp = mine[:, shard + 1, :shard].reshape(width).astype(f32)
+        mine = mine[:, :shard].reshape(width, att_width)
+        other = other[:, :shard].reshape(width, att_width)
+        query_key = pick(mine, other)
+        out_value = pick(other, mine)
+        mine = assemble(by_y, True).reshape(width, -1)
+        gate_up = (mine, swap_core(mine))
+        mine = assemble(down_parts, False).reshape(-1, half_width)
+        down = (mine, swap_core(mine))
+        return gain_attn, gain_mlp, query_key, out_value, gate_up, down
+
     stream = tokens.astype(f32)
     saved = []
+    parts = gather_parts(own_weights(0), None)
+    layers = [whole_weights(parts, None)]
     for l in range(DECODER_LAYERS):
         gain_attn, gain_mlp, query_key, out_value, gate_up, down = layers[l]
         normed = (normalize(stream) * gain_attn).astype(bf16)
         values = matmul(normed, out_value[:, width:]).astype(bf16)
         projected = matmul(normed, query_key)
+        if l + 1 < DECODER_LAYERS:
+            parts = gather_parts(own_weights(l + 1), (parts, projected))
         keys = rotary(projected[:, width:], cosine, sine).astype(bf16)
         kv = gather_pack(jnp.concatenate([keys, values], axis=1))
         queries = rotary(projected[:, :width], cosine, sine).astype(bf16)
         queries = queries * jnp.asarray(HEAD ** (-0.5), bf16)
         mixed, logs = attend(queries, kv, key_place, bounds)
+        if l + 1 < DECODER_LAYERS:
+            layers.append(whole_weights(parts, mixed))
         middle = stream + matmul(mixed, out_value[:, :width])
         normed_mlp = (normalize(middle) * gain_mlp).astype(bf16)
         mine = matmul(normed_mlp, gate_up[0])
@@ -395,6 +405,13 @@
         stream = middle + jnp.concatenate([pick(mine, other), pick(other, mine)], axis=1)
     output = stream.astype(bf16)
 
+    earlier = output
+
+    def next_sum(rows):
+        nonlocal earlier
+        earlier = sum_over_x(after(rows, earlier))
+        return earlier
+
     grad = cotangent.astype(f32)
     results = [None] * DECODER_LAYERS
     for l in reversed(range(DECODER_LAYERS)):
@@ -405,7 +422,7 @@
         grad_mine, grad_other = pick(grad_a, grad_b), pick(grad_b, grad_a)
         received = swap_core(cross_rows(hidden, grad_other).astype(bf16))
         down_sum = (cross_rows(hidden, grad_mine) + received.astype(f32)).astype(bf16)
-        down_sum = sum_over_x(down_sum)
+        down_sum = next_sum(down_sum)
 
         dhidden = matmul_nt(grad_mine, down[0]) + matmul_nt(grad_other, down[1])
         sigmoid = jax.nn.sigmoid(gate)
@@ -414,7 +431,7 @@
         dmine, dother = pick(dgate, dup), pick(dup, dgate)
         received = swap_core(cross_rows(normed_mlp, dother).astype(bf16))
         gate_up_sum = (cross_rows(normed_mlp, dmine) + received.astype(f32)).astype(bf16)
-        gate_up_sum = sum_over_x(gate_up_sum)
+        gate_up_sum = next_sum(gate_up_sum)
 
         dnormed = matmul_nt(dmine, gate_up[0]) + matmul_nt(dother, gate_up[1])
         dmiddle, mlp_gain_grad = normalize_back(middle, gain_mlp, dnormed)
@@ -446,7 +463,7 @@
         gain_grads = gain_grads.reshape(2, -1, shard).swapaxes(0, 1)
         gain_grads = jnp.pad(gain_grads, ((0, 0), (0, 6), (0, att_width - shard)))
         att_sum = jnp.concatenate([att_sum.reshape(-1, shard, att_width), gain_grads], axis=1)
-        att_sum = sum_over_x(att_sum.reshape(-1, att_width))
+        att_sum = next_sum(att_sum.reshape(-1, att_width))
 
         def whole(pair):
             own = finish_sum(pair)

time: 1570 us -> 1020 us (0.65)
  Pallas kernels: 667 us -> 57 us
  waiting for transfers between devices: 419 us -> 487 us
  starting transfers between devices: 216 us -> 190 us
    pallas_call x6, Pallas kernels: 623 us -> 13.7 us  [assemble(): pl.pallas_call(functools.partial(assemble_kernel, len(parts), y_parts), o...]
    ppermute x84, waiting for transfers between devices: 293 us -> 335 us  [swap(): return lax.ppermute(array, axis, [(i, i ^ mask) for i in range(count)])]
    reduce_scatter x6, waiting for transfers between devices: 0.03 us -> 26.1 us  [sum_over_x(): lax.psum_scatter(rows, 'fsdp', scatter_dimension=0, tiled=True, axis_inde...]
    ppermute x84, starting transfers between devices: 156 us -> 133 us  [swap(): return lax.ppermute(array, axis, [(i, i ^ mask) for i in range(count)])]
  transfers between devices with their start and end apart: 114 -> 114, of which waited for: 66 -> 61; matrix products, arithmetic and copies ran while one was open for 12% -> 22% of each run, Pallas kernels for 42% -> 6%
where the time goes in v3:
time: 1020 us; the launch traced here: 1000 us
  waiting for transfers between devices  487 us (48%)
  starting transfers between devices  190 us (19%)
  matrix products  104 us (10%)
  other arithmetic  82.9 us (8%)
  local copies, waits for them, and re-layouts  67.4 us (7%)
  Pallas kernels  57 us (6%)
  between operations  17.2 us (2%)
    ppermute x84, waiting for transfers between devices, swap(): return lax.ppermute(array, axis, [(i, i ^ mask) for i in range(count)])  335 us
    ppermute x84, starting transfers between devices, swap(): return lax.ppermute(array, axis, [(i, i ^ mask) for i in range(count)])  133 us
    ppermute x24, waiting for transfers between devices, send(): return lax.ppermute(block, ('rep', 'fsdp'), moves).astype(f32)  126 us
    ppermute x24, starting transfers between devices, send(): return lax.ppermute(block, ('rep', 'fsdp'), moves).astype(f32)  55.5 us
    dot_general x16, matrix products, cross_rows(): lax.dot_general(left, right, (((0,), (0,)), ((), ())), preferred_element_...  42.2 us
    dot_general x14, matrix products, matmul_nt(): return lax.dot_general(left, right, NT, preferred_element_type=f32)  36.4 us
    unnamed x306, local copies, waits for them, and re-layouts  30 us
    pallas_call x2, Pallas kernels, attend_back(): pl.pallas_call(attention_backward_kernel, out_shape=(jax.ShapeDtypeStruct...  28 us
  transfers between devices with their start and end apart: 114, of which 61 were waited for; matrix products, arithmetic and copies ran while one was open for 22% of the time, Pallas kernels for 6%

profile of v3, /device:TPU:5, one launch (start us, length us, event | category | flops | bytes accessed | tf_op | source)
XLA Modules:
  0.0 1004.5 jit_solution(8991500575709661303)
XLA Ops:
  30.8 6.5 collective-permute-done.3
  43.1 9.8 collective-permute-done.5.refs_1_
  52.9 15.7 %collective-permute-done.6.refs_2_ = bf16[2,128,1280]{2,1,0:T(8,128)(2,1)S(1)} collective-permute-done((bf16[2,128,1280]{2,1,0:T(8,128)(2,1)S(1)}, bf16[2,128,1280]{2,1,0:T(8,128)(2,1)S(1)}, u32[]{:S(2)}, u32[]{:S(2)}) %collective-permute-start.6) | collective-permute-done | bytes 655392 | tf_op jit(solution)/shard_map/ppermute | solution.py:29
  95.1 12.2 %collective-permute-done.13.refs_1_ = bf16[8,120,640]{2,1,0:T(8,128)(2,1)} collective-permute-done((bf16[8,120,640]{2,1,0:T(8,128)(2,1)}, bf16[8,120,640]{2,1,0:T(8,128)(2,1)}, u32[]{:S(2)}, u32[]{:S(2)}) %collective-permute-start.13) | collective-permute-done | bytes 1228832 | tf_op jit(solution)/shard_map/ppermute | solution.py:29
  110.6 25.5 %collective-permute-done.14.refs_2_ = bf16[8,120,640]{2,1,0:T(8,128)(2,1)} collective-permute-done((bf16[8,120,640]{2,1,0:T(8,128)(2,1)}, bf16[8,120,640]{2,1,0:T(8,128)(2,1)}, u32[]{:S(2)}, u32[]{:S(2)}) %collective-permute-start.14) | collective-permute-done | bytes 1228832 | tf_op jit(solution)/shard_map/ppermute | solution.py:29
  140.6 5.0 assemble.7
  158.4 9.9 collective-permute-done.20.refs_3_
  209.0 8.9 collective-permute-done.11
  217.9 16.6 %collective-permute-done.12 = bf16[2,176,640]{2,1,0:T(8,128)(2,1)S(1)} collective-permute-done((bf16[2,176,640]{2,1,0:T(8,128)(2,1)}, bf16[2,176,640]{2,1,0:T(8,128)(2,1)S(1)}, u32[]{:S(2)}, u32[]{:S(2)}) %collective-permute-start.12) | collective-permute-done | bytes 450592 | tf_op jit(solution)/shard_map/ppermute | solution.py:29
  239.7 9.9 collective-permute-done.29.refs_3_
  254.6 7.6 attention_forward.2
  273.7 13.7 %collective-permute-done.32.refs_3_ = bf16[8,120,640]{2,1,0:T(8,128)(2,1)S(1)} collective-permute-done((bf16[8,120,640]{2,1,0:T(8,128)(2,1)S(1)}, bf16[8,120,640]{2,1,0:T(8,128)(2,1)S(1)}, u32[]{:S(2)}, u32[]{:S(2)}) %collective-permute-start.32) | collective-permute-done | bytes 1228832 | tf_op jit(solution)/shard_map/ppermute | solution.py:29
  288.6 6.4 collective-permute-done.35.refs_2_
  295.0 14.1 %collective-permute-done.36.refs_3_ = bf16[2,320,480]{2,1,0:T(8,128)(2,1)S(1)} collective-permute-done((bf16[2,320,480]{2,1,0:T(8,128)(2,1)S(1)}, bf16[2,320,480]{2,1,0:T(8,128)(2,1)S(1)}, u32[]{:S(2)}, u32[]{:S(2)}) %collective-permute-start.36) | collective-permute-done | bytes 614432 | tf_op jit(solution)/shard_map/ppermute | solution.py:29
  338.6 5.4 multiply_convert_fusion.5
  355.2 8.3 collective-permute-done.38
  368.2 7.4 collective-permute-done.39
  375.7 11.3 %collective-permute-done.40 = bf16[2,176,640]{2,1,0:T(8,128)(2,1)S(1)} collective-permute-done((bf16[2,176,640]{2,1,0:T(8,128)(2,1)S(1)}, bf16[2,176,640]{2,1,0:T(8,128)(2,1)S(1)}, u32[]{:S(2)}, u32[]{:S(2)}) %collective-permute-start.40) | collective-permute-done | bytes 450592 | tf_op jit(solution)/shard_map/ppermute | solution.py:29
  388.5 7.7 attention_forward.3
  414.4 5.0 multiply_reduce_fusion
  431.5 5.7 add_convert_fusion.2
  437.3 6.5 add_convert_fusion
  443.9 25.0 %reduce-scatter.7.cloned.1.call-done = bf16[640,480]{1,0:T(8,128)(2,1)} async-done(((bf16[2560,480]{1,0:T(8,128)(2,1)}), bf16[640,480]{1,0:T(8,128)(2,1)}) %reduce-scatter.7.cloned.1.call-update) | async-done | bytes 614416 | tf_op jit(solution)/shard_map/reduce_scatter | solution.py:58
  472.1 13.9 %attention_backward.2 = (f32[176,960]{1,0:T(8,128)S(1)}, bf16[1408,640]{1,0:T(8,128)(2,1)S(1)}) custom-call(bf16[176,960]{1,0:T(8,128)(2,1)S(1)} %fusion.81.q_ref, bf16[1408,640]{1,0:T(8,128)(2,1)S(1)} %bitcast.173, s32[1408,1]{1,0:T(8,128)S(1)} %copy-done.17, s32[8,528]{1,0:T(8,128)S(1)} %pad.19.bounds_ref, ...), custom_call_target="tpu_custom_call" | custom-call | flops 2378956800 | bytes 6291456 | tf_op jit(solution)/shard_map/attention_backward/pallas_call | solution.py:245
  489.9 18.3 %collective-permute-done.44 = bf16[2,176,640]{2,1,0:T(8,128)(2,1)S(1)} collective-permute-done((bf16[2,176,640]{2,1,0:T(8,128)(2,1)S(1)}, bf16[2,176,640]{2,1,0:T(8,128)(2,1)S(1)}, u32[]{:S(2)}, u32[]{:S(2)}) %collective-permute-start.44) | collective-permute-done | bytes 450592 | tf_op jit(solution)/shard_map/ppermute | solution.py:29
  508.2 19.6 %collective-permute-done.45 = bf16[2,176,640]{2,1,0:T(8,128)(2,1)S(1)} collective-permute-done((bf16[2,176,640]{2,1,0:T(8,128)(2,1)S(1)}, bf16[2,176,640]{2,1,0:T(8,128)(2,1)S(1)}, u32[]{:S(2)}, u32[]{:S(2)}) %collective-permute-start.45) | collective-permute-done | bytes 450592 | tf_op jit(solution)/shard_map/ppermute | solution.py:29
  578.7 5.0 fusion.89
  588.0 5.7 add_convert_fusion.3
  602.6 14.0 %attention_backward.3 = (f32[176,960]{1,0:T(8,128)S(1)}, bf16[1408,640]{1,0:T(8,128)(2,1)S(1)}) custom-call(bf16[176,960]{1,0:T(8,128)(2,1)S(1)} %copy-done.26, bf16[1408,640]{1,0:T(8,128)(2,1)S(1)} %bitcast.171, s32[1408,1]{1,0:T(8,128)S(1)} %copy-done.18, s32[8,528]{1,0:T(8,128)S(1)} %pad.19.bounds_ref, bf16[176,960]{1,0:T(8,128)(2,1)S(1)} %copy-done.8, ...), custom_call_target="tpu_custom_call" | custom-call | flops 2378956800 | bytes 6291456 | tf_op jit(solution)/shard_map/attention_backward/pallas_call | solution.py:245
  623.7 15.5 %collective-permute-done.48 = bf16[2,176,640]{2,1,0:T(8,128)(2,1)S(1)} collective-permute-done((bf16[2,176,640]{2,1,0:T(8,128)(2,1)S(1)}, bf16[2,176,640]{2,1,0:T(8,128)(2,1)S(1)}, u32[]{:S(2)}, u32[]{:S(2)}) %collective-permute-start.48) | collective-permute-done | bytes 450592 | tf_op jit(solution)/shard_map/ppermute | solution.py:29
  639.2 9.0 collective-permute-done.49
  656.6 6.1 add_convert_fusion.1
  674.6 7.3 collective-permute-start.100
  691.0 5.1 collective-permute-done.100
  713.2 44.1 %collective-permute-done.103 = bf16[320,480]{1,0:T(8,128)(2,1)S(1)} collective-permute-done((bf16[320,480]{1,0:T(8,128)(2,1)S(1)}, bf16[320,480]{1,0:T(8,128)(2,1)S(1)}, u32[]{:S(2)}, u32[]{:S(2)}) %collective-permute-start.103) | collective-permute-done | bytes 307232 | tf_op jit(solution)/shard_map/ppermute | solution.py:75
  768.2 6.8 collective-permute-done.105
  776.2 5.7 collective-permute-start.107
  782.0 5.5 collective-permute-start.67
  788.7 12.6 %collective-permute-done.89 = bf16[120,2560]{1,0:T(8,128)(2,1)S(1)} collective-permute-done((bf16[120,2560]{1,0:T(8,128)(2,1)S(1)}, bf16[120,2560]{1,0:T(8,128)(2,1)S(1)}, u32[]{:S(2)}, u32[]{:S(2)}) %collective-permute-start.89) | collective-permute-done | bytes 614432 | tf_op jit(solution)/shard_map/ppermute | solution.py:29
  811.2 7.2 collective-permute-done.70
  825.0 7.0 collective-permute-done.72
  867.7 17.4 %collective-permute-done.76 = bf16[120,2560]{1,0:T(8,128)(2,1)S(1)} collective-permute-done((bf16[120,2560]{1,0:T(8,128)(2,1)S(1)}, bf16[120,2560]{1,0:T(8,128)(2,1)S(1)}, u32[]{:S(2)}, u32[]{:S(2)}) %collective-permute-start.76) | collective-permute-done | bytes 614432 | tf_op jit(solution)/shard_map/ppermute | solution.py:75
  885.1 7.0 collective-permute-done.77
  894.7 10.8 %collective-permute-done.78 = bf16[120,2560]{1,0:T(8,128)(2,1)S(1)} collective-permute-done((bf16[120,2560]{1,0:T(8,128)(2,1)S(1)}, bf16[120,2560]{1,0:T(8,128)(2,1)S(1)}, u32[]{:S(2)}, u32[]{:S(2)}) %collective-permute-start.78) | collective-permute-done | bytes 614432 | tf_op jit(solution)/shard_map/ppermute | solution.py:75
  905.5 5.3 collective-permute-done.79
  917.6 8.0 collective-permute-done.80
  925.5 15.5 %collective-permute-done.81 = bf16[120,2560]{1,0:T(8,128)(2,1)S(1)} collective-permute-done((bf16[120,2560]{1,0:T(8,128)(2,1)S(1)}, bf16[120,2560]{1,0:T(8,128)(2,1)S(1)}, u32[]{:S(2)}, u32[]{:S(2)}) %collective-permute-start.81) | collective-permute-done | bytes 614432 | tf_op jit(solution)/shard_map/ppermute | solution.py:29
  979.5 7.0 collective-permute-done.65
  (735 shorter events, 463.6 us)
Async XLA Ops:
  7.2 461.7 %reduce-scatter.7.cloned.1.call-start = ((), (), s32[]{:S(2)}) async-start(), calls=%async_computation.6 | async-start | bytes 3276800 | tf_op jit(solution)/shard_map/reduce_scatter | solution.py:58
  19.2 74.1 %collective-permute-start.17 = (bf16[320,480]{1,0:T(8,128)(2,1)}, bf16[320,480]{1,0:T(8,128)(2,1)}, u32[]{:S(2)}, u32[]{:S(2)}) collective-permute-start(bf16[320,480]{1,0:T(8,128)(2,1)} %slice_select_fusion.1), channel_id=1, source_target_pairs={{0,4},{1,5},{2,6},{3,7},{4,0},{5,1},{6,2},{7,3},{8,12},{9,13},{10,... | collective-permute-start | bytes 921608 | tf_op jit(solution)/shard_map/ppermute | solution.py:29
  40.5 28.1 %collective-permute-start.6 = (bf16[2,128,1280]{2,1,0:T(8,128)(2,1)S(1)}, bf16[2,128,1280]{2,1,0:T(8,128)(2,1)S(1)}, u32[]{:S(2)}, u32[]{:S(2)}) collective-permute-start(bf16[2,128,1280]{2,1,0:T(8,128)(2,1)S(1)} %pad_maximum_fusion.2.refs_0_), channel_id=1, source_target_pairs={{0,2},{1,3},{2,0},{3,1},{4,6},{5,7},{6,4},{7,5},{8,10},{9,11},{10,... | collective-permute-start | bytes 1966088 | tf_op jit(solution)/shard_map/ppermute | solution.py:29
  69.5 76.1 %collective-permute-start.8 = (bf16[8,128,1280]{2,1,0:T(8,128)(2,1)S(1)}, bf16[8,128,1280]{2,1,0:T(8,128)(2,1)}, u32[]{:S(2)}, u32[]{:S(2)}) collective-permute-start(bf16[8,128,1280]{2,1,0:T(8,128)(2,1)S(1)} %assemble.6), channel_id=1, source_target_pairs={{0,8},{8,0},{16,24},{24,16},{32,40},{40,32},{48,56},{56,48},{64,72... | collective-permute-start | bytes 7864328 | tf_op jit(solution)/shard_map/ppermute | solution.py:29
  78.3 28.9 %collective-permute-start.13 = (bf16[8,120,640]{2,1,0:T(8,128)(2,1)}, bf16[8,120,640]{2,1,0:T(8,128)(2,1)}, u32[]{:S(2)}, u32[]{:S(2)}) collective-permute-start(bf16[8,120,640]{2,1,0:T(8,128)(2,1)} %constant_dynamic-update-slice_fusion.5.refs_0_), channel_id=1, source_target_pairs={{0,32},{8,40},{16,48},{24,56},{32,0},{40,8},{48,16},{56,24},{64,96... | collective-permute-start | bytes 3686408 | tf_op jit(solution)/shard_map/ppermute | solution.py:29
  79.6 56.5 %collective-permute-start.14 = (bf16[8,120,640]{2,1,0:T(8,128)(2,1)}, bf16[8,120,640]{2,1,0:T(8,128)(2,1)}, u32[]{:S(2)}, u32[]{:S(2)}) collective-permute-start(bf16[8,120,640]{2,1,0:T(8,128)(2,1)} %constant_dynamic-update-slice_fusion.5.refs_0_), channel_id=1, source_target_pairs={{0,64},{8,72},{16,80},{24,88},{32,96},{40,104},{48,112},{56,120},{... | collective-permute-start | bytes 3686408 | tf_op jit(solution)/shard_map/ppermute | solution.py:29
  82.3 56.4 %collective-permute-start.15 = (bf16[8,120,640]{2,1,0:T(8,128)(2,1)}, bf16[8,120,640]{2,1,0:T(8,128)(2,1)}, u32[]{:S(2)}, u32[]{:S(2)}) collective-permute-start(bf16[8,120,640]{2,1,0:T(8,128)(2,1)} %constant_dynamic-update-slice_fusion.5.refs_0_), channel_id=1, source_target_pairs={{0,96},{8,104},{16,112},{24,120},{32,64},{40,72},{48,80},{56,88},{... | collective-permute-start | bytes 3686408 | tf_op jit(solution)/shard_map/ppermute | solution.py:29
  93.3 61.0 %collective-permute-start.23 = (bf16[120,640]{1,0:T(8,128)(2,1)S(1)}, bf16[120,640]{1,0:T(8,128)(2,1)}, u32[]{:S(2)}, u32[]{:S(2)}) collective-permute-start(bf16[120,640]{1,0:T(8,128)(2,1)S(1)} %bitcast.206), channel_id=1, source_target_pairs={{0,4},{1,5},{2,6},{3,7},{4,0},{5,1},{6,2},{7,3},{8,12},{9,13},{10,... | collective-permute-start | bytes 460808 | tf_op jit(solution)/shard_map/ppermute | solution.py:29
  107.3 48.0 %collective-permute-start.18 = (bf16[2,320,480]{2,1,0:T(8,128)(2,1)S(1)}, bf16[2,320,480]{2,1,0:T(8,128)(2,1)S(1)}, u32[]{:S(2)}, u32[]{:S(2)}) collective-permute-start(bf16[2,320,480]{2,1,0:T(8,128)(2,1)S(1)} %pad_maximum_fusion.3.refs_0_), channel_id=1, source_target_pairs={{0,1},{1,0},{2,3},{3,2},{4,5},{5,4},{6,7},{7,6},{8,9},{9,8},{10,11... | collective-permute-start | bytes 1843208 | tf_op jit(solution)/shard_map/ppermute | solution.py:29
  138.7 29.6 %collective-permute-start.20 = (bf16[2,320,480]{2,1,0:T(8,128)(2,1)S(1)}, bf16[2,320,480]{2,1,0:T(8,128)(2,1)S(1)}, u32[]{:S(2)}, u32[]{:S(2)}) collective-permute-start(bf16[2,320,480]{2,1,0:T(8,128)(2,1)S(1)} %pad_maximum_fusion.3.refs_0_), channel_id=1, source_target_pairs={{0,3},{1,2},{2,1},{3,0},{4,7},{5,6},{6,5},{7,4},{8,11},{9,10},{10,... | collective-permute-start | bytes 1843208 | tf_op jit(solution)/shard_map/ppermute | solution.py:29
  145.7 192.9 %collective-permute-start.16 = (bf16[960,2560]{1,0:T(8,128)(2,1)}, bf16[960,2560]{1,0:T(8,128)(2,1)}, u32[]{:S(2)}, u32[]{:S(2)}) collective-permute-start(bf16[960,2560]{1,0:T(8,128)(2,1)} %bitcast.174), channel_id=1, source_target_pairs={{0,8},{8,0},{16,24},{24,16},{32,40},{40,32},{48,56},{56,48},{64,72... | collective-permute-start | bytes 14745608 | tf_op jit(solution)/shard_map/ppermute | solution.py:29
  186.6 48.3 %collective-permute-start.27 = (bf16[2,128,1280]{2,1,0:T(8,128)(2,1)S(1)}, bf16[2,128,1280]{2,1,0:T(8,128)(2,1)}, u32[]{:S(2)}, u32[]{:S(2)}) collective-permute-start(bf16[2,128,1280]{2,1,0:T(8,128)(2,1)S(1)} %pad_maximum_fusion.4.refs_0_), channel_id=1, source_target_pairs={{0,1},{1,0},{2,3},{3,2},{4,5},{5,4},{6,7},{7,6},{8,9},{9,8},{10,11... | collective-permute-start | bytes 1966088 | tf_op jit(solution)/shard_map/ppermute | solution.py:29
  201.0 33.5 %collective-permute-start.12 = (bf16[2,176,640]{2,1,0:T(8,128)(2,1)}, bf16[2,176,640]{2,1,0:T(8,128)(2,1)S(1)}, u32[]{:S(2)}, u32[]{:S(2)}) collective-permute-start(bf16[2,176,640]{2,1,0:T(8,128)(2,1)} %pad_maximum_fusion.6), channel_id=1, source_target_pairs={{0,3},{1,2},{2,1},{3,0},{4,7},{5,6},{6,5},{7,4},{8,11},{9,10},{10,... | collective-permute-start | bytes 1351688 | tf_op jit(solution)/shard_map/ppermute | solution.py:29
  201.3 35.8 %collective-permute-start.28 = (bf16[2,128,1280]{2,1,0:T(8,128)(2,1)S(1)}, bf16[2,128,1280]{2,1,0:T(8,128)(2,1)S(1)}, u32[]{:S(2)}, u32[]{:S(2)}) collective-permute-start(bf16[2,128,1280]{2,1,0:T(8,128)(2,1)S(1)} %pad_maximum_fusion.4.refs_0_), channel_id=1, source_target_pairs={{0,2},{1,3},{2,0},{3,1},{4,6},{5,7},{6,4},{7,5},{8,10},{9,11},{10,... | collective-permute-start | bytes 1966088 | tf_op jit(solution)/shard_map/ppermute | solution.py:29
  217.9 44.3 %collective-permute-start.30 = (bf16[8,120,640]{2,1,0:T(8,128)(2,1)S(1)}, bf16[8,120,640]{2,1,0:T(8,128)(2,1)S(1)}, u32[]{:S(2)}, u32[]{:S(2)}) collective-permute-start(bf16[8,120,640]{2,1,0:T(8,128)(2,1)S(1)} %constant_dynamic-update-slice_fusion.10.refs_0_), channel_id=1, source_target_pairs={{0,32},{8,40},{16,48},{24,56},{32,0},{40,8},{48,16},{56,24},{64,96... | collective-permute-start | bytes 3686408 | tf_op jit(solution)/shard_map/ppermute | solution.py:29
  234.5 35.6 %collective-permute-start.31 = (bf16[8,120,640]{2,1,0:T(8,128)(2,1)S(1)}, bf16[8,120,640]{2,1,0:T(8,128)(2,1)S(1)}, u32[]{:S(2)}, u32[]{:S(2)}) collective-permute-start(bf16[8,120,640]{2,1,0:T(8,128)(2,1)S(1)} %constant_dynamic-update-slice_fusion.10.refs_0_), channel_id=1, source_target_pairs={{0,64},{8,72},{16,80},{24,88},{32,96},{40,104},{48,112},{56,120},{... | collective-permute-start | bytes 3686408 | tf_op jit(solution)/shard_map/ppermute | solution.py:29
  234.9 52.6 %collective-permute-start.32 = (bf16[8,120,640]{2,1,0:T(8,128)(2,1)S(1)}, bf16[8,120,640]{2,1,0:T(8,128)(2,1)S(1)}, u32[]{:S(2)}, u32[]{:S(2)}) collective-permute-start(bf16[8,120,640]{2,1,0:T(8,128)(2,1)S(1)} %constant_dynamic-update-slice_fusion.10.refs_0_), channel_id=1, source_target_pairs={{0,96},{8,104},{16,112},{24,120},{32,64},{40,72},{48,80},{56,88},{... | collective-permute-start | bytes 3686408 | tf_op jit(solution)/shard_map/ppermute | solution.py:29
  249.6 94.4 %collective-permute-start.21 = (bf16[2560,480]{0,1:T(8,128)(2,1)}, bf16[2560,480]{0,1:T(8,128)(2,1)}, u32[]{:S(2)}, u32[]{:S(2)}) collective-permute-start(bf16[2560,480]{0,1:T(8,128)(2,1)} %copy.139), channel_id=1, source_target_pairs={{0,8},{8,0},{16,24},{24,16},{32,40},{40,32},{48,56},{56,48},{64,72... | collective-permute-start | bytes 7372808 | tf_op jit(solution)/shard_map/ppermute | solution.py:29
  312.0 36.5 %collective-permute-start.37 = (bf16[8,128,1280]{2,1,0:T(8,128)(2,1)}, bf16[8,128,1280]{2,1,0:T(8,128)(2,1)}, u32[]{:S(2)}, u32[]{:S(2)}) collective-permute-start(bf16[8,128,1280]{2,1,0:T(8,128)(2,1)} %assemble.9), channel_id=1, source_target_pairs={{0,8},{8,0},{16,24},{24,16},{32,40},{40,32},{48,56},{56,48},{64,72... | collective-permute-start | bytes 7864328 | tf_op jit(solution)/shard_map/ppermute | solution.py:29
  324.2 77.6 %collective-permute-start.43 = (bf16[2560,480]{0,1:T(8,128)(2,1)}, bf16[2560,480]{0,1:T(8,128)(2,1)}, u32[]{:S(2)}, u32[]{:S(2)}) collective-permute-start(bf16[2560,480]{0,1:T(8,128)(2,1)} %copy.145), channel_id=1, source_target_pairs={{0,8},{8,0},{16,24},{24,16},{32,40},{40,32},{48,56},{56,48},{64,72... | collective-permute-start | bytes 7372808 | tf_op jit(solution)/shard_map/ppermute | solution.py:29
  332.5 65.7 %collective-permute-start.42 = (bf16[960,2560]{1,0:T(8,128)(2,1)}, bf16[960,2560]{1,0:T(8,128)(2,1)}, u32[]{:S(2)}, u32[]{:S(2)}) collective-permute-start(bf16[960,2560]{1,0:T(8,128)(2,1)} %bitcast.177), channel_id=1, source_target_pairs={{0,8},{8,0},{16,24},{24,16},{32,40},{40,32},{48,56},{56,48},{64,72... | collective-permute-start | bytes 14745608 | tf_op jit(solution)/shard_map/ppermute | solution.py:29
  437.3 123.0 %reduce-scatter.9.cloned.1.call-start = ((), (), s32[]{:S(2)}) async-start(), calls=%async_computation.7 | async-start | bytes 6144000 | tf_op jit(solution)/shard_map/reduce_scatter | solution.py:58
  468.9 126.0 %reduce-scatter.11.cloned.1.call-start = ((), (), s32[]{:S(2)}) async-start(), calls=%async_computation.8 | async-start | bytes 3276800 | tf_op jit(solution)/shard_map/reduce_scatter | solution.py:58
  487.0 40.7 %collective-permute-start.45 = (bf16[2,176,640]{2,1,0:T(8,128)(2,1)S(1)}, bf16[2,176,640]{2,1,0:T(8,128)(2,1)S(1)}, u32[]{:S(2)}, u32[]{:S(2)}) collective-permute-start(bf16[2,176,640]{2,1,0:T(8,128)(2,1)S(1)} %bitcast.213), channel_id=1, source_target_pairs={{0,2},{1,3},{2,0},{3,1},{4,6},{5,7},{6,4},{7,5},{8,10},{9,11},{10,... | collective-permute-start | bytes 1351688 | tf_op jit(solution)/shard_map/ppermute | solution.py:29
  488.3 39.4 %collective-permute-start.46 = (bf16[2,176,640]{2,1,0:T(8,128)(2,1)S(1)}, bf16[2,176,640]{2,1,0:T(8,128)(2,1)S(1)}, u32[]{:S(2)}, u32[]{:S(2)}) collective-permute-start(bf16[2,176,640]{2,1,0:T(8,128)(2,1)S(1)} %bitcast.212), channel_id=1, source_target_pairs={{0,3},{1,2},{2,1},{3,0},{4,7},{5,6},{6,5},{7,4},{8,11},{9,10},{10,... | collective-permute-start | bytes 1351688 | tf_op jit(solution)/shard_map/ppermute | solution.py:29
  560.3 102.4 %reduce-scatter.13.cloned.1.call-start = ((), (), s32[]{:S(2)}) async-start(), calls=%async_computation.9 | async-start | bytes 3276800 | tf_op jit(solution)/shard_map/reduce_scatter | solution.py:58
  575.4 81.2 %collective-permute-start.54 = (bf16[960,2560]{1,0:T(8,128)(2,1)}, bf16[960,2560]{1,0:T(8,128)(2,1)}, u32[]{:S(2)}, u32[]{:S(2)}) collective-permute-start(bf16[960,2560]{1,0:T(8,128)(2,1)} %convolution_convert_fusion.1), channel_id=1, source_target_pairs={{0,8},{8,0},{16,24},{24,16},{32,40},{40,32},{48,56},{56,48},{64,72... | collective-permute-start | bytes 14745608 | tf_op jit(solution)/shard_map/ppermute | solution.py:29
  594.9 252.6 %reduce-scatter.15.cloned.1.call-start = ((), (), s32[]{:S(2)}) async-start(), calls=%async_computation.10 | async-start | bytes 6144000 | tf_op jit(solution)/shard_map/reduce_scatter | solution.py:58
  618.6 29.6 %collective-permute-start.49 = (bf16[2,176,640]{2,1,0:T(8,128)(2,1)S(1)}, bf16[2,176,640]{2,1,0:T(8,128)(2,1)S(1)}, u32[]{:S(2)}, u32[]{:S(2)}) collective-permute-start(bf16[2,176,640]{2,1,0:T(8,128)(2,1)S(1)} %bitcast.210), channel_id=1, source_target_pairs={{0,2},{1,3},{2,0},{3,1},{4,6},{5,7},{6,4},{7,5},{8,10},{9,11},{10,... | collective-permute-start | bytes 1351688 | tf_op jit(solution)/shard_map/ppermute | solution.py:29
  618.9 29.3 %collective-permute-start.50 = (bf16[2,176,640]{2,1,0:T(8,128)(2,1)S(1)}, bf16[2,176,640]{2,1,0:T(8,128)(2,1)S(1)}, u32[]{:S(2)}, u32[]{:S(2)}) collective-permute-start(bf16[2,176,640]{2,1,0:T(8,128)(2,1)S(1)} %bitcast.209), channel_id=1, source_target_pairs={{0,3},{1,2},{2,1},{3,0},{4,7},{5,6},{6,5},{7,4},{8,11},{9,10},{10,... | collective-permute-start | bytes 1351688 | tf_op jit(solution)/shard_map/ppermute | solution.py:29
  662.7 285.7 %reduce-scatter.17.cloned.1.call-start = ((), (), s32[]{:S(2)}) async-start(), calls=%async_computation.11 | async-start | bytes 3276800 | tf_op jit(solution)/shard_map/reduce_scatter | solution.py:58
  682.0 28.2 %collective-permute-start.102 = (bf16[320,480]{1,0:T(8,128)(2,1)S(1)}, bf16[320,480]{1,0:T(8,128)(2,1)S(1)}, u32[]{:S(2)}, u32[]{:S(2)}) collective-permute-start(bf16[320,480]{1,0:T(8,128)(2,1)S(1)} %get-tuple-element.220), channel_id=1, source_target_pairs={{0,16},{1,18},{2,20},{3,22},{4,17},{5,19},{6,21},{7,23},{8,24},{9,... | collective-permute-start | bytes 921608 | tf_op jit(solution)/shard_map/ppermute | solution.py:75
  684.9 73.9 %collective-permute-start.84 = (bf16[120,2560]{1,0:T(8,128)(2,1)S(1)}, bf16[120,2560]{1,0:T(8,128)(2,1)S(1)}, u32[]{:S(2)}, u32[]{:S(2)}) collective-permute-start(bf16[120,2560]{1,0:T(8,128)(2,1)S(1)} %get-tuple-element.178), channel_id=1, source_target_pairs={{0,0},{1,2},{2,4},{3,6},{4,1},{5,3},{6,5},{7,7},{8,8},{9,10},{10,1... | collective-permute-start | bytes 1843208 | tf_op jit(solution)/shard_map/ppermute | solution.py:75
  686.8 74.6 %collective-permute-start.86 = (bf16[120,2560]{1,0:T(8,128)(2,1)S(1)}, bf16[120,2560]{1,0:T(8,128)(2,1)S(1)}, u32[]{:S(2)}, u32[]{:S(2)}) collective-permute-start(bf16[120,2560]{1,0:T(8,128)(2,1)S(1)} %get-tuple-element.178), channel_id=1, source_target_pairs={{0,16},{1,18},{2,20},{3,22},{4,17},{5,19},{6,21},{7,23},{8,24},{9,... | collective-permute-start | bytes 1843208 | tf_op jit(solution)/shard_map/ppermute | solution.py:75
  696.1 65.1 %collective-permute-start.85 = (bf16[120,2560]{1,0:T(8,128)(2,1)S(1)}, bf16[120,2560]{1,0:T(8,128)(2,1)S(1)}, u32[]{:S(2)}, u32[]{:S(2)}) collective-permute-start(bf16[120,2560]{1,0:T(8,128)(2,1)S(1)} %get-tuple-element.179), channel_id=1, source_target_pairs={{0,1},{1,3},{2,5},{3,7},{4,0},{5,2},{6,4},{7,6},{8,9},{9,11},{10,1... | collective-permute-start | bytes 1843208 | tf_op jit(solution)/shard_map/ppermute | solution.py:75
  701.4 60.0 %collective-permute-start.87 = (bf16[120,2560]{1,0:T(8,128)(2,1)S(1)}, bf16[120,2560]{1,0:T(8,128)(2,1)S(1)}, u32[]{:S(2)}, u32[]{:S(2)}) collective-permute-start(bf16[120,2560]{1,0:T(8,128)(2,1)S(1)} %get-tuple-element.179), channel_id=1, source_target_pairs={{0,17},{1,19},{2,21},{3,23},{4,16},{5,18},{6,20},{7,22},{8,25},{9,... | collective-permute-start | bytes 1843208 | tf_op jit(solution)/shard_map/ppermute | solution.py:75
  710.2 47.1 %collective-permute-start.103 = (bf16[320,480]{1,0:T(8,128)(2,1)S(1)}, bf16[320,480]{1,0:T(8,128)(2,1)S(1)}, u32[]{:S(2)}, u32[]{:S(2)}) collective-permute-start(bf16[320,480]{1,0:T(8,128)(2,1)S(1)} %get-tuple-element.221), channel_id=1, source_target_pairs={{0,17},{1,19},{2,21},{3,23},{4,16},{5,18},{6,20},{7,22},{8,25},{9,... | collective-permute-start | bytes 921608 | tf_op jit(solution)/shard_map/ppermute | solution.py:75
  761.9 39.5 %collective-permute-start.89 = (bf16[120,2560]{1,0:T(8,128)(2,1)S(1)}, bf16[120,2560]{1,0:T(8,128)(2,1)S(1)}, u32[]{:S(2)}, u32[]{:S(2)}) collective-permute-start(bf16[120,2560]{1,0:T(8,128)(2,1)S(1)} %add_convert_fusion.5), channel_id=1, source_target_pairs={{0,64},{8,72},{16,80},{24,88},{32,96},{40,104},{48,112},{56,120},{... | collective-permute-start | bytes 1843208 | tf_op jit(solution)/shard_map/ppermute | solution.py:29
  765.7 37.7 %collective-permute-start.90 = (bf16[120,2560]{1,0:T(8,128)(2,1)S(1)}, bf16[120,2560]{1,0:T(8,128)(2,1)S(1)}, u32[]{:S(2)}, u32[]{:S(2)}) collective-permute-start(bf16[120,2560]{1,0:T(8,128)(2,1)S(1)} %add_convert_fusion.5), channel_id=1, source_target_pairs={{0,96},{8,104},{16,112},{24,120},{32,64},{40,72},{48,80},{56,88},{... | collective-permute-start | bytes 1843208 | tf_op jit(solution)/shard_map/ppermute | solution.py:29
  776.2 29.0 %collective-permute-start.107 = (bf16[320,480]{1,0:T(8,128)(2,1)S(1)}, bf16[320,480]{1,0:T(8,128)(2,1)S(1)}, u32[]{:S(2)}, u32[]{:S(2)}) collective-permute-start(bf16[320,480]{1,0:T(8,128)(2,1)S(1)} %add_convert_fusion.8), channel_id=1, source_target_pairs={{0,8},{8,0},{16,24},{24,16},{32,40},{40,32},{48,56},{56,48},{64,72... | collective-permute-start | bytes 921608 | tf_op jit(solution)/shard_map/ppermute | solution.py:29
  848.9 36.1 %collective-permute-start.76 = (bf16[120,2560]{1,0:T(8,128)(2,1)S(1)}, bf16[120,2560]{1,0:T(8,128)(2,1)S(1)}, u32[]{:S(2)}, u32[]{:S(2)}) collective-permute-start(bf16[120,2560]{1,0:T(8,128)(2,1)S(1)} %get-tuple-element.176), channel_id=1, source_target_pairs={{0,0},{1,2},{2,4},{3,6},{4,1},{5,3},{6,5},{7,7},{8,8},{9,10},{10,1... | collective-permute-start | bytes 1843208 | tf_op jit(solution)/shard_map/ppermute | solution.py:75
  852.7 52.8 %collective-permute-start.78 = (bf16[120,2560]{1,0:T(8,128)(2,1)S(1)}, bf16[120,2560]{1,0:T(8,128)(2,1)S(1)}, u32[]{:S(2)}, u32[]{:S(2)}) collective-permute-start(bf16[120,2560]{1,0:T(8,128)(2,1)S(1)} %get-tuple-element.176), channel_id=1, source_target_pairs={{0,16},{1,18},{2,20},{3,22},{4,17},{5,19},{6,21},{7,23},{8,24},{9,... | collective-permute-start | bytes 1843208 | tf_op jit(solution)/shard_map/ppermute | solution.py:75
  857.0 35.0 %collective-permute-start.77 = (bf16[120,2560]{1,0:T(8,128)(2,1)S(1)}, bf16[120,2560]{1,0:T(8,128)(2,1)S(1)}, u32[]{:S(2)}, u32[]{:S(2)}) collective-permute-start(bf16[120,2560]{1,0:T(8,128)(2,1)S(1)} %get-tuple-element.177), channel_id=1, source_target_pairs={{0,1},{1,3},{2,5},{3,7},{4,0},{5,2},{6,4},{7,6},{8,9},{9,11},{10,1... | collective-permute-start | bytes 1843208 | tf_op jit(solution)/shard_map/ppermute | solution.py:75
  858.8 52.0 %collective-permute-start.79 = (bf16[120,2560]{1,0:T(8,128)(2,1)S(1)}, bf16[120,2560]{1,0:T(8,128)(2,1)S(1)}, u32[]{:S(2)}, u32[]{:S(2)}) collective-permute-start(bf16[120,2560]{1,0:T(8,128)(2,1)S(1)} %get-tuple-element.177), channel_id=1, source_target_pairs={{0,17},{1,19},{2,21},{3,23},{4,16},{5,18},{6,20},{7,22},{8,25},{9,... | collective-permute-start | bytes 1843208 | tf_op jit(solution)/shard_map/ppermute | solution.py:75
  867.6 47.5 %collective-permute-start.96 = (bf16[320,480]{1,0:T(8,128)(2,1)S(1)}, bf16[320,480]{1,0:T(8,128)(2,1)S(1)}, u32[]{:S(2)}, u32[]{:S(2)}) collective-permute-start(bf16[320,480]{1,0:T(8,128)(2,1)S(1)} %add_convert_fusion.11), channel_id=1, source_target_pairs={{0,32},{8,40},{16,48},{24,56},{32,0},{40,8},{48,16},{56,24},{64,96... | collective-permute-start | bytes 921608 | tf_op jit(solution)/shard_map/ppermute | solution.py:29
  885.1 30.3 %collective-permute-start.97 = (bf16[320,480]{1,0:T(8,128)(2,1)S(1)}, bf16[320,480]{1,0:T(8,128)(2,1)S(1)}, u32[]{:S(2)}, u32[]{:S(2)}) collective-permute-start(bf16[320,480]{1,0:T(8,128)(2,1)S(1)} %add_convert_fusion.11), channel_id=1, source_target_pairs={{0,64},{8,72},{16,80},{24,88},{32,96},{40,104},{48,112},{56,120},{... | collective-permute-start | bytes 921608 | tf_op jit(solution)/shard_map/ppermute | solution.py:29
  911.3 29.7 %collective-permute-start.81 = (bf16[120,2560]{1,0:T(8,128)(2,1)S(1)}, bf16[120,2560]{1,0:T(8,128)(2,1)S(1)}, u32[]{:S(2)}, u32[]{:S(2)}) collective-permute-start(bf16[120,2560]{1,0:T(8,128)(2,1)S(1)} %add_convert_fusion.7), channel_id=1, source_target_pairs={{0,64},{8,72},{16,80},{24,88},{32,96},{40,104},{48,112},{56,120},{... | collective-permute-start | bytes 1843208 | tf_op jit(solution)/shard_map/ppermute | solution.py:29
  915.5 30.8 %collective-permute-start.99 = (bf16[320,480]{1,0:T(8,128)(2,1)S(1)}, bf16[320,480]{1,0:T(8,128)(2,1)S(1)}, u32[]{:S(2)}, u32[]{:S(2)}) collective-permute-start(bf16[320,480]{1,0:T(8,128)(2,1)S(1)} %add_convert_fusion.10), channel_id=1, source_target_pairs={{0,8},{8,0},{16,24},{24,16},{32,40},{40,32},{48,56},{56,48},{64,72... | collective-permute-start | bytes 921608 | tf_op jit(solution)/shard_map/ppermute | solution.py:29
  (209 other events, 3135.1 us)
Sparse Core Ops, SparseCore 0:
  437.4 31.4 reduce-scatter.6
  471.3 71.7 reduce-scatter.8
  560.5 34.3 reduce-scatter.10
  597.3 43.1 reduce-scatter.12
  662.9 88.5 reduce-scatter.14
  847.7 54.7 reduce-scatter.16

commit v4 on v3

--- a/solution.py
+++ b/solution.py
@@ -79,11 +79,38 @@
     return (near + far).astype(bf16)
 
 
-def finish_sum(pair):
-    total = to_owners(pair)
-    parts = [total] + [swap(total, "rep", 4 * m) for m in range(1, 4)]
-    parts = [part.astype(f32) for part in parts]
-    return ((parts[0] + parts[1]) + (parts[2] + parts[3])).astype(bf16)
+def y_position():
+    return lax.axis_index("rep") // 4
+
+
+def sum_over_y(block_of):
+    y = y_position()
+    total = block_of(y).astype(f32)
+    for m in range(1, 4):
+        total = total + swap(block_of(jnp.bitwise_xor(y, m)), "rep", 4 * m).astype(f32)
+    return total.astype(bf16)
+
+
+def spread_over_y(block, axis):
+    y = y_position()
+    parts = [block] + [swap(block, "rep", 4 * m) for m in range(1, 4)]
+    parts = [jnp.where(y % 2 == 1, parts[m ^ 1], parts[m]) for m in range(4)]
+    parts = [jnp.where(y >= 2, parts[m ^ 2], parts[m]) for m in range(4)]
+    return jnp.concatenate(parts, axis=axis)
+
+
+def finish_rows(rows):
+    count, columns = rows.shape
+    blocks = rows.reshape(2, 4, count // 8, columns)
+    total = sum_over_y(lambda k: lax.dynamic_index_in_dim(blocks, k, axis=1, keepdims=False))
+    own = spread_over_y(to_owners(total), 0)
+    return own, swap_core(own)
+
+
+def finish_columns(columns):
+    count, width = columns.shape
+    own = spread_over_y(to_owners(columns.reshape(2, count // 2, width)), 1)
+    return own, swap_core(own)
 
 
 def kernel_params():
@@ -144,7 +171,7 @@
 
 def gather_by_y(part, earlier):
     columns = part.shape[1] // 4
-    y = lax.axis_index("rep") // 4
+    y = y_position()
     quarter = lax.dynamic_slice_in_dim(part, y * columns, columns, axis=1)
     blocks = gather_blocks(quarter, earlier)
     joined = jnp.concatenate(blocks, axis=0)
@@ -351,47 +378,46 @@
         down = pick(down_weight[l][:, :half_width], down_weight[l][:, half_width:])
         return att, gate_up, down
 
-    def gather_parts(own, earlier):
+    def gather_parts(own):
         att, gate_up, down = own
-        by_y, blocks = gather_by_y(gate_up, earlier)
-        att_parts = gather_blocks(att, blocks)
-        down_parts = gather_blocks(down, att_parts)
-        return att_parts, by_y, down_parts
-
-    def whole_weights(parts, earlier):
-        att_parts, by_y, down_parts = parts if earlier is None else after(parts, earlier)
+        by_y, _ = gather_by_y(gate_up, None)
+        att_parts = gather_blocks(att, None)
+        return att_parts, by_y, gather_blocks(down, att_parts)
+
+    def attention_weights(att_parts):
         mine = assemble(att_parts, False)
         other = swap_core(mine)
         gain_attn = mine[:, shard, :shard].reshape(width).astype(f32)
         gain_mlp = mine[:, shard + 1, :shard].reshape(width).astype(f32)
         mine = mine[:, :shard].reshape(width, att_width)
         other = other[:, :shard].reshape(width, att_width)
-        query_key = pick(mine, other)
-        out_value = pick(other, mine)
+        return gain_attn, gain_mlp, pick(mine, other), pick(other, mine)
+
+    def mlp_weights(by_y, down_parts):
         mine = assemble(by_y, True).reshape(width, -1)
         gate_up = (mine, swap_core(mine))
         mine = assemble(down_parts, False).reshape(-1, half_width)
-        down = (mine, swap_core(mine))
-        return gain_attn, gain_mlp, query_key, out_value, gate_up, down
+        return gate_up, (mine, swap_core(mine))
 
     stream = tokens.astype(f32)
     saved = []
-    parts = gather_parts(own_weights(0), None)
-    layers = [whole_weights(parts, None)]
+    layers = []
+    parts = gather_parts(own_weights(0))
     for l in range(DECODER_LAYERS):
-        gain_attn, gain_mlp, query_key, out_value, gate_up, down = layers[l]
+        att_parts, by_y, down_parts = parts
+        gain_attn, gain_mlp, query_key, out_value = attention_weights(att_parts)
         normed = (normalize(stream) * gain_attn).astype(bf16)
         values = matmul(normed, out_value[:, width:]).astype(bf16)
         projected = matmul(normed, query_key)
-        if l + 1 < DECODER_LAYERS:
-            parts = gather_parts(own_weights(l + 1), (parts, projected))
         keys = rotary(projected[:, width:], cosine, sine).astype(bf16)
         kv = gather_pack(jnp.concatenate([keys, values], axis=1))
+        if l + 1 < DECODER_LAYERS:
+            parts = gather_parts(after(own_weights(l + 1), kv))
         queries = rotary(projected[:, :width], cosine, sine).astype(bf16)
         queries = queries * jnp.asarray(HEAD ** (-0.5), bf16)
         mixed, logs = attend(queries, kv, key_place, bounds)
-        if l + 1 < DECODER_LAYERS:
-            layers.append(whole_weights(parts, mixed))
+        gate_up, down = mlp_weights(*after((by_y, down_parts), mixed))
+        layers.append((gain_attn, gain_mlp, query_key, out_value, gate_up, down))
         middle = stream + matmul(mixed, out_value[:, :width])
         normed_mlp = (normalize(middle) * gain_mlp).astype(bf16)
         mine = matmul(normed_mlp, gate_up[0])
@@ -405,13 +431,8 @@
         stream = middle + jnp.concatenate([pick(mine, other), pick(other, mine)], axis=1)
     output = stream.astype(bf16)
 
-    earlier = output
-
-    def next_sum(rows):
-        nonlocal earlier
-        earlier = sum_over_x(after(rows, earlier))
-        return earlier
-
+    sums = ()
+    mlp_done = att_done = ()
     grad = cotangent.astype(f32)
     results = [None] * DECODER_LAYERS
     for l in reversed(range(DECODER_LAYERS)):
@@ -420,26 +441,33 @@
         grad_low = grad.astype(bf16)
         grad_a, grad_b = grad_low[:, :half_width], grad_low[:, half_width:]
         grad_mine, grad_other = pick(grad_a, grad_b), pick(grad_b, grad_a)
-        received = swap_core(cross_rows(hidden, grad_other).astype(bf16))
-        down_sum = (cross_rows(hidden, grad_mine) + received.astype(f32)).astype(bf16)
-        down_sum = next_sum(down_sum)
+        down_received = swap_core(cross_rows(hidden, grad_other).astype(bf16))
+        down_sum = (cross_rows(hidden, grad_mine) + down_received.astype(f32)).astype(bf16)
+        down_sum = sum_over_x(after(down_sum, sums))
 
         dhidden = matmul_nt(grad_mine, down[0]) + matmul_nt(grad_other, down[1])
         sigmoid = jax.nn.sigmoid(gate)
         dgate = (dhidden * up * sigmoid * (1.0 + gate * (1.0 - sigmoid))).astype(bf16)
         dup = (dhidden * gate * sigmoid).astype(bf16)
         dmine, dother = pick(dgate, dup), pick(dup, dgate)
-        received = swap_core(cross_rows(normed_mlp, dother).astype(bf16))
-        gate_up_sum = (cross_rows(normed_mlp, dmine) + received.astype(f32)).astype(bf16)
-        gate_up_sum = next_sum(gate_up_sum)
+        gate_up_received = swap_core(cross_rows(normed_mlp, dother).astype(bf16))
+        gate_up_sum = cross_rows(normed_mlp, dmine) + gate_up_received.astype(f32)
+        gate_up_sum = gate_up_sum.astype(bf16)
+        columns = gate_up_sum.shape[1] // 4
+        gate_up_sum = sum_over_y(
+            lambda k: lax.dynamic_slice_in_dim(gate_up_sum, k * columns, columns, axis=1)
+        )
+        gate_up_sum = sum_over_x(after(gate_up_sum, sums))
 
         dnormed = matmul_nt(dmine, gate_up[0]) + matmul_nt(dother, gate_up[1])
         dmiddle, mlp_gain_grad = normalize_back(middle, gain_mlp, dnormed)
         dmiddle = dmiddle + grad
         dmiddle_low = dmiddle.astype(bf16)
         dmixed = matmul_nt(dmiddle_low, out_value[:, :width]).astype(bf16)
+        dmixed = after(dmixed, mlp_done)
         dq, dkv = attend_back(queries, kv, key_place, bounds, mixed, logs, dmixed)
-        dkv = scatter_pack(dkv)
+        dkv = after(dkv, (down_received, gate_up_received))
+        dkv = after(scatter_pack(dkv), att_done)
         dq = rotary_back(dq, cosine, sine).astype(bf16)
         dk = rotary_back(dkv[:, :key_width], cosine, sine).astype(bf16)
         dv = dkv[:, key_width:].astype(bf16)
@@ -463,15 +491,13 @@
         gain_grads = gain_grads.reshape(2, -1, shard).swapaxes(0, 1)
         gain_grads = jnp.pad(gain_grads, ((0, 0), (0, 6), (0, att_width - shard)))
         att_sum = jnp.concatenate([att_sum.reshape(-1, shard, att_width), gain_grads], axis=1)
-        att_sum = next_sum(att_sum.reshape(-1, att_width))
-
-        def whole(pair):
-            own = finish_sum(pair)
-            return own, swap_core(own)
-
-        gate_up_own, gate_up_other = whole(gate_up_sum.reshape(2, shard, -1))
-        down_own, down_other = whole(down_sum.reshape(2, -1, half_width))
-        att_own, att_other = whole(att_sum.reshape(2, shard + 8, att_width))
+        att_sum = sum_over_x(att_sum.reshape(-1, att_width))
+        sums = (down_sum, gate_up_sum, att_sum)
+
+        mlp_done = (*finish_columns(gate_up_sum), *finish_rows(down_sum))
+        gate_up_own, gate_up_other, down_own, down_other = mlp_done
+        att_done = finish_rows(att_sum)
+        att_own, att_other = att_done
         att_a, att_b = pick(att_own, att_other), pick(att_other, att_own)
         results[l] = (
             att_own[shard, :shard],

time: 1020 us -> 892 us (0.87)
  waiting for transfers between devices: 487 us -> 322 us
  local copies, waits for them, and re-layouts: 67.4 us -> 85.9 us
  starting transfers between devices: 190 us -> 206 us
    ppermute x24, waiting for transfers between devices: 126 us -> 30.2 us  [send(): return lax.ppermute(block, ('rep', 'fsdp'), moves).astype(f32)]
    ppermute x84 -> x102, waiting for transfers between devices: 335 us -> 291 us  [swap(): return lax.ppermute(array, axis, [(i, i ^ mask) for i in range(count)])]
    reduce_scatter x6, waiting for transfers between devices: 26.1 us -> 0.08 us  [sum_over_x(): lax.psum_scatter(rows, 'fsdp', scatter_dimension=0, tiled=True, axis_inde...]
    ppermute x84 -> x102, starting transfers between devices: 133 us -> 152 us  [swap(): return lax.ppermute(array, axis, [(i, i ^ mask) for i in range(count)])]
    unnamed x306 -> x349, local copies, waits for them, and re-layouts: 30 us -> 43.2 us
  transfers between devices with their start and end apart: 114 -> 132, of which waited for: 61 -> 58; matrix products, arithmetic and copies ran while one was open for 22% -> 26% of each run, Pallas kernels for 6% -> 6%
where the time goes in v4:
time: 892 us; the launch traced here: 881 us
  waiting for transfers between devices  322 us (36%)
  starting transfers between devices  206 us (23%)
  matrix products  107 us (12%)
  other arithmetic  88.3 us (10%)
  local copies, waits for them, and re-layouts  85.9 us (10%)
  Pallas kernels  54.8 us (6%)
  between operations  17.2 us (2%)
    ppermute x102, waiting for transfers between devices, swap(): return lax.ppermute(array, axis, [(i, i ^ mask) for i in range(count)])  291 us
    ppermute x102, starting transfers between devices, swap(): return lax.ppermute(array, axis, [(i, i ^ mask) for i in range(count)])  152 us
    ppermute x24, starting transfers between devices, send(): return lax.ppermute(block, ('rep', 'fsdp'), moves).astype(f32)  53.7 us
    unnamed x349, local copies, waits for them, and re-layouts  43.2 us
    dot_general x16, matrix products, cross_rows(): lax.dot_general(left, right, (((0,), (0,)), ((), ())), preferred_element_...  43 us
    dot_general x14, matrix products, matmul_nt(): return lax.dot_general(left, right, NT, preferred_element_type=f32)  33.4 us
    dot_general x14, matrix products, matmul(): return jnp.dot(left, right, preferred_element_type=f32)  30.8 us
    ppermute x24, waiting for transfers between devices, send(): return lax.ppermute(block, ('rep', 'fsdp'), moves).astype(f32)  30.2 us
  transfers between devices with their start and end apart: 132, of which 58 were waited for; matrix products, arithmetic and copies ran while one was open for 26% of the time, Pallas kernels for 6%

profile of v4, /device:TPU:5, one launch (start us, length us, event | category | flops | bytes accessed | tf_op | source)
XLA Modules:
  0.0 881.5 jit_solution(10448016035636715299)
XLA Ops:
  44.8 13.2 %collective-permute-done.2.refs_2_ = bf16[2,128,1280]{2,1,0:T(8,128)(2,1)S(1)} collective-permute-done((bf16[2,128,1280]{2,1,0:T(8,128)(2,1)S(1)}, bf16[2,128,1280]{2,1,0:T(8,128)(2,1)S(1)}, u32[]{:S(2)}, u32[]{:S(2)}) %collective-permute-start.2) | collective-permute-done | bytes 655392 | tf_op jit(solution)/shard_map/ppermute | solution.py:29
  92.6 8.1 collective-permute-done.11
  105.6 7.5 collective-permute-done.17.refs_1_
  115.9 6.9 collective-permute-done.6
  125.3 8.8 collective-permute-done.7
  135.1 22.9 %collective-permute-done.8 = bf16[2,176,640]{2,1,0:T(8,128)(2,1)S(1)} collective-permute-done((bf16[2,176,640]{2,1,0:T(8,128)(2,1)S(1)}, bf16[2,176,640]{2,1,0:T(8,128)(2,1)S(1)}, u32[]{:S(2)}, u32[]{:S(2)}) %collective-permute-start.8) | collective-permute-done | bytes 450592 | tf_op jit(solution)/shard_map/ppermute | solution.py:29
  158.5 7.6 attention_forward.2
  166.9 7.1 collective-permute-done.19.refs_3_
  181.5 8.1 collective-permute-done.22
  194.3 13.0 %collective-permute-done.23.refs_1_ = bf16[2,128,1280]{2,1,0:T(8,128)(2,1)S(1)} collective-permute-done((bf16[2,128,1280]{2,1,0:T(8,128)(2,1)S(1)}, bf16[2,128,1280]{2,1,0:T(8,128)(2,1)S(1)}, u32[]{:S(2)}, u32[]{:S(2)}) %collective-permute-start.23) | collective-permute-done | bytes 655392 | tf_op jit(solution)/shard_map/ppermute | solution.py:29
  207.4 13.4 %collective-permute-done.24.refs_2_ = bf16[2,128,1280]{2,1,0:T(8,128)(2,1)S(1)} collective-permute-done((bf16[2,128,1280]{2,1,0:T(8,128)(2,1)S(1)}, bf16[2,128,1280]{2,1,0:T(8,128)(2,1)S(1)}, u32[]{:S(2)}, u32[]{:S(2)}) %collective-permute-start.24) | collective-permute-done | bytes 655392 | tf_op jit(solution)/shard_map/ppermute | solution.py:29
  242.3 4.8 fusion.196
  252.9 7.2 multiply_convert_fusion.5
  280.9 8.2 collective-permute-done.33
  294.0 7.6 collective-permute-done.39.refs_1_
  304.3 6.9 collective-permute-done.28
  313.8 8.7 collective-permute-done.29
  323.5 22.9 %collective-permute-done.30 = bf16[2,176,640]{2,1,0:T(8,128)(2,1)S(1)} collective-permute-done((bf16[2,176,640]{2,1,0:T(8,128)(2,1)S(1)}, bf16[2,176,640]{2,1,0:T(8,128)(2,1)S(1)}, u32[]{:S(2)}, u32[]{:S(2)}) %collective-permute-start.30) | collective-permute-done | bytes 450592 | tf_op jit(solution)/shard_map/ppermute | solution.py:29
  347.1 7.8 attention_forward.3
  354.9 7.8 collective-permute-done.41.refs_3_
  369.6 4.4 copy.144
  397.8 4.1 fusion.87
  401.9 4.2 multiply_reduce_fusion.1
  412.1 14.2 %attention_backward.2 = (f32[176,960]{1,0:T(8,128)S(1)}, bf16[1408,640]{1,0:T(8,128)(2,1)S(1)}) custom-call(bf16[176,960]{1,0:T(8,128)(2,1)S(1)} %copy-done.26, bf16[1408,640]{1,0:T(8,128)(2,1)S(1)} %bitcast.239, s32[1408,1]{1,0:T(8,128)S(1)} %copy-done.9, s32[8,528]{1,0:T(8,128)S(1)} %pad.19.bounds_ref, bf16[176,960]{1,0:T(8,128)(2,1)S(1)} %get-tuple-element.57.mixed_ref, ...), custom_call_target="tpu_custom_call" | custom-call | flops 2378956800 | bytes 6291456 | tf_op jit(solution)/shard_map/attention_backward/pallas_call | solution.py:272
  438.4 4.1 add_convert_fusion.3
  442.5 4.3 copy.166
  447.0 8.2 collective-permute-done.47
  500.5 21.8 %collective-permute-done.51 = bf16[960,640]{1,0:T(8,128)(2,1)} collective-permute-done((bf16[960,640]{1,0:T(8,128)(2,1)}, bf16[960,640]{1,0:T(8,128)(2,1)}, u32[]{:S(2)}, u32[]{:S(2)}) %collective-permute-start.51) | collective-permute-done | bytes 1228832 | tf_op jit(solution)/shard_map/ppermute | solution.py:29
  524.3 4.0 add_convert_fusion.5
  533.5 5.0 multiply_reduce_fusion
  544.4 4.3 fusion.2
  554.1 8.6 collective-permute-start.64
  581.0 5.0 collective-permute-done.54
  587.7 5.2 collective-permute-done.56
  596.7 4.3 collective-permute-done.57
  601.0 7.7 collective-permute-start.71
  612.8 4.3 add_convert_fusion.2
  618.0 13.9 %attention_backward.3 = (f32[176,960]{1,0:T(8,128)S(1)}, bf16[1408,640]{1,0:T(8,128)(2,1)S(1)}) custom-call(bf16[176,960]{1,0:T(8,128)(2,1)S(1)} %copy-done.24, bf16[1408,640]{1,0:T(8,128)(2,1)S(1)} %bitcast.237, s32[1408,1]{1,0:T(8,128)S(1)} %copy-done.10, s32[8,528]{1,0:T(8,128)S(1)} %pad.19.bounds_ref, bf16[176,960]{1,0:T(8,128)(2,1)S(1)} %copy-done.6, ...), custom_call_target="tpu_custom_call" | custom-call | flops 2378956800 | bytes 6291456 | tf_op jit(solution)/shard_map/attention_backward/pallas_call | solution.py:272
  647.0 21.2 %collective-permute-done.104 = bf16[960,640]{1,0:T(8,128)(2,1)} collective-permute-done((bf16[960,640]{1,0:T(8,128)(2,1)}, bf16[960,640]{1,0:T(8,128)(2,1)}, u32[]{:S(2)}, u32[]{:S(2)}) %collective-permute-start.104) | collective-permute-done | bytes 1228832 | tf_op jit(solution)/shard_map/ppermute | solution.py:29
  668.2 27.7 %collective-permute-done.105 = bf16[960,640]{1,0:T(8,128)(2,1)} collective-permute-done((bf16[960,640]{1,0:T(8,128)(2,1)}, bf16[960,640]{1,0:T(8,128)(2,1)}, u32[]{:S(2)}, u32[]{:S(2)}) %collective-permute-start.105) | collective-permute-done | bytes 1228832 | tf_op jit(solution)/shard_map/ppermute | solution.py:29
  699.0 4.1 add_convert_fusion.4
  729.4 8.1 collective-permute-start.90
  739.7 4.4 copy.168
  759.3 4.3 fusion.3
  788.7 4.0 collective-permute-done.111
  812.6 5.1 collective-permute-start.118
  835.4 4.2 collective-permute-start.125
  860.8 7.8 collective-permute-start.103
  (825 shorter events, 447.2 us)
Async XLA Ops:
  7.2 531.5 %reduce-scatter.19.cloned.1.call-start = ((), (), s32[]{:S(2)}) async-start(), calls=%async_computation.10 | async-start | bytes 3276800 | tf_op jit(solution)/shard_map/reduce_scatter | solution.py:58
  22.2 59.7 %collective-permute-start.9 = (bf16[120,640]{1,0:T(8,128)(2,1)}, bf16[120,640]{1,0:T(8,128)(2,1)S(1)}, u32[]{:S(2)}, u32[]{:S(2)}) collective-permute-start(bf16[120,640]{1,0:T(8,128)(2,1)} %bitcast.17), channel_id=1, source_target_pairs={{0,4},{1,5},{2,6},{3,7},{4,0},{5,1},{6,2},{7,3},{8,12},{9,13},{10,... | collective-permute-start | bytes 460808 | tf_op jit(solution)/shard_map/ppermute | solution.py:29
  24.9 62.0 %collective-permute-start.16 = (bf16[320,480]{1,0:T(8,128)(2,1)}, bf16[320,480]{1,0:T(8,128)(2,1)}, u32[]{:S(2)}, u32[]{:S(2)}) collective-permute-start(bf16[320,480]{1,0:T(8,128)(2,1)} %slice_select_fusion.1), channel_id=1, source_target_pairs={{0,4},{1,5},{2,6},{3,7},{4,0},{5,1},{6,2},{7,3},{8,12},{9,13},{10,... | collective-permute-start | bytes 921608 | tf_op jit(solution)/shard_map/ppermute | solution.py:29
  30.2 27.9 %collective-permute-start.2 = (bf16[2,128,1280]{2,1,0:T(8,128)(2,1)S(1)}, bf16[2,128,1280]{2,1,0:T(8,128)(2,1)S(1)}, u32[]{:S(2)}, u32[]{:S(2)}) collective-permute-start(bf16[2,128,1280]{2,1,0:T(8,128)(2,1)S(1)} %pad_maximum_fusion.2.refs_0_), channel_id=1, source_target_pairs={{0,2},{1,3},{2,0},{3,1},{4,6},{5,7},{6,4},{7,5},{8,10},{9,11},{10,... | collective-permute-start | bytes 1966088 | tf_op jit(solution)/shard_map/ppermute | solution.py:29
  30.7 28.2 %collective-permute-start.3 = (bf16[2,128,1280]{2,1,0:T(8,128)(2,1)S(1)}, bf16[2,128,1280]{2,1,0:T(8,128)(2,1)S(1)}, u32[]{:S(2)}, u32[]{:S(2)}) collective-permute-start(bf16[2,128,1280]{2,1,0:T(8,128)(2,1)S(1)} %pad_maximum_fusion.2.refs_0_), channel_id=1, source_target_pairs={{0,3},{1,2},{2,1},{3,0},{4,7},{5,6},{6,5},{7,4},{8,11},{9,10},{10,... | collective-permute-start | bytes 1966088 | tf_op jit(solution)/shard_map/ppermute | solution.py:29
  88.0 25.2 %collective-permute-start.17 = (bf16[2,320,480]{2,1,0:T(8,128)(2,1)S(1)}, bf16[2,320,480]{2,1,0:T(8,128)(2,1)S(1)}, u32[]{:S(2)}, u32[]{:S(2)}) collective-permute-start(bf16[2,320,480]{2,1,0:T(8,128)(2,1)S(1)} %pad_maximum_fusion.3.refs_0_), channel_id=1, source_target_pairs={{0,1},{1,0},{2,3},{3,2},{4,5},{5,4},{6,7},{7,6},{8,9},{9,8},{10,11... | collective-permute-start | bytes 1843208 | tf_op jit(solution)/shard_map/ppermute | solution.py:29
  90.4 32.4 %collective-permute-start.6 = (bf16[2,176,640]{2,1,0:T(8,128)(2,1)S(1)}, bf16[2,176,640]{2,1,0:T(8,128)(2,1)S(1)}, u32[]{:S(2)}, u32[]{:S(2)}) collective-permute-start(bf16[2,176,640]{2,1,0:T(8,128)(2,1)S(1)} %pad_maximum_fusion.8), channel_id=1, source_target_pairs={{0,1},{1,0},{2,3},{3,2},{4,5},{5,4},{6,7},{7,6},{8,9},{9,8},{10,11... | collective-permute-start | bytes 1351688 | tf_op jit(solution)/shard_map/ppermute | solution.py:29
  101.6 72.4 %collective-permute-start.13 = (bf16[8,120,640]{2,1,0:T(8,128)(2,1)S(1)}, bf16[8,120,640]{2,1,0:T(8,128)(2,1)S(1)}, u32[]{:S(2)}, u32[]{:S(2)}) collective-permute-start(bf16[8,120,640]{2,1,0:T(8,128)(2,1)S(1)} %constant_dynamic-update-slice_fusion.5.refs_0_), channel_id=1, source_target_pairs={{0,32},{8,40},{16,48},{24,56},{32,0},{40,8},{48,16},{56,24},{64,96... | collective-permute-start | bytes 3686408 | tf_op jit(solution)/shard_map/ppermute | solution.py:29
  103.0 71.1 %collective-permute-start.14 = (bf16[8,120,640]{2,1,0:T(8,128)(2,1)S(1)}, bf16[8,120,640]{2,1,0:T(8,128)(2,1)S(1)}, u32[]{:S(2)}, u32[]{:S(2)}) collective-permute-start(bf16[8,120,640]{2,1,0:T(8,128)(2,1)S(1)} %constant_dynamic-update-slice_fusion.5.refs_0_), channel_id=1, source_target_pairs={{0,64},{8,72},{16,80},{24,88},{32,96},{40,104},{48,112},{56,120},{... | collective-permute-start | bytes 3686408 | tf_op jit(solution)/shard_map/ppermute | solution.py:29
  105.6 68.4 %collective-permute-start.15 = (bf16[8,120,640]{2,1,0:T(8,128)(2,1)S(1)}, bf16[8,120,640]{2,1,0:T(8,128)(2,1)S(1)}, u32[]{:S(2)}, u32[]{:S(2)}) collective-permute-start(bf16[8,120,640]{2,1,0:T(8,128)(2,1)S(1)} %constant_dynamic-update-slice_fusion.5.refs_0_), channel_id=1, source_target_pairs={{0,96},{8,104},{16,112},{24,120},{32,64},{40,72},{48,80},{56,88},{... | collective-permute-start | bytes 3686408 | tf_op jit(solution)/shard_map/ppermute | solution.py:29
  113.2 20.9 %collective-permute-start.7 = (bf16[2,176,640]{2,1,0:T(8,128)(2,1)S(1)}, bf16[2,176,640]{2,1,0:T(8,128)(2,1)S(1)}, u32[]{:S(2)}, u32[]{:S(2)}) collective-permute-start(bf16[2,176,640]{2,1,0:T(8,128)(2,1)S(1)} %pad_maximum_fusion.8), channel_id=1, source_target_pairs={{0,2},{1,3},{2,0},{3,1},{4,6},{5,7},{6,4},{7,5},{8,10},{9,11},{10,... | collective-permute-start | bytes 1351688 | tf_op jit(solution)/shard_map/ppermute | solution.py:29
  122.8 35.3 %collective-permute-start.8 = (bf16[2,176,640]{2,1,0:T(8,128)(2,1)S(1)}, bf16[2,176,640]{2,1,0:T(8,128)(2,1)S(1)}, u32[]{:S(2)}, u32[]{:S(2)}) collective-permute-start(bf16[2,176,640]{2,1,0:T(8,128)(2,1)S(1)} %pad_maximum_fusion.8), channel_id=1, source_target_pairs={{0,3},{1,2},{2,1},{3,0},{4,7},{5,6},{6,5},{7,4},{8,11},{9,10},{10,... | collective-permute-start | bytes 1351688 | tf_op jit(solution)/shard_map/ppermute | solution.py:29
  134.1 32.8 %collective-permute-start.18 = (bf16[2,320,480]{2,1,0:T(8,128)(2,1)S(1)}, bf16[2,320,480]{2,1,0:T(8,128)(2,1)S(1)}, u32[]{:S(2)}, u32[]{:S(2)}) collective-permute-start(bf16[2,320,480]{2,1,0:T(8,128)(2,1)S(1)} %pad_maximum_fusion.3.refs_0_), channel_id=1, source_target_pairs={{0,2},{1,3},{2,0},{3,1},{4,6},{5,7},{6,4},{7,5},{8,10},{9,11},{10,... | collective-permute-start | bytes 1843208 | tf_op jit(solution)/shard_map/ppermute | solution.py:29
  177.3 75.6 %collective-permute-start.20 = (bf16[960,2560]{1,0:T(8,128)(2,1)}, bf16[960,2560]{1,0:T(8,128)(2,1)}, u32[]{:S(2)}, u32[]{:S(2)}) collective-permute-start(bf16[960,2560]{1,0:T(8,128)(2,1)} %bitcast.240), channel_id=1, source_target_pairs={{0,8},{8,0},{16,24},{24,16},{32,40},{40,32},{48,56},{56,48},{64,72... | collective-permute-start | bytes 14745608 | tf_op jit(solution)/shard_map/ppermute | solution.py:29
  193.0 27.7 %collective-permute-start.24 = (bf16[2,128,1280]{2,1,0:T(8,128)(2,1)S(1)}, bf16[2,128,1280]{2,1,0:T(8,128)(2,1)S(1)}, u32[]{:S(2)}, u32[]{:S(2)}) collective-permute-start(bf16[2,128,1280]{2,1,0:T(8,128)(2,1)S(1)} %pad_maximum_fusion.4.refs_0_), channel_id=1, source_target_pairs={{0,2},{1,3},{2,0},{3,1},{4,6},{5,7},{6,4},{7,5},{8,10},{9,11},{10,... | collective-permute-start | bytes 1966088 | tf_op jit(solution)/shard_map/ppermute | solution.py:29
  193.0 29.2 %collective-permute-start.25 = (bf16[2,128,1280]{2,1,0:T(8,128)(2,1)S(1)}, bf16[2,128,1280]{2,1,0:T(8,128)(2,1)S(1)}, u32[]{:S(2)}, u32[]{:S(2)}) collective-permute-start(bf16[2,128,1280]{2,1,0:T(8,128)(2,1)S(1)} %pad_maximum_fusion.4.refs_0_), channel_id=1, source_target_pairs={{0,3},{1,2},{2,1},{3,0},{4,7},{5,6},{6,5},{7,4},{8,11},{9,10},{10,... | collective-permute-start | bytes 1966088 | tf_op jit(solution)/shard_map/ppermute | solution.py:29
  224.6 25.3 %collective-permute-start.26 = (bf16[8,128,1280]{2,1,0:T(8,128)(2,1)}, bf16[8,128,1280]{2,1,0:T(8,128)(2,1)}, u32[]{:S(2)}, u32[]{:S(2)}) collective-permute-start(bf16[8,128,1280]{2,1,0:T(8,128)(2,1)} %assemble.9), channel_id=1, source_target_pairs={{0,8},{8,0},{16,24},{24,16},{32,40},{40,32},{48,56},{56,48},{64,72... | collective-permute-start | bytes 7864328 | tf_op jit(solution)/shard_map/ppermute | solution.py:29
  226.8 48.5 %collective-permute-start.38 = (bf16[320,480]{1,0:T(8,128)(2,1)}, bf16[320,480]{1,0:T(8,128)(2,1)}, u32[]{:S(2)}, u32[]{:S(2)}) collective-permute-start(bf16[320,480]{1,0:T(8,128)(2,1)} %slice_select_fusion), channel_id=1, source_target_pairs={{0,4},{1,5},{2,6},{3,7},{4,0},{5,1},{6,2},{7,3},{8,12},{9,13},{10,... | collective-permute-start | bytes 921608 | tf_op jit(solution)/shard_map/ppermute | solution.py:29
  231.2 38.6 %collective-permute-start.31 = (bf16[120,640]{1,0:T(8,128)(2,1)}, bf16[120,640]{1,0:T(8,128)(2,1)S(1)}, u32[]{:S(2)}, u32[]{:S(2)}) collective-permute-start(bf16[120,640]{1,0:T(8,128)(2,1)} %get-tuple-element.153), channel_id=1, source_target_pairs={{0,4},{1,5},{2,6},{3,7},{4,0},{5,1},{6,2},{7,3},{8,12},{9,13},{10,... | collective-permute-start | bytes 460808 | tf_op jit(solution)/shard_map/ppermute | solution.py:29
  238.3 22.4 %collective-permute-start.21 = (bf16[2560,480]{0,1:T(8,128)(2,1)}, bf16[2560,480]{0,1:T(8,128)(2,1)}, u32[]{:S(2)}, u32[]{:S(2)}) collective-permute-start(bf16[2560,480]{0,1:T(8,128)(2,1)} %copy.138), channel_id=1, source_target_pairs={{0,8},{8,0},{16,24},{24,16},{32,40},{40,32},{48,56},{56,48},{64,72... | collective-permute-start | bytes 7372808 | tf_op jit(solution)/shard_map/ppermute | solution.py:29
  276.5 25.1 %collective-permute-start.39 = (bf16[2,320,480]{2,1,0:T(8,128)(2,1)S(1)}, bf16[2,320,480]{2,1,0:T(8,128)(2,1)S(1)}, u32[]{:S(2)}, u32[]{:S(2)}) collective-permute-start(bf16[2,320,480]{2,1,0:T(8,128)(2,1)S(1)} %pad_maximum_fusion.5.refs_0_), channel_id=1, source_target_pairs={{0,1},{1,0},{2,3},{3,2},{4,5},{5,4},{6,7},{7,6},{8,9},{9,8},{10,11... | collective-permute-start | bytes 1843208 | tf_op jit(solution)/shard_map/ppermute | solution.py:29
  278.6 32.6 %collective-permute-start.28 = (bf16[2,176,640]{2,1,0:T(8,128)(2,1)S(1)}, bf16[2,176,640]{2,1,0:T(8,128)(2,1)S(1)}, u32[]{:S(2)}, u32[]{:S(2)}) collective-permute-start(bf16[2,176,640]{2,1,0:T(8,128)(2,1)S(1)} %pad_maximum_fusion.9), channel_id=1, source_target_pairs={{0,1},{1,0},{2,3},{3,2},{4,5},{5,4},{6,7},{7,6},{8,9},{9,8},{10,11... | collective-permute-start | bytes 1351688 | tf_op jit(solution)/shard_map/ppermute | solution.py:29
  290.0 72.7 %collective-permute-start.35 = (bf16[8,120,640]{2,1,0:T(8,128)(2,1)S(1)}, bf16[8,120,640]{2,1,0:T(8,128)(2,1)S(1)}, u32[]{:S(2)}, u32[]{:S(2)}) collective-permute-start(bf16[8,120,640]{2,1,0:T(8,128)(2,1)S(1)} %constant_dynamic-update-slice_fusion.15.refs_0_), channel_id=1, source_target_pairs={{0,32},{8,40},{16,48},{24,56},{32,0},{40,8},{48,16},{56,24},{64,96... | collective-permute-start | bytes 3686408 | tf_op jit(solution)/shard_map/ppermute | solution.py:29
  291.4 71.3 %collective-permute-start.36 = (bf16[8,120,640]{2,1,0:T(8,128)(2,1)S(1)}, bf16[8,120,640]{2,1,0:T(8,128)(2,1)S(1)}, u32[]{:S(2)}, u32[]{:S(2)}) collective-permute-start(bf16[8,120,640]{2,1,0:T(8,128)(2,1)S(1)} %constant_dynamic-update-slice_fusion.15.refs_0_), channel_id=1, source_target_pairs={{0,64},{8,72},{16,80},{24,88},{32,96},{40,104},{48,112},{56,120},{... | collective-permute-start | bytes 3686408 | tf_op jit(solution)/shard_map/ppermute | solution.py:29
  294.0 68.7 %collective-permute-start.37 = (bf16[8,120,640]{2,1,0:T(8,128)(2,1)S(1)}, bf16[8,120,640]{2,1,0:T(8,128)(2,1)S(1)}, u32[]{:S(2)}, u32[]{:S(2)}) collective-permute-start(bf16[8,120,640]{2,1,0:T(8,128)(2,1)S(1)} %constant_dynamic-update-slice_fusion.15.refs_0_), channel_id=1, source_target_pairs={{0,96},{8,104},{16,112},{24,120},{32,64},{40,72},{48,80},{56,88},{... | collective-permute-start | bytes 3686408 | tf_op jit(solution)/shard_map/ppermute | solution.py:29
  301.5 20.9 %collective-permute-start.29 = (bf16[2,176,640]{2,1,0:T(8,128)(2,1)S(1)}, bf16[2,176,640]{2,1,0:T(8,128)(2,1)S(1)}, u32[]{:S(2)}, u32[]{:S(2)}) collective-permute-start(bf16[2,176,640]{2,1,0:T(8,128)(2,1)S(1)} %pad_maximum_fusion.9), channel_id=1, source_target_pairs={{0,2},{1,3},{2,0},{3,1},{4,6},{5,7},{6,4},{7,5},{8,10},{9,11},{10,... | collective-permute-start | bytes 1351688 | tf_op jit(solution)/shard_map/ppermute | solution.py:29
  311.2 35.3 %collective-permute-start.30 = (bf16[2,176,640]{2,1,0:T(8,128)(2,1)S(1)}, bf16[2,176,640]{2,1,0:T(8,128)(2,1)S(1)}, u32[]{:S(2)}, u32[]{:S(2)}) collective-permute-start(bf16[2,176,640]{2,1,0:T(8,128)(2,1)S(1)} %pad_maximum_fusion.9), channel_id=1, source_target_pairs={{0,3},{1,2},{2,1},{3,0},{4,7},{5,6},{6,5},{7,4},{8,11},{9,10},{10,... | collective-permute-start | bytes 1351688 | tf_op jit(solution)/shard_map/ppermute | solution.py:29
  322.5 32.4 %collective-permute-start.40 = (bf16[2,320,480]{2,1,0:T(8,128)(2,1)S(1)}, bf16[2,320,480]{2,1,0:T(8,128)(2,1)S(1)}, u32[]{:S(2)}, u32[]{:S(2)}) collective-permute-start(bf16[2,320,480]{2,1,0:T(8,128)(2,1)S(1)} %pad_maximum_fusion.5.refs_0_), channel_id=1, source_target_pairs={{0,2},{1,3},{2,0},{3,1},{4,6},{5,7},{6,4},{7,5},{8,10},{9,11},{10,... | collective-permute-start | bytes 1843208 | tf_op jit(solution)/shard_map/ppermute | solution.py:29
  393.4 37.2 %collective-permute-start.45 = (bf16[960,2560]{1,0:T(8,128)(2,1)}, bf16[960,2560]{1,0:T(8,128)(2,1)}, u32[]{:S(2)}, u32[]{:S(2)}) collective-permute-start(bf16[960,2560]{1,0:T(8,128)(2,1)} %convolution_convert_fusion.1), channel_id=1, source_target_pairs={{0,8},{8,0},{16,24},{24,16},{32,40},{40,32},{48,56},{56,48},{64,72... | collective-permute-start | bytes 14745608 | tf_op jit(solution)/shard_map/ppermute | solution.py:29
  396.3 34.2 %collective-permute-start.44 = (bf16[2560,480]{0,1:T(8,128)(2,1)S(1)}, bf16[2560,480]{0,1:T(8,128)(2,1)}, u32[]{:S(2)}, u32[]{:S(2)}) collective-permute-start(bf16[2560,480]{0,1:T(8,128)(2,1)S(1)} %convolution_convert_fusion.3), channel_id=1, source_target_pairs={{0,8},{8,0},{16,24},{24,16},{32,40},{40,32},{48,56},{56,48},{64,72... | collective-permute-start | bytes 7372808 | tf_op jit(solution)/shard_map/ppermute | solution.py:29
  435.2 21.6 %collective-permute-start.48 = (bf16[2,176,640]{2,1,0:T(8,128)(2,1)}, bf16[2,176,640]{2,1,0:T(8,128)(2,1)}, u32[]{:S(2)}, u32[]{:S(2)}) collective-permute-start(bf16[2,176,640]{2,1,0:T(8,128)(2,1)} %bitcast.46), channel_id=1, source_target_pairs={{0,3},{1,2},{2,1},{3,0},{4,7},{5,6},{6,5},{7,4},{8,11},{9,10},{10,... | collective-permute-start | bytes 1351688 | tf_op jit(solution)/shard_map/ppermute | solution.py:29
  446.9 116.9 %reduce-scatter.11.cloned.1.call-start = ((), (), s32[]{:S(2)}) async-start(), calls=%async_computation.6 | async-start | bytes 1536000 | tf_op jit(solution)/shard_map/reduce_scatter | solution.py:58
  466.0 34.5 %collective-permute-start.50 = (bf16[960,640]{1,0:T(8,128)(2,1)}, bf16[960,640]{1,0:T(8,128)(2,1)}, u32[]{:S(2)}, u32[]{:S(2)}) collective-permute-start(bf16[960,640]{1,0:T(8,128)(2,1)} %get-tuple-element.173), channel_id=1, source_target_pairs={{0,32},{8,40},{16,48},{24,56},{32,0},{40,8},{48,16},{56,24},{64,96... | collective-permute-start | bytes 3686408 | tf_op jit(solution)/shard_map/ppermute | solution.py:29
  467.4 54.9 %collective-permute-start.51 = (bf16[960,640]{1,0:T(8,128)(2,1)}, bf16[960,640]{1,0:T(8,128)(2,1)}, u32[]{:S(2)}, u32[]{:S(2)}) collective-permute-start(bf16[960,640]{1,0:T(8,128)(2,1)} %get-tuple-element.175), channel_id=1, source_target_pairs={{0,64},{8,72},{16,80},{24,88},{32,96},{40,104},{48,112},{56,120},{... | collective-permute-start | bytes 3686408 | tf_op jit(solution)/shard_map/ppermute | solution.py:29
  470.0 54.3 %collective-permute-start.52 = (bf16[960,640]{1,0:T(8,128)(2,1)}, bf16[960,640]{1,0:T(8,128)(2,1)}, u32[]{:S(2)}, u32[]{:S(2)}) collective-permute-start(bf16[960,640]{1,0:T(8,128)(2,1)} %get-tuple-element.174), channel_id=1, source_target_pairs={{0,96},{8,104},{16,112},{24,120},{32,64},{40,72},{48,80},{56,88},{... | collective-permute-start | bytes 3686408 | tf_op jit(solution)/shard_map/ppermute | solution.py:29
  479.2 133.6 %collective-permute-start.72 = (bf16[2560,480]{0,1:T(8,128)(2,1)}, bf16[2560,480]{0,1:T(8,128)(2,1)}, u32[]{:S(2)}, u32[]{:S(2)}) collective-permute-start(bf16[2560,480]{0,1:T(8,128)(2,1)} %convolution_convert_fusion.2), channel_id=1, source_target_pairs={{0,8},{8,0},{16,24},{24,16},{32,40},{40,32},{48,56},{56,48},{64,72... | collective-permute-start | bytes 7372808 | tf_op jit(solution)/shard_map/ppermute | solution.py:29
  488.8 52.9 %collective-permute-start.78 = (bf16[960,1280]{1,0:T(8,128)(2,1)}, bf16[960,1280]{1,0:T(8,128)(2,1)}, u32[]{:S(2)}, u32[]{:S(2)}) collective-permute-start(bf16[960,1280]{1,0:T(8,128)(2,1)} %pad_maximum_fusion), channel_id=1, source_target_pairs={{0,8},{8,0},{16,24},{24,16},{32,40},{40,32},{48,56},{56,48},{64,72... | collective-permute-start | bytes 7372808 | tf_op jit(solution)/shard_map/ppermute | solution.py:29
  528.4 116.8 %reduce-scatter.13.cloned.1.call-start = ((), (), s32[]{:S(2)}) async-start(), calls=%async_computation.7 | async-start | bytes 3276800 | tf_op jit(solution)/shard_map/reduce_scatter | solution.py:58
  531.5 100.5 %collective-permute-start.73 = (bf16[960,2560]{1,0:T(8,128)(2,1)}, bf16[960,2560]{1,0:T(8,128)(2,1)}, u32[]{:S(2)}, u32[]{:S(2)}) collective-permute-start(bf16[960,2560]{1,0:T(8,128)(2,1)} %convolution_convert_fusion), channel_id=1, source_target_pairs={{0,8},{8,0},{16,24},{24,16},{32,40},{40,32},{48,56},{56,48},{64,72... | collective-permute-start | bytes 14745608 | tf_op jit(solution)/shard_map/ppermute | solution.py:29
  550.5 216.9 %reduce-scatter.17.cloned.1.call-start = ((), (), s32[]{:S(2)}) async-start(), calls=%async_computation.9 | async-start | bytes 1536000 | tf_op jit(solution)/shard_map/reduce_scatter | solution.py:58
  639.3 28.9 %collective-permute-start.104 = (bf16[960,640]{1,0:T(8,128)(2,1)}, bf16[960,640]{1,0:T(8,128)(2,1)}, u32[]{:S(2)}, u32[]{:S(2)}) collective-permute-start(bf16[960,640]{1,0:T(8,128)(2,1)} %get-tuple-element.170), channel_id=1, source_target_pairs={{0,32},{8,40},{16,48},{24,56},{32,0},{40,8},{48,16},{56,24},{64,96... | collective-permute-start | bytes 3686408 | tf_op jit(solution)/shard_map/ppermute | solution.py:29
  639.3 56.6 %collective-permute-start.105 = (bf16[960,640]{1,0:T(8,128)(2,1)}, bf16[960,640]{1,0:T(8,128)(2,1)}, u32[]{:S(2)}, u32[]{:S(2)}) collective-permute-start(bf16[960,640]{1,0:T(8,128)(2,1)} %get-tuple-element.172), channel_id=1, source_target_pairs={{0,64},{8,72},{16,80},{24,88},{32,96},{40,104},{48,112},{56,120},{... | collective-permute-start | bytes 3686408 | tf_op jit(solution)/shard_map/ppermute | solution.py:29
  642.2 55.7 %collective-permute-start.106 = (bf16[960,640]{1,0:T(8,128)(2,1)}, bf16[960,640]{1,0:T(8,128)(2,1)}, u32[]{:S(2)}, u32[]{:S(2)}) collective-permute-start(bf16[960,640]{1,0:T(8,128)(2,1)} %get-tuple-element.171), channel_id=1, source_target_pairs={{0,96},{8,104},{16,112},{24,120},{32,64},{40,72},{48,80},{56,88},{... | collective-permute-start | bytes 3686408 | tf_op jit(solution)/shard_map/ppermute | solution.py:29
  645.2 66.0 %collective-permute-start.74 = (bf16[2,176,640]{2,1,0:T(8,128)(2,1)}, bf16[2,176,640]{2,1,0:T(8,128)(2,1)}, u32[]{:S(2)}, u32[]{:S(2)}) collective-permute-start(bf16[2,176,640]{2,1,0:T(8,128)(2,1)} %bitcast.57), channel_id=1, source_target_pairs={{0,1},{1,0},{2,3},{3,2},{4,5},{5,4},{6,7},{7,6},{8,9},{9,8},{10,11... | collective-permute-start | bytes 1351688 | tf_op jit(solution)/shard_map/ppermute | solution.py:29
  645.2 66.2 %collective-permute-start.75 = (bf16[2,176,640]{2,1,0:T(8,128)(2,1)}, bf16[2,176,640]{2,1,0:T(8,128)(2,1)}, u32[]{:S(2)}, u32[]{:S(2)}) collective-permute-start(bf16[2,176,640]{2,1,0:T(8,128)(2,1)} %bitcast.58), channel_id=1, source_target_pairs={{0,2},{1,3},{2,0},{3,1},{4,6},{5,7},{6,4},{7,5},{8,10},{9,11},{10,... | collective-permute-start | bytes 1351688 | tf_op jit(solution)/shard_map/ppermute | solution.py:29
  668.2 34.9 %collective-permute-start.80 = (bf16[2,32,1280]{2,1,0:T(8,128)(2,1)}, bf16[2,32,1280]{2,1,0:T(8,128)(2,1)S(1)}, u32[]{:S(2)}, u32[]{:S(2)}) collective-permute-start(bf16[2,32,1280]{2,1,0:T(8,128)(2,1)} %get-tuple-element.239), channel_id=1, source_target_pairs={{0,32},{8,40},{16,48},{24,56},{32,0},{40,8},{48,16},{56,24},{64,96... | collective-permute-start | bytes 491528 | tf_op jit(solution)/shard_map/ppermute | solution.py:29
  703.0 95.3 %reduce-scatter.21.cloned.1.call-start = ((), (), s32[]{:S(2)}) async-start(), calls=%async_computation.11 | async-start | bytes 3276800 | tf_op jit(solution)/shard_map/reduce_scatter | solution.py:58
  744.2 86.1 %reduce-scatter.15.cloned.1.call-start = ((), (), s32[]{:S(2)}) async-start(), calls=%async_computation.8 | async-start | bytes 3276800 | tf_op jit(solution)/shard_map/reduce_scatter | solution.py:58
  (247 other events, 2089.2 us)
Sparse Core Ops, SparseCore 0:
  447.0 33.4 reduce-scatter.18
  528.5 24.1 reduce-scatter.10
  555.8 42.1 reduce-scatter.12
  703.2 27.0 reduce-scatter.16
  744.3 32.3 reduce-scatter.20
  779.5 37.5 reduce-scatter.14

commit v5 on v4

--- a/solution.py
+++ b/solution.py
@@ -99,18 +99,42 @@
     return jnp.concatenate(parts, axis=axis)
 
 
-def finish_rows(rows):
-    count, columns = rows.shape
-    blocks = rows.reshape(2, 4, count // 8, columns)
+LAST = 640
+
+
+def as_rows(array):
+    columns = array.shape[2]
+    parts = []
+    for first in range(0, columns, LAST):
+        part = array[:, :, first : first + LAST]
+        parts.append(jnp.pad(part, ((0, 0), (0, 0), (0, LAST - part.shape[2]))))
+    return jnp.concatenate(parts, axis=1)
+
+
+def finish_sums(summed, quarter):
+    joined = jnp.concatenate([as_rows(array) for array in summed], axis=1)
+    height = joined.shape[1] // 4
+    blocks = joined.reshape(2, 4, height, LAST)
     total = sum_over_y(lambda k: lax.dynamic_index_in_dim(blocks, k, axis=1, keepdims=False))
-    own = spread_over_y(to_owners(total), 0)
-    return own, swap_core(own)
-
-
-def finish_columns(columns):
-    count, width = columns.shape
-    own = spread_over_y(to_owners(columns.reshape(2, count // 2, width)), 1)
-    return own, swap_core(own)
+    if quarter is not None:
+        total = jnp.concatenate([total, quarter], axis=1)
+    own = spread_over_y(to_owners(total)[None], 0)
+
+    def take_apart(spread):
+        rows = spread[:, :height].reshape(4 * height, LAST)
+        results, first = [], 0
+        for array in summed:
+            count, columns = array.shape[1:]
+            parts = []
+            for start in range(0, columns, LAST):
+                parts.append(rows[first : first + count, : min(LAST, columns - start)])
+                first += count
+            results.append(jnp.concatenate(parts, axis=1))
+        if quarter is not None:
+            results.append(jnp.concatenate([spread[k, height:] for k in range(4)], axis=1))
+        return results
+
+    return take_apart(own), take_apart(swap_core(own))
 
 
 def kernel_params():
@@ -176,7 +200,7 @@
     blocks = gather_blocks(quarter, earlier)
     joined = jnp.concatenate(blocks, axis=0)
     parts = [joined] + [swap(joined, "rep", 4 * m) for m in range(1, 4)]
-    return parts, blocks
+    return parts, joined
 
 
 def stacked_heads(array, kv_head):
@@ -380,9 +404,9 @@
 
     def gather_parts(own):
         att, gate_up, down = own
-        by_y, _ = gather_by_y(gate_up, None)
         att_parts = gather_blocks(att, None)
-        return att_parts, by_y, gather_blocks(down, att_parts)
+        by_y, by_x = gather_by_y(gate_up, None)
+        return att_parts, by_y, by_x, down
 
     def attention_weights(att_parts):
         mine = assemble(att_parts, False)
@@ -404,13 +428,15 @@
     layers = []
     parts = gather_parts(own_weights(0))
     for l in range(DECODER_LAYERS):
-        att_parts, by_y, down_parts = parts
+        att_parts, by_y, by_x, own_down = parts
+        att_parts = after(att_parts, stream)
         gain_attn, gain_mlp, query_key, out_value = attention_weights(att_parts)
         normed = (normalize(stream) * gain_attn).astype(bf16)
         values = matmul(normed, out_value[:, width:]).astype(bf16)
         projected = matmul(normed, query_key)
         keys = rotary(projected[:, width:], cosine, sine).astype(bf16)
-        kv = gather_pack(jnp.concatenate([keys, values], axis=1))
+        kv = gather_pack(after(jnp.concatenate([keys, values], axis=1), by_x))
+        down_parts = gather_blocks(own_down, kv)
         if l + 1 < DECODER_LAYERS:
             parts = gather_parts(after(own_weights(l + 1), kv))
         queries = rotary(projected[:, :width], cosine, sine).astype(bf16)
@@ -431,8 +457,7 @@
         stream = middle + jnp.concatenate([pick(mine, other), pick(other, mine)], axis=1)
     output = stream.astype(bf16)
 
-    sums = ()
-    mlp_done = att_done = ()
+    latest = done = ()
     grad = cotangent.astype(f32)
     results = [None] * DECODER_LAYERS
     for l in reversed(range(DECODER_LAYERS)):
@@ -443,7 +468,6 @@
         grad_mine, grad_other = pick(grad_a, grad_b), pick(grad_b, grad_a)
         down_received = swap_core(cross_rows(hidden, grad_other).astype(bf16))
         down_sum = (cross_rows(hidden, grad_mine) + down_received.astype(f32)).astype(bf16)
-        down_sum = sum_over_x(after(down_sum, sums))
 
         dhidden = matmul_nt(grad_mine, down[0]) + matmul_nt(grad_other, down[1])
         sigmoid = jax.nn.sigmoid(gate)
@@ -453,21 +477,21 @@
         gate_up_received = swap_core(cross_rows(normed_mlp, dother).astype(bf16))
         gate_up_sum = cross_rows(normed_mlp, dmine) + gate_up_received.astype(f32)
         gate_up_sum = gate_up_sum.astype(bf16)
-        columns = gate_up_sum.shape[1] // 4
-        gate_up_sum = sum_over_y(
-            lambda k: lax.dynamic_slice_in_dim(gate_up_sum, k * columns, columns, axis=1)
-        )
-        gate_up_sum = sum_over_x(after(gate_up_sum, sums))
 
         dnormed = matmul_nt(dmine, gate_up[0]) + matmul_nt(dother, gate_up[1])
         dmiddle, mlp_gain_grad = normalize_back(middle, gain_mlp, dnormed)
         dmiddle = dmiddle + grad
         dmiddle_low = dmiddle.astype(bf16)
         dmixed = matmul_nt(dmiddle_low, out_value[:, :width]).astype(bf16)
-        dmixed = after(dmixed, mlp_done)
+        dmixed = after(dmixed, (down_sum, gate_up_sum))
         dq, dkv = attend_back(queries, kv, key_place, bounds, mixed, logs, dmixed)
-        dkv = after(dkv, (down_received, gate_up_received))
-        dkv = after(scatter_pack(dkv), att_done)
+        down_sum = sum_over_x(after(down_sum, latest))
+        dkv = after(scatter_pack(dkv), done)
+        columns = gate_up_sum.shape[1] // 4
+        gate_up_sum = sum_over_y(
+            lambda k: lax.dynamic_slice_in_dim(gate_up_sum, k * columns, columns, axis=1)
+        )
+        gate_up_sum = sum_over_x(after(gate_up_sum, down_sum))
         dq = rotary_back(dq, cosine, sine).astype(bf16)
         dk = rotary_back(dkv[:, :key_width], cosine, sine).astype(bf16)
         dv = dkv[:, key_width:].astype(bf16)
@@ -491,13 +515,19 @@
         gain_grads = gain_grads.reshape(2, -1, shard).swapaxes(0, 1)
         gain_grads = jnp.pad(gain_grads, ((0, 0), (0, 6), (0, att_width - shard)))
         att_sum = jnp.concatenate([att_sum.reshape(-1, shard, att_width), gain_grads], axis=1)
-        att_sum = sum_over_x(att_sum.reshape(-1, att_width))
-        sums = (down_sum, gate_up_sum, att_sum)
-
-        mlp_done = (*finish_columns(gate_up_sum), *finish_rows(down_sum))
-        gate_up_own, gate_up_other, down_own, down_other = mlp_done
-        att_done = finish_rows(att_sum)
-        att_own, att_other = att_done
+        att_sum = sum_over_x(after(att_sum.reshape(-1, att_width), gate_up_sum))
+        latest = att_sum
+
+        att_pair = att_sum.reshape(2, shard + 8, att_width)
+        down_pair = down_sum.reshape(2, -1, half_width)
+        gate_up_pair = gate_up_sum.reshape(2, shard, columns)
+        if l > 0:
+            done = finish_sums([att_pair, down_pair], gate_up_pair)
+            (att_own, down_own, gate_up_own), (att_other, down_other, gate_up_other) = done
+        else:
+            mlp = finish_sums([down_pair], gate_up_pair)
+            (down_own, gate_up_own), (down_other, gate_up_other) = mlp
+            (att_own,), (att_other,) = finish_sums([att_pair], None)
         att_a, att_b = pick(att_own, att_other), pick(att_other, att_own)
         results[l] = (
             att_own[shard, :shard],

time: 892 us -> 830 us (0.930)
  starting transfers between devices: 206 us -> 154 us
    ppermute x102 -> x87, starting transfers between devices: 152 us -> 124 us  [swap(): return lax.ppermute(array, axis, [(i, i ^ mask) for i in range(count)])]
    ppermute x102 -> x87, waiting for transfers between devices: 291 us -> 317 us  [swap(): return lax.ppermute(array, axis, [(i, i ^ mask) for i in range(count)])]
    ppermute x24 -> x12, starting transfers between devices: 53.7 us -> 29 us  [send(): return lax.ppermute(block, ('rep', 'fsdp'), moves).astype(f32)]
    ppermute x24 -> x12, waiting for transfers between devices: 30.2 us -> 8.82 us  [send(): return lax.ppermute(block, ('rep', 'fsdp'), moves).astype(f32)]
    unnamed x349 -> x311, local copies, waits for them, and re-layouts: 43.2 us -> 34.9 us
  transfers between devices with their start and end apart: 132 -> 105, of which waited for: 58 -> 52; matrix products, arithmetic and copies ran while one was open for 26% -> 26% of each run, Pallas kernels for 6% -> 4%
where the time goes in v5:
time: 830 us; the launch traced here: 819 us
  waiting for transfers between devices  330 us (40%)
  starting transfers between devices  154 us (19%)
  matrix products  103 us (12%)
  local copies, waits for them, and re-layouts  80.2 us (10%)
  other arithmetic  79.5 us (10%)
  Pallas kernels  55.5 us (7%)
  between operations  16.8 us (2%)
    ppermute x87, waiting for transfers between devices, swap(): return lax.ppermute(array, axis, [(i, i ^ mask) for i in range(count)])  317 us
    ppermute x87, starting transfers between devices, swap(): return lax.ppermute(array, axis, [(i, i ^ mask) for i in range(count)])  124 us
    dot_general x16, matrix products, cross_rows(): lax.dot_general(left, right, (((0,), (0,)), ((), ())), preferred_element_...  40.1 us
    unnamed x311, local copies, waits for them, and re-layouts  34.9 us
    dot_general x14, matrix products, matmul_nt(): return lax.dot_general(left, right, NT, preferred_element_type=f32)  34.3 us
    ppermute x12, starting transfers between devices, send(): return lax.ppermute(block, ('rep', 'fsdp'), moves).astype(f32)  29 us
    dot_general x14, matrix products, matmul(): return jnp.dot(left, right, preferred_element_type=f32)  28.4 us
    pallas_call x2, Pallas kernels, attend_back(): pl.pallas_call(attention_backward_kernel, out_shape=(jax.ShapeDtypeStruct...  28 us
  transfers between devices with their start and end apart: 105, of which 52 were waited for; matrix products, arithmetic and copies ran while one was open for 26% of the time, Pallas kernels for 4%

profile of v5, /device:TPU:5, one launch (start us, length us, event | category | flops | bytes accessed | tf_op | source)
XLA Modules:
  0.0 818.5 jit_solution(15786276381098958192)
XLA Ops:
  32.7 11.2 %collective-permute-done.1.refs_1_ = bf16[2,128,1280]{2,1,0:T(8,128)(2,1)S(1)} collective-permute-done((bf16[2,128,1280]{2,1,0:T(8,128)(2,1)S(1)}, bf16[2,128,1280]{2,1,0:T(8,128)(2,1)S(1)}, u32[]{:S(2)}, u32[]{:S(2)}) %collective-permute-start.1) | collective-permute-done | bytes 655392 | tf_op jit(solution)/shard_map/ppermute | solution.py:29
  43.9 14.1 %collective-permute-done.2.refs_2_ = bf16[2,128,1280]{2,1,0:T(8,128)(2,1)S(1)} collective-permute-done((bf16[2,128,1280]{2,1,0:T(8,128)(2,1)S(1)}, bf16[2,128,1280]{2,1,0:T(8,128)(2,1)S(1)}, u32[]{:S(2)}, u32[]{:S(2)}) %collective-permute-start.2) | collective-permute-done | bytes 655392 | tf_op jit(solution)/shard_map/ppermute | solution.py:29
  58.9 3.9 collective-permute-start.4
  77.1 4.5 collective-permute-done.6
  82.3 7.5 collective-permute-done.7
  119.2 7.9 collective-permute-done.11
  127.3 11.9 %collective-permute-done.12 = bf16[2,176,640]{2,1,0:T(8,128)(2,1)S(1)} collective-permute-done((bf16[2,176,640]{2,1,0:T(8,128)(2,1)S(1)}, bf16[2,176,640]{2,1,0:T(8,128)(2,1)S(1)}, u32[]{:S(2)}, u32[]{:S(2)}) %collective-permute-start.12) | collective-permute-done | bytes 450592 | tf_op jit(solution)/shard_map/ppermute | solution.py:29
  143.5 7.6 attention_forward.2
  151.9 5.1 collective-permute-done.14.refs_2_
  157.0 10.2 %collective-permute-done.15.refs_3_ = bf16[8,120,640]{2,1,0:T(8,128)(2,1)S(1)} collective-permute-done((bf16[8,120,640]{2,1,0:T(8,128)(2,1)S(1)}, bf16[8,120,640]{2,1,0:T(8,128)(2,1)S(1)}, u32[]{:S(2)}, u32[]{:S(2)}) %collective-permute-start.15) | collective-permute-done | bytes 1228832 | tf_op jit(solution)/shard_map/ppermute | solution.py:29
  188.5 7.1 collective-permute-done.22
  203.8 6.0 multiply_convert_fusion.5
  214.4 12.9 %collective-permute-done.24.refs_2_ = bf16[2,128,1280]{2,1,0:T(8,128)(2,1)S(1)} collective-permute-done((bf16[2,128,1280]{2,1,0:T(8,128)(2,1)S(1)}, bf16[2,128,1280]{2,1,0:T(8,128)(2,1)S(1)}, u32[]{:S(2)}, u32[]{:S(2)}) %collective-permute-start.24) | collective-permute-done | bytes 655392 | tf_op jit(solution)/shard_map/ppermute | solution.py:29
  229.7 4.0 collective-permute-start.26
  236.3 6.0 collective-permute-done.27
  247.6 4.9 collective-permute-done.28
  253.2 5.0 collective-permute-done.29
  278.3 4.9 collective-permute-done.38
  290.6 8.1 collective-permute-done.33
  298.7 12.8 %collective-permute-done.34 = bf16[2,176,640]{2,1,0:T(8,128)(2,1)S(1)} collective-permute-done((bf16[2,176,640]{2,1,0:T(8,128)(2,1)S(1)}, bf16[2,176,640]{2,1,0:T(8,128)(2,1)S(1)}, u32[]{:S(2)}, u32[]{:S(2)}) %collective-permute-start.34) | collective-permute-done | bytes 450592 | tf_op jit(solution)/shard_map/ppermute | solution.py:29
  315.8 7.6 attention_forward.3
  323.5 3.9 collective-permute-done.36.refs_2_
  327.4 11.7 %collective-permute-done.37.refs_3_ = bf16[8,120,640]{2,1,0:T(8,128)(2,1)S(1)} collective-permute-done((bf16[8,120,640]{2,1,0:T(8,128)(2,1)}, bf16[8,120,640]{2,1,0:T(8,128)(2,1)S(1)}, u32[]{:S(2)}, u32[]{:S(2)}) %collective-permute-start.37) | collective-permute-done | bytes 1228832 | tf_op jit(solution)/shard_map/ppermute | solution.py:29
  343.2 3.9 assemble.10
  351.4 4.6 copy.142
  378.8 4.0 fusion.84
  382.9 4.9 multiply_reduce_fusion.3
  396.2 4.0 add_convert_fusion.1
  400.3 13.9 %attention_backward.2 = (f32[176,960]{1,0:T(8,128)S(1)}, bf16[1408,640]{1,0:T(8,128)(2,1)S(1)}) custom-call(bf16[176,960]{1,0:T(8,128)(2,1)S(1)} %copy-done.19, bf16[1408,640]{1,0:T(8,128)(2,1)S(1)} %bitcast.235, s32[1408,1]{1,0:T(8,128)S(1)} %copy-done.8, s32[8,528]{1,0:T(8,128)S(1)} %pad.26.bounds_ref, bf16[176,960]{1,0:T(8,128)(2,1)S(1)} %get-tuple-element.80.mixed_ref, ...), custom_call_target="tpu_custom_call" | custom-call | flops 2378956800 | bytes 6291456 | tf_op jit(solution)/shard_map/attention_backward/pallas_call | solution.py:296
  415.1 4.4 collective-permute-start.47
  424.2 11.4 %collective-permute-done.48 = bf16[2,176,640]{2,1,0:T(8,128)(2,1)S(1)} collective-permute-done((bf16[2,176,640]{2,1,0:T(8,128)(2,1)S(1)}, bf16[2,176,640]{2,1,0:T(8,128)(2,1)S(1)}, u32[]{:S(2)}, u32[]{:S(2)}) %collective-permute-start.48) | collective-permute-done | bytes 450592 | tf_op jit(solution)/shard_map/ppermute | solution.py:29
  441.7 4.0 collective-permute-done.49
  456.1 21.0 %collective-permute-done.60 = bf16[960,640]{1,0:T(8,128)(2,1)} collective-permute-done((bf16[960,640]{1,0:T(8,128)(2,1)}, bf16[960,640]{1,0:T(8,128)(2,1)}, u32[]{:S(2)}, u32[]{:S(2)}) %collective-permute-start.60) | collective-permute-done | bytes 1228832 | tf_op jit(solution)/shard_map/ppermute | solution.py:29
  477.6 4.1 add_convert_fusion.5
  494.0 4.3 fusion.2
  522.7 4.1 fusion.86
  526.8 3.9 add_convert_fusion
  534.4 4.3 multiply_reduce_fusion
  543.9 43.1 %collective-permute-done.76 = bf16[960,640]{1,0:T(8,128)(2,1)S(1)} collective-permute-done((bf16[960,640]{1,0:T(8,128)(2,1)S(1)}, bf16[960,640]{1,0:T(8,128)(2,1)S(1)}, u32[]{:S(2)}, u32[]{:S(2)}) %collective-permute-start.76) | collective-permute-done | bytes 1228832 | tf_op jit(solution)/shard_map/ppermute | solution.py:29
  590.8 14.1 %attention_backward.3 = (f32[176,960]{1,0:T(8,128)S(1)}, bf16[1408,640]{1,0:T(8,128)(2,1)S(1)}) custom-call(bf16[176,960]{1,0:T(8,128)(2,1)S(1)} %copy-done.17, bf16[1408,640]{1,0:T(8,128)(2,1)S(1)} %bitcast.233, s32[1408,1]{1,0:T(8,128)S(1)} %copy-done.9, s32[8,528]{1,0:T(8,128)S(1)} %pad.26.bounds_ref, bf16[176,960]{1,0:T(8,128)(2,1)S(1)} %copy-done.5, ...), custom_call_target="tpu_custom_call" | custom-call | flops 2378956800 | bytes 6291456 | tf_op jit(solution)/shard_map/attention_backward/pallas_call | solution.py:296
  610.1 20.1 %collective-permute-done.54 = bf16[2,176,640]{2,1,0:T(8,128)(2,1)S(1)} collective-permute-done((bf16[2,176,640]{2,1,0:T(8,128)(2,1)S(1)}, bf16[2,176,640]{2,1,0:T(8,128)(2,1)S(1)}, u32[]{:S(2)}, u32[]{:S(2)}) %collective-permute-start.54) | collective-permute-done | bytes 450592 | tf_op jit(solution)/shard_map/ppermute | solution.py:29
  639.1 4.5 copy.165
  670.9 12.4 %collective-permute-done.63 = bf16[2,144,640]{2,1,0:T(8,128)(2,1)S(1)} collective-permute-done((bf16[2,144,640]{2,1,0:T(8,128)(2,1)S(1)}, bf16[2,144,640]{2,1,0:T(8,128)(2,1)S(1)}, u32[]{:S(2)}, u32[]{:S(2)}) %collective-permute-start.63) | collective-permute-done | bytes 368672 | tf_op jit(solution)/shard_map/ppermute | solution.py:29
  689.3 4.2 collective-permute-start.64
  696.4 6.2 collective-permute-done.65
  706.2 13.4 %collective-permute-done.68 = bf16[1,264,640]{2,1,0:T(8,128)(2,1)S(1)} collective-permute-done((bf16[1,264,640]{2,1,0:T(8,128)(2,1)S(1)}, bf16[1,264,640]{2,1,0:T(8,128)(2,1)S(1)}, u32[]{:S(2)}, u32[]{:S(2)}) %collective-permute-start.68) | collective-permute-done | bytes 337952 | tf_op jit(solution)/shard_map/ppermute | solution.py:29
  733.8 7.7 collective-permute-done.90
  767.2 9.2 %collective-permute-done.95 = bf16[1,200,640]{2,1,0:T(8,128)(2,1)S(1)} collective-permute-done((bf16[1,200,640]{2,1,0:T(8,128)(2,1)S(1)}, bf16[1,200,640]{2,1,0:T(8,128)(2,1)S(1)}, u32[]{:S(2)}, u32[]{:S(2)}) %collective-permute-start.95) | collective-permute-done | bytes 256032 | tf_op jit(solution)/shard_map/ppermute | solution.py:29
  (742 shorter events, 391.3 us)
Async XLA Ops:
  7.2 496.7 %reduce-scatter.11.cloned.1.call-start = ((), (), s32[]{:S(2)}) async-start(), calls=%async_computation.6 | async-start | bytes 1536000 | tf_op jit(solution)/shard_map/reduce_scatter | solution.py:58
  23.1 47.6 %collective-permute-start.5 = (bf16[120,640]{1,0:T(8,128)(2,1)}, bf16[120,640]{1,0:T(8,128)(2,1)S(1)}, u32[]{:S(2)}, u32[]{:S(2)}) collective-permute-start(bf16[120,640]{1,0:T(8,128)(2,1)} %bitcast.14), channel_id=1, source_target_pairs={{0,4},{1,5},{2,6},{3,7},{4,0},{5,1},{6,2},{7,3},{8,12},{9,13},{10,... | collective-permute-start | bytes 460808 | tf_op jit(solution)/shard_map/ppermute | solution.py:29
  24.9 85.0 %collective-permute-start.16 = (bf16[320,480]{1,0:T(8,128)(2,1)}, bf16[320,480]{1,0:T(8,128)(2,1)}, u32[]{:S(2)}, u32[]{:S(2)}) collective-permute-start(bf16[320,480]{1,0:T(8,128)(2,1)} %slice_select_fusion.1), channel_id=1, source_target_pairs={{0,4},{1,5},{2,6},{3,7},{4,0},{5,1},{6,2},{7,3},{8,12},{9,13},{10,... | collective-permute-start | bytes 921608 | tf_op jit(solution)/shard_map/ppermute | solution.py:29
  30.1 27.9 %collective-permute-start.2 = (bf16[2,128,1280]{2,1,0:T(8,128)(2,1)S(1)}, bf16[2,128,1280]{2,1,0:T(8,128)(2,1)S(1)}, u32[]{:S(2)}, u32[]{:S(2)}) collective-permute-start(bf16[2,128,1280]{2,1,0:T(8,128)(2,1)S(1)} %pad_maximum_fusion.4.refs_0_), channel_id=1, source_target_pairs={{0,2},{1,3},{2,0},{3,1},{4,6},{5,7},{6,4},{7,5},{8,10},{9,11},{10,... | collective-permute-start | bytes 1966088 | tf_op jit(solution)/shard_map/ppermute | solution.py:29
  30.6 27.3 %collective-permute-start.3 = (bf16[2,128,1280]{2,1,0:T(8,128)(2,1)S(1)}, bf16[2,128,1280]{2,1,0:T(8,128)(2,1)S(1)}, u32[]{:S(2)}, u32[]{:S(2)}) collective-permute-start(bf16[2,128,1280]{2,1,0:T(8,128)(2,1)S(1)} %pad_maximum_fusion.4.refs_0_), channel_id=1, source_target_pairs={{0,3},{1,2},{2,1},{3,0},{4,7},{5,6},{6,5},{7,4},{8,11},{9,10},{10,... | collective-permute-start | bytes 1966088 | tf_op jit(solution)/shard_map/ppermute | solution.py:29
  58.9 33.8 %collective-permute-start.4 = (bf16[8,128,1280]{2,1,0:T(8,128)(2,1)S(1)}, bf16[8,128,1280]{2,1,0:T(8,128)(2,1)}, u32[]{:S(2)}, u32[]{:S(2)}) collective-permute-start(bf16[8,128,1280]{2,1,0:T(8,128)(2,1)S(1)} %assemble.6), channel_id=1, source_target_pairs={{0,8},{8,0},{16,24},{24,16},{32,40},{40,32},{48,56},{56,48},{64,72... | collective-permute-start | bytes 7864328 | tf_op jit(solution)/shard_map/ppermute | solution.py:29
  101.0 39.0 %collective-permute-start.13 = (bf16[8,120,640]{2,1,0:T(8,128)(2,1)S(1)}, bf16[8,120,640]{2,1,0:T(8,128)(2,1)S(1)}, u32[]{:S(2)}, u32[]{:S(2)}) collective-permute-start(bf16[8,120,640]{2,1,0:T(8,128)(2,1)S(1)} %copy-done.3), channel_id=1, source_target_pairs={{0,32},{8,40},{16,48},{24,56},{32,0},{40,8},{48,16},{56,24},{64,96... | collective-permute-start | bytes 3686408 | tf_op jit(solution)/shard_map/ppermute | solution.py:29
  111.1 45.9 %collective-permute-start.14 = (bf16[8,120,640]{2,1,0:T(8,128)(2,1)S(1)}, bf16[8,120,640]{2,1,0:T(8,128)(2,1)S(1)}, u32[]{:S(2)}, u32[]{:S(2)}) collective-permute-start(bf16[8,120,640]{2,1,0:T(8,128)(2,1)S(1)} %copy-done.3), channel_id=1, source_target_pairs={{0,64},{8,72},{16,80},{24,88},{32,96},{40,104},{48,112},{56,120},{... | collective-permute-start | bytes 3686408 | tf_op jit(solution)/shard_map/ppermute | solution.py:29
  114.1 53.1 %collective-permute-start.15 = (bf16[8,120,640]{2,1,0:T(8,128)(2,1)S(1)}, bf16[8,120,640]{2,1,0:T(8,128)(2,1)S(1)}, u32[]{:S(2)}, u32[]{:S(2)}) collective-permute-start(bf16[8,120,640]{2,1,0:T(8,128)(2,1)S(1)} %copy-done.3), channel_id=1, source_target_pairs={{0,96},{8,104},{16,112},{24,120},{32,64},{40,72},{48,80},{56,88},{... | collective-permute-start | bytes 3686408 | tf_op jit(solution)/shard_map/ppermute | solution.py:29
  118.2 20.9 %collective-permute-start.12 = (bf16[2,176,640]{2,1,0:T(8,128)(2,1)S(1)}, bf16[2,176,640]{2,1,0:T(8,128)(2,1)S(1)}, u32[]{:S(2)}, u32[]{:S(2)}) collective-permute-start(bf16[2,176,640]{2,1,0:T(8,128)(2,1)S(1)} %pad_maximum_fusion.13), channel_id=1, source_target_pairs={{0,3},{1,2},{2,1},{3,0},{4,7},{5,6},{6,5},{7,4},{8,11},{9,10},{10,... | collective-permute-start | bytes 1351688 | tf_op jit(solution)/shard_map/ppermute | solution.py:29
  139.2 28.0 %collective-permute-start.17 = (bf16[2,320,480]{2,1,0:T(8,128)(2,1)S(1)}, bf16[2,320,480]{2,1,0:T(8,128)(2,1)S(1)}, u32[]{:S(2)}, u32[]{:S(2)}) collective-permute-start(bf16[2,320,480]{2,1,0:T(8,128)(2,1)S(1)} %pad_maximum_fusion.5.refs_0_), channel_id=1, source_target_pairs={{0,1},{1,0},{2,3},{3,2},{4,5},{5,4},{6,7},{7,6},{8,9},{9,8},{10,11... | collective-permute-start | bytes 1843208 | tf_op jit(solution)/shard_map/ppermute | solution.py:29
  140.1 27.2 %collective-permute-start.18 = (bf16[2,320,480]{2,1,0:T(8,128)(2,1)S(1)}, bf16[2,320,480]{2,1,0:T(8,128)(2,1)S(1)}, u32[]{:S(2)}, u32[]{:S(2)}) collective-permute-start(bf16[2,320,480]{2,1,0:T(8,128)(2,1)S(1)} %pad_maximum_fusion.5.refs_0_), channel_id=1, source_target_pairs={{0,2},{1,3},{2,0},{3,1},{4,6},{5,7},{6,4},{7,5},{8,10},{9,11},{10,... | collective-permute-start | bytes 1843208 | tf_op jit(solution)/shard_map/ppermute | solution.py:29
  140.1 29.3 %collective-permute-start.19 = (bf16[2,320,480]{2,1,0:T(8,128)(2,1)S(1)}, bf16[2,320,480]{2,1,0:T(8,128)(2,1)S(1)}, u32[]{:S(2)}, u32[]{:S(2)}) collective-permute-start(bf16[2,320,480]{2,1,0:T(8,128)(2,1)S(1)} %pad_maximum_fusion.5.refs_0_), channel_id=1, source_target_pairs={{0,3},{1,2},{2,1},{3,0},{4,7},{5,6},{6,5},{7,4},{8,11},{9,10},{10,... | collective-permute-start | bytes 1843208 | tf_op jit(solution)/shard_map/ppermute | solution.py:29
  172.6 31.1 %collective-permute-start.20 = (bf16[960,2560]{1,0:T(8,128)(2,1)}, bf16[960,2560]{1,0:T(8,128)(2,1)}, u32[]{:S(2)}, u32[]{:S(2)}) collective-permute-start(bf16[960,2560]{1,0:T(8,128)(2,1)} %bitcast.236), channel_id=1, source_target_pairs={{0,8},{8,0},{16,24},{24,16},{32,40},{40,32},{48,56},{56,48},{64,72... | collective-permute-start | bytes 14745608 | tf_op jit(solution)/shard_map/ppermute | solution.py:29
  183.1 27.3 %collective-permute-start.21 = (bf16[2560,480]{0,1:T(8,128)(2,1)}, bf16[2560,480]{0,1:T(8,128)(2,1)}, u32[]{:S(2)}, u32[]{:S(2)}) collective-permute-start(bf16[2560,480]{0,1:T(8,128)(2,1)} %copy.136), channel_id=1, source_target_pairs={{0,8},{8,0},{16,24},{24,16},{32,40},{40,32},{48,56},{56,48},{64,72... | collective-permute-start | bytes 7372808 | tf_op jit(solution)/shard_map/ppermute | solution.py:29
  195.6 18.8 %collective-permute-start.23 = (bf16[2,128,1280]{2,1,0:T(8,128)(2,1)S(1)}, bf16[2,128,1280]{2,1,0:T(8,128)(2,1)S(1)}, u32[]{:S(2)}, u32[]{:S(2)}) collective-permute-start(bf16[2,128,1280]{2,1,0:T(8,128)(2,1)S(1)} %pad_maximum_fusion.6.refs_0_), channel_id=1, source_target_pairs={{0,1},{1,0},{2,3},{3,2},{4,5},{5,4},{6,7},{7,6},{8,9},{9,8},{10,11... | collective-permute-start | bytes 1966088 | tf_op jit(solution)/shard_map/ppermute | solution.py:29
  197.7 29.6 %collective-permute-start.24 = (bf16[2,128,1280]{2,1,0:T(8,128)(2,1)S(1)}, bf16[2,128,1280]{2,1,0:T(8,128)(2,1)S(1)}, u32[]{:S(2)}, u32[]{:S(2)}) collective-permute-start(bf16[2,128,1280]{2,1,0:T(8,128)(2,1)S(1)} %pad_maximum_fusion.6.refs_0_), channel_id=1, source_target_pairs={{0,2},{1,3},{2,0},{3,1},{4,6},{5,7},{6,4},{7,5},{8,10},{9,11},{10,... | collective-permute-start | bytes 1966088 | tf_op jit(solution)/shard_map/ppermute | solution.py:29
  200.0 27.3 %collective-permute-start.25 = (bf16[2,128,1280]{2,1,0:T(8,128)(2,1)S(1)}, bf16[2,128,1280]{2,1,0:T(8,128)(2,1)S(1)}, u32[]{:S(2)}, u32[]{:S(2)}) collective-permute-start(bf16[2,128,1280]{2,1,0:T(8,128)(2,1)S(1)} %pad_maximum_fusion.6.refs_0_), channel_id=1, source_target_pairs={{0,3},{1,2},{2,1},{3,0},{4,7},{5,6},{6,5},{7,4},{8,11},{9,10},{10,... | collective-permute-start | bytes 1966088 | tf_op jit(solution)/shard_map/ppermute | solution.py:29
  229.7 33.7 %collective-permute-start.26 = (bf16[8,128,1280]{2,1,0:T(8,128)(2,1)}, bf16[8,128,1280]{2,1,0:T(8,128)(2,1)}, u32[]{:S(2)}, u32[]{:S(2)}) collective-permute-start(bf16[8,128,1280]{2,1,0:T(8,128)(2,1)} %assemble.9), channel_id=1, source_target_pairs={{0,8},{8,0},{16,24},{24,16},{32,40},{40,32},{48,56},{56,48},{64,72... | collective-permute-start | bytes 7864328 | tf_op jit(solution)/shard_map/ppermute | solution.py:29
  272.7 40.9 %collective-permute-start.35 = (bf16[8,120,640]{2,1,0:T(8,128)(2,1)}, bf16[8,120,640]{2,1,0:T(8,128)(2,1)S(1)}, u32[]{:S(2)}, u32[]{:S(2)}) collective-permute-start(bf16[8,120,640]{2,1,0:T(8,128)(2,1)} %constant_dynamic-update-slice_fusion.10.refs_0_), channel_id=1, source_target_pairs={{0,32},{8,40},{16,48},{24,56},{32,0},{40,8},{48,16},{56,24},{64,96... | collective-permute-start | bytes 3686408 | tf_op jit(solution)/shard_map/ppermute | solution.py:29
  283.4 44.0 %collective-permute-start.36 = (bf16[8,120,640]{2,1,0:T(8,128)(2,1)}, bf16[8,120,640]{2,1,0:T(8,128)(2,1)S(1)}, u32[]{:S(2)}, u32[]{:S(2)}) collective-permute-start(bf16[8,120,640]{2,1,0:T(8,128)(2,1)} %constant_dynamic-update-slice_fusion.10.refs_0_), channel_id=1, source_target_pairs={{0,64},{8,72},{16,80},{24,88},{32,96},{40,104},{48,112},{56,120},{... | collective-permute-start | bytes 3686408 | tf_op jit(solution)/shard_map/ppermute | solution.py:29
  286.0 53.1 %collective-permute-start.37 = (bf16[8,120,640]{2,1,0:T(8,128)(2,1)}, bf16[8,120,640]{2,1,0:T(8,128)(2,1)S(1)}, u32[]{:S(2)}, u32[]{:S(2)}) collective-permute-start(bf16[8,120,640]{2,1,0:T(8,128)(2,1)} %constant_dynamic-update-slice_fusion.10.refs_0_), channel_id=1, source_target_pairs={{0,96},{8,104},{16,112},{24,120},{32,64},{40,72},{48,80},{56,88},{... | collective-permute-start | bytes 3686408 | tf_op jit(solution)/shard_map/ppermute | solution.py:29
  290.4 21.1 %collective-permute-start.34 = (bf16[2,176,640]{2,1,0:T(8,128)(2,1)S(1)}, bf16[2,176,640]{2,1,0:T(8,128)(2,1)S(1)}, u32[]{:S(2)}, u32[]{:S(2)}) collective-permute-start(bf16[2,176,640]{2,1,0:T(8,128)(2,1)S(1)} %pad_maximum_fusion.14), channel_id=1, source_target_pairs={{0,3},{1,2},{2,1},{3,0},{4,7},{5,6},{6,5},{7,4},{8,11},{9,10},{10,... | collective-permute-start | bytes 1351688 | tf_op jit(solution)/shard_map/ppermute | solution.py:29
  311.6 27.5 %collective-permute-start.39 = (bf16[2,320,480]{2,1,0:T(8,128)(2,1)S(1)}, bf16[2,320,480]{2,1,0:T(8,128)(2,1)S(1)}, u32[]{:S(2)}, u32[]{:S(2)}) collective-permute-start(bf16[2,320,480]{2,1,0:T(8,128)(2,1)S(1)} %pad_maximum_fusion.7.refs_0_), channel_id=1, source_target_pairs={{0,1},{1,0},{2,3},{3,2},{4,5},{5,4},{6,7},{7,6},{8,9},{9,8},{10,11... | collective-permute-start | bytes 1843208 | tf_op jit(solution)/shard_map/ppermute | solution.py:29
  311.7 30.5 %collective-permute-start.40 = (bf16[2,320,480]{2,1,0:T(8,128)(2,1)S(1)}, bf16[2,320,480]{2,1,0:T(8,128)(2,1)S(1)}, u32[]{:S(2)}, u32[]{:S(2)}) collective-permute-start(bf16[2,320,480]{2,1,0:T(8,128)(2,1)S(1)} %pad_maximum_fusion.7.refs_0_), channel_id=1, source_target_pairs={{0,2},{1,3},{2,0},{3,1},{4,6},{5,7},{6,4},{7,5},{8,10},{9,11},{10,... | collective-permute-start | bytes 1843208 | tf_op jit(solution)/shard_map/ppermute | solution.py:29
  313.7 29.5 %collective-permute-start.41 = (bf16[2,320,480]{2,1,0:T(8,128)(2,1)S(1)}, bf16[2,320,480]{2,1,0:T(8,128)(2,1)S(1)}, u32[]{:S(2)}, u32[]{:S(2)}) collective-permute-start(bf16[2,320,480]{2,1,0:T(8,128)(2,1)S(1)} %pad_maximum_fusion.7.refs_0_), channel_id=1, source_target_pairs={{0,3},{1,2},{2,1},{3,0},{4,7},{5,6},{6,5},{7,4},{8,11},{9,10},{10,... | collective-permute-start | bytes 1843208 | tf_op jit(solution)/shard_map/ppermute | solution.py:29
  375.3 20.9 %collective-permute-start.45 = (bf16[960,2560]{1,0:T(8,128)(2,1)}, bf16[960,2560]{1,0:T(8,128)(2,1)}, u32[]{:S(2)}, u32[]{:S(2)}) collective-permute-start(bf16[960,2560]{1,0:T(8,128)(2,1)} %convolution_convert_fusion.1), channel_id=1, source_target_pairs={{0,8},{8,0},{16,24},{24,16},{32,40},{40,32},{48,56},{56,48},{64,72... | collective-permute-start | bytes 14745608 | tf_op jit(solution)/shard_map/ppermute | solution.py:29
  414.4 21.3 %collective-permute-start.48 = (bf16[2,176,640]{2,1,0:T(8,128)(2,1)S(1)}, bf16[2,176,640]{2,1,0:T(8,128)(2,1)S(1)}, u32[]{:S(2)}, u32[]{:S(2)}) collective-permute-start(bf16[2,176,640]{2,1,0:T(8,128)(2,1)S(1)} %bitcast.295), channel_id=1, source_target_pairs={{0,3},{1,2},{2,1},{3,0},{4,7},{5,6},{6,5},{7,4},{8,11},{9,10},{10,... | collective-permute-start | bytes 1351688 | tf_op jit(solution)/shard_map/ppermute | solution.py:29
  415.1 20.6 %collective-permute-start.47 = (bf16[2,176,640]{2,1,0:T(8,128)(2,1)S(1)}, bf16[2,176,640]{2,1,0:T(8,128)(2,1)S(1)}, u32[]{:S(2)}, u32[]{:S(2)}) collective-permute-start(bf16[2,176,640]{2,1,0:T(8,128)(2,1)S(1)} %bitcast.294), channel_id=1, source_target_pairs={{0,2},{1,3},{2,0},{3,1},{4,6},{5,7},{6,4},{7,5},{8,10},{9,11},{10,... | collective-permute-start | bytes 1351688 | tf_op jit(solution)/shard_map/ppermute | solution.py:29
  419.4 18.7 %collective-permute-start.46 = (bf16[2,176,640]{2,1,0:T(8,128)(2,1)S(1)}, bf16[2,176,640]{2,1,0:T(8,128)(2,1)S(1)}, u32[]{:S(2)}, u32[]{:S(2)}) collective-permute-start(bf16[2,176,640]{2,1,0:T(8,128)(2,1)S(1)} %bitcast.293), channel_id=1, source_target_pairs={{0,1},{1,0},{2,3},{3,2},{4,5},{5,4},{6,7},{7,6},{8,9},{9,8},{10,11... | collective-permute-start | bytes 1351688 | tf_op jit(solution)/shard_map/ppermute | solution.py:29
  421.8 55.3 %collective-permute-start.60 = (bf16[960,640]{1,0:T(8,128)(2,1)}, bf16[960,640]{1,0:T(8,128)(2,1)}, u32[]{:S(2)}, u32[]{:S(2)}) collective-permute-start(bf16[960,640]{1,0:T(8,128)(2,1)} %get-tuple-element.194), channel_id=1, source_target_pairs={{0,96},{8,104},{16,112},{24,120},{32,64},{40,72},{48,80},{56,88},{... | collective-permute-start | bytes 3686408 | tf_op jit(solution)/shard_map/ppermute | solution.py:29
  423.7 53.4 %collective-permute-start.59 = (bf16[960,640]{1,0:T(8,128)(2,1)}, bf16[960,640]{1,0:T(8,128)(2,1)}, u32[]{:S(2)}, u32[]{:S(2)}) collective-permute-start(bf16[960,640]{1,0:T(8,128)(2,1)} %get-tuple-element.195), channel_id=1, source_target_pairs={{0,64},{8,72},{16,80},{24,88},{32,96},{40,104},{48,112},{56,120},{... | collective-permute-start | bytes 3686408 | tf_op jit(solution)/shard_map/ppermute | solution.py:29
  435.6 41.9 %collective-permute-start.58 = (bf16[960,640]{1,0:T(8,128)(2,1)}, bf16[960,640]{1,0:T(8,128)(2,1)}, u32[]{:S(2)}, u32[]{:S(2)}) collective-permute-start(bf16[960,640]{1,0:T(8,128)(2,1)} %get-tuple-element.193), channel_id=1, source_target_pairs={{0,32},{8,40},{16,48},{24,56},{32,0},{40,8},{48,16},{56,24},{64,96... | collective-permute-start | bytes 3686408 | tf_op jit(solution)/shard_map/ppermute | solution.py:29
  453.7 40.3 %collective-permute-start.56 = (bf16[960,1280]{1,0:T(8,128)(2,1)}, bf16[960,1280]{1,0:T(8,128)(2,1)}, u32[]{:S(2)}, u32[]{:S(2)}) collective-permute-start(bf16[960,1280]{1,0:T(8,128)(2,1)} %pad_maximum_fusion), channel_id=1, source_target_pairs={{0,8},{8,0},{16,24},{24,16},{32,40},{40,32},{48,56},{56,48},{64,72... | collective-permute-start | bytes 7372808 | tf_op jit(solution)/shard_map/ppermute | solution.py:29
  481.7 157.5 %reduce-scatter.13.cloned.1.call-start = ((), (), s32[]{:S(2)}) async-start(), calls=%async_computation.7 | async-start | bytes 3276800 | tf_op jit(solution)/shard_map/reduce_scatter | solution.py:58
  503.9 158.8 %reduce-scatter.19.cloned.1.call-start = ((), (), s32[]{:S(2)}) async-start(), calls=%async_computation.10 | async-start | bytes 3276800 | tf_op jit(solution)/shard_map/reduce_scatter | solution.py:58
  520.2 175.0 %reduce-scatter.15.cloned.1.call-start = ((), (), s32[]{:S(2)}) async-start(), calls=%async_computation.8 | async-start | bytes 1536000 | tf_op jit(solution)/shard_map/reduce_scatter | solution.py:58
  522.4 18.8 %collective-permute-start.50 = (bf16[2560,480]{0,1:T(8,128)(2,1)S(1)}, bf16[2560,480]{0,1:T(8,128)(2,1)S(1)}, u32[]{:S(2)}, u32[]{:S(2)}) collective-permute-start(bf16[2560,480]{0,1:T(8,128)(2,1)S(1)} %convolution_convert_fusion.2), channel_id=1, source_target_pairs={{0,8},{8,0},{16,24},{24,16},{32,40},{40,32},{48,56},{56,48},{64,72... | collective-permute-start | bytes 7372808 | tf_op jit(solution)/shard_map/ppermute | solution.py:29
  531.1 55.9 %collective-permute-start.76 = (bf16[960,640]{1,0:T(8,128)(2,1)S(1)}, bf16[960,640]{1,0:T(8,128)(2,1)S(1)}, u32[]{:S(2)}, u32[]{:S(2)}) collective-permute-start(bf16[960,640]{1,0:T(8,128)(2,1)S(1)} %get-tuple-element.191), channel_id=1, source_target_pairs={{0,96},{8,104},{16,112},{24,120},{32,64},{40,72},{48,80},{56,88},{... | collective-permute-start | bytes 3686408 | tf_op jit(solution)/shard_map/ppermute | solution.py:29
  533.6 53.4 %collective-permute-start.75 = (bf16[960,640]{1,0:T(8,128)(2,1)S(1)}, bf16[960,640]{1,0:T(8,128)(2,1)S(1)}, u32[]{:S(2)}, u32[]{:S(2)}) collective-permute-start(bf16[960,640]{1,0:T(8,128)(2,1)S(1)} %get-tuple-element.192), channel_id=1, source_target_pairs={{0,64},{8,72},{16,80},{24,88},{32,96},{40,104},{48,112},{56,120},{... | collective-permute-start | bytes 3686408 | tf_op jit(solution)/shard_map/ppermute | solution.py:29
  534.2 53.2 %collective-permute-start.74 = (bf16[960,640]{1,0:T(8,128)(2,1)S(1)}, bf16[960,640]{1,0:T(8,128)(2,1)S(1)}, u32[]{:S(2)}, u32[]{:S(2)}) collective-permute-start(bf16[960,640]{1,0:T(8,128)(2,1)S(1)} %get-tuple-element.190), channel_id=1, source_target_pairs={{0,32},{8,40},{16,48},{24,56},{32,0},{40,8},{48,16},{56,24},{64,96... | collective-permute-start | bytes 3686408 | tf_op jit(solution)/shard_map/ppermute | solution.py:29
  589.1 139.4 %reduce-scatter.21.cloned.1.call-start = ((), (), s32[]{:S(2)}) async-start(), calls=%async_computation.11 | async-start | bytes 3276800 | tf_op jit(solution)/shard_map/reduce_scatter | solution.py:58
  605.1 25.0 %collective-permute-start.54 = (bf16[2,176,640]{2,1,0:T(8,128)(2,1)S(1)}, bf16[2,176,640]{2,1,0:T(8,128)(2,1)S(1)}, u32[]{:S(2)}, u32[]{:S(2)}) collective-permute-start(bf16[2,176,640]{2,1,0:T(8,128)(2,1)S(1)} %bitcast.298), channel_id=1, source_target_pairs={{0,3},{1,2},{2,1},{3,0},{4,7},{5,6},{6,5},{7,4},{8,11},{9,10},{10,... | collective-permute-start | bytes 1351688 | tf_op jit(solution)/shard_map/ppermute | solution.py:29
  605.2 24.9 %collective-permute-start.53 = (bf16[2,176,640]{2,1,0:T(8,128)(2,1)S(1)}, bf16[2,176,640]{2,1,0:T(8,128)(2,1)S(1)}, u32[]{:S(2)}, u32[]{:S(2)}) collective-permute-start(bf16[2,176,640]{2,1,0:T(8,128)(2,1)S(1)} %bitcast.297), channel_id=1, source_target_pairs={{0,2},{1,3},{2,0},{3,1},{4,6},{5,7},{6,4},{7,5},{8,10},{9,11},{10,... | collective-permute-start | bytes 1351688 | tf_op jit(solution)/shard_map/ppermute | solution.py:29
  607.5 23.4 %collective-permute-start.52 = (bf16[2,176,640]{2,1,0:T(8,128)(2,1)S(1)}, bf16[2,176,640]{2,1,0:T(8,128)(2,1)S(1)}, u32[]{:S(2)}, u32[]{:S(2)}) collective-permute-start(bf16[2,176,640]{2,1,0:T(8,128)(2,1)S(1)} %bitcast.296), channel_id=1, source_target_pairs={{0,1},{1,0},{2,3},{3,2},{4,5},{5,4},{6,7},{7,6},{8,9},{9,8},{10,11... | collective-permute-start | bytes 1351688 | tf_op jit(solution)/shard_map/ppermute | solution.py:29
  643.6 109.9 %reduce-scatter.17.cloned.1.call-start = ((), (), s32[]{:S(2)}) async-start(), calls=%async_computation.9 | async-start | bytes 3276800 | tf_op jit(solution)/shard_map/reduce_scatter | solution.py:58
  664.3 18.9 %collective-permute-start.63 = (bf16[2,144,640]{2,1,0:T(8,128)(2,1)S(1)}, bf16[2,144,640]{2,1,0:T(8,128)(2,1)S(1)}, u32[]{:S(2)}, u32[]{:S(2)}) collective-permute-start(bf16[2,144,640]{2,1,0:T(8,128)(2,1)S(1)} %get-tuple-element.209), channel_id=1, source_target_pairs={{0,96},{8,104},{16,112},{24,120},{32,64},{40,72},{48,80},{56,88},{... | collective-permute-start | bytes 1105928 | tf_op jit(solution)/shard_map/ppermute | solution.py:29
  763.5 20.3 %collective-permute-start.83 = (bf16[64,640]{1,0:T(8,128)(2,1)S(1)}, bf16[64,640]{1,0:T(8,128)(2,1)S(1)}, u32[]{:S(2)}, u32[]{:S(2)}) collective-permute-start(bf16[64,640]{1,0:T(8,128)(2,1)S(1)} %get-tuple-element.315), channel_id=1, source_target_pairs={{0,17},{1,19},{2,21},{3,23},{4,16},{5,18},{6,20},{7,22},{8,25},{9,... | collective-permute-start | bytes 245768 | tf_op jit(solution)/shard_map/ppermute | solution.py:75
  (200 other events, 1671.0 us)
Sparse Core Ops, SparseCore 0:
  481.8 22.1 reduce-scatter.10
  506.5 34.8 reduce-scatter.12
  544.5 33.6 reduce-scatter.18
  589.2 34.6 reduce-scatter.14
  643.7 35.4 reduce-scatter.20
  695.3 34.4 reduce-scatter.16

commit v6 on v5

--- a/solution.py
+++ b/solution.py
@@ -111,27 +111,23 @@
     return jnp.concatenate(parts, axis=1)
 
 
-def finish_sums(summed, quarter):
+def rows_over_y(summed):
     joined = jnp.concatenate([as_rows(array) for array in summed], axis=1)
-    height = joined.shape[1] // 4
-    blocks = joined.reshape(2, 4, height, LAST)
-    total = sum_over_y(lambda k: lax.dynamic_index_in_dim(blocks, k, axis=1, keepdims=False))
-    if quarter is not None:
-        total = jnp.concatenate([total, quarter], axis=1)
-    own = spread_over_y(to_owners(total)[None], 0)
-
-    def take_apart(spread):
-        rows = spread[:, :height].reshape(4 * height, LAST)
+    blocks = joined.reshape(2, 4, joined.shape[1] // 4, LAST)
+    return sum_over_y(lambda k: lax.dynamic_index_in_dim(blocks, k, axis=1, keepdims=False))
+
+
+def whole_sums(over_y, shapes):
+    own = spread_over_y(to_owners(over_y), 0)
+
+    def take_apart(rows):
         results, first = [], 0
-        for array in summed:
-            count, columns = array.shape[1:]
+        for count, columns in shapes:
             parts = []
             for start in range(0, columns, LAST):
                 parts.append(rows[first : first + count, : min(LAST, columns - start)])
                 first += count
             results.append(jnp.concatenate(parts, axis=1))
-        if quarter is not None:
-            results.append(jnp.concatenate([spread[k, height:] for k in range(4)], axis=1))
         return results
 
     return take_apart(own), take_apart(swap_core(own))
@@ -141,7 +137,7 @@
     return pltpu.CompilerParams(vmem_limit_bytes=48 * 1024 * 1024)
 
 
-def assemble_kernel(count, y_parts, *refs):
+def assemble_kernel(count, y_parts, ready_ref, *refs):
     parts, out, sems = refs[:count], refs[count], refs[count + 1]
     me = lax.axis_index("fsdp")
     copies = []
@@ -166,7 +162,8 @@
         copy.wait()
 
 
-def assemble(parts, y_parts):
+def assemble(parts, y_parts, *earlier):
+    ready = token(earlier).reshape(1)
     rows, columns = parts[0].shape[1:]
     blocks = len(BLOCK_ORDER)
     columns = columns * len(parts) if y_parts else columns
@@ -174,33 +171,46 @@
     return pl.pallas_call(
         functools.partial(assemble_kernel, len(parts), y_parts),
         out_shape=jax.ShapeDtypeStruct((blocks, rows, columns), parts[0].dtype),
-        in_specs=[pl.BlockSpec(memory_space=pl.ANY)] * len(parts),
+        in_specs=[pl.BlockSpec(memory_space=pltpu.SMEM)]
+        + [pl.BlockSpec(memory_space=pl.ANY)] * len(parts),
         out_specs=pl.BlockSpec(memory_space=pltpu.VMEM),
         compiler_params=kernel_params(),
         scratch_shapes=[pltpu.SemaphoreType.DMA((blocks * (len(parts) if y_parts else 1),))],
         cost_estimate=pl.CostEstimate(flops=0, bytes_accessed=size, transcendentals=0),
         name="assemble",
-    )(*parts)
-
-
-def after(array, earlier):
-    return lax.optimization_barrier((array, earlier))[0]
-
-
-def gather_blocks(part, earlier):
-    pair = jnp.stack([part, swap(part, "fsdp", 4)])
-    pair = pair if earlier is None else after(pair, earlier)
+    )(ready, *parts)
+
+
+def token(arrays):
+    total = jnp.zeros((), f32)
+    for array in arrays:
+        last = lax.slice(array, tuple(n - 1 for n in array.shape), array.shape).reshape(())
+        total = total + (last != last).astype(f32)
+    return total
+
+
+def after(array, *earlier):
+    return array + token(earlier).astype(array.dtype) if earlier else array
+
+
+def z_pair(part):
+    return jnp.stack([part, swap(part, "fsdp", 4)])
+
+
+def gather_blocks(pair, *earlier):
+    pair = after(pair, *earlier)
     return [pair] + [swap(pair, "fsdp", m) for m in range(1, X_SIZE)]
 
 
-def gather_by_y(part, earlier):
+def quarter_by_y(part):
     columns = part.shape[1] // 4
-    y = y_position()
-    quarter = lax.dynamic_slice_in_dim(part, y * columns, columns, axis=1)
-    blocks = gather_blocks(quarter, earlier)
-    joined = jnp.concatenate(blocks, axis=0)
-    parts = [joined] + [swap(joined, "rep", 4 * m) for m in range(1, 4)]
-    return parts, joined
+    return lax.dynamic_slice_in_dim(part, y_position() * columns, columns, axis=1)
+
+
+def gather_by_y(blocks, earlier, later):
+    joined = after(jnp.concatenate(blocks, axis=0), earlier)
+    near = [swap(joined, "rep", 4 * m) for m in (1, 2)]
+    return [joined, *near, swap(after(joined, later), "rep", 12)]
 
 
 def stacked_heads(array, kv_head):
@@ -390,7 +400,7 @@
     key_place = blocks[:, None] * rows + jnp.arange(rows, dtype=jnp.int32)[None, :]
     key_place = key_place.reshape(-1, 1)
 
-    def own_weights(l):
+    def own_weights(l, *earlier):
         gains = jnp.stack([attn_gain[l], mlp_gain[l]])
         gains = jnp.pad(gains, ((0, 6), (0, att_width - shard)))
         att = pick(
@@ -400,16 +410,15 @@
         att = jnp.concatenate([att, gains], axis=0)
         gate_up = pick(gate_weight[l], up_weight[l])
         down = pick(down_weight[l][:, :half_width], down_weight[l][:, half_width:])
-        return att, gate_up, down
-
-    def gather_parts(own):
+        return after(att, *earlier), after(gate_up, *earlier), after(down, *earlier)
+
+    def gather_parts(own, *earlier):
         att, gate_up, down = own
-        att_parts = gather_blocks(att, None)
-        by_y, by_x = gather_by_y(gate_up, None)
-        return att_parts, by_y, by_x, down
-
-    def attention_weights(att_parts):
-        mine = assemble(att_parts, False)
+        att_parts = gather_blocks(z_pair(att), *earlier)
+        return att_parts, gather_blocks(z_pair(quarter_by_y(gate_up)), *earlier), z_pair(down)
+
+    def attention_weights(att_parts, *earlier):
+        mine = assemble(att_parts, False, *earlier)
         other = swap_core(mine)
         gain_attn = mine[:, shard, :shard].reshape(width).astype(f32)
         gain_mlp = mine[:, shard + 1, :shard].reshape(width).astype(f32)
@@ -417,10 +426,10 @@
         other = other[:, :shard].reshape(width, att_width)
         return gain_attn, gain_mlp, pick(mine, other), pick(other, mine)
 
-    def mlp_weights(by_y, down_parts):
-        mine = assemble(by_y, True).reshape(width, -1)
+    def mlp_weights(by_y, down_parts, mixed):
+        mine = assemble(by_y, True, mixed).reshape(width, -1)
         gate_up = (mine, swap_core(mine))
-        mine = assemble(down_parts, False).reshape(-1, half_width)
+        mine = assemble(down_parts, False, mixed).reshape(-1, half_width)
         return gate_up, (mine, swap_core(mine))
 
     stream = tokens.astype(f32)
@@ -428,21 +437,23 @@
     layers = []
     parts = gather_parts(own_weights(0))
     for l in range(DECODER_LAYERS):
-        att_parts, by_y, by_x, own_down = parts
-        att_parts = after(att_parts, stream)
-        gain_attn, gain_mlp, query_key, out_value = attention_weights(att_parts)
+        att_parts, quarters, down_pair = parts
+        gain_attn, gain_mlp, query_key, out_value = attention_weights(
+            att_parts, stream, *quarters
+        )
         normed = (normalize(stream) * gain_attn).astype(bf16)
         values = matmul(normed, out_value[:, width:]).astype(bf16)
         projected = matmul(normed, query_key)
         keys = rotary(projected[:, width:], cosine, sine).astype(bf16)
-        kv = gather_pack(after(jnp.concatenate([keys, values], axis=1), by_x))
-        down_parts = gather_blocks(own_down, kv)
-        if l + 1 < DECODER_LAYERS:
-            parts = gather_parts(after(own_weights(l + 1), kv))
+        kv = gather_pack(after(jnp.concatenate([keys, values], axis=1), down_pair))
+        by_y = gather_by_y(quarters, projected, kv)
+        down_parts = gather_blocks(down_pair, kv)
         queries = rotary(projected[:, :width], cosine, sine).astype(bf16)
         queries = queries * jnp.asarray(HEAD ** (-0.5), bf16)
+        if l + 1 < DECODER_LAYERS:
+            parts = gather_parts(own_weights(l + 1, projected), kv)
         mixed, logs = attend(queries, kv, key_place, bounds)
-        gate_up, down = mlp_weights(*after((by_y, down_parts), mixed))
+        gate_up, down = mlp_weights(by_y, down_parts, mixed)
         layers.append((gain_attn, gain_mlp, query_key, out_value, gate_up, down))
         middle = stream + matmul(mixed, out_value[:, :width])
         normed_mlp = (normalize(middle) * gain_mlp).astype(bf16)
@@ -457,7 +468,8 @@
         stream = middle + jnp.concatenate([pick(mine, other), pick(other, mine)], axis=1)
     output = stream.astype(bf16)
 
-    latest = done = ()
+    done = ()
+    pending = []
     grad = cotangent.astype(f32)
     results = [None] * DECODER_LAYERS
     for l in reversed(range(DECODER_LAYERS)):
@@ -483,20 +495,16 @@
         dmiddle = dmiddle + grad
         dmiddle_low = dmiddle.astype(bf16)
         dmixed = matmul_nt(dmiddle_low, out_value[:, :width]).astype(bf16)
-        dmixed = after(dmixed, (down_sum, gate_up_sum))
+        dmixed = after(dmixed, down_sum, gate_up_sum)
         dq, dkv = attend_back(queries, kv, key_place, bounds, mixed, logs, dmixed)
-        down_sum = sum_over_x(after(down_sum, latest))
-        dkv = after(scatter_pack(dkv), done)
-        columns = gate_up_sum.shape[1] // 4
-        gate_up_sum = sum_over_y(
-            lambda k: lax.dynamic_slice_in_dim(gate_up_sum, k * columns, columns, axis=1)
-        )
-        gate_up_sum = sum_over_x(after(gate_up_sum, down_sum))
+        down_sum = sum_over_x(down_sum)
+        gate_up_sum = sum_over_x(gate_up_sum)
+        dkv = scatter_pack(dkv)
         dq = rotary_back(dq, cosine, sine).astype(bf16)
         dk = rotary_back(dkv[:, :key_width], cosine, sine).astype(bf16)
         dv = dkv[:, key_width:].astype(bf16)
 
-        dqk = jnp.concatenate([dq, dk], axis=1)
+        dqk = after(jnp.concatenate([dq, dk], axis=1), *done)
         dnormed = matmul_nt(dqk, query_key) + matmul_nt(dv, out_value[:, width:])
         dstream, attn_gain_grad = normalize_back(stream, gain_attn, dnormed)
         grad = dstream + dmiddle
@@ -515,19 +523,36 @@
         gain_grads = gain_grads.reshape(2, -1, shard).swapaxes(0, 1)
         gain_grads = jnp.pad(gain_grads, ((0, 0), (0, 6), (0, att_width - shard)))
         att_sum = jnp.concatenate([att_sum.reshape(-1, shard, att_width), gain_grads], axis=1)
-        att_sum = sum_over_x(after(att_sum.reshape(-1, att_width), gate_up_sum))
-        latest = att_sum
+        att_sum = after(att_sum.reshape(-1, att_width), gate_up_sum)
+        late = att_sum
+        att_sum = sum_over_x(att_sum)
 
         att_pair = att_sum.reshape(2, shard + 8, att_width)
         down_pair = down_sum.reshape(2, -1, half_width)
-        gate_up_pair = gate_up_sum.reshape(2, shard, columns)
+        gate_up_pair = gate_up_sum.reshape(2, shard, -1)
         if l > 0:
-            done = finish_sums([att_pair, down_pair], gate_up_pair)
-            (att_own, down_own, gate_up_own), (att_other, down_other, gate_up_other) = done
+            groups = [(l, (att_pair, down_pair, gate_up_pair))]
         else:
-            mlp = finish_sums([down_pair], gate_up_pair)
-            (down_own, gate_up_own), (down_other, gate_up_other) = mlp
-            (att_own,), (att_other,) = finish_sums([att_pair], None)
+            groups = [(l, (down_pair, gate_up_pair)), (l, (att_pair,))]
+        for layer, arrays in groups:
+            shapes = [array.shape[1:] for array in arrays]
+            pending.append((layer, rows_over_y(arrays), shapes))
+        done = (pending[-1][1],)
+
+    found = {}
+    for layer, over_y, shapes in pending:
+        if shapes != pending[-1][2]:
+            over_y = after(over_y, late)
+        own, other = whole_sums(over_y, shapes)
+        for shape, pair in zip(shapes, zip(own, other)):
+            found[layer, shape] = pair
+    att_shape = (shard + 8, att_width)
+    down_shape = (down_weight.shape[1], half_width)
+    gate_up_shape = (shard, gate_weight.shape[2])
+    for l in range(DECODER_LAYERS):
+        att_own, att_other = found[l, att_shape]
+        down_own, down_other = found[l, down_shape]
+        gate_up_own, gate_up_other = found[l, gate_up_shape]
         att_a, att_b = pick(att_own, att_other), pick(att_other, att_own)
         results[l] = (
             att_own[shard, :shard],

time: 830 us -> 965 us (1.16)
  waiting for transfers between devices: 330 us -> 374 us
  local copies, waits for them, and re-layouts: 80.2 us -> 119 us
  between operations: 16.8 us -> 50.9 us
  other arithmetic: 79.5 us -> 90.4 us
    ppermute x87 -> x81, waiting for transfers between devices: 317 us -> 350 us  [swap(): return lax.ppermute(array, axis, [(i, i ^ mask) for i in range(count)])]
    slice x14 -> x27, local copies, waits for them, and re-layouts: 6.01 us -> 23.8 us  [the longest x26 22.5 us: token(): lax.slice(array, tuple((n - 1 for n in array.shape)), array.shape)]
    add x0 -> x16, other arithmetic: none -> 17.2 us  [after(): return array + token(earlier).astype(array.dtype) if earlier else array]
    convert_element_type x0 -> x6, other arithmetic: none -> 14 us  [the longest x2 11.4 us: body(): (cross_rows(hidden, grad_mine) + down_received.astype(f32)).astype(bf16)]
    reduce_scatter x6, waiting for transfers between devices: 3.88 us -> 17 us  [sum_over_x(): lax.psum_scatter(rows, 'fsdp', scatter_dimension=0, tiled=True, axis_inde...]
    unnamed x311 -> x313, local copies, waits for them, and re-layouts: 34.9 us -> 45.8 us
    ppermute x87 -> x81, starting transfers between devices: 124 us -> 132 us  [swap(): return lax.ppermute(array, axis, [(i, i ^ mask) for i in range(count)])]
  transfers between devices with their start and end apart: 105 -> 99, of which waited for: 52 -> 53; matrix products, arithmetic and copies ran while one was open for 26% -> 26% of each run, Pallas kernels for 4% -> 5%
where the time goes in v6:
time: 965 us; the launch traced here: 950 us
  waiting for transfers between devices  374 us (39%)
  starting transfers between devices  158 us (16%)
  local copies, waits for them, and re-layouts  119 us (12%)
  matrix products  101 us (10%)
  other arithmetic  90.4 us (9%)
  Pallas kernels  57.2 us (6%)
  between operations  50.9 us (5%)
    ppermute x81, waiting for transfers between devices, swap(): return lax.ppermute(array, axis, [(i, i ^ mask) for i in range(count)])  350 us
    ppermute x81, starting transfers between devices, swap(): return lax.ppermute(array, axis, [(i, i ^ mask) for i in range(count)])  132 us
    unnamed x313, local copies, waits for them, and re-layouts  45.8 us
    dot_general x16, matrix products, cross_rows(): lax.dot_general(left, right, (((0,), (0,)), ((), ())), preferred_element_...  39.3 us
    dot_general x14, matrix products, matmul_nt(): return lax.dot_general(left, right, NT, preferred_element_type=f32)  34.2 us
    pallas_call x2, Pallas kernels, attend_back(): pl.pallas_call(attention_backward_kernel, out_shape=(jax.ShapeDtypeStruct...  28.2 us
    dot_general x14, matrix products, matmul(): return jnp.dot(left, right, preferred_element_type=f32)  27.9 us
    ppermute x12, starting transfers between devices, send(): return lax.ppermute(block, ('rep', 'fsdp'), moves).astype(f32)  24.7 us
  transfers between devices with their start and end apart: 99, of which 53 were waited for; matrix products, arithmetic and copies ran while one was open for 26% of the time, Pallas kernels for 5%

profile of v6, /device:TPU:5, one launch (start us, length us, event | category | flops | bytes accessed | tf_op | source)
XLA Modules:
  0.0 950.2 jit_solution(16161191149910322780)
XLA Ops:
  21.9 4.8 collective-permute-done.4
  33.3 29.4 %collective-permute-done.1 = bf16[2,120,640]{2,1,0:T(8,128)(2,1)} collective-permute-done((bf16[2,120,640]{2,1,0:T(8,128)(2,1)}, bf16[2,120,640]{2,1,0:T(8,128)(2,1)}, u32[]{:S(2)}, u32[]{:S(2)}) %collective-permute-start.1) | collective-permute-done | bytes 307232 | tf_op jit(solution)/shard_map/ppermute | solution.py:29
  115.7 6.4 collective-permute-done.10
  127.1 5.7 collective-permute-done.11
  132.9 10.7 %collective-permute-done.12 = bf16[2,176,640]{2,1,0:T(8,128)(2,1)S(1)} collective-permute-done((bf16[2,176,640]{2,1,0:T(8,128)(2,1)S(1)}, bf16[2,176,640]{2,1,0:T(8,128)(2,1)S(1)}, u32[]{:S(2)}, u32[]{:S(2)}) %collective-permute-start.12) | collective-permute-done | bytes 450592 | tf_op jit(solution)/shard_map/ppermute | solution.py:29
  159.5 7.6 attention_forward.2
  169.1 8.1 collective-permute-done.14.refs_1_
  177.2 28.8 %collective-permute-done.15.refs_2_ = bf16[8,120,640]{2,1,0:T(8,128)(2,1)} collective-permute-done((bf16[8,120,640]{2,1,0:T(8,128)(2,1)S(1)}, bf16[8,120,640]{2,1,0:T(8,128)(2,1)}, u32[]{:S(2)}, u32[]{:S(2)}) %collective-permute-start.15) | collective-permute-done | bytes 1228832 | tf_op jit(solution)/shard_map/ppermute | solution.py:29
  206.0 4.6 assemble.7
  210.7 6.6 collective-permute-start.17
  226.4 10.4 %collective-permute-done.18.refs_1_ = bf16[2,320,480]{2,1,0:T(8,128)(2,1)S(1)} collective-permute-done((bf16[2,320,480]{2,1,0:T(8,128)(2,1)S(1)}, bf16[2,320,480]{2,1,0:T(8,128)(2,1)S(1)}, u32[]{:S(2)}, u32[]{:S(2)}) %collective-permute-start.18) | collective-permute-done | bytes 614432 | tf_op jit(solution)/shard_map/ppermute | solution.py:29
  238.1 12.2 %collective-permute-done.19.refs_2_ = bf16[2,320,480]{2,1,0:T(8,128)(2,1)S(1)} collective-permute-done((bf16[2,320,480]{2,1,0:T(8,128)(2,1)S(1)}, bf16[2,320,480]{2,1,0:T(8,128)(2,1)S(1)}, u32[]{:S(2)}, u32[]{:S(2)}) %collective-permute-start.19) | collective-permute-done | bytes 614432 | tf_op jit(solution)/shard_map/ppermute | solution.py:29
  288.2 6.1 multiply_convert_fusion.5
  299.2 9.2 collective-permute-done.28.refs_2_
  318.6 10.8 %collective-permute-done.31 = bf16[320,480]{1,0:T(8,128)(2,1)S(1)} collective-permute-done((bf16[320,480]{1,0:T(8,128)(2,1)S(1)}, bf16[320,480]{1,0:T(8,128)(2,1)S(1)}, u32[]{:S(2)}, u32[]{:S(2)}) %collective-permute-start.31) | collective-permute-done | bytes 307232 | tf_op jit(solution)/shard_map/ppermute | solution.py:29
  340.8 7.4 collective-permute-done.32
  353.2 5.4 collective-permute-done.33
  358.7 10.7 %collective-permute-done.34 = bf16[2,176,640]{2,1,0:T(8,128)(2,1)S(1)} collective-permute-done((bf16[2,176,640]{2,1,0:T(8,128)(2,1)S(1)}, bf16[2,176,640]{2,1,0:T(8,128)(2,1)S(1)}, u32[]{:S(2)}, u32[]{:S(2)}) %collective-permute-start.34) | collective-permute-done | bytes 450592 | tf_op jit(solution)/shard_map/ppermute | solution.py:29
  380.2 7.7 attention_forward.3
  389.8 10.4 %collective-permute-done.36.refs_1_ = bf16[8,120,640]{2,1,0:T(8,128)(2,1)S(1)} collective-permute-done((bf16[8,120,640]{2,1,0:T(8,128)(2,1)S(1)}, bf16[8,120,640]{2,1,0:T(8,128)(2,1)S(1)}, u32[]{:S(2)}, u32[]{:S(2)}) %collective-permute-start.36) | collective-permute-done | bytes 1228832 | tf_op jit(solution)/shard_map/ppermute | solution.py:29
  400.2 26.1 %collective-permute-done.37.refs_2_ = bf16[8,120,640]{2,1,0:T(8,128)(2,1)S(1)} collective-permute-done((bf16[8,120,640]{2,1,0:T(8,128)(2,1)S(1)}, bf16[8,120,640]{2,1,0:T(8,128)(2,1)S(1)}, u32[]{:S(2)}, u32[]{:S(2)}) %collective-permute-start.37) | collective-permute-done | bytes 1228832 | tf_op jit(solution)/shard_map/ppermute | solution.py:29
  429.5 6.9 collective-permute-start.39
  441.1 13.8 %collective-permute-done.40.refs_1_ = bf16[2,320,480]{2,1,0:T(8,128)(2,1)S(1)} collective-permute-done((bf16[2,320,480]{2,1,0:T(8,128)(2,1)S(1)}, bf16[2,320,480]{2,1,0:T(8,128)(2,1)S(1)}, u32[]{:S(2)}, u32[]{:S(2)}) %collective-permute-start.40) | collective-permute-done | bytes 614432 | tf_op jit(solution)/shard_map/ppermute | solution.py:29
  454.9 13.9 %collective-permute-done.41.refs_2_ = bf16[2,320,480]{2,1,0:T(8,128)(2,1)S(1)} collective-permute-done((bf16[2,320,480]{2,1,0:T(8,128)(2,1)S(1)}, bf16[2,320,480]{2,1,0:T(8,128)(2,1)S(1)}, u32[]{:S(2)}, u32[]{:S(2)}) %collective-permute-start.41) | collective-permute-done | bytes 614432 | tf_op jit(solution)/shard_map/ppermute | solution.py:29
  472.3 4.5 copy.210
  519.2 4.5 copy.211
  523.7 5.7 add_convert_fusion.3
  537.4 14.0 %attention_backward.2 = (f32[176,960]{1,0:T(8,128)S(1)}, bf16[1408,640]{1,0:T(8,128)(2,1)S(1)}) custom-call(bf16[176,960]{1,0:T(8,128)(2,1)S(1)} %fusion.84.q_ref, bf16[1408,640]{1,0:T(8,128)(2,1)S(1)} %bitcast.285, s32[1408,1]{1,0:T(8,128)S(1)} %copy-done.7, s32[8,528]{1,0:T(8,128)S(1)} %pad.26.bounds_ref, ...), custom_call_target="tpu_custom_call" | custom-call | flops 2378956800 | bytes 6291456 | tf_op jit(solution)/shard_map/attention_backward/pallas_call | solution.py:306
  557.6 24.3 %collective-permute-done.48 = bf16[2,176,640]{2,1,0:T(8,128)(2,1)S(1)} collective-permute-done((bf16[2,176,640]{2,1,0:T(8,128)(2,1)S(1)}, bf16[2,176,640]{2,1,0:T(8,128)(2,1)S(1)}, u32[]{:S(2)}, u32[]{:S(2)}) %collective-permute-start.48) | collective-permute-done | bytes 450592 | tf_op jit(solution)/shard_map/ppermute | solution.py:29
  586.1 5.0 collective-permute-done.49
  607.0 5.7 add_convert_fusion.2
  629.8 5.8 fusion.2
  653.0 4.9 fusion.92
  661.2 6.1 add_convert_fusion
  668.4 4.4 multiply_reduce_fusion
  679.3 14.2 %attention_backward.3 = (f32[176,960]{1,0:T(8,128)S(1)}, bf16[1408,640]{1,0:T(8,128)(2,1)S(1)}) custom-call(bf16[176,960]{1,0:T(8,128)(2,1)S(1)} %copy-done.22, bf16[1408,640]{1,0:T(8,128)(2,1)S(1)} %bitcast.282, s32[1408,1]{1,0:T(8,128)S(1)} %copy-done.8, s32[8,528]{1,0:T(8,128)S(1)} %pad.26.bounds_ref, bf16[176,960]{1,0:T(8,128)(2,1)S(1)} %copy-done.4, ...), custom_call_target="tpu_custom_call" | custom-call | flops 2378956800 | bytes 6291456 | tf_op jit(solution)/shard_map/attention_backward/pallas_call | solution.py:306
  698.6 26.7 %collective-permute-done.54 = bf16[2,176,640]{2,1,0:T(8,128)(2,1)S(1)} collective-permute-done((bf16[2,176,640]{2,1,0:T(8,128)(2,1)S(1)}, bf16[2,176,640]{2,1,0:T(8,128)(2,1)S(1)}, u32[]{:S(2)}, u32[]{:S(2)}) %collective-permute-start.54) | collective-permute-done | bytes 450592 | tf_op jit(solution)/shard_map/ppermute | solution.py:29
  725.3 9.5 collective-permute-done.52
  760.5 5.3 fusion.3
  780.9 12.5 %reduce-scatter.23.cloned.1.call-done = bf16[240,2560]{1,0:T(8,128)(2,1)} async-done(((bf16[960,2560]{1,0:T(8,128)(2,1)}), bf16[240,2560]{1,0:T(8,128)(2,1)}) %reduce-scatter.23.cloned.1.call-update) | async-done | bytes 1228816 | tf_op jit(solution)/shard_map/reduce_scatter | solution.py:58
  804.2 4.9 collective-permute-done.60
  843.8 4.6 collective-permute-done.74
  851.5 11.2 %collective-permute-start.78 = (bf16[264,640]{1,0:T(8,128)(2,1)S(1)}, bf16[264,640]{1,0:T(8,128)(2,1)S(1)}, u32[]{:S(2)}, u32[]{:S(2)}) collective-permute-start(bf16[264,640]{1,0:T(8,128)(2,1)S(1)} %add_convert_fusion.4), channel_id=1, source_target_pairs={{0,64},{8,72},{16,80},{24,88},{32,96},{40,104},{48,112},{56,120},{... | collective-permute-start | bytes 1013768 | tf_op jit(solution)/shard_map/ppermute | solution.py:29
  867.6 5.0 collective-permute-start.90
  872.6 5.5 collective-permute-done.77
  880.7 4.9 collective-permute-done.90
  898.2 4.5 reduce-scatter.17.cloned.1.call-done
  907.6 5.5 collective-permute-done.65
  (755 shorter events, 436.3 us)
Async XLA Ops:
  7.2 628.4 %reduce-scatter.19.cloned.1.call-start = ((), (), s32[]{:S(2)}) async-start(), calls=%async_computation.8 | async-start | bytes 6144000 | tf_op jit(solution)/shard_map/reduce_scatter | solution.py:58
  27.7 50.3 %collective-permute-start.5 = (bf16[2,128,1280]{2,1,0:T(8,128)(2,1)S(1)}, bf16[2,128,1280]{2,1,0:T(8,128)(2,1)S(1)}, u32[]{:S(2)}, u32[]{:S(2)}) collective-permute-start(bf16[2,128,1280]{2,1,0:T(8,128)(2,1)S(1)} %pad_maximum_fusion.4.refs_0_), channel_id=1, source_target_pairs={{0,1},{1,0},{2,3},{3,2},{4,5},{5,4},{6,7},{7,6},{8,9},{9,8},{10,11... | collective-permute-start | bytes 1966088 | tf_op jit(solution)/shard_map/ppermute | solution.py:29
  28.7 50.1 %collective-permute-start.6 = (bf16[2,128,1280]{2,1,0:T(8,128)(2,1)S(1)}, bf16[2,128,1280]{2,1,0:T(8,128)(2,1)S(1)}, u32[]{:S(2)}, u32[]{:S(2)}) collective-permute-start(bf16[2,128,1280]{2,1,0:T(8,128)(2,1)S(1)} %pad_maximum_fusion.4.refs_0_), channel_id=1, source_target_pairs={{0,2},{1,3},{2,0},{3,1},{4,6},{5,7},{6,4},{7,5},{8,10},{9,11},{10,... | collective-permute-start | bytes 1966088 | tf_op jit(solution)/shard_map/ppermute | solution.py:29
  29.2 50.5 %collective-permute-start.7 = (bf16[2,128,1280]{2,1,0:T(8,128)(2,1)S(1)}, bf16[2,128,1280]{2,1,0:T(8,128)(2,1)S(1)}, u32[]{:S(2)}, u32[]{:S(2)}) collective-permute-start(bf16[2,128,1280]{2,1,0:T(8,128)(2,1)S(1)} %pad_maximum_fusion.4.refs_0_), channel_id=1, source_target_pairs={{0,3},{1,2},{2,1},{3,0},{4,7},{5,6},{6,5},{7,4},{8,11},{9,10},{10,... | collective-permute-start | bytes 1966088 | tf_op jit(solution)/shard_map/ppermute | solution.py:29
  31.2 31.5 %collective-permute-start.1 = (bf16[2,120,640]{2,1,0:T(8,128)(2,1)}, bf16[2,120,640]{2,1,0:T(8,128)(2,1)}, u32[]{:S(2)}, u32[]{:S(2)}) collective-permute-start(bf16[2,120,640]{2,1,0:T(8,128)(2,1)} %pad_maximum_fusion.20), channel_id=1, source_target_pairs={{0,1},{1,0},{2,3},{3,2},{4,5},{5,4},{6,7},{7,6},{8,9},{9,8},{10,11... | collective-permute-start | bytes 921608 | tf_op jit(solution)/shard_map/ppermute | solution.py:29
  33.3 39.1 %collective-permute-start.2 = (bf16[2,120,640]{2,1,0:T(8,128)(2,1)}, bf16[2,120,640]{2,1,0:T(8,128)(2,1)S(1)}, u32[]{:S(2)}, u32[]{:S(2)}) collective-permute-start(bf16[2,120,640]{2,1,0:T(8,128)(2,1)} %pad_maximum_fusion.20), channel_id=1, source_target_pairs={{0,2},{1,3},{2,0},{3,1},{4,6},{5,7},{6,4},{7,5},{8,10},{9,11},{10,... | collective-permute-start | bytes 921608 | tf_op jit(solution)/shard_map/ppermute | solution.py:29
  84.7 22.0 %collective-permute-start.8 = (bf16[8,128,1280]{2,1,0:T(8,128)(2,1)S(1)}, bf16[8,128,1280]{2,1,0:T(8,128)(2,1)}, u32[]{:S(2)}, u32[]{:S(2)}) collective-permute-start(bf16[8,128,1280]{2,1,0:T(8,128)(2,1)S(1)} %assemble.6), channel_id=1, source_target_pairs={{0,8},{8,0},{16,24},{24,16},{32,40},{40,32},{48,56},{56,48},{64,72... | collective-permute-start | bytes 7864328 | tf_op jit(solution)/shard_map/ppermute | solution.py:29
  123.1 20.5 %collective-permute-start.12 = (bf16[2,176,640]{2,1,0:T(8,128)(2,1)S(1)}, bf16[2,176,640]{2,1,0:T(8,128)(2,1)S(1)}, u32[]{:S(2)}, u32[]{:S(2)}) collective-permute-start(bf16[2,176,640]{2,1,0:T(8,128)(2,1)S(1)} %pad_maximum_fusion.10), channel_id=1, source_target_pairs={{0,2},{1,3},{2,0},{3,1},{4,6},{5,7},{6,4},{7,5},{8,10},{9,11},{10,... | collective-permute-start | bytes 1351688 | tf_op jit(solution)/shard_map/ppermute | solution.py:29
  151.2 26.0 %collective-permute-start.14 = (bf16[8,120,640]{2,1,0:T(8,128)(2,1)S(1)}, bf16[8,120,640]{2,1,0:T(8,128)(2,1)S(1)}, u32[]{:S(2)}, u32[]{:S(2)}) collective-permute-start(bf16[8,120,640]{2,1,0:T(8,128)(2,1)S(1)} %get-tuple-element.120.refs_0_), channel_id=1, source_target_pairs={{0,32},{8,40},{16,48},{24,56},{32,0},{40,8},{48,16},{56,24},{64,96... | collective-permute-start | bytes 3686408 | tf_op jit(solution)/shard_map/ppermute | solution.py:29
  152.5 53.6 %collective-permute-start.15 = (bf16[8,120,640]{2,1,0:T(8,128)(2,1)S(1)}, bf16[8,120,640]{2,1,0:T(8,128)(2,1)}, u32[]{:S(2)}, u32[]{:S(2)}) collective-permute-start(bf16[8,120,640]{2,1,0:T(8,128)(2,1)S(1)} %get-tuple-element.120.refs_0_), channel_id=1, source_target_pairs={{0,64},{8,72},{16,80},{24,88},{32,96},{40,104},{48,112},{56,120},{... | collective-permute-start | bytes 3686408 | tf_op jit(solution)/shard_map/ppermute | solution.py:29
  155.1 50.9 %collective-permute-start.16 = (bf16[8,120,640]{2,1,0:T(8,128)(2,1)}, bf16[8,120,640]{2,1,0:T(8,128)(2,1)}, u32[]{:S(2)}, u32[]{:S(2)}) collective-permute-start(bf16[8,120,640]{2,1,0:T(8,128)(2,1)} %get-tuple-element.119), channel_id=1, source_target_pairs={{0,96},{8,104},{16,112},{24,120},{32,64},{40,72},{48,80},{56,88},{... | collective-permute-start | bytes 3686408 | tf_op jit(solution)/shard_map/ppermute | solution.py:29
  210.7 77.5 %collective-permute-start.17 = (bf16[960,2560]{1,0:T(8,128)(2,1)}, bf16[960,2560]{1,0:T(8,128)(2,1)}, u32[]{:S(2)}, u32[]{:S(2)}) collective-permute-start(bf16[960,2560]{1,0:T(8,128)(2,1)} %bitcast.286), channel_id=1, source_target_pairs={{0,8},{8,0},{16,24},{24,16},{32,40},{40,32},{48,56},{56,48},{64,72... | collective-permute-start | bytes 14745608 | tf_op jit(solution)/shard_map/ppermute | solution.py:29
  221.8 28.5 %collective-permute-start.19 = (bf16[2,320,480]{2,1,0:T(8,128)(2,1)S(1)}, bf16[2,320,480]{2,1,0:T(8,128)(2,1)S(1)}, u32[]{:S(2)}, u32[]{:S(2)}) collective-permute-start(bf16[2,320,480]{2,1,0:T(8,128)(2,1)S(1)} %maximum_add_fusion.5.refs_0_), channel_id=1, source_target_pairs={{0,2},{1,3},{2,0},{3,1},{4,6},{5,7},{6,4},{7,5},{8,10},{9,11},{10,... | collective-permute-start | bytes 1843208 | tf_op jit(solution)/shard_map/ppermute | solution.py:29
  221.8 30.1 %collective-permute-start.20 = (bf16[2,320,480]{2,1,0:T(8,128)(2,1)S(1)}, bf16[2,320,480]{2,1,0:T(8,128)(2,1)S(1)}, u32[]{:S(2)}, u32[]{:S(2)}) collective-permute-start(bf16[2,320,480]{2,1,0:T(8,128)(2,1)S(1)} %maximum_add_fusion.5.refs_0_), channel_id=1, source_target_pairs={{0,3},{1,2},{2,1},{3,0},{4,7},{5,6},{6,5},{7,4},{8,11},{9,10},{10,... | collective-permute-start | bytes 1843208 | tf_op jit(solution)/shard_map/ppermute | solution.py:29
  225.6 35.1 %collective-permute-start.22 = (bf16[120,640]{1,0:T(8,128)(2,1)S(1)}, bf16[120,640]{1,0:T(8,128)(2,1)}, u32[]{:S(2)}, u32[]{:S(2)}) collective-permute-start(bf16[120,640]{1,0:T(8,128)(2,1)S(1)} %bitcast.339), channel_id=1, source_target_pairs={{0,4},{1,5},{2,6},{3,7},{4,0},{5,1},{6,2},{7,3},{8,12},{9,13},{10,... | collective-permute-start | bytes 460808 | tf_op jit(solution)/shard_map/ppermute | solution.py:29
  237.7 28.3 %collective-permute-start.26 = (bf16[128,1280]{1,0:T(8,128)(2,1)}, bf16[128,1280]{1,0:T(8,128)(2,1)}, u32[]{:S(2)}, u32[]{:S(2)}) collective-permute-start(bf16[128,1280]{1,0:T(8,128)(2,1)} %maximum_add_fusion.11), channel_id=1, source_target_pairs={{0,4},{1,5},{2,6},{3,7},{4,0},{5,1},{6,2},{7,3},{8,12},{9,13},{10,... | collective-permute-start | bytes 983048 | tf_op jit(solution)/shard_map/ppermute | solution.py:29
  259.5 34.9 %collective-permute-start.21 = (bf16[2560,480]{0,1:T(8,128)(2,1)}, bf16[2560,480]{0,1:T(8,128)(2,1)S(1)}, u32[]{:S(2)}, u32[]{:S(2)}) collective-permute-start(bf16[2560,480]{0,1:T(8,128)(2,1)} %copy.204), channel_id=1, source_target_pairs={{0,8},{8,0},{16,24},{24,16},{32,40},{40,32},{48,56},{56,48},{64,72... | collective-permute-start | bytes 7372808 | tf_op jit(solution)/shard_map/ppermute | solution.py:29
  271.9 27.3 %collective-permute-start.27 = (bf16[2,128,1280]{2,1,0:T(8,128)(2,1)S(1)}, bf16[2,128,1280]{2,1,0:T(8,128)(2,1)}, u32[]{:S(2)}, u32[]{:S(2)}) collective-permute-start(bf16[2,128,1280]{2,1,0:T(8,128)(2,1)S(1)} %maximum_add_fusion.6.refs_0_), channel_id=1, source_target_pairs={{0,1},{1,0},{2,3},{3,2},{4,5},{5,4},{6,7},{7,6},{8,9},{9,8},{10,11... | collective-permute-start | bytes 1966088 | tf_op jit(solution)/shard_map/ppermute | solution.py:29
  280.1 28.2 %collective-permute-start.28 = (bf16[2,128,1280]{2,1,0:T(8,128)(2,1)S(1)}, bf16[2,128,1280]{2,1,0:T(8,128)(2,1)}, u32[]{:S(2)}, u32[]{:S(2)}) collective-permute-start(bf16[2,128,1280]{2,1,0:T(8,128)(2,1)S(1)} %maximum_add_fusion.6.refs_0_), channel_id=1, source_target_pairs={{0,2},{1,3},{2,0},{3,1},{4,6},{5,7},{6,4},{7,5},{8,10},{9,11},{10,... | collective-permute-start | bytes 1966088 | tf_op jit(solution)/shard_map/ppermute | solution.py:29
  283.2 29.6 %collective-permute-start.29 = (bf16[2,128,1280]{2,1,0:T(8,128)(2,1)S(1)}, bf16[2,128,1280]{2,1,0:T(8,128)(2,1)}, u32[]{:S(2)}, u32[]{:S(2)}) collective-permute-start(bf16[2,128,1280]{2,1,0:T(8,128)(2,1)S(1)} %maximum_add_fusion.6.refs_0_), channel_id=1, source_target_pairs={{0,3},{1,2},{2,1},{3,0},{4,7},{5,6},{6,5},{7,4},{8,11},{9,10},{10,... | collective-permute-start | bytes 1966088 | tf_op jit(solution)/shard_map/ppermute | solution.py:29
  374.7 25.5 %collective-permute-start.36 = (bf16[8,120,640]{2,1,0:T(8,128)(2,1)S(1)}, bf16[8,120,640]{2,1,0:T(8,128)(2,1)S(1)}, u32[]{:S(2)}, u32[]{:S(2)}) collective-permute-start(bf16[8,120,640]{2,1,0:T(8,128)(2,1)S(1)} %get-tuple-element.112.refs_0_), channel_id=1, source_target_pairs={{0,32},{8,40},{16,48},{24,56},{32,0},{40,8},{48,16},{56,24},{64,96... | collective-permute-start | bytes 3686408 | tf_op jit(solution)/shard_map/ppermute | solution.py:29
  374.8 51.5 %collective-permute-start.37 = (bf16[8,120,640]{2,1,0:T(8,128)(2,1)S(1)}, bf16[8,120,640]{2,1,0:T(8,128)(2,1)S(1)}, u32[]{:S(2)}, u32[]{:S(2)}) collective-permute-start(bf16[8,120,640]{2,1,0:T(8,128)(2,1)S(1)} %get-tuple-element.112.refs_0_), channel_id=1, source_target_pairs={{0,64},{8,72},{16,80},{24,88},{32,96},{40,104},{48,112},{56,120},{... | collective-permute-start | bytes 3686408 | tf_op jit(solution)/shard_map/ppermute | solution.py:29
  376.0 50.3 %collective-permute-start.38 = (bf16[8,120,640]{2,1,0:T(8,128)(2,1)S(1)}, bf16[8,120,640]{2,1,0:T(8,128)(2,1)S(1)}, u32[]{:S(2)}, u32[]{:S(2)}) collective-permute-start(bf16[8,120,640]{2,1,0:T(8,128)(2,1)S(1)} %get-tuple-element.111), channel_id=1, source_target_pairs={{0,96},{8,104},{16,112},{24,120},{32,64},{40,72},{48,80},{56,88},{... | collective-permute-start | bytes 3686408 | tf_op jit(solution)/shard_map/ppermute | solution.py:29
  429.5 57.5 %collective-permute-start.39 = (bf16[960,2560]{1,0:T(8,128)(2,1)}, bf16[960,2560]{1,0:T(8,128)(2,1)}, u32[]{:S(2)}, u32[]{:S(2)}) collective-permute-start(bf16[960,2560]{1,0:T(8,128)(2,1)} %bitcast.289), channel_id=1, source_target_pairs={{0,8},{8,0},{16,24},{24,16},{32,40},{40,32},{48,56},{56,48},{64,72... | collective-permute-start | bytes 14745608 | tf_op jit(solution)/shard_map/ppermute | solution.py:29
  439.8 29.0 %collective-permute-start.41 = (bf16[2,320,480]{2,1,0:T(8,128)(2,1)S(1)}, bf16[2,320,480]{2,1,0:T(8,128)(2,1)S(1)}, u32[]{:S(2)}, u32[]{:S(2)}) collective-permute-start(bf16[2,320,480]{2,1,0:T(8,128)(2,1)S(1)} %maximum_add_fusion.7.refs_0_), channel_id=1, source_target_pairs={{0,2},{1,3},{2,0},{3,1},{4,6},{5,7},{6,4},{7,5},{8,10},{9,11},{10,... | collective-permute-start | bytes 1843208 | tf_op jit(solution)/shard_map/ppermute | solution.py:29
  439.9 30.1 %collective-permute-start.42 = (bf16[2,320,480]{2,1,0:T(8,128)(2,1)S(1)}, bf16[2,320,480]{2,1,0:T(8,128)(2,1)S(1)}, u32[]{:S(2)}, u32[]{:S(2)}) collective-permute-start(bf16[2,320,480]{2,1,0:T(8,128)(2,1)S(1)} %maximum_add_fusion.7.refs_0_), channel_id=1, source_target_pairs={{0,3},{1,2},{2,1},{3,0},{4,7},{5,6},{6,5},{7,4},{8,11},{9,10},{10,... | collective-permute-start | bytes 1843208 | tf_op jit(solution)/shard_map/ppermute | solution.py:29
  497.2 22.1 %collective-permute-start.44 = (bf16[2560,480]{0,1:T(8,128)(2,1)}, bf16[2560,480]{0,1:T(8,128)(2,1)}, u32[]{:S(2)}, u32[]{:S(2)}) collective-permute-start(bf16[2560,480]{0,1:T(8,128)(2,1)} %convolution_convert_fusion.3), channel_id=1, source_target_pairs={{0,8},{8,0},{16,24},{24,16},{32,40},{40,32},{48,56},{56,48},{64,72... | collective-permute-start | bytes 7372808 | tf_op jit(solution)/shard_map/ppermute | solution.py:29
  512.8 245.6 %reduce-scatter.25.cloned.1.call-start = ((), (), s32[]{:S(2)}) async-start(), calls=%async_computation.11 | async-start | bytes 3276800 | tf_op jit(solution)/shard_map/reduce_scatter | solution.py:58
  551.5 30.5 %collective-permute-start.48 = (bf16[2,176,640]{2,1,0:T(8,128)(2,1)S(1)}, bf16[2,176,640]{2,1,0:T(8,128)(2,1)S(1)}, u32[]{:S(2)}, u32[]{:S(2)}) collective-permute-start(bf16[2,176,640]{2,1,0:T(8,128)(2,1)S(1)} %bitcast.348), channel_id=1, source_target_pairs={{0,3},{1,2},{2,1},{3,0},{4,7},{5,6},{6,5},{7,4},{8,11},{9,10},{10,... | collective-permute-start | bytes 1351688 | tf_op jit(solution)/shard_map/ppermute | solution.py:29
  553.0 29.0 %collective-permute-start.47 = (bf16[2,176,640]{2,1,0:T(8,128)(2,1)S(1)}, bf16[2,176,640]{2,1,0:T(8,128)(2,1)S(1)}, u32[]{:S(2)}, u32[]{:S(2)}) collective-permute-start(bf16[2,176,640]{2,1,0:T(8,128)(2,1)S(1)} %bitcast.347), channel_id=1, source_target_pairs={{0,2},{1,3},{2,0},{3,1},{4,6},{5,7},{6,4},{7,5},{8,10},{9,11},{10,... | collective-permute-start | bytes 1351688 | tf_op jit(solution)/shard_map/ppermute | solution.py:29
  556.5 26.1 %collective-permute-start.46 = (bf16[2,176,640]{2,1,0:T(8,128)(2,1)S(1)}, bf16[2,176,640]{2,1,0:T(8,128)(2,1)S(1)}, u32[]{:S(2)}, u32[]{:S(2)}) collective-permute-start(bf16[2,176,640]{2,1,0:T(8,128)(2,1)S(1)} %bitcast.346), channel_id=1, source_target_pairs={{0,1},{1,0},{2,3},{3,2},{4,5},{5,4},{6,7},{7,6},{8,9},{9,8},{10,11... | collective-permute-start | bytes 1351688 | tf_op jit(solution)/shard_map/ppermute | solution.py:29
  612.7 153.1 %reduce-scatter.15.cloned.1.call-start = ((), (), s32[]{:S(2)}) async-start(), calls=%async_computation.6 | async-start | bytes 3276800 | tf_op jit(solution)/shard_map/reduce_scatter | solution.py:58
  641.9 127.5 %reduce-scatter.21.cloned.1.call-start = ((), (), s32[]{:S(2)}) async-start(), calls=%async_computation.9 | async-start | bytes 3276800 | tf_op jit(solution)/shard_map/reduce_scatter | solution.py:58
  652.9 140.4 %reduce-scatter.23.cloned.1.call-start = ((), (), s32[]{:S(2)}) async-start(), calls=%async_computation.10 | async-start | bytes 6144000 | tf_op jit(solution)/shard_map/reduce_scatter | solution.py:58
  667.4 235.3 %reduce-scatter.17.cloned.1.call-start = ((), (), s32[]{:S(2)}) async-start(), calls=%async_computation.7 | async-start | bytes 3276800 | tf_op jit(solution)/shard_map/reduce_scatter | solution.py:58
  693.7 31.7 %collective-permute-start.54 = (bf16[2,176,640]{2,1,0:T(8,128)(2,1)S(1)}, bf16[2,176,640]{2,1,0:T(8,128)(2,1)S(1)}, u32[]{:S(2)}, u32[]{:S(2)}) collective-permute-start(bf16[2,176,640]{2,1,0:T(8,128)(2,1)S(1)} %bitcast.345), channel_id=1, source_target_pairs={{0,3},{1,2},{2,1},{3,0},{4,7},{5,6},{6,5},{7,4},{8,11},{9,10},{10,... | collective-permute-start | bytes 1351688 | tf_op jit(solution)/shard_map/ppermute | solution.py:29
  694.3 31.1 %collective-permute-start.53 = (bf16[2,176,640]{2,1,0:T(8,128)(2,1)S(1)}, bf16[2,176,640]{2,1,0:T(8,128)(2,1)S(1)}, u32[]{:S(2)}, u32[]{:S(2)}) collective-permute-start(bf16[2,176,640]{2,1,0:T(8,128)(2,1)S(1)} %bitcast.344), channel_id=1, source_target_pairs={{0,2},{1,3},{2,0},{3,1},{4,6},{5,7},{6,4},{7,5},{8,10},{9,11},{10,... | collective-permute-start | bytes 1351688 | tf_op jit(solution)/shard_map/ppermute | solution.py:29
  696.0 38.8 %collective-permute-start.52 = (bf16[2,176,640]{2,1,0:T(8,128)(2,1)S(1)}, bf16[2,176,640]{2,1,0:T(8,128)(2,1)S(1)}, u32[]{:S(2)}, u32[]{:S(2)}) collective-permute-start(bf16[2,176,640]{2,1,0:T(8,128)(2,1)S(1)} %bitcast.343), channel_id=1, source_target_pairs={{0,1},{1,0},{2,3},{3,2},{4,5},{5,4},{6,7},{7,6},{8,9},{9,8},{10,11... | collective-permute-start | bytes 1351688 | tf_op jit(solution)/shard_map/ppermute | solution.py:29
  777.5 31.6 %collective-permute-start.60 = (bf16[2,264,640]{2,1,0:T(8,128)(2,1)}, bf16[2,264,640]{2,1,0:T(8,128)(2,1)}, u32[]{:S(2)}, u32[]{:S(2)}) collective-permute-start(bf16[2,264,640]{2,1,0:T(8,128)(2,1)} %get-tuple-element.132), channel_id=1, source_target_pairs={{0,96},{8,104},{16,112},{24,120},{32,64},{40,72},{48,80},{56,88},{... | collective-permute-start | bytes 2027528 | tf_op jit(solution)/shard_map/ppermute | solution.py:29
  779.7 29.4 %collective-permute-start.59 = (bf16[2,264,640]{2,1,0:T(8,128)(2,1)}, bf16[2,264,640]{2,1,0:T(8,128)(2,1)}, u32[]{:S(2)}, u32[]{:S(2)}) collective-permute-start(bf16[2,264,640]{2,1,0:T(8,128)(2,1)} %get-tuple-element.133), channel_id=1, source_target_pairs={{0,64},{8,72},{16,80},{24,88},{32,96},{40,104},{48,112},{56,120},{... | collective-permute-start | bytes 2027528 | tf_op jit(solution)/shard_map/ppermute | solution.py:29
  780.2 29.4 %collective-permute-start.58 = (bf16[2,264,640]{2,1,0:T(8,128)(2,1)}, bf16[2,264,640]{2,1,0:T(8,128)(2,1)}, u32[]{:S(2)}, u32[]{:S(2)}) collective-permute-start(bf16[2,264,640]{2,1,0:T(8,128)(2,1)} %get-tuple-element.131), channel_id=1, source_target_pairs={{0,32},{8,40},{16,48},{24,56},{32,0},{40,8},{48,16},{56,24},{64,96... | collective-permute-start | bytes 2027528 | tf_op jit(solution)/shard_map/ppermute | solution.py:29
  801.2 31.4 %collective-permute-start.84 = (bf16[2,200,640]{2,1,0:T(8,128)(2,1)}, bf16[2,200,640]{2,1,0:T(8,128)(2,1)}, u32[]{:S(2)}, u32[]{:S(2)}) collective-permute-start(bf16[2,200,640]{2,1,0:T(8,128)(2,1)} %get-tuple-element.135), channel_id=1, source_target_pairs={{0,96},{8,104},{16,112},{24,120},{32,64},{40,72},{48,80},{56,88},{... | collective-permute-start | bytes 1536008 | tf_op jit(solution)/shard_map/ppermute | solution.py:29
  803.6 28.9 %collective-permute-start.83 = (bf16[2,200,640]{2,1,0:T(8,128)(2,1)}, bf16[2,200,640]{2,1,0:T(8,128)(2,1)}, u32[]{:S(2)}, u32[]{:S(2)}) collective-permute-start(bf16[2,200,640]{2,1,0:T(8,128)(2,1)} %get-tuple-element.136), channel_id=1, source_target_pairs={{0,64},{8,72},{16,80},{24,88},{32,96},{40,104},{48,112},{56,120},{... | collective-permute-start | bytes 1536008 | tf_op jit(solution)/shard_map/ppermute | solution.py:29
  809.1 27.6 %collective-permute-start.82 = (bf16[2,200,640]{2,1,0:T(8,128)(2,1)}, bf16[2,200,640]{2,1,0:T(8,128)(2,1)}, u32[]{:S(2)}, u32[]{:S(2)}) collective-permute-start(bf16[2,200,640]{2,1,0:T(8,128)(2,1)} %get-tuple-element.134), channel_id=1, source_target_pairs={{0,32},{8,40},{16,48},{24,56},{32,0},{40,8},{48,16},{56,24},{64,96... | collective-permute-start | bytes 1536008 | tf_op jit(solution)/shard_map/ppermute | solution.py:29
  838.4 24.3 %collective-permute-start.88 = (bf16[200,640]{1,0:T(8,128)(2,1)S(1)}, bf16[200,640]{1,0:T(8,128)(2,1)S(1)}, u32[]{:S(2)}, u32[]{:S(2)}) collective-permute-start(bf16[200,640]{1,0:T(8,128)(2,1)S(1)} %get-tuple-element.219), channel_id=1, source_target_pairs={{0,17},{1,19},{2,21},{3,23},{4,16},{5,18},{6,20},{7,22},{8,25},{9,... | collective-permute-start | bytes 768008 | tf_op jit(solution)/shard_map/ppermute | solution.py:75
  841.1 24.9 %collective-permute-start.86 = (bf16[200,640]{1,0:T(8,128)(2,1)S(1)}, bf16[200,640]{1,0:T(8,128)(2,1)S(1)}, u32[]{:S(2)}, u32[]{:S(2)}) collective-permute-start(bf16[200,640]{1,0:T(8,128)(2,1)S(1)} %get-tuple-element.219), channel_id=1, source_target_pairs={{0,1},{1,3},{2,5},{3,7},{4,0},{5,2},{6,4},{7,6},{8,9},{9,11},{10,1... | collective-permute-start | bytes 768008 | tf_op jit(solution)/shard_map/ppermute | solution.py:75
  842.9 20.7 %collective-permute-start.87 = (bf16[200,640]{1,0:T(8,128)(2,1)S(1)}, bf16[200,640]{1,0:T(8,128)(2,1)}, u32[]{:S(2)}, u32[]{:S(2)}) collective-permute-start(bf16[200,640]{1,0:T(8,128)(2,1)S(1)} %get-tuple-element.218), channel_id=1, source_target_pairs={{0,16},{1,18},{2,20},{3,22},{4,17},{5,19},{6,21},{7,23},{8,24},{9,... | collective-permute-start | bytes 768008 | tf_op jit(solution)/shard_map/ppermute | solution.py:75
  851.5 21.2 %collective-permute-start.78 = (bf16[264,640]{1,0:T(8,128)(2,1)S(1)}, bf16[264,640]{1,0:T(8,128)(2,1)S(1)}, u32[]{:S(2)}, u32[]{:S(2)}) collective-permute-start(bf16[264,640]{1,0:T(8,128)(2,1)S(1)} %add_convert_fusion.4), channel_id=1, source_target_pairs={{0,64},{8,72},{16,80},{24,88},{32,96},{40,104},{48,112},{56,120},{... | collective-permute-start | bytes 1013768 | tf_op jit(solution)/shard_map/ppermute | solution.py:29
  (194 other events, 1697.8 us)
Sparse Core Ops, SparseCore 0:
  512.9 68.7 reduce-scatter.18
  612.8 33.3 reduce-scatter.24
  648.7 33.6 reduce-scatter.14
  685.4 52.7 reduce-scatter.20
  740.6 52.6 reduce-scatter.22
  866.0 36.5 reduce-scatter.16

commit v7 on v5

--- a/solution.py
+++ b/solution.py
@@ -111,17 +111,13 @@
     return jnp.concatenate(parts, axis=1)
 
 
-def finish_sums(summed, quarter):
+def finish_sums(summed):
     joined = jnp.concatenate([as_rows(array) for array in summed], axis=1)
-    height = joined.shape[1] // 4
-    blocks = joined.reshape(2, 4, height, LAST)
+    blocks = joined.reshape(2, 4, joined.shape[1] // 4, LAST)
     total = sum_over_y(lambda k: lax.dynamic_index_in_dim(blocks, k, axis=1, keepdims=False))
-    if quarter is not None:
-        total = jnp.concatenate([total, quarter], axis=1)
-    own = spread_over_y(to_owners(total)[None], 0)
-
-    def take_apart(spread):
-        rows = spread[:, :height].reshape(4 * height, LAST)
+    own = spread_over_y(to_owners(total), 0)
+
+    def take_apart(rows):
         results, first = [], 0
         for array in summed:
             count, columns = array.shape[1:]
@@ -130,8 +126,6 @@
                 parts.append(rows[first : first + count, : min(LAST, columns - start)])
                 first += count
             results.append(jnp.concatenate(parts, axis=1))
-        if quarter is not None:
-            results.append(jnp.concatenate([spread[k, height:] for k in range(4)], axis=1))
         return results
 
     return take_apart(own), take_apart(swap_core(own))
@@ -485,13 +479,9 @@
         dmixed = matmul_nt(dmiddle_low, out_value[:, :width]).astype(bf16)
         dmixed = after(dmixed, (down_sum, gate_up_sum))
         dq, dkv = attend_back(queries, kv, key_place, bounds, mixed, logs, dmixed)
-        down_sum = sum_over_x(after(down_sum, latest))
+        gate_up_sum = sum_over_x(after(gate_up_sum, latest))
+        down_sum = sum_over_x(after(down_sum, gate_up_sum))
         dkv = after(scatter_pack(dkv), done)
-        columns = gate_up_sum.shape[1] // 4
-        gate_up_sum = sum_over_y(
-            lambda k: lax.dynamic_slice_in_dim(gate_up_sum, k * columns, columns, axis=1)
-        )
-        gate_up_sum = sum_over_x(after(gate_up_sum, down_sum))
         dq = rotary_back(dq, cosine, sine).astype(bf16)
         dk = rotary_back(dkv[:, :key_width], cosine, sine).astype(bf16)
         dv = dkv[:, key_width:].astype(bf16)
@@ -515,19 +505,19 @@
         gain_grads = gain_grads.reshape(2, -1, shard).swapaxes(0, 1)
         gain_grads = jnp.pad(gain_grads, ((0, 0), (0, 6), (0, att_width - shard)))
         att_sum = jnp.concatenate([att_sum.reshape(-1, shard, att_width), gain_grads], axis=1)
-        att_sum = sum_over_x(after(att_sum.reshape(-1, att_width), gate_up_sum))
+        att_sum = sum_over_x(after(att_sum.reshape(-1, att_width), down_sum))
         latest = att_sum
 
         att_pair = att_sum.reshape(2, shard + 8, att_width)
         down_pair = down_sum.reshape(2, -1, half_width)
-        gate_up_pair = gate_up_sum.reshape(2, shard, columns)
+        gate_up_pair = gate_up_sum.reshape(2, shard, -1)
         if l > 0:
-            done = finish_sums([att_pair, down_pair], gate_up_pair)
+            done = finish_sums([att_pair, down_pair, gate_up_pair])
             (att_own, down_own, gate_up_own), (att_other, down_other, gate_up_other) = done
         else:
-            mlp = finish_sums([down_pair], gate_up_pair)
+            mlp = finish_sums([down_pair, gate_up_pair])
             (down_own, gate_up_own), (down_other, gate_up_other) = mlp
-            (att_own,), (att_other,) = finish_sums([att_pair], None)
+            (att_own,), (att_other,) = finish_sums([att_pair])
         att_a, att_b = pick(att_own, att_other), pick(att_other, att_own)
         results[l] = (
             att_own[shard, :shard],

time: 830 us -> 837 us (level)
  starting transfers between devices: 154 us -> 141 us
    reduce_scatter x6, waiting for transfers between devices: 3.88 us -> 34.6 us  [sum_over_x(): lax.psum_scatter(rows, 'fsdp', scatter_dimension=0, tiled=True, axis_inde...]
    ppermute x87 -> x81, waiting for transfers between devices: 317 us -> 288 us  [swap(): return lax.ppermute(array, axis, [(i, i ^ mask) for i in range(count)])]
    unnamed x311 -> x357, local copies, waits for them, and re-layouts: 34.9 us -> 47 us
    ppermute x87 -> x81, starting transfers between devices: 124 us -> 115 us  [swap(): return lax.ppermute(array, axis, [(i, i ^ mask) for i in range(count)])]
    dot_general x16, matrix products: 40.1 us -> 48.8 us  [cross_rows(): lax.dot_general(left, right, (((0,), (0,)), ((), ())), preferred_element_...]
  transfers between devices with their start and end apart: 105 -> 99, of which waited for: 52 -> 51; matrix products, arithmetic and copies ran while one was open for 26% -> 28% of each run, Pallas kernels for 4% -> 6%
where the time goes in v7:
time: 837 us; the launch traced here: 823 us
  waiting for transfers between devices  332 us (40%)
  starting transfers between devices  141 us (17%)
  matrix products  111 us (13%)
  local copies, waits for them, and re-layouts  87.9 us (11%)
  other arithmetic  77.7 us (9%)
  Pallas kernels  55.4 us (7%)
  between operations  17.2 us (2%)
    ppermute x81, waiting for transfers between devices, swap(): return lax.ppermute(array, axis, [(i, i ^ mask) for i in range(count)])  288 us
    ppermute x81, starting transfers between devices, swap(): return lax.ppermute(array, axis, [(i, i ^ mask) for i in range(count)])  115 us
    dot_general x16, matrix products, cross_rows(): lax.dot_general(left, right, (((0,), (0,)), ((), ())), preferred_element_...  48.8 us
    unnamed x357, local copies, waits for them, and re-layouts  47 us
    reduce_scatter x6, waiting for transfers between devices, sum_over_x(): lax.psum_scatter(rows, 'fsdp', scatter_dimension=0, tiled=True, axis_inde...  34.6 us
    dot_general x14, matrix products, matmul_nt(): return lax.dot_general(left, right, NT, preferred_element_type=f32)  34 us
    dot_general x14, matrix products, matmul(): return jnp.dot(left, right, preferred_element_type=f32)  28.5 us
    pallas_call x2, Pallas kernels, attend_back(): pl.pallas_call(attention_backward_kernel, out_shape=(jax.ShapeDtypeStruct...  27.9 us
  transfers between devices with their start and end apart: 99, of which 51 were waited for; matrix products, arithmetic and copies ran while one was open for 28% of the time, Pallas kernels for 6%

profile of v7, /device:TPU:5, one launch (start us, length us, event | category | flops | bytes accessed | tf_op | source)
XLA Modules:
  0.0 823.0 jit_solution(16818031097784744835)
XLA Ops:
  32.7 11.2 %collective-permute-done.1.refs_1_ = bf16[2,128,1280]{2,1,0:T(8,128)(2,1)S(1)} collective-permute-done((bf16[2,128,1280]{2,1,0:T(8,128)(2,1)S(1)}, bf16[2,128,1280]{2,1,0:T(8,128)(2,1)S(1)}, u32[]{:S(2)}, u32[]{:S(2)}) %collective-permute-start.1) | collective-permute-done | bytes 655392 | tf_op jit(solution)/shard_map/ppermute | solution.py:29
  43.9 14.1 %collective-permute-done.2.refs_2_ = bf16[2,128,1280]{2,1,0:T(8,128)(2,1)S(1)} collective-permute-done((bf16[2,128,1280]{2,1,0:T(8,128)(2,1)S(1)}, bf16[2,128,1280]{2,1,0:T(8,128)(2,1)S(1)}, u32[]{:S(2)}, u32[]{:S(2)}) %collective-permute-start.2) | collective-permute-done | bytes 655392 | tf_op jit(solution)/shard_map/ppermute | solution.py:29
  77.1 4.5 collective-permute-done.6
  82.4 7.5 collective-permute-done.7
  119.3 8.0 collective-permute-done.11
  127.4 11.9 %collective-permute-done.12 = bf16[2,176,640]{2,1,0:T(8,128)(2,1)S(1)} collective-permute-done((bf16[2,176,640]{2,1,0:T(8,128)(2,1)S(1)}, bf16[2,176,640]{2,1,0:T(8,128)(2,1)S(1)}, u32[]{:S(2)}, u32[]{:S(2)}) %collective-permute-start.12) | collective-permute-done | bytes 450592 | tf_op jit(solution)/shard_map/ppermute | solution.py:29
  143.6 7.6 attention_forward.2
  152.0 5.1 collective-permute-done.14.refs_2_
  157.1 10.2 %collective-permute-done.15.refs_3_ = bf16[8,120,640]{2,1,0:T(8,128)(2,1)S(1)} collective-permute-done((bf16[8,120,640]{2,1,0:T(8,128)(2,1)S(1)}, bf16[8,120,640]{2,1,0:T(8,128)(2,1)S(1)}, u32[]{:S(2)}, u32[]{:S(2)}) %collective-permute-start.15) | collective-permute-done | bytes 1228832 | tf_op jit(solution)/shard_map/ppermute | solution.py:29
  188.5 7.1 collective-permute-done.22
  203.9 6.1 multiply_convert_fusion.5
  214.5 12.9 %collective-permute-done.24.refs_2_ = bf16[2,128,1280]{2,1,0:T(8,128)(2,1)S(1)} collective-permute-done((bf16[2,128,1280]{2,1,0:T(8,128)(2,1)S(1)}, bf16[2,128,1280]{2,1,0:T(8,128)(2,1)S(1)}, u32[]{:S(2)}, u32[]{:S(2)}) %collective-permute-start.24) | collective-permute-done | bytes 655392 | tf_op jit(solution)/shard_map/ppermute | solution.py:29
  236.4 6.1 collective-permute-done.27
  247.7 4.9 collective-permute-done.28
  253.3 5.0 collective-permute-done.29
  278.5 4.9 collective-permute-done.38
  290.7 8.1 collective-permute-done.33
  298.9 12.8 %collective-permute-done.34 = bf16[2,176,640]{2,1,0:T(8,128)(2,1)S(1)} collective-permute-done((bf16[2,176,640]{2,1,0:T(8,128)(2,1)S(1)}, bf16[2,176,640]{2,1,0:T(8,128)(2,1)S(1)}, u32[]{:S(2)}, u32[]{:S(2)}) %collective-permute-start.34) | collective-permute-done | bytes 450592 | tf_op jit(solution)/shard_map/ppermute | solution.py:29
  316.0 7.6 attention_forward.3
  327.4 11.7 %collective-permute-done.37.refs_3_ = bf16[8,120,640]{2,1,0:T(8,128)(2,1)S(1)} collective-permute-done((bf16[8,120,640]{2,1,0:T(8,128)(2,1)}, bf16[8,120,640]{2,1,0:T(8,128)(2,1)S(1)}, u32[]{:S(2)}, u32[]{:S(2)}) %collective-permute-start.37) | collective-permute-done | bytes 1228832 | tf_op jit(solution)/shard_map/ppermute | solution.py:29
  351.5 4.5 copy.153
  379.9 4.2 collective-permute-done.45
  384.2 6.1 add_convert_fusion.1
  390.7 4.5 fusion.82
  395.3 4.9 multiply_reduce_fusion.3
  406.2 4.3 add_convert_fusion.3
  410.5 13.9 %attention_backward.2 = (f32[176,960]{1,0:T(8,128)S(1)}, bf16[1408,640]{1,0:T(8,128)(2,1)S(1)}) custom-call(bf16[176,960]{1,0:T(8,128)(2,1)S(1)} %copy-done.19, bf16[1408,640]{1,0:T(8,128)(2,1)S(1)} %bitcast.255, s32[1408,1]{1,0:T(8,128)S(1)} %copy-done.8, s32[8,528]{1,0:T(8,128)S(1)} %pad.26.bounds_ref, bf16[176,960]{1,0:T(8,128)(2,1)S(1)} %get-tuple-element.80.mixed_ref, ...), custom_call_target="tpu_custom_call" | custom-call | flops 2378956800 | bytes 6291456 | tf_op jit(solution)/shard_map/attention_backward/pallas_call | solution.py:290
  425.3 4.5 collective-permute-start.47
  431.4 25.0 %collective-permute-done.48 = bf16[2,176,640]{2,1,0:T(8,128)(2,1)S(1)} collective-permute-done((bf16[2,176,640]{2,1,0:T(8,128)(2,1)S(1)}, bf16[2,176,640]{2,1,0:T(8,128)(2,1)S(1)}, u32[]{:S(2)}, u32[]{:S(2)}) %collective-permute-start.48) | collective-permute-done | bytes 450592 | tf_op jit(solution)/shard_map/ppermute | solution.py:29
  486.3 4.2 fusion.2
  507.9 5.4 collective-permute-done.51
  513.3 6.1 add_convert_fusion
  519.4 6.5 reduce-scatter.13.cloned.1.call-done
  533.3 4.3 multiply_reduce_fusion
  540.2 22.0 %reduce-scatter.19.cloned.1.call-done = bf16[640,480]{1,0:T(8,128)(2,1)} async-done(((bf16[2560,480]{1,0:T(8,128)(2,1)}), bf16[640,480]{1,0:T(8,128)(2,1)}) %reduce-scatter.19.cloned.1.call-update) | async-done | bytes 614416 | tf_op jit(solution)/shard_map/reduce_scatter | solution.py:58
  577.2 4.1 add_convert_fusion.2
  581.3 23.6 %collective-permute-done.60 = bf16[2,264,640]{2,1,0:T(8,128)(2,1)S(1)} collective-permute-done((bf16[2,264,640]{2,1,0:T(8,128)(2,1)S(1)}, bf16[2,264,640]{2,1,0:T(8,128)(2,1)S(1)}, u32[]{:S(2)}, u32[]{:S(2)}) %collective-permute-start.60) | collective-permute-done | bytes 675872 | tf_op jit(solution)/shard_map/ppermute | solution.py:29
  615.8 14.0 %attention_backward.3 = (f32[176,960]{1,0:T(8,128)S(1)}, bf16[1408,640]{1,0:T(8,128)(2,1)S(1)}) custom-call(bf16[176,960]{1,0:T(8,128)(2,1)S(1)} %copy-done.17, bf16[1408,640]{1,0:T(8,128)(2,1)S(1)} %bitcast.253, s32[1408,1]{1,0:T(8,128)S(1)} %copy-done.9, s32[8,528]{1,0:T(8,128)S(1)} %pad.26.bounds_ref, bf16[176,960]{1,0:T(8,128)(2,1)S(1)} %copy-done.5, ...), custom_call_target="tpu_custom_call" | custom-call | flops 2378956800 | bytes 6291456 | tf_op jit(solution)/shard_map/attention_backward/pallas_call | solution.py:290
  637.7 13.1 %collective-permute-done.65 = bf16[264,640]{1,0:T(8,128)(2,1)S(1)} collective-permute-done((bf16[264,640]{1,0:T(8,128)(2,1)S(1)}, bf16[264,640]{1,0:T(8,128)(2,1)S(1)}, u32[]{:S(2)}, u32[]{:S(2)}) %collective-permute-start.65) | collective-permute-done | bytes 337952 | tf_op jit(solution)/shard_map/ppermute | solution.py:29
  654.3 6.2 collective-permute-done.52
  668.6 4.5 copy.177
  678.9 4.1 collective-permute-start.69
  693.6 4.3 fusion.3
  703.6 6.0 reduce-scatter.21.cloned.1.call-done
  717.5 20.5 %collective-permute-done.84 = bf16[2,200,640]{2,1,0:T(8,128)(2,1)S(1)} collective-permute-done((bf16[2,200,640]{2,1,0:T(8,128)(2,1)S(1)}, bf16[2,200,640]{2,1,0:T(8,128)(2,1)S(1)}, u32[]{:S(2)}, u32[]{:S(2)}) %collective-permute-start.84) | collective-permute-done | bytes 512032 | tf_op jit(solution)/shard_map/ppermute | solution.py:29
  751.7 6.2 collective-permute-done.86
  766.8 5.6 collective-permute-done.89
  793.6 4.2 collective-permute-start.74
  (760 shorter events, 401.6 us)
Async XLA Ops:
  7.2 498.0 %reduce-scatter.11.cloned.1.call-start = ((), (), s32[]{:S(2)}) async-start(), calls=%async_computation.6 | async-start | bytes 6144000 | tf_op jit(solution)/shard_map/reduce_scatter | solution.py:58
  23.1 47.6 %collective-permute-start.5 = (bf16[120,640]{1,0:T(8,128)(2,1)}, bf16[120,640]{1,0:T(8,128)(2,1)S(1)}, u32[]{:S(2)}, u32[]{:S(2)}) collective-permute-start(bf16[120,640]{1,0:T(8,128)(2,1)} %bitcast.14), channel_id=1, source_target_pairs={{0,4},{1,5},{2,6},{3,7},{4,0},{5,1},{6,2},{7,3},{8,12},{9,13},{10,... | collective-permute-start | bytes 460808 | tf_op jit(solution)/shard_map/ppermute | solution.py:29
  25.0 85.1 %collective-permute-start.16 = (bf16[320,480]{1,0:T(8,128)(2,1)}, bf16[320,480]{1,0:T(8,128)(2,1)}, u32[]{:S(2)}, u32[]{:S(2)}) collective-permute-start(bf16[320,480]{1,0:T(8,128)(2,1)} %slice_select_fusion.1), channel_id=1, source_target_pairs={{0,4},{1,5},{2,6},{3,7},{4,0},{5,1},{6,2},{7,3},{8,12},{9,13},{10,... | collective-permute-start | bytes 921608 | tf_op jit(solution)/shard_map/ppermute | solution.py:29
  30.1 27.9 %collective-permute-start.2 = (bf16[2,128,1280]{2,1,0:T(8,128)(2,1)S(1)}, bf16[2,128,1280]{2,1,0:T(8,128)(2,1)S(1)}, u32[]{:S(2)}, u32[]{:S(2)}) collective-permute-start(bf16[2,128,1280]{2,1,0:T(8,128)(2,1)S(1)} %pad_maximum_fusion.4.refs_0_), channel_id=1, source_target_pairs={{0,2},{1,3},{2,0},{3,1},{4,6},{5,7},{6,4},{7,5},{8,10},{9,11},{10,... | collective-permute-start | bytes 1966088 | tf_op jit(solution)/shard_map/ppermute | solution.py:29
  30.7 27.3 %collective-permute-start.3 = (bf16[2,128,1280]{2,1,0:T(8,128)(2,1)S(1)}, bf16[2,128,1280]{2,1,0:T(8,128)(2,1)S(1)}, u32[]{:S(2)}, u32[]{:S(2)}) collective-permute-start(bf16[2,128,1280]{2,1,0:T(8,128)(2,1)S(1)} %pad_maximum_fusion.4.refs_0_), channel_id=1, source_target_pairs={{0,3},{1,2},{2,1},{3,0},{4,7},{5,6},{6,5},{7,4},{8,11},{9,10},{10,... | collective-permute-start | bytes 1966088 | tf_op jit(solution)/shard_map/ppermute | solution.py:29
  58.9 33.9 %collective-permute-start.4 = (bf16[8,128,1280]{2,1,0:T(8,128)(2,1)S(1)}, bf16[8,128,1280]{2,1,0:T(8,128)(2,1)}, u32[]{:S(2)}, u32[]{:S(2)}) collective-permute-start(bf16[8,128,1280]{2,1,0:T(8,128)(2,1)S(1)} %assemble.6), channel_id=1, source_target_pairs={{0,8},{8,0},{16,24},{24,16},{32,40},{40,32},{48,56},{56,48},{64,72... | collective-permute-start | bytes 7864328 | tf_op jit(solution)/shard_map/ppermute | solution.py:29
  101.1 39.1 %collective-permute-start.13 = (bf16[8,120,640]{2,1,0:T(8,128)(2,1)S(1)}, bf16[8,120,640]{2,1,0:T(8,128)(2,1)S(1)}, u32[]{:S(2)}, u32[]{:S(2)}) collective-permute-start(bf16[8,120,640]{2,1,0:T(8,128)(2,1)S(1)} %copy-done.3), channel_id=1, source_target_pairs={{0,32},{8,40},{16,48},{24,56},{32,0},{40,8},{48,16},{56,24},{64,96... | collective-permute-start | bytes 3686408 | tf_op jit(solution)/shard_map/ppermute | solution.py:29
  111.2 45.9 %collective-permute-start.14 = (bf16[8,120,640]{2,1,0:T(8,128)(2,1)S(1)}, bf16[8,120,640]{2,1,0:T(8,128)(2,1)S(1)}, u32[]{:S(2)}, u32[]{:S(2)}) collective-permute-start(bf16[8,120,640]{2,1,0:T(8,128)(2,1)S(1)} %copy-done.3), channel_id=1, source_target_pairs={{0,64},{8,72},{16,80},{24,88},{32,96},{40,104},{48,112},{56,120},{... | collective-permute-start | bytes 3686408 | tf_op jit(solution)/shard_map/ppermute | solution.py:29
  114.2 53.1 %collective-permute-start.15 = (bf16[8,120,640]{2,1,0:T(8,128)(2,1)S(1)}, bf16[8,120,640]{2,1,0:T(8,128)(2,1)S(1)}, u32[]{:S(2)}, u32[]{:S(2)}) collective-permute-start(bf16[8,120,640]{2,1,0:T(8,128)(2,1)S(1)} %copy-done.3), channel_id=1, source_target_pairs={{0,96},{8,104},{16,112},{24,120},{32,64},{40,72},{48,80},{56,88},{... | collective-permute-start | bytes 3686408 | tf_op jit(solution)/shard_map/ppermute | solution.py:29
  118.3 20.9 %collective-permute-start.12 = (bf16[2,176,640]{2,1,0:T(8,128)(2,1)S(1)}, bf16[2,176,640]{2,1,0:T(8,128)(2,1)S(1)}, u32[]{:S(2)}, u32[]{:S(2)}) collective-permute-start(bf16[2,176,640]{2,1,0:T(8,128)(2,1)S(1)} %pad_maximum_fusion.13), channel_id=1, source_target_pairs={{0,3},{1,2},{2,1},{3,0},{4,7},{5,6},{6,5},{7,4},{8,11},{9,10},{10,... | collective-permute-start | bytes 1351688 | tf_op jit(solution)/shard_map/ppermute | solution.py:29
  139.3 28.0 %collective-permute-start.17 = (bf16[2,320,480]{2,1,0:T(8,128)(2,1)S(1)}, bf16[2,320,480]{2,1,0:T(8,128)(2,1)S(1)}, u32[]{:S(2)}, u32[]{:S(2)}) collective-permute-start(bf16[2,320,480]{2,1,0:T(8,128)(2,1)S(1)} %pad_maximum_fusion.5.refs_0_), channel_id=1, source_target_pairs={{0,1},{1,0},{2,3},{3,2},{4,5},{5,4},{6,7},{7,6},{8,9},{9,8},{10,11... | collective-permute-start | bytes 1843208 | tf_op jit(solution)/shard_map/ppermute | solution.py:29
  140.2 27.1 %collective-permute-start.18 = (bf16[2,320,480]{2,1,0:T(8,128)(2,1)S(1)}, bf16[2,320,480]{2,1,0:T(8,128)(2,1)S(1)}, u32[]{:S(2)}, u32[]{:S(2)}) collective-permute-start(bf16[2,320,480]{2,1,0:T(8,128)(2,1)S(1)} %pad_maximum_fusion.5.refs_0_), channel_id=1, source_target_pairs={{0,2},{1,3},{2,0},{3,1},{4,6},{5,7},{6,4},{7,5},{8,10},{9,11},{10,... | collective-permute-start | bytes 1843208 | tf_op jit(solution)/shard_map/ppermute | solution.py:29
  140.2 29.3 %collective-permute-start.19 = (bf16[2,320,480]{2,1,0:T(8,128)(2,1)S(1)}, bf16[2,320,480]{2,1,0:T(8,128)(2,1)S(1)}, u32[]{:S(2)}, u32[]{:S(2)}) collective-permute-start(bf16[2,320,480]{2,1,0:T(8,128)(2,1)S(1)} %pad_maximum_fusion.5.refs_0_), channel_id=1, source_target_pairs={{0,3},{1,2},{2,1},{3,0},{4,7},{5,6},{6,5},{7,4},{8,11},{9,10},{10,... | collective-permute-start | bytes 1843208 | tf_op jit(solution)/shard_map/ppermute | solution.py:29
  172.7 31.2 %collective-permute-start.20 = (bf16[960,2560]{1,0:T(8,128)(2,1)}, bf16[960,2560]{1,0:T(8,128)(2,1)}, u32[]{:S(2)}, u32[]{:S(2)}) collective-permute-start(bf16[960,2560]{1,0:T(8,128)(2,1)} %bitcast.256), channel_id=1, source_target_pairs={{0,8},{8,0},{16,24},{24,16},{32,40},{40,32},{48,56},{56,48},{64,72... | collective-permute-start | bytes 14745608 | tf_op jit(solution)/shard_map/ppermute | solution.py:29
  183.2 27.3 %collective-permute-start.21 = (bf16[2560,480]{0,1:T(8,128)(2,1)}, bf16[2560,480]{0,1:T(8,128)(2,1)}, u32[]{:S(2)}, u32[]{:S(2)}) collective-permute-start(bf16[2560,480]{0,1:T(8,128)(2,1)} %copy.147), channel_id=1, source_target_pairs={{0,8},{8,0},{16,24},{24,16},{32,40},{40,32},{48,56},{56,48},{64,72... | collective-permute-start | bytes 7372808 | tf_op jit(solution)/shard_map/ppermute | solution.py:29
  195.7 18.8 %collective-permute-start.23 = (bf16[2,128,1280]{2,1,0:T(8,128)(2,1)S(1)}, bf16[2,128,1280]{2,1,0:T(8,128)(2,1)S(1)}, u32[]{:S(2)}, u32[]{:S(2)}) collective-permute-start(bf16[2,128,1280]{2,1,0:T(8,128)(2,1)S(1)} %pad_maximum_fusion.6.refs_0_), channel_id=1, source_target_pairs={{0,1},{1,0},{2,3},{3,2},{4,5},{5,4},{6,7},{7,6},{8,9},{9,8},{10,11... | collective-permute-start | bytes 1966088 | tf_op jit(solution)/shard_map/ppermute | solution.py:29
  197.8 29.6 %collective-permute-start.24 = (bf16[2,128,1280]{2,1,0:T(8,128)(2,1)S(1)}, bf16[2,128,1280]{2,1,0:T(8,128)(2,1)S(1)}, u32[]{:S(2)}, u32[]{:S(2)}) collective-permute-start(bf16[2,128,1280]{2,1,0:T(8,128)(2,1)S(1)} %pad_maximum_fusion.6.refs_0_), channel_id=1, source_target_pairs={{0,2},{1,3},{2,0},{3,1},{4,6},{5,7},{6,4},{7,5},{8,10},{9,11},{10,... | collective-permute-start | bytes 1966088 | tf_op jit(solution)/shard_map/ppermute | solution.py:29
  200.1 27.3 %collective-permute-start.25 = (bf16[2,128,1280]{2,1,0:T(8,128)(2,1)S(1)}, bf16[2,128,1280]{2,1,0:T(8,128)(2,1)S(1)}, u32[]{:S(2)}, u32[]{:S(2)}) collective-permute-start(bf16[2,128,1280]{2,1,0:T(8,128)(2,1)S(1)} %pad_maximum_fusion.6.refs_0_), channel_id=1, source_target_pairs={{0,3},{1,2},{2,1},{3,0},{4,7},{5,6},{6,5},{7,4},{8,11},{9,10},{10,... | collective-permute-start | bytes 1966088 | tf_op jit(solution)/shard_map/ppermute | solution.py:29
  229.8 33.7 %collective-permute-start.26 = (bf16[8,128,1280]{2,1,0:T(8,128)(2,1)}, bf16[8,128,1280]{2,1,0:T(8,128)(2,1)}, u32[]{:S(2)}, u32[]{:S(2)}) collective-permute-start(bf16[8,128,1280]{2,1,0:T(8,128)(2,1)} %assemble.9), channel_id=1, source_target_pairs={{0,8},{8,0},{16,24},{24,16},{32,40},{40,32},{48,56},{56,48},{64,72... | collective-permute-start | bytes 7864328 | tf_op jit(solution)/shard_map/ppermute | solution.py:29
  272.9 41.0 %collective-permute-start.35 = (bf16[8,120,640]{2,1,0:T(8,128)(2,1)}, bf16[8,120,640]{2,1,0:T(8,128)(2,1)S(1)}, u32[]{:S(2)}, u32[]{:S(2)}) collective-permute-start(bf16[8,120,640]{2,1,0:T(8,128)(2,1)} %constant_dynamic-update-slice_fusion.10.refs_0_), channel_id=1, source_target_pairs={{0,32},{8,40},{16,48},{24,56},{32,0},{40,8},{48,16},{56,24},{64,96... | collective-permute-start | bytes 3686408 | tf_op jit(solution)/shard_map/ppermute | solution.py:29
  283.5 44.0 %collective-permute-start.36 = (bf16[8,120,640]{2,1,0:T(8,128)(2,1)}, bf16[8,120,640]{2,1,0:T(8,128)(2,1)S(1)}, u32[]{:S(2)}, u32[]{:S(2)}) collective-permute-start(bf16[8,120,640]{2,1,0:T(8,128)(2,1)} %constant_dynamic-update-slice_fusion.10.refs_0_), channel_id=1, source_target_pairs={{0,64},{8,72},{16,80},{24,88},{32,96},{40,104},{48,112},{56,120},{... | collective-permute-start | bytes 3686408 | tf_op jit(solution)/shard_map/ppermute | solution.py:29
  286.1 53.1 %collective-permute-start.37 = (bf16[8,120,640]{2,1,0:T(8,128)(2,1)}, bf16[8,120,640]{2,1,0:T(8,128)(2,1)S(1)}, u32[]{:S(2)}, u32[]{:S(2)}) collective-permute-start(bf16[8,120,640]{2,1,0:T(8,128)(2,1)} %constant_dynamic-update-slice_fusion.10.refs_0_), channel_id=1, source_target_pairs={{0,96},{8,104},{16,112},{24,120},{32,64},{40,72},{48,80},{56,88},{... | collective-permute-start | bytes 3686408 | tf_op jit(solution)/shard_map/ppermute | solution.py:29
  290.5 21.1 %collective-permute-start.34 = (bf16[2,176,640]{2,1,0:T(8,128)(2,1)S(1)}, bf16[2,176,640]{2,1,0:T(8,128)(2,1)S(1)}, u32[]{:S(2)}, u32[]{:S(2)}) collective-permute-start(bf16[2,176,640]{2,1,0:T(8,128)(2,1)S(1)} %pad_maximum_fusion.14), channel_id=1, source_target_pairs={{0,3},{1,2},{2,1},{3,0},{4,7},{5,6},{6,5},{7,4},{8,11},{9,10},{10,... | collective-permute-start | bytes 1351688 | tf_op jit(solution)/shard_map/ppermute | solution.py:29
  311.7 27.5 %collective-permute-start.39 = (bf16[2,320,480]{2,1,0:T(8,128)(2,1)S(1)}, bf16[2,320,480]{2,1,0:T(8,128)(2,1)S(1)}, u32[]{:S(2)}, u32[]{:S(2)}) collective-permute-start(bf16[2,320,480]{2,1,0:T(8,128)(2,1)S(1)} %pad_maximum_fusion.7.refs_0_), channel_id=1, source_target_pairs={{0,1},{1,0},{2,3},{3,2},{4,5},{5,4},{6,7},{7,6},{8,9},{9,8},{10,11... | collective-permute-start | bytes 1843208 | tf_op jit(solution)/shard_map/ppermute | solution.py:29
  311.8 30.5 %collective-permute-start.40 = (bf16[2,320,480]{2,1,0:T(8,128)(2,1)S(1)}, bf16[2,320,480]{2,1,0:T(8,128)(2,1)S(1)}, u32[]{:S(2)}, u32[]{:S(2)}) collective-permute-start(bf16[2,320,480]{2,1,0:T(8,128)(2,1)S(1)} %pad_maximum_fusion.7.refs_0_), channel_id=1, source_target_pairs={{0,2},{1,3},{2,0},{3,1},{4,6},{5,7},{6,4},{7,5},{8,10},{9,11},{10,... | collective-permute-start | bytes 1843208 | tf_op jit(solution)/shard_map/ppermute | solution.py:29
  313.8 29.5 %collective-permute-start.41 = (bf16[2,320,480]{2,1,0:T(8,128)(2,1)S(1)}, bf16[2,320,480]{2,1,0:T(8,128)(2,1)S(1)}, u32[]{:S(2)}, u32[]{:S(2)}) collective-permute-start(bf16[2,320,480]{2,1,0:T(8,128)(2,1)S(1)} %pad_maximum_fusion.7.refs_0_), channel_id=1, source_target_pairs={{0,3},{1,2},{2,1},{3,0},{4,7},{5,6},{6,5},{7,4},{8,11},{9,10},{10,... | collective-permute-start | bytes 1843208 | tf_op jit(solution)/shard_map/ppermute | solution.py:29
  379.9 26.3 %collective-permute-start.44 = (bf16[2560,480]{0,1:T(8,128)(2,1)}, bf16[2560,480]{0,1:T(8,128)(2,1)}, u32[]{:S(2)}, u32[]{:S(2)}) collective-permute-start(bf16[2560,480]{0,1:T(8,128)(2,1)} %convolution_convert_fusion.3), channel_id=1, source_target_pairs={{0,8},{8,0},{16,24},{24,16},{32,40},{40,32},{48,56},{56,48},{64,72... | collective-permute-start | bytes 7372808 | tf_op jit(solution)/shard_map/ppermute | solution.py:29
  390.3 135.7 %reduce-scatter.13.cloned.1.call-start = ((), (), s32[]{:S(2)}) async-start(), calls=%async_computation.7 | async-start | bytes 3276800 | tf_op jit(solution)/shard_map/reduce_scatter | solution.py:58
  424.6 31.8 %collective-permute-start.48 = (bf16[2,176,640]{2,1,0:T(8,128)(2,1)S(1)}, bf16[2,176,640]{2,1,0:T(8,128)(2,1)S(1)}, u32[]{:S(2)}, u32[]{:S(2)}) collective-permute-start(bf16[2,176,640]{2,1,0:T(8,128)(2,1)S(1)} %bitcast.313), channel_id=1, source_target_pairs={{0,3},{1,2},{2,1},{3,0},{4,7},{5,6},{6,5},{7,4},{8,11},{9,10},{10,... | collective-permute-start | bytes 1351688 | tf_op jit(solution)/shard_map/ppermute | solution.py:29
  425.3 31.2 %collective-permute-start.47 = (bf16[2,176,640]{2,1,0:T(8,128)(2,1)S(1)}, bf16[2,176,640]{2,1,0:T(8,128)(2,1)S(1)}, u32[]{:S(2)}, u32[]{:S(2)}) collective-permute-start(bf16[2,176,640]{2,1,0:T(8,128)(2,1)S(1)} %bitcast.312), channel_id=1, source_target_pairs={{0,2},{1,3},{2,0},{3,1},{4,6},{5,7},{6,4},{7,5},{8,10},{9,11},{10,... | collective-permute-start | bytes 1351688 | tf_op jit(solution)/shard_map/ppermute | solution.py:29
  429.8 30.1 %collective-permute-start.46 = (bf16[2,176,640]{2,1,0:T(8,128)(2,1)S(1)}, bf16[2,176,640]{2,1,0:T(8,128)(2,1)S(1)}, u32[]{:S(2)}, u32[]{:S(2)}) collective-permute-start(bf16[2,176,640]{2,1,0:T(8,128)(2,1)S(1)} %bitcast.311), channel_id=1, source_target_pairs={{0,1},{1,0},{2,3},{3,2},{4,5},{5,4},{6,7},{7,6},{8,9},{9,8},{10,11... | collective-permute-start | bytes 1351688 | tf_op jit(solution)/shard_map/ppermute | solution.py:29
  492.3 69.9 %reduce-scatter.19.cloned.1.call-start = ((), (), s32[]{:S(2)}) async-start(), calls=%async_computation.10 | async-start | bytes 3276800 | tf_op jit(solution)/shard_map/reduce_scatter | solution.py:58
  507.8 160.8 %reduce-scatter.15.cloned.1.call-start = ((), (), s32[]{:S(2)}) async-start(), calls=%async_computation.8 | async-start | bytes 6144000 | tf_op jit(solution)/shard_map/reduce_scatter | solution.py:58
  526.0 183.6 %reduce-scatter.21.cloned.1.call-start = ((), (), s32[]{:S(2)}) async-start(), calls=%async_computation.11 | async-start | bytes 3276800 | tf_op jit(solution)/shard_map/reduce_scatter | solution.py:58
  528.5 48.6 %collective-permute-start.50 = (bf16[2560,480]{0,1:T(8,128)(2,1)}, bf16[2560,480]{0,1:T(8,128)(2,1)}, u32[]{:S(2)}, u32[]{:S(2)}) collective-permute-start(bf16[2560,480]{0,1:T(8,128)(2,1)} %convolution_convert_fusion.2), channel_id=1, source_target_pairs={{0,8},{8,0},{16,24},{24,16},{32,40},{40,32},{48,56},{56,48},{64,72... | collective-permute-start | bytes 7372808 | tf_op jit(solution)/shard_map/ppermute | solution.py:29
  573.1 31.9 %collective-permute-start.60 = (bf16[2,264,640]{2,1,0:T(8,128)(2,1)S(1)}, bf16[2,264,640]{2,1,0:T(8,128)(2,1)S(1)}, u32[]{:S(2)}, u32[]{:S(2)}) collective-permute-start(bf16[2,264,640]{2,1,0:T(8,128)(2,1)S(1)} %get-tuple-element.195), channel_id=1, source_target_pairs={{0,96},{8,104},{16,112},{24,120},{32,64},{40,72},{48,80},{56,88},{... | collective-permute-start | bytes 2027528 | tf_op jit(solution)/shard_map/ppermute | solution.py:29
  575.6 29.3 %collective-permute-start.59 = (bf16[2,264,640]{2,1,0:T(8,128)(2,1)S(1)}, bf16[2,264,640]{2,1,0:T(8,128)(2,1)S(1)}, u32[]{:S(2)}, u32[]{:S(2)}) collective-permute-start(bf16[2,264,640]{2,1,0:T(8,128)(2,1)S(1)} %get-tuple-element.196), channel_id=1, source_target_pairs={{0,64},{8,72},{16,80},{24,88},{32,96},{40,104},{48,112},{56,120},{... | collective-permute-start | bytes 2027528 | tf_op jit(solution)/shard_map/ppermute | solution.py:29
  576.1 29.3 %collective-permute-start.58 = (bf16[2,264,640]{2,1,0:T(8,128)(2,1)S(1)}, bf16[2,264,640]{2,1,0:T(8,128)(2,1)S(1)}, u32[]{:S(2)}, u32[]{:S(2)}) collective-permute-start(bf16[2,264,640]{2,1,0:T(8,128)(2,1)S(1)} %get-tuple-element.194), channel_id=1, source_target_pairs={{0,32},{8,40},{16,48},{24,56},{32,0},{40,8},{48,16},{56,24},{64,96... | collective-permute-start | bytes 2027528 | tf_op jit(solution)/shard_map/ppermute | solution.py:29
  606.9 24.1 %collective-permute-start.64 = (bf16[264,640]{1,0:T(8,128)(2,1)S(1)}, bf16[264,640]{1,0:T(8,128)(2,1)S(1)}, u32[]{:S(2)}, u32[]{:S(2)}) collective-permute-start(bf16[264,640]{1,0:T(8,128)(2,1)S(1)} %get-tuple-element.268), channel_id=1, source_target_pairs={{0,17},{1,19},{2,21},{3,23},{4,16},{5,18},{6,20},{7,22},{8,25},{9,... | collective-permute-start | bytes 1013768 | tf_op jit(solution)/shard_map/ppermute | solution.py:75
  609.9 23.8 %collective-permute-start.62 = (bf16[264,640]{1,0:T(8,128)(2,1)S(1)}, bf16[264,640]{1,0:T(8,128)(2,1)S(1)}, u32[]{:S(2)}, u32[]{:S(2)}) collective-permute-start(bf16[264,640]{1,0:T(8,128)(2,1)S(1)} %get-tuple-element.268), channel_id=1, source_target_pairs={{0,1},{1,3},{2,5},{3,7},{4,0},{5,2},{6,4},{7,6},{8,9},{9,11},{10,1... | collective-permute-start | bytes 1013768 | tf_op jit(solution)/shard_map/ppermute | solution.py:75
  610.9 22.9 %collective-permute-start.63 = (bf16[264,640]{1,0:T(8,128)(2,1)S(1)}, bf16[264,640]{1,0:T(8,128)(2,1)S(1)}, u32[]{:S(2)}, u32[]{:S(2)}) collective-permute-start(bf16[264,640]{1,0:T(8,128)(2,1)S(1)} %get-tuple-element.267), channel_id=1, source_target_pairs={{0,16},{1,18},{2,20},{3,22},{4,17},{5,19},{6,21},{7,23},{8,24},{9,... | collective-permute-start | bytes 1013768 | tf_op jit(solution)/shard_map/ppermute | solution.py:75
  612.2 21.6 %collective-permute-start.61 = (bf16[264,640]{1,0:T(8,128)(2,1)S(1)}, bf16[264,640]{1,0:T(8,128)(2,1)S(1)}, u32[]{:S(2)}, u32[]{:S(2)}) collective-permute-start(bf16[264,640]{1,0:T(8,128)(2,1)S(1)} %get-tuple-element.267), channel_id=1, source_target_pairs={{0,0},{1,2},{2,4},{3,6},{4,1},{5,3},{6,5},{7,7},{8,8},{9,10},{10,1... | collective-permute-start | bytes 1013768 | tf_op jit(solution)/shard_map/ppermute | solution.py:75
  629.9 24.4 %collective-permute-start.54 = (bf16[2,176,640]{2,1,0:T(8,128)(2,1)S(1)}, bf16[2,176,640]{2,1,0:T(8,128)(2,1)S(1)}, u32[]{:S(2)}, u32[]{:S(2)}) collective-permute-start(bf16[2,176,640]{2,1,0:T(8,128)(2,1)S(1)} %bitcast.310), channel_id=1, source_target_pairs={{0,3},{1,2},{2,1},{3,0},{4,7},{5,6},{6,5},{7,4},{8,11},{9,10},{10,... | collective-permute-start | bytes 1351688 | tf_op jit(solution)/shard_map/ppermute | solution.py:29
  631.0 23.3 %collective-permute-start.53 = (bf16[2,176,640]{2,1,0:T(8,128)(2,1)S(1)}, bf16[2,176,640]{2,1,0:T(8,128)(2,1)S(1)}, u32[]{:S(2)}, u32[]{:S(2)}) collective-permute-start(bf16[2,176,640]{2,1,0:T(8,128)(2,1)S(1)} %bitcast.309), channel_id=1, source_target_pairs={{0,2},{1,3},{2,0},{3,1},{4,6},{5,7},{6,4},{7,5},{8,10},{9,11},{10,... | collective-permute-start | bytes 1351688 | tf_op jit(solution)/shard_map/ppermute | solution.py:29
  673.1 104.0 %reduce-scatter.17.cloned.1.call-start = ((), (), s32[]{:S(2)}) async-start(), calls=%async_computation.9 | async-start | bytes 3276800 | tf_op jit(solution)/shard_map/reduce_scatter | solution.py:58
  713.1 24.8 %collective-permute-start.84 = (bf16[2,200,640]{2,1,0:T(8,128)(2,1)S(1)}, bf16[2,200,640]{2,1,0:T(8,128)(2,1)S(1)}, u32[]{:S(2)}, u32[]{:S(2)}) collective-permute-start(bf16[2,200,640]{2,1,0:T(8,128)(2,1)S(1)} %get-tuple-element.198), channel_id=1, source_target_pairs={{0,96},{8,104},{16,112},{24,120},{32,64},{40,72},{48,80},{56,88},{... | collective-permute-start | bytes 1536008 | tf_op jit(solution)/shard_map/ppermute | solution.py:29
  715.6 22.3 %collective-permute-start.83 = (bf16[2,200,640]{2,1,0:T(8,128)(2,1)S(1)}, bf16[2,200,640]{2,1,0:T(8,128)(2,1)S(1)}, u32[]{:S(2)}, u32[]{:S(2)}) collective-permute-start(bf16[2,200,640]{2,1,0:T(8,128)(2,1)S(1)} %get-tuple-element.199), channel_id=1, source_target_pairs={{0,64},{8,72},{16,80},{24,88},{32,96},{40,104},{48,112},{56,120},{... | collective-permute-start | bytes 1536008 | tf_op jit(solution)/shard_map/ppermute | solution.py:29
  716.2 22.2 %collective-permute-start.82 = (bf16[2,200,640]{2,1,0:T(8,128)(2,1)S(1)}, bf16[2,200,640]{2,1,0:T(8,128)(2,1)S(1)}, u32[]{:S(2)}, u32[]{:S(2)}) collective-permute-start(bf16[2,200,640]{2,1,0:T(8,128)(2,1)S(1)} %get-tuple-element.197), channel_id=1, source_target_pairs={{0,32},{8,40},{16,48},{24,56},{32,0},{40,8},{48,16},{56,24},{64,96... | collective-permute-start | bytes 1536008 | tf_op jit(solution)/shard_map/ppermute | solution.py:29
  (212 other events, 1754.0 us)
Sparse Core Ops, SparseCore 0:
  390.4 70.3 reduce-scatter.10
  492.4 33.4 reduce-scatter.12
  528.5 33.6 reduce-scatter.18
  564.6 53.5 reduce-scatter.14
  673.2 36.3 reduce-scatter.20
  712.4 33.6 reduce-scatter.16
